TPU v7x, 32 devices: a whole 2x2x4 slice. The times are simulated.
32 devices in a mesh: dp: 8 (over y, x, core), tensor: 4 (over z).
Axes of the slice: x: 2, y: 2, z: 4, core: 2. Of those that a mesh axis runs over, the one named last changes fastest.
Arguments:
- teacher_rows: bfloat16 [1024, 16384], P('dp', 'tensor'), may hold values from -6 to 6
- row_map: int32 [1024], P('dp'), may hold values from 0 to 1023, as said below
- student_hidden: bfloat16 [1024, 8192], P('dp', 'tensor'), may hold values from -6 to 6
- projected: bfloat16 [1024, 8192], P('dp', 'tensor'), may hold values from -6 to 6
- mlp_input: bfloat16 [1024, 8192], P('dp', 'tensor'), may hold values from -6 to 6
- gate_bucket: bfloat16 [8192, 512], P(None, 'tensor'), may hold values from -0.0625 to 0.0625
- up_bucket: bfloat16 [8192, 512], P(None, 'tensor'), may hold values from -0.0625 to 0.0625
- down_bucket: bfloat16 [512, 8192], P('tensor'), may hold values from -0.03125 to 0.03125
Outputs:
- grad_proj: float32 [128, 4, 4096], P(None, 'tensor', 'dp')
- grad_gate: float32 [512, 8192], P('tensor', 'dp')
- grad_up: float32 [512, 8192], P('tensor', 'dp')
Inputs may be any that keep to these rules, and one draw needn't show every extreme that they name: `row_map`: a permutation of the token ids; token id t belongs to student group t // 128; the rows of one device (aligned blocks of 128) send exactly 16 rows to every student group.
All inputs are finite; a program needn't handle non-finite values.
Results may differ from a plain program's by a relative error of at most 0.0042.
Values may be sent and summed in bfloat16 or wider, within the bound.
No kernel may reach another device: no remote copies, remote signals or barrier semaphores. Data moves between devices by JAX's collectives and lax.ppermute only.
A program may use at most 128 MiB of HBM per device.

v0:
```python
import math

import jax
import jax.numpy as jnp
from jax import lax
from jax.sharding import PartitionSpec as P

PB = 128


def contract_rows(left, right):
    return lax.dot_general(
        left, right, (((0,), (0,)), ((), ())), preferred_element_type=jnp.float32
    )


def body(
    teacher_rows, row_map, student_hidden, projected, mlp_input, gate_bucket, up_bucket, down_bucket
):
    tok_dev = row_map.shape[0]
    dp_count = lax.axis_size("dp")
    factor = 1.0 / math.sqrt(tok_dev * dp_count)
    difference = (student_hidden.astype(jnp.float32) - projected.astype(jnp.float32)) * factor
    err_local = difference.astype(jnp.bfloat16)
    err_full, inputs_full = (
        lax.all_gather(err_local, "tensor", axis=1, tiled=True),
        lax.all_gather(mlp_input, "tensor", axis=1, tiled=True),
    )
    act_grad = lax.dot_general(
        err_full, down_bucket, (((1,), (1,)), ((), ())), preferred_element_type=jnp.float32
    )
    gate_pre = jnp.dot(inputs_full, gate_bucket, preferred_element_type=jnp.float32)
    up_pre = jnp.dot(inputs_full, up_bucket, preferred_element_type=jnp.float32)
    sigmoid_gate = jax.nn.sigmoid(gate_pre)
    gate_grad = (act_grad * up_pre * sigmoid_gate * (1.0 + gate_pre * (1.0 - sigmoid_gate))).astype(
        jnp.bfloat16
    )
    up_grad = (act_grad * gate_pre * sigmoid_gate).astype(jnp.bfloat16)
    inputs_across = jnp.transpose(inputs_full)
    feature_cols = lax.all_to_all(inputs_across, "dp", split_axis=0, concat_axis=1, tiled=True)
    gate_add = lax.dot_general(
        lax.all_gather(gate_grad, "dp", axis=0, tiled=True),
        feature_cols,
        (((0,), (1,)), ((), ())),
        preferred_element_type=jnp.float32,
    )
    up_add = lax.dot_general(
        lax.all_gather(up_grad, "dp", axis=0, tiled=True),
        feature_cols,
        (((0,), (1,)), ((), ())),
        preferred_element_type=jnp.float32,
    )
    target = row_map // tok_dev
    arrangement = jnp.argsort(target, stable=True)
    sorted_rows = jnp.take(teacher_rows, arrangement, axis=0)
    sorted_slots = jnp.take(row_map % tok_dev, arrangement, axis=0)
    bucket_err = err_full[:, :PB]
    got_rows, got_slots = (
        lax.all_to_all(sorted_rows, "dp", split_axis=0, concat_axis=0, tiled=True),
        lax.all_to_all(sorted_slots, "dp", split_axis=0, concat_axis=0, tiled=True),
    )
    placed = jnp.take(got_rows, jnp.argsort(got_slots), axis=0)
    proj_term = contract_rows(bucket_err, placed)
    grad_proj = lax.psum_scatter(proj_term, "dp", scatter_dimension=1, tiled=True)
    return (grad_proj[:, None, :], gate_add, up_add)


def solution(mesh):
    in_specs = (
        P("dp", "tensor"),
        P("dp"),
        P("dp", "tensor"),
        P("dp", "tensor"),
        P("dp", "tensor"),
        P(None, "tensor"),
        P(None, "tensor"),
        P("tensor", None),
    )
    out_specs = (P(None, "tensor", "dp"), P("tensor", "dp"), P("tensor", "dp"))
    return jax.shard_map(body, mesh=mesh, in_specs=in_specs, out_specs=out_specs, check_vma=False)
```

profile of v0, /device:TPU:0, one launch (start us, length us, event | category | flops | bytes accessed | tf_op | source)
XLA Modules:
  0.0 171.1 jit_solution(9949525473633267266)
XLA Ops:
  7.2 2.3 %multiply_convert_fusion = bf16[128,2048]{1,0:T(8,128)(2,1)} fusion(bf16[128,2048]{1,0:T(8,128)(2,1)} %param.13, bf16[128,2048]{1,0:T(8,128)(2,1)} %param.12), kind=kLoop, calls=%fused_computation.9 | loop fusion | flops 1310720 | bytes 1572864 | tf_op jit(solution)/shard_map/convert_element_type | solution.py:24
  9.6 0.0 all-gather.5.cloned.1.call-start
  9.6 2.0 %copy.17 = bf16[128,2048]{0,1:T(8,128)(2,1)} copy(bf16[128,2048]{1,0:T(8,128)(2,1)} %param.14) | data formatting | bytes 1048576 | tf_op args[4]
  11.7 2.5 %sort.34 = (s32[128]{0:T(128)}, s32[128]{0:T(128)S(1)}) sort(s32[128]{0:T(128)S(1)} %get-tuple-element.23, s32[128]{0:T(128)S(1)} %iota.8), dimensions={0}, to_apply=%region_0.1 | sort | flops 896 | bytes 2048 | tf_op jit(solution)/shard_map/jit(argsort)/sort | solution.py:54
  14.3 1.2 gather_fusion
  15.5 0.7 select_n.40
  16.2 5.2 %all-to-all-start.1 = ((s32[8,16,1]{1,2,0:T(1,128)}), s32[8,16,1]{1,2,0:T(1,128)S(1)}, u32[]{:S(2)}, u32[]{:S(2)}) async-start(s32[8,16,1]{1,2,0:T(1,128)} %bitcast), calls=%async_computation.1 | async-start | bytes 8192 | tf_op jit(solution)/shard_map/all_to_all | solution.py:60
  21.4 2.2 %gather_fusion.1 = bf16[128,4096]{1,0:T(8,128)(2,1)} fusion(bf16[128,4096]{1,0:T(8,128)(2,1)S(1)} %copy-done.1, s32[1024]{0:T(1024)S(1)} %pad_clamp_fusion.1), kind=kCustom, calls=%fused_computation.clone | custom fusion | bytes 2097664 | tf_op jit(solution)/shard_map/jit(_take)/gather | solution.py:55
  23.5 2.4 %broadcast_select_fusion = bf16[128,4096]{1,0:T(8,128)(2,1)} fusion(bf16[128,4096]{1,0:T(8,128)(2,1)} %gather_fusion.1, pred[128]{0:T(512)(128)(4,1)S(1)} %get-tuple-element.21), kind=kLoop, calls=%fused_computation.11 | loop fusion | flops 524288 | bytes 2097280 | tf_op jit(solution)/shard_map/jit(_take)/select_n | solution.py:55
  25.9 0.1 all-to-all-done.1
  26.0 4.1 %all-to-all-start = ((bf16[8,16,4096]{2,1,0:T(8,128)(2,1)}), bf16[8,16,4096]{2,1,0:T(8,128)(2,1)S(1)}, u32[]{:S(2)}, u32[]{:S(2)}) async-start(bf16[8,16,4096]{2,1,0:T(8,128)(2,1)} %bitcast.24), calls=%async_computation | async-start | bytes 2097152 | tf_op jit(solution)/shard_map/all_to_all | solution.py:59
  30.1 0.5 broadcast.65
  30.7 0.7 reduce.3
  31.3 0.1 all_to_all.32
  31.4 2.5 %sort.35 = (s32[128]{0:T(128)}, s32[128]{0:T(128)S(1)}) sort(s32[128]{0:T(128)S(1)} %all_to_all.32, s32[128]{0:T(128)S(1)} %iota.9), dimensions={0}, to_apply=%region_1.3 | sort | flops 896 | bytes 2048 | tf_op jit(solution)/shard_map/jit(argsort)/sort | solution.py:62
  34.0 11.5 %all-to-all-done = bf16[8,16,4096]{2,1,0:T(8,128)(2,1)S(1)} async-done(((bf16[8,16,4096]{2,1,0:T(8,128)(2,1)}), bf16[8,16,4096]{2,1,0:T(8,128)(2,1)S(1)}, u32[]{:S(2)}, u32[]{:S(2)}) %all-to-all-start) | async-done | bytes 1048608 | tf_op jit(solution)/shard_map/all_to_all | solution.py:59
  45.5 2.2 %gather_fusion.2 = bf16[128,4096]{1,0:T(8,128)(2,1)} fusion(bf16[128,4096]{1,0:T(8,128)(2,1)S(1)} %bitcast.20, s32[1024]{0:T(1024)S(1)} %pad_clamp_fusion), kind=kCustom, calls=%fused_computation.1.clone | custom fusion | bytes 2097664 | tf_op jit(solution)/shard_map/jit(_take)/gather | solution.py:62
  47.7 11.1 %all-gather.3.cloned.1.call-done = bf16[128,8192]{1,0:T(8,128)(2,1)} async-done(((bf16[128,2048]{1,0:T(8,128)(2,1)}), bf16[128,8192]{1,0:T(8,128)(2,1)}) %all-gather.3.cloned.1.call-update) | async-done | bytes 2097168 | tf_op jit(solution)/shard_map/all_gather | solution.py:26
  58.9 3.1 %fusion.3 = f32[128,4096]{1,0:T(8,128)} fusion(bf16[128,4096]{1,0:T(8,128)(2,1)} %gather_fusion.2, pred[128]{0:T(512)(128)(4,1)S(1)} %compare_and_fusion, bf16[128,8192]{1,0:T(8,128)(2,1)} %all-gather.3.cloned.1.call-done), kind=kOutput, calls=%fused_computation.7 | convolution fusion | flops 134742016 | bytes 3178624 | tf_op jit(solution)/shard_map/dot_general | solution.py:12
  61.9 43.8 %all-gather.5.cloned.1.call-done = bf16[128,8192]{0,1:T(8,128)(2,1)} async-done(((bf16[128,2048]{0,1:T(8,128)(2,1)}), bf16[128,8192]{0,1:T(8,128)(2,1)}) %all-gather.5.cloned.1.call-update) | async-done | bytes 2097168 | tf_op jit(solution)/shard_map/all_gather | solution.py:27
  105.7 4.4 %all-to-all-start.2 = ((bf16[8,1024,128]{2,1,0:T(8,128)(2,1)}), bf16[8,1024,128]{2,1,0:T(8,128)(2,1)}, u32[]{:S(2)}, u32[]{:S(2)}) async-start(bf16[8,1024,128]{2,1,0:T(8,128)(2,1)} %bitcast.21), calls=%async_computation.3 | async-start | bytes 4194304 | tf_op jit(solution)/shard_map/all_to_all | solution.py:40
  110.0 3.1 %fusion.9 = f32[128,128]{1,0:T(8,128)S(1)} fusion(bf16[128,8192]{0,1:T(8,128)(2,1)} %all-gather.5.cloned.1.call-done, bf16[8192,128]{1,0:T(8,128)(2,1)} %param.15), kind=kOutput, calls=%fused_computation.29 | convolution fusion | flops 268435456 | bytes 4259840 | tf_op jit(solution)/shard_map/dot_general | solution.py:32
  113.2 0.7 multiply_convert_fusion.1
  113.9 0.9 copy-done.2
  114.8 0.8 copy-done.5
  115.6 0.8 fusion.2
  116.3 29.4 %all_gather.14 = bf16[1024,128]{1,0:T(8,128)(2,1)S(1)} all-gather(bf16[128,128]{1,0:T(8,128)(2,1)S(1)} %fusion.2), channel_id=1, replica_groups=mesh['dp'=8,'tensor'=4] {'dp'}, dimensions={0}, use_global_device_ids=true | all-gather | bytes 294912 | tf_op jit(solution)/shard_map/all_gather | solution.py:42
  145.7 8.7 %all_gather.15 = bf16[1024,128]{1,0:T(8,128)(2,1)S(1)} all-gather(bf16[128,128]{1,0:T(8,128)(2,1)S(1)} %get-tuple-element.24), channel_id=1, replica_groups=mesh['dp'=8,'tensor'=4] {'dp'}, dimensions={0}, use_global_device_ids=true | all-gather | bytes 294912 | tf_op jit(solution)/shard_map/all_gather | solution.py:48
  154.4 3.9 %copy.18 = bf16[1024,8,128]{0,2,1:T(8,128)(2,1)} copy(bf16[1024,8,128]{2,0,1:T(8,128)(2,1)} %bitcast.6) | data formatting | bytes 4194304 | tf_op jit(solution)/shard_map/all_to_all | solution.py:40
  158.3 3.0 %fusion.10 = f32[128,1024]{1,0:T(8,128)} fusion(bf16[1024,128]{1,0:T(8,128)(2,1)S(1)} %all_gather.14, bf16[1024,1024]{0,1:T(8,128)(2,1)} %bitcast.22), kind=kOutput, calls=%fused_computation.30 | convolution fusion | flops 268435456 | bytes 2883584 | tf_op jit(solution)/shard_map/dot_general | solution.py:41
  161.4 1.3 fusion.11
  162.6 1.9 %copy.19 = f32[128,1,512]{2,1,0:T(1,128)} copy(f32[128,1,512]{2,0,1:T(8,128)} %bitcast.25) | data formatting | bytes 524288
  (28 shorter events, 0.2 us)
Async XLA Ops:
  7.2 106.0 %copy-start = (bf16[128,8192]{1,0:T(8,128)(2,1)S(1)}, bf16[128,8192]{1,0:T(8,128)(2,1)}, u32[]{:S(2)}) copy-start(bf16[128,8192]{1,0:T(8,128)(2,1)} %param.17) | copy-start | bytes 6291460
  7.2 4.5 %copy-start.6 = (s32[128]{0:T(128)S(1)}, s32[128]{0:T(128)}, u32[]{:S(2)}) copy-start(s32[128]{0:T(128)} %param.11) | copy-start | bytes 1540
  7.2 14.2 %copy-start.1 = (bf16[128,4096]{1,0:T(8,128)(2,1)S(1)}, bf16[128,4096]{1,0:T(8,128)(2,1)}, u32[]{:S(2)}) copy-start(bf16[128,4096]{1,0:T(8,128)(2,1)} %param.10) | copy-start | bytes 3145732
  7.2 51.7 %all-gather.3.cloned.1.call-start = ((), (), s32[]{:S(2)}) async-start(), calls=%async_computation.4 | async-start | bytes 2621440 | tf_op jit(solution)/shard_map/all_gather | solution.py:26
  9.6 96.1 %all-gather.5.cloned.1.call-start = ((), (), s32[]{:S(2)}) async-start(), calls=%async_computation.6 | async-start | bytes 2621440 | tf_op jit(solution)/shard_map/all_gather | solution.py:27
  16.2 9.8 %all-to-all-start.1 = ((s32[8,16,1]{1,2,0:T(1,128)}), s32[8,16,1]{1,2,0:T(1,128)S(1)}, u32[]{:S(2)}, u32[]{:S(2)}) async-start(s32[8,16,1]{1,2,0:T(1,128)} %bitcast), calls=%async_computation.1 | async-start | bytes 8192 | tf_op jit(solution)/shard_map/all_to_all | solution.py:60
  26.0 19.6 %all-to-all-start = ((bf16[8,16,4096]{2,1,0:T(8,128)(2,1)}), bf16[8,16,4096]{2,1,0:T(8,128)(2,1)S(1)}, u32[]{:S(2)}, u32[]{:S(2)}) async-start(bf16[8,16,4096]{2,1,0:T(8,128)(2,1)} %bitcast.24), calls=%async_computation | async-start | bytes 2097152 | tf_op jit(solution)/shard_map/all_to_all | solution.py:59
  30.1 132.5 %reduce-scatter.2.cloned.1.call-start = ((), (), s32[]{:S(2)}) async-start(), calls=%async_computation.5 | async-start | bytes 2359296 | tf_op jit(solution)/shard_map/reduce_scatter | solution.py:64
  105.7 48.8 %all-to-all-start.2 = ((bf16[8,1024,128]{2,1,0:T(8,128)(2,1)}), bf16[8,1024,128]{2,1,0:T(8,128)(2,1)}, u32[]{:S(2)}, u32[]{:S(2)}) async-start(bf16[8,1024,128]{2,1,0:T(8,128)(2,1)} %bitcast.21), calls=%async_computation.3 | async-start | bytes 4194304 | tf_op jit(solution)/shard_map/all_to_all | solution.py:40
  110.0 3.1 %copy-start.4 = (bf16[128,8192]{1,0:T(8,128)(2,1)S(1)}, bf16[128,8192]{1,0:T(8,128)(2,1)}, u32[]{:S(2)}) copy-start(bf16[128,8192]{1,0:T(8,128)(2,1)} %all-gather.3.cloned.1.call-done) | copy-start | bytes 6291460
  113.2 1.6 copy-start.2
  113.2 2.4 %copy-start.5 = (bf16[8192,128]{1,0:T(8,128)(2,1)S(1)}, bf16[8192,128]{1,0:T(8,128)(2,1)}, u32[]{:S(2)}) copy-start(bf16[8192,128]{1,0:T(8,128)(2,1)} %param.16) | copy-start | bytes 6291460
  158.3 3.0 %copy-start.3 = (bf16[1024,8,128]{0,2,1:T(8,128)(2,1)S(1)}, bf16[1024,8,128]{0,2,1:T(8,128)(2,1)}, u32[]{:S(2)}) copy-start(bf16[1024,8,128]{0,2,1:T(8,128)(2,1)} %copy.18) | copy-start | bytes 6291460
Sparse Core Ops, SparseCore 0:
  10.2 48.6 all-gather.2
  61.0 44.6 all-gather.4
  109.0 43.8 reduce-scatter.1
where the time goes:
time: 172 us; the launch traced here: 171 us
  waiting for transfers between devices  66.5 us (39%)
  blocking collectives  38.1 us (22%)
  local copies, waits for them, and re-layouts  16.4 us (10%)
  between operations  13.9 us (8%)
  starting transfers between devices  13.8 us (8%)
  matrix products  11.9 us (7%)
  other arithmetic  10.4 us (6%)
    all_gather x1, waiting for transfers between devices, body(): lax.all_gather(mlp_input, 'tensor', axis=1, tiled=True)  43.8 us
    all_gather x1, blocking collectives, body(): lax.all_gather(gate_grad, 'dp', axis=0, tiled=True)  29.4 us
    all_to_all x1, waiting for transfers between devices, body(): lax.all_to_all(sorted_rows, 'dp', split_axis=0, concat_axis=0, tiled=True)  11.5 us
    all_gather x1, waiting for transfers between devices, body(): lax.all_gather(err_local, 'tensor', axis=1, tiled=True)  11.1 us
    all_gather x1, blocking collectives, body(): lax.all_gather(up_grad, 'dp', axis=0, tiled=True)  8.73 us
    unnamed x16, local copies, waits for them, and re-layouts  5.64 us
    all_to_all x1, starting transfers between devices, body(): lax.all_to_all(sorted_slots, 'dp', split_axis=0, concat_axis=0, tiled=True)  5.17 us
    all_to_all x1, starting transfers between devices, body(): lax.all_to_all(inputs_across, 'dp', split_axis=0, concat_axis=1, tiled=True)  4.35 us
  transfers between devices with their start and end apart: 6, of which 4 were waited for; matrix products, arithmetic and copies ran while one was open for 19% of the time, Pallas kernels for 0%

commit v1 on v0

v1 whole, which is shorter than its diff:
```python
import math

import jax
import jax.numpy as jnp
from jax import lax
from jax.experimental import pallas as pl
from jax.experimental.pallas import tpu as pltpu
from jax.sharding import PartitionSpec as P

PB = 128
LANES = 128
GROUP = 8
FIRST = 96
MIB = 1 << 20

VMEM = pl.BlockSpec(memory_space=pltpu.VMEM)


def params(mib):
    return pltpu.CompilerParams(vmem_limit_bytes=mib * MIB)


def cost(flops, nbytes):
    return pl.CostEstimate(flops=int(flops), bytes_accessed=int(nbytes), transcendentals=0)


def struct(shape, dtype=jnp.bfloat16):
    return jax.ShapeDtypeStruct(shape, dtype)


def shift(x, count, by):
    return lax.ppermute(x, "tensor", [(i, (i + by) % count) for i in range(count)])


def swap(x, count, mask):
    return lax.ppermute(x, "dp", [(i, i ^ mask) for i in range(count)])


def contract_rows(left, right):
    return lax.dot_general(
        left, right, (((0,), (0,)), ((), ())), preferred_element_type=jnp.float32
    )


def contract_cols(left, right):
    return lax.dot_general(
        left, right, (((1,), (1,)), ((), ())), preferred_element_type=jnp.float32
    )


def scaled_difference(student, projected, factor):
    wide = student.astype(jnp.float32) - projected.astype(jnp.float32)
    return (wide * factor).astype(jnp.bfloat16)


def prepare(row_map, teacher, mlp_input, student, projected, down, n_dp, n_t, rows, factor):
    tok, width = mlp_input.shape
    wide = teacher.shape[1] // n_dp
    second = tok - FIRST
    hbm = pl.BlockSpec(memory_space=pltpu.HBM)
    if wide % LANES:
        blocks = teacher.reshape(tok, n_dp, wide).transpose(1, 0, 2)
        wide = 0

    def kernel(m_ref, t_ref, x_ref, s_ref, p_ref, d_ref, one_ref, two_ref, *refs):
        pieces, outs, (s_buf, p_buf, m_buf, sems) = refs[:n_t], refs[n_t:-4], refs[-4:]
        row = pl.multiple_of((lax.axis_index("dp") % GROUP) * rows, rows)
        pairs = [
            (s_ref.at[:, :PB], s_buf),
            (p_ref.at[:, :PB], p_buf),
            (m_ref, m_buf),
            (x_ref.at[:FIRST], one_ref.at[:, :width]),
            (x_ref.at[FIRST:], two_ref),
        ]
        for k in range(n_t):
            col = pl.multiple_of(((lax.axis_index("tensor") + k) % n_t) * width, width)
            pairs.append((d_ref.at[pl.ds(row, rows), pl.ds(col, width)], pieces[k]))
        if wide:
            for i in range(n_dp):
                pairs.append((t_ref.at[:, i * wide : (i + 1) * wide], outs[0].at[i]))
        copies = [
            pltpu.make_async_copy(src, dst, sems.at[i]) for i, (src, dst) in enumerate(pairs)
        ]
        for c in copies:
            c.start()
        for c in copies[:3]:
            c.wait()
        bucket = scaled_difference(s_buf[...], p_buf[...], factor)
        one_ref[:, width : width + PB] = bucket[:FIRST]
        one_ref[:second, width + PB :] = bucket[FIRST:]
        one_ref[second + 16 :, width + PB :] = jnp.zeros((FIRST - second - 16, PB), jnp.bfloat16)
        line = lax.broadcasted_iota(jnp.int32, (16, tok), 0)
        number = jnp.broadcast_to(m_buf[...], (16, tok))
        high, low = number // LANES, number % LANES
        digits = jnp.where(line == 0, high, jnp.where(line == 1, low, 0))
        one_ref[second : second + 16, width + PB :] = digits.astype(jnp.float32).astype(jnp.bfloat16)
        for c in copies[3:]:
            c.wait()

    shapes = [(FIRST, width + 2 * PB), (second, width)] + [(rows, width)] * n_t
    if wide:
        shapes.append((n_dp, tok, wide))
    count = 5 + n_t + n_dp
    out = pl.pallas_call(
        kernel,
        in_specs=[hbm] * 6,
        out_specs=[VMEM] * len(shapes),
        out_shape=[struct(s) for s in shapes],
        scratch_shapes=[
            pltpu.VMEM((tok, PB), jnp.bfloat16),
            pltpu.VMEM((tok, PB), jnp.bfloat16),
            pltpu.VMEM((1, tok), jnp.int32),
            pltpu.SemaphoreType.DMA((count,)),
        ],
        compiler_params=params(60),
        cost_estimate=cost(0, 1024),
        name="prepare",
    )(row_map.reshape(1, tok), teacher, mlp_input, student, projected, down)
    return out if wide else [*out, blocks]


def stack_rows(parts, after=()):
    height = [p.shape[0] for p in parts]

    def kernel(*refs):
        out_ref, at = refs[-1], 0
        for ref, h in zip(refs, height):
            out_ref[at : at + h] = ref[...]
            at += h

    return pl.pallas_call(
        kernel,
        in_specs=[VMEM] * len(parts) + [pl.BlockSpec(memory_space=pl.ANY)] * len(after),
        out_specs=VMEM,
        out_shape=struct((sum(height),) + parts[0].shape[1:]),
        compiler_params=params(16),
        cost_estimate=cost(0, 1024),
        name="stack_rows",
    )(*parts, *after)


def join(gate, up, student, projected, factor, after):
    def kernel(gate_ref, up_ref, s_ref, p_ref, *refs):
        w_ref, err_ref = refs[len(after) :]
        hb = gate_ref.shape[1]
        w_ref[:, :hb] = gate_ref[...]
        w_ref[:, hb:] = up_ref[...]
        err_ref[...] = scaled_difference(s_ref[...], p_ref[...], factor)

    return pl.pallas_call(
        kernel,
        in_specs=[VMEM] * 4 + [pl.BlockSpec(memory_space=pl.ANY)] * len(after),
        out_specs=[VMEM] * 2,
        out_shape=[struct((gate.shape[0], 2 * gate.shape[1])), struct(student.shape)],
        compiler_params=params(24),
        cost_estimate=cost(0, 1024),
        name="join",
    )(gate, up, student, projected, *after)


def ordered(x, *after):
    def kernel(*refs):
        pass

    return pl.pallas_call(
        kernel,
        in_specs=[pl.BlockSpec(memory_space=pl.ANY)] * (1 + len(after)),
        out_specs=pl.BlockSpec(memory_space=pl.ANY),
        out_shape=struct(x.shape, x.dtype),
        input_output_aliases={0: 0},
        cost_estimate=cost(0, 1024),
        name="ordered",
    )(x, *after)


def partial_products(near, far, err, n_t, rows, after):
    tok, width = err.shape
    hb = rows * GROUP
    half = GROUP // 2

    def kernel(near_ref, far_ref, e_ref, *refs):
        outs = refs[len(after) :]
        place = lax.axis_index("dp") % GROUP
        for side, ref in enumerate((near_ref, far_ref)):
            product = contract_cols(ref[...], e_ref[...])
            for j in range(half):
                row = pl.multiple_of((place ^ (2 * j + side)) * rows, rows)
                for k in range(n_t):
                    at = (j * n_t + k) * rows
                    outs[k][pl.ds(row, rows), :] = product[at : at + rows]

    return pl.pallas_call(
        kernel,
        in_specs=[VMEM] * 3
        + [pl.BlockSpec(memory_space=pl.ANY)] * len(after),
        out_specs=[VMEM] * n_t,
        out_shape=[struct((hb, tok), jnp.float32)] * n_t,
        compiler_params=params(16),
        cost_estimate=cost(0, 1024),
        name="partial_products",
    )(near, far, err, *after)


def features(slices, weights, n_dp, rest=None, after=()):
    n_t = len(slices)
    count, width = slices[0].shape[0], weights.shape[0] // n_t
    hb = weights.shape[1] // 2
    cols = width * n_t // n_dp
    per = width // cols
    if rest is None:
        base = 2 * PB
        others = []
    else:
        pre, acts = rest
        tok = pre.shape[0] + count
        base = (tok // count) * 2 * hb
        others = [pre, *acts]

    def kernel(*refs):
        xs, refs = refs[:n_t], refs[n_t:]
        w_ref, refs = refs[0], refs[1:]
        if rest is None:
            out_ref, pre_ref, bucket_ref = refs[len(after) :]
        else:
            pre_ref, act_refs, out_ref = refs[0], refs[1 : 1 + n_t], refs[-1]
        pre = jnp.zeros((count, 2 * hb), jnp.float32)
        for k in range(n_t):
            slot = (lax.axis_index("tensor") + n_t - k) % n_t
            at = pl.ds(pl.multiple_of(slot * width, width), width)
            x = xs[k][:, :width]
            pre += jnp.dot(x, w_ref[at, :], preferred_element_type=jnp.float32)
            for b in range(per):
                out_ref[slot * per + b, :, base:] = xs[k][:, b * cols : (b + 1) * cols]
            if rest is None:

                @pl.when(slot == 0)
                def _(k=k):
                    bucket_ref[...] = xs[k][:, width:]

        if rest is None:
            pre_ref[...] = pre
            for i in range(n_dp):
                out_ref[i, :, :base] = bucket_ref[...]
            return
        act = act_refs[0][...]
        for ref in act_refs[1:]:
            act += ref[...]
        act = act.T
        pre = jnp.concatenate([pre_ref[...], pre])
        gate_pre, up_pre = pre[:, :hb], pre[:, hb:]
        s = jax.nn.sigmoid(gate_pre)
        gate_grad = (act * up_pre * s * (1.0 + gate_pre * (1.0 - s))).astype(jnp.bfloat16)
        up_grad = (act * gate_pre * s).astype(jnp.bfloat16)
        for b in range(tok // count):
            for j, grad in enumerate((gate_grad, up_grad)):
                part = grad[b * count : (b + 1) * count]
                for i in range(n_dp):
                    out_ref[i, :, (2 * b + j) * hb : (2 * b + j + 1) * hb] = part

    payload = struct((n_dp, count, base + cols))
    first = rest is None
    return pl.pallas_call(
        kernel,
        in_specs=[VMEM] * (n_t + 1 + len(others)) + [pl.BlockSpec(memory_space=pl.ANY)] * len(after),
        out_specs=[VMEM, VMEM] if first else VMEM,
        out_shape=[payload, struct((count, 2 * hb), jnp.float32)] if first else payload,
        scratch_shapes=[pltpu.VMEM((count, 2 * PB), jnp.bfloat16)] if first else [],
        compiler_params=params(24),
        cost_estimate=cost(0, 1024),
        name="first_features" if first else "last_features",
    )(*slices, weights, *others, *after)


def projector(came, teach):
    n_dp, tok, wide = teach.shape
    second = tok - FIRST
    groups = n_dp // GROUP
    span = GROUP * tok

    def kernel(came_ref, teach_ref, out_ref, flipped_ref):
        def flip(g, carry):
            parts = []
            for i in range(GROUP):
                parts.append(came_ref[g * GROUP + i, :, :PB])
                parts.append(came_ref[g * GROUP + i, :second, PB : 2 * PB])
            flipped_ref[g] = jnp.concatenate(parts).astype(jnp.float32).T.astype(jnp.bfloat16)
            return carry

        lax.fori_loop(0, groups, flip, 0)
        out_ref[...] = jnp.zeros_like(out_ref)

        def sender(g, carry):
            digits = came_ref[g, second : second + 16, PB : 2 * PB].astype(jnp.float32)
            number = (digits[0:1] * float(LANES) + digits[1:2]).astype(jnp.int32)

            def block(h, total):
                token = lax.broadcasted_iota(jnp.int32, (span, tok), 0) + h * span
                picks = (token == number).astype(jnp.float32).astype(jnp.bfloat16)
                return total + jnp.dot(flipped_ref[h], picks, preferred_element_type=jnp.float32)

            rows = lax.fori_loop(0, groups, block, jnp.zeros((PB, tok), jnp.float32))
            out_ref[...] += jnp.dot(
                rows.astype(jnp.bfloat16), teach_ref[g], preferred_element_type=jnp.float32
            )
            return carry

        lax.fori_loop(0, n_dp, sender, 0)

    return pl.pallas_call(
        kernel,
        in_specs=[VMEM, VMEM],
        out_specs=VMEM,
        out_shape=struct((PB, wide), jnp.float32),
        scratch_shapes=[pltpu.VMEM((groups, PB, span), jnp.bfloat16)],
        compiler_params=params(24),
        cost_estimate=cost(0, 1024),
        name="projector",
    )(came, teach)


def final_product(first, last, hb, cols):
    n_dp, count = last.shape[:2]
    blocks = (last.shape[2] - cols) // (2 * hb)

    def kernel(first_ref, last_ref, gate_ref, up_ref):
        def group(g, total):
            here = pl.ds(g * GROUP, GROUP)
            for b in range(blocks):
                grads = last_ref[here, :, 2 * b * hb : 2 * (b + 1) * hb]
                if b < blocks - 1:
                    feats = first_ref[here, b * count : (b + 1) * count, 2 * PB :]
                else:
                    feats = last_ref[here, :, 2 * blocks * hb :]
                total = total + contract_rows(
                    grads.reshape(GROUP * count, 2 * hb), feats.reshape(GROUP * count, cols)
                )
            return total

        total = jnp.zeros((2 * hb, cols), jnp.float32)
        if n_dp == GROUP:
            total = group(0, total)
        else:
            total = lax.fori_loop(0, n_dp // GROUP, group, total)
        gate_ref[...] = total[:hb]
        up_ref[...] = total[hb:]

    return pl.pallas_call(
        kernel,
        in_specs=[VMEM] * 2,
        out_specs=[VMEM] * 2,
        out_shape=[struct((hb, cols), jnp.float32)] * 2,
        compiler_params=params(24),
        cost_estimate=cost(0, 1024),
        name="final_product",
    )(first, last)


def body(
    teacher_rows, row_map, student_hidden, projected, mlp_input, gate_bucket, up_bucket, down_bucket
):
    tok = row_map.shape[0]
    n_dp = lax.axis_size("dp")
    n_t = lax.axis_size("tensor")
    hb, width = down_bucket.shape[0], student_hidden.shape[1]
    cols = width * n_t // n_dp
    factor = 1.0 / math.sqrt(tok * n_dp)
    rows = hb // GROUP

    one, two, *pieces, teach = prepare(
        row_map, teacher_rows, mlp_input, student_hidden, projected, down_bucket,
        n_dp, n_t, rows, factor,
    )
    teach = lax.all_to_all(teach, "dp", split_axis=0, concat_axis=0, tiled=True)

    pieces = [pieces[0]] + [shift(pieces[k], n_t, k) for k in range(1, n_t)]
    before, beyond = shift(one, n_t, 1), shift(one, n_t, -1)
    mine = stack_rows(pieces)
    weights, err = join(gate_bucket, up_bucket, student_hidden, projected, factor, after=[mine])
    before = ordered(before, mine, weights)
    first = [one, before, shift(before, n_t, 1), beyond]
    others = [swap(mine, n_dp, mask) for mask in (2, 4, 6)]
    near = stack_rows([mine] + others)
    far = swap(near, n_dp, 1)
    before, beyond = shift(two, n_t, 1), shift(two, n_t, -1)
    second = [two, before, shift(before, n_t, 1), beyond]

    sent, pre = features(first, weights, n_dp, after=[near])
    came_first = lax.all_to_all(sent, "dp", split_axis=0, concat_axis=0, tiled=True)

    partial = partial_products(near, far, err, n_t, rows, after=[pre, before, beyond, teach])
    acts = [partial[0]] + [shift(partial[k], n_t, -k) for k in range(1, n_t)]

    sent = features(second, weights, n_dp, rest=(pre, acts))
    came_last = lax.all_to_all(sent, "dp", split_axis=0, concat_axis=0, tiled=True)
    grad_proj = projector(came_first, teach)
    grad_gate, grad_up = final_product(came_first, came_last, hb, cols)
    return (grad_proj[:, None, :], grad_gate, grad_up)


def solution(mesh):
    in_specs = (
        P("dp", "tensor"),
        P("dp"),
        P("dp", "tensor"),
        P("dp", "tensor"),
        P("dp", "tensor"),
        P(None, "tensor"),
        P(None, "tensor"),
        P("tensor", None),
    )
    out_specs = (P(None, "tensor", "dp"), P("tensor", "dp"), P("tensor", "dp"))
    return jax.shard_map(body, mesh=mesh, in_specs=in_specs, out_specs=out_specs, check_vma=False)
```

time: 172 us -> 123 us (0.72)
  blocking collectives: 38.1 us -> 0 us
  starting transfers between devices: 13.8 us -> 44.5 us
  waiting for transfers between devices: 66.5 us -> 43.3 us
  Pallas kernels: 0 us -> 13.9 us
  between operations: 13.9 us -> 0.83 us
  matrix products: 11.9 us -> 0 us
  other arithmetic: 10.4 us -> 0 us
  local copies, waits for them, and re-layouts: 16.4 us -> 19.6 us
    all_gather x2 -> x0, waiting for transfers between devices: 54.9 us -> none  [the longest x1 43.8 us: body(): lax.all_gather(mlp_input, 'tensor', axis=1, tiled=True)]
    all_gather x2 -> x0, blocking collectives: 38.1 us -> none  [the longest x1 29.4 us: body(): lax.all_gather(gate_grad, 'dp', axis=0, tiled=True)]
    ppermute x0 -> x16, waiting for transfers between devices: none -> 31.9 us  [the longest x12 21.2 us: shift(): lax.ppermute(x, 'tensor', [(i, (i + by) % count) for i in range(count)])]
    ppermute x0 -> x16, starting transfers between devices: none -> 31.2 us  [the longest x12 27.3 us: shift(): lax.ppermute(x, 'tensor', [(i, (i + by) % count) for i in range(count)])]
    unnamed x16 -> x45, local copies, waits for them, and re-layouts: 5.64 us -> 19.6 us
    pallas_call x0 -> x10, Pallas kernels: none -> 13.9 us  [the longest x2 3.47 us: features(): pl.pallas_call(kernel, in_specs=[VMEM] * (n_t + 1 + len(others)) + [pl.Bl...]
    dot_general x6 -> x0, matrix products: 11.9 us -> none  [the longest x1 3.12 us: body(): jnp.dot(inputs_full, gate_bucket, preferred_element_type=jnp.float32)]
    gather x3 -> x0, local copies, waits for them, and re-layouts: 5.58 us -> none  [the longest x1 2.19 us: body(): placed = jnp.take(got_rows, jnp.argsort(got_slots), axis=0)]
  transfers between devices with their start and end apart: 6 -> 19, of which waited for: 4 -> 9; matrix products, arithmetic and copies ran while one was open for 19% -> 1% of each run, Pallas kernels for 0% -> 7%
where the time goes in v1:
time: 123 us; the launch traced here: 122 us
  starting transfers between devices  44.5 us (36%)
  waiting for transfers between devices  43.3 us (35%)
  local copies, waits for them, and re-layouts  19.6 us (16%)
  Pallas kernels  13.9 us (11%)
    ppermute x12, starting transfers between devices, shift(): lax.ppermute(x, 'tensor', [(i, (i + by) % count) for i in range(count)])  27.3 us
    ppermute x12, waiting for transfers between devices, shift(): lax.ppermute(x, 'tensor', [(i, (i + by) % count) for i in range(count)])  21.2 us
    unnamed x45, local copies, waits for them, and re-layouts  19.6 us
    all_to_all x2, waiting for transfers between devices, body(): lax.all_to_all(sent, 'dp', split_axis=0, concat_axis=0, tiled=True)  11.5 us
    ppermute x4, waiting for transfers between devices, swap(): return lax.ppermute(x, 'dp', [(i, i ^ mask) for i in range(count)])  10.6 us
    all_to_all x2, starting transfers between devices, body(): lax.all_to_all(sent, 'dp', split_axis=0, concat_axis=0, tiled=True)  7.97 us
    all_to_all x1, starting transfers between devices, body(): teach = lax.all_to_all(teach, 'dp', split_axis=0, concat_axis=0, tiled=True)  5.31 us
    ppermute x4, starting transfers between devices, swap(): return lax.ppermute(x, 'dp', [(i, i ^ mask) for i in range(count)])  3.89 us
  transfers between devices with their start and end apart: 19, of which 9 were waited for; matrix products, arithmetic and copies ran while one was open for 1% of the time, Pallas kernels for 7%

profile of v1, /device:TPU:0, one launch (start us, length us, event | category | flops | bytes accessed | tf_op | source)
XLA Modules:
  0.0 122.1 jit_solution(14394128297189922205)
XLA Ops:
  0.6 2.9 %prepare.1 = (bf16[96,2304]{1,0:T(8,128)(2,1)}, bf16[32,2048]{1,0:T(8,128)(2,1)}, bf16[16,2048]{1,0:T(8,128)(2,1)}, bf16[16,2048]{1,0:T(8,128)(2,1)}, bf16[16,20...) custom-call(s32[1,128]{1,0:T(1,128)} %bitcast.3, bf16[128,4096]{1,0:T(8,128)(2,1)} %t_ref.1, ...), custom_call_target="tpu_custom_call" | custom-call | bytes 1024 | tf_op jit(solution)/shard_map/prepare/pallas_call | solution.py:104
  3.6 5.3 %all-to-all-start.1 = ((bf16[8,128,512]{2,1,0:T(8,128)(2,1)}), bf16[8,128,512]{2,1,0:T(8,128)(2,1)S(1)}, u32[]{:S(2)}, u32[]{:S(2)}) async-start(bf16[8,128,512]{2,1,0:T(8,128)(2,1)} %get-tuple-element.27), calls=%async_computation.1 | async-start | bytes 2097152 | tf_op jit(solution)/shard_map/all_to_all | solution.py:373
  8.9 1.6 %collective-permute-start = (bf16[96,2304]{1,0:T(8,128)(2,1)}, bf16[96,2304]{1,0:T(8,128)(2,1)S(1)}, u32[]{:S(2)}, u32[]{:S(2)}) collective-permute-start(bf16[96,2304]{1,0:T(8,128)(2,1)} %get-tuple-element.20.refs_0_), channel_id=1, source_target_pairs={{0,1},{1,2},{2,3},{3,0},{4,5},{5,6},{6,7},{7,4},{8,9},{9,10},{10,1... | collective-permute-start | bytes 1327112 | tf_op jit(solution)/shard_map/ppermute | solution.py:32
  10.5 1.6 %collective-permute-start.1 = (bf16[16,2048]{1,0:T(8,128)(2,1)}, bf16[16,2048]{1,0:T(8,128)(2,1)S(1)}, u32[]{:S(2)}, u32[]{:S(2)}) collective-permute-start(bf16[16,2048]{1,0:T(8,128)(2,1)} %get-tuple-element.22), channel_id=1, source_target_pairs={{0,1},{1,2},{2,3},{3,0},{4,5},{5,6},{6,7},{7,4},{8,9},{9,10},{10,1... | collective-permute-start | bytes 196616 | tf_op jit(solution)/shard_map/ppermute | solution.py:32
  12.0 1.2 %collective-permute-start.2 = (bf16[16,2048]{1,0:T(8,128)(2,1)}, bf16[16,2048]{1,0:T(8,128)(2,1)S(1)}, u32[]{:S(2)}, u32[]{:S(2)}) collective-permute-start(bf16[16,2048]{1,0:T(8,128)(2,1)} %get-tuple-element.23), channel_id=1, source_target_pairs={{0,2},{1,3},{2,0},{3,1},{4,6},{5,7},{6,4},{7,5},{8,10},{9,11},{10,... | collective-permute-start | bytes 196616 | tf_op jit(solution)/shard_map/ppermute | solution.py:32
  13.3 2.7 %collective-permute-start.3 = (bf16[16,2048]{1,0:T(8,128)(2,1)}, bf16[16,2048]{1,0:T(8,128)(2,1)S(1)}, u32[]{:S(2)}, u32[]{:S(2)}) collective-permute-start(bf16[16,2048]{1,0:T(8,128)(2,1)} %get-tuple-element.24), channel_id=1, source_target_pairs={{0,3},{1,0},{2,1},{3,2},{4,7},{5,4},{6,5},{7,6},{8,11},{9,8},{10,9... | collective-permute-start | bytes 196616 | tf_op jit(solution)/shard_map/ppermute | solution.py:32
  16.4 9.0 %collective-permute-done.1.refs_1_ = bf16[16,2048]{1,0:T(8,128)(2,1)S(1)} collective-permute-done((bf16[16,2048]{1,0:T(8,128)(2,1)}, bf16[16,2048]{1,0:T(8,128)(2,1)S(1)}, u32[]{:S(2)}, u32[]{:S(2)}) %collective-permute-start.1) | collective-permute-done | bytes 65568 | tf_op jit(solution)/shard_map/ppermute | solution.py:32
  25.4 2.5 %collective-permute-done.2.refs_2_ = bf16[16,2048]{1,0:T(8,128)(2,1)S(1)} collective-permute-done((bf16[16,2048]{1,0:T(8,128)(2,1)}, bf16[16,2048]{1,0:T(8,128)(2,1)S(1)}, u32[]{:S(2)}, u32[]{:S(2)}) %collective-permute-start.2) | collective-permute-done | bytes 65568 | tf_op jit(solution)/shard_map/ppermute | solution.py:32
  28.8 1.6 %copy-done.9 = bf16[8192,128]{1,0:T(8,128)(2,1)S(1)} copy-done((bf16[8192,128]{1,0:T(8,128)(2,1)S(1)}, bf16[8192,128]{1,0:T(8,128)(2,1)}, u32[]{:S(2)}) %copy-start.9) | copy-done | bytes 2097176
  33.4 2.0 %copy-done = bf16[8192,256]{1,0:T(8,128)(2,1)} copy-done((bf16[8192,256]{1,0:T(8,128)(2,1)}, bf16[8192,256]{1,0:T(8,128)(2,1)S(1)}, u32[]{:S(2)}) %copy-start) | copy-done | bytes 4194328
  36.9 9.6 %collective-permute-start.4 = (bf16[96,2304]{1,0:T(8,128)(2,1)}, bf16[96,2304]{1,0:T(8,128)(2,1)S(1)}, u32[]{:S(2)}, u32[]{:S(2)}) collective-permute-start(bf16[96,2304]{1,0:T(8,128)(2,1)} %ordered.1.refs_1_), channel_id=1, source_target_pairs={{0,1},{1,2},{2,3},{3,0},{4,5},{5,6},{6,7},{7,4},{8,9},{9,10},{10,1... | collective-permute-start | bytes 1327112 | tf_op jit(solution)/shard_map/ppermute | solution.py:32
  46.5 1.7 %collective-permute-start.6 = (bf16[64,2048]{1,0:T(8,128)(2,1)S(1)}, bf16[64,2048]{1,0:T(8,128)(2,1)S(1)}, u32[]{:S(2)}, u32[]{:S(2)}) collective-permute-start(bf16[64,2048]{1,0:T(8,128)(2,1)S(1)} %copy-done.7), channel_id=1, source_target_pairs={{0,8},{4,12},{8,0},{12,4},{16,24},{20,28},{24,16},{28,20},{1,9},{5... | collective-permute-start | bytes 786440 | tf_op jit(solution)/shard_map/ppermute | solution.py:36
  48.2 1.5 %collective-permute-start.7 = (bf16[64,2048]{1,0:T(8,128)(2,1)S(1)}, bf16[64,2048]{1,0:T(8,128)(2,1)S(1)}, u32[]{:S(2)}, u32[]{:S(2)}) collective-permute-start(bf16[64,2048]{1,0:T(8,128)(2,1)S(1)} %copy-done.7), channel_id=1, source_target_pairs={{0,16},{4,20},{8,24},{12,28},{16,0},{20,4},{24,8},{28,12},{1,17},{... | collective-permute-start | bytes 786440 | tf_op jit(solution)/shard_map/ppermute | solution.py:36
  50.0 5.8 %collective-permute-done.6.refs_1_ = bf16[64,2048]{1,0:T(8,128)(2,1)S(1)} collective-permute-done((bf16[64,2048]{1,0:T(8,128)(2,1)S(1)}, bf16[64,2048]{1,0:T(8,128)(2,1)S(1)}, u32[]{:S(2)}, u32[]{:S(2)}) %collective-permute-start.6) | collective-permute-done | bytes 262176 | tf_op jit(solution)/shard_map/ppermute | solution.py:36
  55.8 4.9 %collective-permute-done.7.refs_2_ = bf16[64,2048]{1,0:T(8,128)(2,1)S(1)} collective-permute-done((bf16[64,2048]{1,0:T(8,128)(2,1)S(1)}, bf16[64,2048]{1,0:T(8,128)(2,1)S(1)}, u32[]{:S(2)}, u32[]{:S(2)}) %collective-permute-start.7) | collective-permute-done | bytes 262176 | tf_op jit(solution)/shard_map/ppermute | solution.py:36
  60.8 2.2 %copy-done.1 = bf16[8192,256]{1,0:T(8,128)(2,1)S(1)} copy-done((bf16[8192,256]{1,0:T(8,128)(2,1)S(1)}, bf16[8192,256]{1,0:T(8,128)(2,1)}, u32[]{:S(2)}) %copy-start.1) | copy-done | bytes 4194328
  63.0 2.6 %first_features.1 = (bf16[8,96,1280]{2,1,0:T(8,128)(2,1)S(1)}, f32[96,256]{1,0:T(8,128)S(1)}) custom-call(bf16[96,2304]{1,0:T(8,128)(2,1)S(1)} %copy-done.17, bf16[96,2304]{1,0:T(8,128)(2,1)S(1)} %copy-done.14, bf16[96,2304]{1,0:T(8,128)(2,1)S(1)} %collective-permute-done.4.refs_2_, bf16[96,2304]{1,0:T(8,128)(2,1)} %collective-permute-done.5.refs_3_, ...), custom_call_target="tpu_custom_call" | custom-call | bytes 1024 | tf_op jit(solution)/shard_map/first_features/pallas_call | solution.py:262
  66.7 1.3 %copy-done.12 = bf16[8,96,1280]{2,1,0:T(8,128)(2,1)} copy-done((bf16[8,96,1280]{2,1,0:T(8,128)(2,1)}, bf16[8,96,1280]{2,1,0:T(8,128)(2,1)S(1)}, u32[]{:S(2)}) %copy-start.12) | copy-done | bytes 1966104
  68.7 3.7 %all-to-all-start = ((bf16[8,96,1280]{2,1,0:T(8,128)(2,1)}), bf16[8,96,1280]{2,1,0:T(8,128)(2,1)S(1)}, u32[]{:S(2)}, u32[]{:S(2)}) async-start(bf16[8,96,1280]{2,1,0:T(8,128)(2,1)} %copy-done.12), calls=%async_computation | async-start | bytes 3932160 | tf_op jit(solution)/shard_map/all_to_all | solution.py:388
  74.0 2.6 %collective-permute-start.11 = (bf16[32,2048]{1,0:T(8,128)(2,1)}, bf16[32,2048]{1,0:T(8,128)(2,1)S(1)}, u32[]{:S(2)}, u32[]{:S(2)}) collective-permute-start(bf16[32,2048]{1,0:T(8,128)(2,1)} %get-tuple-element.28.refs_0_), channel_id=1, source_target_pairs={{0,3},{1,0},{2,1},{3,2},{4,7},{5,4},{6,5},{7,6},{8,11},{9,8},{10,9... | collective-permute-start | bytes 393224 | tf_op jit(solution)/shard_map/ppermute | solution.py:32
  76.6 4.5 %collective-permute-done.9.refs_1_ = bf16[32,2048]{1,0:T(8,128)(2,1)S(1)} collective-permute-done((bf16[32,2048]{1,0:T(8,128)(2,1)}, bf16[32,2048]{1,0:T(8,128)(2,1)S(1)}, u32[]{:S(2)}, u32[]{:S(2)}) %collective-permute-start.9) | collective-permute-done | bytes 131104 | tf_op jit(solution)/shard_map/ppermute | solution.py:32
  81.1 1.6 %collective-permute-start.10 = (bf16[32,2048]{1,0:T(8,128)(2,1)S(1)}, bf16[32,2048]{1,0:T(8,128)(2,1)S(1)}, u32[]{:S(2)}, u32[]{:S(2)}) collective-permute-start(bf16[32,2048]{1,0:T(8,128)(2,1)S(1)} %collective-permute-done.9.refs_1_), channel_id=1, source_target_pairs={{0,1},{1,2},{2,3},{3,0},{4,5},{5,6},{6,7},{7,4},{8,9},{9,10},{10,1... | collective-permute-start | bytes 393224 | tf_op jit(solution)/shard_map/ppermute | solution.py:32
  83.1 1.2 %copy-done.4 = bf16[256,2048]{1,0:T(8,128)(2,1)S(1)} copy-done((bf16[256,2048]{1,0:T(8,128)(2,1)S(1)}, bf16[256,2048]{1,0:T(8,128)(2,1)}, u32[]{:S(2)}) %copy-start.4) | copy-done | bytes 1048600
  85.9 2.1 %collective-permute-start.13 = (f32[128,128]{1,0:T(8,128)S(1)}, f32[128,128]{1,0:T(8,128)S(1)}, u32[]{:S(2)}, u32[]{:S(2)}) collective-permute-start(f32[128,128]{1,0:T(8,128)S(1)} %get-tuple-element.32), channel_id=1, source_target_pairs={{0,3},{1,0},{2,1},{3,2},{4,7},{5,4},{6,5},{7,6},{8,11},{9,8},{10,9... | collective-permute-start | bytes 196616 | tf_op jit(solution)/shard_map/ppermute | solution.py:32
  88.1 1.4 %collective-permute-start.14 = (f32[128,128]{1,0:T(8,128)S(1)}, f32[128,128]{1,0:T(8,128)S(1)}, u32[]{:S(2)}, u32[]{:S(2)}) collective-permute-start(f32[128,128]{1,0:T(8,128)S(1)} %get-tuple-element.33), channel_id=1, source_target_pairs={{0,2},{1,3},{2,0},{3,1},{4,6},{5,7},{6,4},{7,5},{8,10},{9,11},{10,... | collective-permute-start | bytes 196616 | tf_op jit(solution)/shard_map/ppermute | solution.py:32
  89.4 1.2 %collective-permute-start.15 = (f32[128,128]{1,0:T(8,128)S(1)}, f32[128,128]{1,0:T(8,128)S(1)}, u32[]{:S(2)}, u32[]{:S(2)}) collective-permute-start(f32[128,128]{1,0:T(8,128)S(1)} %get-tuple-element.34), channel_id=1, source_target_pairs={{0,1},{1,2},{2,3},{3,0},{4,5},{5,6},{6,7},{7,4},{8,9},{9,10},{10,1... | collective-permute-start | bytes 196616 | tf_op jit(solution)/shard_map/ppermute | solution.py:32
  90.7 3.8 %collective-permute-done.14.refs_8_ = f32[128,128]{1,0:T(8,128)S(1)} collective-permute-done((f32[128,128]{1,0:T(8,128)S(1)}, f32[128,128]{1,0:T(8,128)S(1)}, u32[]{:S(2)}, u32[]{:S(2)}) %collective-permute-start.14) | collective-permute-done | bytes 65568 | tf_op jit(solution)/shard_map/ppermute | solution.py:32
  95.5 2.2 %copy-done.2 = bf16[8192,256]{1,0:T(8,128)(2,1)S(1)} copy-done((bf16[8192,256]{1,0:T(8,128)(2,1)S(1)}, bf16[8192,256]{1,0:T(8,128)(2,1)}, u32[]{:S(2)}) %copy-start.2) | copy-done | bytes 4194328
  99.6 4.2 %all-to-all-start.2 = ((bf16[8,32,2048]{2,1,0:T(8,128)(2,1)}), bf16[8,32,2048]{2,1,0:T(8,128)(2,1)}, u32[]{:S(2)}, u32[]{:S(2)}) async-start(bf16[8,32,2048]{2,1,0:T(8,128)(2,1)} %copy-done.5), calls=%async_computation.2 | async-start | bytes 2097152 | tf_op jit(solution)/shard_map/all_to_all | solution.py:394
  103.8 3.0 %projector.1 = f32[128,512]{1,0:T(8,128)S(1)} custom-call(bf16[8,96,1280]{2,1,0:T(8,128)(2,1)S(1)} %all-to-all-done.came_ref.first_ref, bf16[8,128,512]{2,1,0:T(8,128)(2,1)S(1)} %all-to-all-done.1.teach_ref.refs_3_), custom_call_target="tpu_custom_call" | custom-call | bytes 1024 | tf_op jit(solution)/shard_map/projector/pallas_call | solution.py:309
  107.8 11.5 %all-to-all-done.2.last_ref = bf16[8,32,2048]{2,1,0:T(8,128)(2,1)} async-done(((bf16[8,32,2048]{2,1,0:T(8,128)(2,1)}), bf16[8,32,2048]{2,1,0:T(8,128)(2,1)}, u32[]{:S(2)}, u32[]{:S(2)}) %all-to-all-start.2) | async-done | bytes 1048608 | tf_op jit(solution)/shard_map/all_to_all | solution.py:394
  119.2 2.9 %final_product.1 = (f32[128,1024]{1,0:T(8,128)}, f32[128,1024]{1,0:T(8,128)}) custom-call(bf16[8,96,1280]{2,1,0:T(8,128)(2,1)S(1)} %all-to-all-done.came_ref.first_ref, bf16[8,32,2048]{2,1,0:T(8,128)(2,1)} %all-to-all-done.2.last_ref), custom_call_target="tpu_custom_call" | custom-call | bytes 1024 | tf_op jit(solution)/shard_map/final_product/pallas_call | solution.py:347
  (61 shorter events, 15.5 us)
Async XLA Ops:
  3.5 25.2 %copy-start.8 = (bf16[8192,128]{1,0:T(8,128)(2,1)S(1)}, bf16[8192,128]{1,0:T(8,128)(2,1)}, u32[]{:S(2)}) copy-start(bf16[8192,128]{1,0:T(8,128)(2,1)} %gate_ref.1) | copy-start | bytes 6291460
  3.6 65.1 %all-to-all-start.1 = ((bf16[8,128,512]{2,1,0:T(8,128)(2,1)}), bf16[8,128,512]{2,1,0:T(8,128)(2,1)S(1)}, u32[]{:S(2)}, u32[]{:S(2)}) async-start(bf16[8,128,512]{2,1,0:T(8,128)(2,1)} %get-tuple-element.27), calls=%async_computation.1 | async-start | bytes 2097152 | tf_op jit(solution)/shard_map/all_to_all | solution.py:373
  8.9 27.2 %collective-permute-start = (bf16[96,2304]{1,0:T(8,128)(2,1)}, bf16[96,2304]{1,0:T(8,128)(2,1)S(1)}, u32[]{:S(2)}, u32[]{:S(2)}) collective-permute-start(bf16[96,2304]{1,0:T(8,128)(2,1)} %get-tuple-element.20.refs_0_), channel_id=1, source_target_pairs={{0,1},{1,2},{2,3},{3,0},{4,5},{5,6},{6,7},{7,4},{8,9},{9,10},{10,1... | collective-permute-start | bytes 1327112 | tf_op jit(solution)/shard_map/ppermute | solution.py:32
  10.5 14.9 %collective-permute-start.1 = (bf16[16,2048]{1,0:T(8,128)(2,1)}, bf16[16,2048]{1,0:T(8,128)(2,1)S(1)}, u32[]{:S(2)}, u32[]{:S(2)}) collective-permute-start(bf16[16,2048]{1,0:T(8,128)(2,1)} %get-tuple-element.22), channel_id=1, source_target_pairs={{0,1},{1,2},{2,3},{3,0},{4,5},{5,6},{6,7},{7,4},{8,9},{9,10},{10,1... | collective-permute-start | bytes 196616 | tf_op jit(solution)/shard_map/ppermute | solution.py:32
  12.0 15.9 %collective-permute-start.2 = (bf16[16,2048]{1,0:T(8,128)(2,1)}, bf16[16,2048]{1,0:T(8,128)(2,1)S(1)}, u32[]{:S(2)}, u32[]{:S(2)}) collective-permute-start(bf16[16,2048]{1,0:T(8,128)(2,1)} %get-tuple-element.23), channel_id=1, source_target_pairs={{0,2},{1,3},{2,0},{3,1},{4,6},{5,7},{6,4},{7,5},{8,10},{9,11},{10,... | collective-permute-start | bytes 196616 | tf_op jit(solution)/shard_map/ppermute | solution.py:32
  13.3 14.6 %collective-permute-start.3 = (bf16[16,2048]{1,0:T(8,128)(2,1)}, bf16[16,2048]{1,0:T(8,128)(2,1)S(1)}, u32[]{:S(2)}, u32[]{:S(2)}) collective-permute-start(bf16[16,2048]{1,0:T(8,128)(2,1)} %get-tuple-element.24), channel_id=1, source_target_pairs={{0,3},{1,0},{2,1},{3,2},{4,7},{5,4},{6,5},{7,6},{8,11},{9,8},{10,9... | collective-permute-start | bytes 196616 | tf_op jit(solution)/shard_map/ppermute | solution.py:32
  16.0 44.8 %collective-permute-start.5 = (bf16[96,2304]{1,0:T(8,128)(2,1)}, bf16[96,2304]{1,0:T(8,128)(2,1)}, u32[]{:S(2)}, u32[]{:S(2)}) collective-permute-start(bf16[96,2304]{1,0:T(8,128)(2,1)} %get-tuple-element.20.refs_0_), channel_id=1, source_target_pairs={{0,3},{1,0},{2,1},{3,2},{4,7},{5,4},{6,5},{7,6},{8,11},{9,8},{10,9... | collective-permute-start | bytes 1327112 | tf_op jit(solution)/shard_map/ppermute | solution.py:32
  28.8 1.6 %copy-start.9 = (bf16[8192,128]{1,0:T(8,128)(2,1)S(1)}, bf16[8192,128]{1,0:T(8,128)(2,1)}, u32[]{:S(2)}) copy-start(bf16[8192,128]{1,0:T(8,128)(2,1)} %up_ref.1) | copy-start | bytes 6291460
  33.3 2.0 %copy-start = (bf16[8192,256]{1,0:T(8,128)(2,1)}, bf16[8192,256]{1,0:T(8,128)(2,1)S(1)}, u32[]{:S(2)}) copy-start(bf16[8192,256]{1,0:T(8,128)(2,1)S(1)} %get-tuple-element.25.refs_2_.refs_4_) | copy-start | bytes 12582916
  36.9 9.6 %copy-start.7 = (bf16[64,2048]{1,0:T(8,128)(2,1)S(1)}, bf16[64,2048]{1,0:T(8,128)(2,1)}, u32[]{:S(2)}) copy-start(bf16[64,2048]{1,0:T(8,128)(2,1)} %copy-done.6) | copy-start | bytes 786436
  36.9 23.9 %copy-start.14 = (bf16[96,2304]{1,0:T(8,128)(2,1)S(1)}, bf16[96,2304]{1,0:T(8,128)(2,1)}, u32[]{:S(2)}) copy-start(bf16[96,2304]{1,0:T(8,128)(2,1)} %ordered.1.refs_1_) | copy-start | bytes 1327108
  36.9 23.9 %copy-start.17 = (bf16[96,2304]{1,0:T(8,128)(2,1)S(1)}, bf16[96,2304]{1,0:T(8,128)(2,1)}, u32[]{:S(2)}) copy-start(bf16[96,2304]{1,0:T(8,128)(2,1)} %get-tuple-element.20.refs_0_) | copy-start | bytes 1327108
  36.9 23.8 %collective-permute-start.4 = (bf16[96,2304]{1,0:T(8,128)(2,1)}, bf16[96,2304]{1,0:T(8,128)(2,1)S(1)}, u32[]{:S(2)}, u32[]{:S(2)}) collective-permute-start(bf16[96,2304]{1,0:T(8,128)(2,1)} %ordered.1.refs_1_), channel_id=1, source_target_pairs={{0,1},{1,2},{2,3},{3,0},{4,5},{5,6},{6,7},{7,4},{8,9},{9,10},{10,1... | collective-permute-start | bytes 1327112 | tf_op jit(solution)/shard_map/ppermute | solution.py:32
  46.5 9.2 %collective-permute-start.6 = (bf16[64,2048]{1,0:T(8,128)(2,1)S(1)}, bf16[64,2048]{1,0:T(8,128)(2,1)S(1)}, u32[]{:S(2)}, u32[]{:S(2)}) collective-permute-start(bf16[64,2048]{1,0:T(8,128)(2,1)S(1)} %copy-done.7), channel_id=1, source_target_pairs={{0,8},{4,12},{8,0},{12,4},{16,24},{20,28},{24,16},{28,20},{1,9},{5... | collective-permute-start | bytes 786440 | tf_op jit(solution)/shard_map/ppermute | solution.py:36
  48.2 12.4 %collective-permute-start.7 = (bf16[64,2048]{1,0:T(8,128)(2,1)S(1)}, bf16[64,2048]{1,0:T(8,128)(2,1)S(1)}, u32[]{:S(2)}, u32[]{:S(2)}) collective-permute-start(bf16[64,2048]{1,0:T(8,128)(2,1)S(1)} %copy-done.7), channel_id=1, source_target_pairs={{0,16},{4,20},{8,24},{12,28},{16,0},{20,4},{24,8},{28,12},{1,17},{... | collective-permute-start | bytes 786440 | tf_op jit(solution)/shard_map/ppermute | solution.py:36
  49.7 11.0 %collective-permute-start.8 = (bf16[64,2048]{1,0:T(8,128)(2,1)S(1)}, bf16[64,2048]{1,0:T(8,128)(2,1)S(1)}, u32[]{:S(2)}, u32[]{:S(2)}) collective-permute-start(bf16[64,2048]{1,0:T(8,128)(2,1)S(1)} %copy-done.7), channel_id=1, source_target_pairs={{0,24},{4,28},{8,16},{12,20},{16,8},{20,12},{24,0},{28,4},{1,25},{... | collective-permute-start | bytes 786440 | tf_op jit(solution)/shard_map/ppermute | solution.py:36
  60.8 2.2 %copy-start.1 = (bf16[8192,256]{1,0:T(8,128)(2,1)S(1)}, bf16[8192,256]{1,0:T(8,128)(2,1)}, u32[]{:S(2)}) copy-start(bf16[8192,256]{1,0:T(8,128)(2,1)} %copy-done) | copy-start | bytes 12582916
  65.6 1.1 copy-start.3
  66.7 1.3 %copy-start.12 = (bf16[8,96,1280]{2,1,0:T(8,128)(2,1)}, bf16[8,96,1280]{2,1,0:T(8,128)(2,1)S(1)}, u32[]{:S(2)}) copy-start(bf16[8,96,1280]{2,1,0:T(8,128)(2,1)S(1)} %get-tuple-element.26) | copy-start | bytes 5898244
  68.6 14.4 %copy-start.16 = (bf16[128,2048]{1,0:T(8,128)(2,1)S(1)}, bf16[128,2048]{1,0:T(8,128)(2,1)}, u32[]{:S(2)}) copy-start(bf16[128,2048]{1,0:T(8,128)(2,1)} %copy-done.15) | copy-start | bytes 1572868
  68.7 30.9 %all-to-all-start = ((bf16[8,96,1280]{2,1,0:T(8,128)(2,1)}), bf16[8,96,1280]{2,1,0:T(8,128)(2,1)S(1)}, u32[]{:S(2)}, u32[]{:S(2)}) async-start(bf16[8,96,1280]{2,1,0:T(8,128)(2,1)} %copy-done.12), calls=%async_computation | async-start | bytes 3932160 | tf_op jit(solution)/shard_map/all_to_all | solution.py:388
  72.4 10.7 %collective-permute-start.12 = (bf16[256,2048]{1,0:T(8,128)(2,1)}, bf16[256,2048]{1,0:T(8,128)(2,1)S(1)}, u32[]{:S(2)}, u32[]{:S(2)}) collective-permute-start(bf16[256,2048]{1,0:T(8,128)(2,1)} %copy-done.3), channel_id=1, source_target_pairs={{0,4},{4,0},{8,12},{12,8},{16,20},{20,16},{24,28},{28,24},{1,5},{5... | collective-permute-start | bytes 3145736 | tf_op jit(solution)/shard_map/ppermute | solution.py:36
  72.8 8.3 %collective-permute-start.9 = (bf16[32,2048]{1,0:T(8,128)(2,1)}, bf16[32,2048]{1,0:T(8,128)(2,1)S(1)}, u32[]{:S(2)}, u32[]{:S(2)}) collective-permute-start(bf16[32,2048]{1,0:T(8,128)(2,1)} %get-tuple-element.28.refs_0_), channel_id=1, source_target_pairs={{0,1},{1,2},{2,3},{3,0},{4,5},{5,6},{6,7},{7,4},{8,9},{9,10},{10,1... | collective-permute-start | bytes 393224 | tf_op jit(solution)/shard_map/ppermute | solution.py:32
  74.0 9.1 %collective-permute-start.11 = (bf16[32,2048]{1,0:T(8,128)(2,1)}, bf16[32,2048]{1,0:T(8,128)(2,1)S(1)}, u32[]{:S(2)}, u32[]{:S(2)}) collective-permute-start(bf16[32,2048]{1,0:T(8,128)(2,1)} %get-tuple-element.28.refs_0_), channel_id=1, source_target_pairs={{0,3},{1,0},{2,1},{3,2},{4,7},{5,4},{6,5},{7,6},{8,11},{9,8},{10,9... | collective-permute-start | bytes 393224 | tf_op jit(solution)/shard_map/ppermute | solution.py:32
  81.1 9.5 %collective-permute-start.10 = (bf16[32,2048]{1,0:T(8,128)(2,1)S(1)}, bf16[32,2048]{1,0:T(8,128)(2,1)S(1)}, u32[]{:S(2)}, u32[]{:S(2)}) collective-permute-start(bf16[32,2048]{1,0:T(8,128)(2,1)S(1)} %collective-permute-done.9.refs_1_), channel_id=1, source_target_pairs={{0,1},{1,2},{2,3},{3,0},{4,5},{5,6},{6,7},{7,4},{8,9},{9,10},{10,1... | collective-permute-start | bytes 393224 | tf_op jit(solution)/shard_map/ppermute | solution.py:32
  83.1 1.2 %copy-start.4 = (bf16[256,2048]{1,0:T(8,128)(2,1)S(1)}, bf16[256,2048]{1,0:T(8,128)(2,1)}, u32[]{:S(2)}) copy-start(bf16[256,2048]{1,0:T(8,128)(2,1)} %copy-done.3) | copy-start | bytes 3145732
  85.2 10.3 %copy-start.20 = (bf16[32,2048]{1,0:T(8,128)(2,1)S(1)}, bf16[32,2048]{1,0:T(8,128)(2,1)}, u32[]{:S(2)}) copy-start(bf16[32,2048]{1,0:T(8,128)(2,1)} %get-tuple-element.28.refs_0_) | copy-start | bytes 393220
  85.9 4.7 %collective-permute-start.13 = (f32[128,128]{1,0:T(8,128)S(1)}, f32[128,128]{1,0:T(8,128)S(1)}, u32[]{:S(2)}, u32[]{:S(2)}) collective-permute-start(f32[128,128]{1,0:T(8,128)S(1)} %get-tuple-element.32), channel_id=1, source_target_pairs={{0,3},{1,0},{2,1},{3,2},{4,7},{5,4},{6,5},{7,6},{8,11},{9,8},{10,9... | collective-permute-start | bytes 196616 | tf_op jit(solution)/shard_map/ppermute | solution.py:32
  88.1 6.4 %collective-permute-start.14 = (f32[128,128]{1,0:T(8,128)S(1)}, f32[128,128]{1,0:T(8,128)S(1)}, u32[]{:S(2)}, u32[]{:S(2)}) collective-permute-start(f32[128,128]{1,0:T(8,128)S(1)} %get-tuple-element.33), channel_id=1, source_target_pairs={{0,2},{1,3},{2,0},{3,1},{4,6},{5,7},{6,4},{7,5},{8,10},{9,11},{10,... | collective-permute-start | bytes 196616 | tf_op jit(solution)/shard_map/ppermute | solution.py:32
  89.4 6.1 %collective-permute-start.15 = (f32[128,128]{1,0:T(8,128)S(1)}, f32[128,128]{1,0:T(8,128)S(1)}, u32[]{:S(2)}, u32[]{:S(2)}) collective-permute-start(f32[128,128]{1,0:T(8,128)S(1)} %get-tuple-element.34), channel_id=1, source_target_pairs={{0,1},{1,2},{2,3},{3,0},{4,5},{5,6},{6,7},{7,4},{8,9},{9,10},{10,1... | collective-permute-start | bytes 196616 | tf_op jit(solution)/shard_map/ppermute | solution.py:32
  95.5 2.2 %copy-start.2 = (bf16[8192,256]{1,0:T(8,128)(2,1)S(1)}, bf16[8192,256]{1,0:T(8,128)(2,1)}, u32[]{:S(2)}) copy-start(bf16[8192,256]{1,0:T(8,128)(2,1)} %copy-done) | copy-start | bytes 12582916
  99.6 19.7 %all-to-all-start.2 = ((bf16[8,32,2048]{2,1,0:T(8,128)(2,1)}), bf16[8,32,2048]{2,1,0:T(8,128)(2,1)}, u32[]{:S(2)}, u32[]{:S(2)}) async-start(bf16[8,32,2048]{2,1,0:T(8,128)(2,1)} %copy-done.5), calls=%async_computation.2 | async-start | bytes 2097152 | tf_op jit(solution)/shard_map/all_to_all | solution.py:394
  (9 other events, 7.9 us)

commit v2 on v1

v2 whole, which is shorter than its diff:
```python
import math

import jax
import jax.numpy as jnp
from jax import lax
from jax.experimental import pallas as pl
from jax.experimental.pallas import tpu as pltpu
from jax.sharding import PartitionSpec as P

PB = 128
LANES = 128
GROUP = 8
FIRST = 80
MIB = 1 << 20

VMEM = pl.BlockSpec(memory_space=pltpu.VMEM)


def params(mib):
    return pltpu.CompilerParams(vmem_limit_bytes=mib * MIB)


def cost(flops, nbytes):
    return pl.CostEstimate(flops=int(flops), bytes_accessed=int(nbytes), transcendentals=0)


def struct(shape, dtype=jnp.bfloat16):
    return jax.ShapeDtypeStruct(shape, dtype)


def shift(x, count, by):
    return lax.ppermute(x, "tensor", [(i, (i + by) % count) for i in range(count)])


def swap(x, count, mask):
    return lax.ppermute(x, "dp", [(i, i ^ mask) for i in range(count)])


def contract_rows(left, right):
    return lax.dot_general(
        left, right, (((0,), (0,)), ((), ())), preferred_element_type=jnp.float32
    )


def contract_cols(left, right):
    return lax.dot_general(
        left, right, (((1,), (1,)), ((), ())), preferred_element_type=jnp.float32
    )


def scaled_difference(student, projected, factor):
    wide = student.astype(jnp.float32) - projected.astype(jnp.float32)
    return (wide * factor).astype(jnp.bfloat16)


def prepare(row_map, teacher, mlp_input, student, projected, down, n_dp, n_t, factor):
    tok, width = mlp_input.shape
    rows = down.shape[0] // GROUP
    wide = teacher.shape[1] // n_dp
    second = tok - FIRST
    hbm = pl.BlockSpec(memory_space=pltpu.HBM)
    if wide % LANES:
        blocks = teacher.reshape(tok, n_dp, wide).transpose(1, 0, 2)
        wide = 0

    def kernel(m_ref, t_ref, x_ref, s_ref, p_ref, d_ref, right_ref, left_ref, *refs):
        two_ref, digits_ref, here_ref, far_ref = refs[:4]
        s_buf, p_buf, m_buf, sems = refs[-4:]
        row = pl.multiple_of((lax.axis_index("dp") % GROUP) * rows, rows)
        pairs = [
            (s_ref.at[:, :PB], s_buf),
            (p_ref.at[:, :PB], p_buf),
            (m_ref, m_buf),
            (x_ref.at[:FIRST], right_ref.at[:FIRST, :width]),
            (x_ref.at[:FIRST], left_ref.at[:FIRST, :width]),
            (x_ref.at[FIRST:], two_ref),
        ]
        pieces = [here_ref, right_ref.at[FIRST:, :width], far_ref, left_ref.at[FIRST:, :width]]
        for k in range(n_t):
            col = pl.multiple_of(((lax.axis_index("tensor") + k) % n_t) * width, width)
            pairs.append((d_ref.at[pl.ds(row, rows), pl.ds(col, width)], pieces[k]))
        if wide:
            for i in range(n_dp):
                pairs.append((t_ref.at[:, i * wide : (i + 1) * wide], refs[4].at[i]))
        copies = [
            pltpu.make_async_copy(src, dst, sems.at[i]) for i, (src, dst) in enumerate(pairs)
        ]
        for c in copies:
            c.start()
        for c in copies[:3]:
            c.wait()
        bucket = scaled_difference(s_buf[...], p_buf[...], factor)
        for ref in (right_ref, left_ref):
            ref[:FIRST, width : width + PB] = bucket[:FIRST]
            ref[:second, width + PB :] = bucket[FIRST:]
            ref[second:, width + PB :] = jnp.zeros((FIRST + rows - second, PB), jnp.bfloat16)
            ref[FIRST:, width : width + PB] = jnp.zeros((rows, PB), jnp.bfloat16)
        line = lax.broadcasted_iota(jnp.int32, (16, tok), 0)
        number = jnp.broadcast_to(m_buf[...], (16, tok))
        high, low = number // LANES, number % LANES
        digits = jnp.where(line == 0, high, jnp.where(line == 1, low, 0))
        digits_ref[...] = digits.astype(jnp.float32).astype(jnp.bfloat16)
        for c in copies[3:]:
            c.wait()

    shapes = [(FIRST + rows, width + 2 * PB)] * 2 + [(second, width), (16, tok)] + [(rows, width)] * 2
    if wide:
        shapes.append((n_dp, tok, wide))
    out = pl.pallas_call(
        kernel,
        in_specs=[hbm] * 6,
        out_specs=[VMEM] * len(shapes),
        out_shape=[struct(s) for s in shapes],
        scratch_shapes=[
            pltpu.VMEM((tok, PB), jnp.bfloat16),
            pltpu.VMEM((tok, PB), jnp.bfloat16),
            pltpu.VMEM((1, tok), jnp.int32),
            pltpu.SemaphoreType.DMA((6 + n_t + n_dp,)),
        ],
        compiler_params=params(60),
        cost_estimate=cost(0, 1024),
        name="prepare",
    )(row_map.reshape(1, tok), teacher, mlp_input, student, projected, down)
    return out if wide else [*out, blocks]


def stack_rows(parts, rows, width, after=()):
    def kernel(*refs):
        out_ref = refs[-1]
        for i, ref in enumerate(refs[: len(parts)]):
            out_ref[i * rows : (i + 1) * rows] = ref[ref.shape[0] - rows :, :width]

    return pl.pallas_call(
        kernel,
        in_specs=[VMEM] * len(parts) + [pl.BlockSpec(memory_space=pl.ANY)] * len(after),
        out_specs=VMEM,
        out_shape=struct((len(parts) * rows, width)),
        compiler_params=params(8),
        cost_estimate=cost(0, 1024),
        name="stack_rows",
    )(*parts, *after)


def partial_products(near, far, student, projected, n_t, rows, factor, after):
    tok, width = student.shape
    hb = rows * GROUP
    half = GROUP // 2

    def kernel(near_ref, far_ref, s_ref, p_ref, *refs):
        outs = refs[len(after) :]
        err = scaled_difference(s_ref[...], p_ref[...], factor)
        place = lax.axis_index("dp") % GROUP
        for side, ref in enumerate((near_ref, far_ref)):
            product = contract_cols(ref[...], err)
            for j in range(half):
                row = pl.multiple_of((place ^ (2 * j + side)) * rows, rows)
                for k in range(n_t):
                    at = (j * n_t + k) * rows
                    outs[k][pl.ds(row, rows), :] = product[at : at + rows]

    return pl.pallas_call(
        kernel,
        in_specs=[VMEM] * 4
        + [pl.BlockSpec(memory_space=pl.ANY)] * len(after),
        out_specs=[VMEM] * n_t,
        out_shape=[struct((hb, tok), jnp.float32)] * n_t,
        compiler_params=params(60),
        cost_estimate=cost(0, 1024),
        name="partial_products",
    )(near, far, student, projected, *after)


def features(slices, gate, up, n_dp, digits=None, rest=None, after=()):
    n_t = len(slices)
    width, hb = gate.shape[0] // n_t, gate.shape[1]
    cols = width * n_t // n_dp
    per = width // cols
    first = rest is None
    if first:
        count, base, others = FIRST, 2 * PB, [digits]
        second = digits.shape[1] - FIRST
    else:
        count, others = slices[0].shape[0], [rest[0], *rest[1]]
        base = (1 + pl.cdiv(FIRST, count)) * 2 * hb

    def kernel(*refs):
        xs, gate_ref, up_ref, refs = refs[:n_t], refs[n_t], refs[n_t + 1], refs[n_t + 2 :]
        w_ref, sems = refs[-2:]
        if first:
            digits_ref, (out_ref, pre_ref) = refs[0], refs[-4:-2]
        else:
            pre_ref, act_refs, out_ref = refs[0], refs[1 : 1 + n_t], refs[-3]
        t = lax.axis_index("tensor")
        slots = [(t + n_t - k) % n_t for k in range(n_t)]
        copies = []
        for k in range(n_t):
            at = pl.ds(pl.multiple_of(slots[k] * width, width), width)
            for j, ref in enumerate((gate_ref, up_ref)):
                copies.append(
                    pltpu.make_async_copy(
                        ref.at[at], w_ref.at[k, :, j * hb : (j + 1) * hb], sems.at[2 * k + j]
                    )
                )
        for c in copies:
            c.start()
        for k in range(n_t):
            for b in range(per):
                out_ref[slots[k] * per + b, :, base:] = xs[k][:count, b * cols : (b + 1) * cols]
            if first:

                @pl.when(slots[k] == 0)
                def _(k=k):
                    for i in range(n_dp):
                        out_ref[i, :, :base] = xs[k][:count, width:]

        if first:
            for i in range(n_dp):
                out_ref[i, second : second + 16, PB : 2 * PB] = digits_ref[...]
        pre = jnp.zeros((count, 2 * hb), jnp.float32)
        for k in range(n_t):
            copies[2 * k].wait()
            copies[2 * k + 1].wait()
            pre += jnp.dot(xs[k][:count, :width], w_ref[k], preferred_element_type=jnp.float32)
        if first:
            pre_ref[...] = pre
            return
        act = act_refs[0][...]
        for ref in act_refs[1:]:
            act += ref[...]
        act = act.T
        pre = jnp.concatenate([pre_ref[...], pre])
        gate_pre, up_pre = pre[:, :hb], pre[:, hb:]
        s = jax.nn.sigmoid(gate_pre)
        gate_grad = (act * up_pre * s * (1.0 + gate_pre * (1.0 - s))).astype(jnp.bfloat16)
        up_grad = (act * gate_pre * s).astype(jnp.bfloat16)
        starts = [*range(0, FIRST, count), FIRST]
        for b, low in enumerate(starts):
            size = min(count, FIRST - low) if low < FIRST else count
            for j, grad in enumerate((gate_grad, up_grad)):
                at = slice((2 * b + j) * hb, (2 * b + j + 1) * hb)
                for i in range(n_dp):
                    out_ref[i, :size, at] = grad[low : low + size]
                    if size < count:
                        out_ref[i, size:, at] = jnp.zeros((count - size, hb), jnp.bfloat16)

    payload = struct((n_dp, count, base + cols))
    anywhere = pl.BlockSpec(memory_space=pl.ANY)
    return pl.pallas_call(
        kernel,
        in_specs=[VMEM] * n_t
        + [pl.BlockSpec(memory_space=pltpu.HBM)] * 2
        + [VMEM] * len(others)
        + [anywhere] * len(after),
        out_specs=[VMEM, VMEM] if first else VMEM,
        out_shape=[payload, struct((count, 2 * hb), jnp.float32)] if first else payload,
        scratch_shapes=[
            pltpu.VMEM((n_t, width, 2 * hb), jnp.bfloat16),
            pltpu.SemaphoreType.DMA((2 * n_t,)),
        ],
        compiler_params=params(60),
        cost_estimate=cost(0, 1024),
        name="first_features" if first else "last_features",
    )(*slices, gate, up, *others, *after)


def projector(came, teach):
    n_dp, tok, wide = teach.shape
    second = tok - FIRST
    groups = n_dp // GROUP
    span = GROUP * tok

    def kernel(came_ref, teach_ref, out_ref, flipped_ref):
        def flip(g, carry):
            parts = []
            for i in range(GROUP):
                parts.append(came_ref[g * GROUP + i, :, :PB])
                parts.append(came_ref[g * GROUP + i, :second, PB : 2 * PB])
            flipped_ref[g] = jnp.concatenate(parts).astype(jnp.float32).T.astype(jnp.bfloat16)
            return carry

        lax.fori_loop(0, groups, flip, 0)
        out_ref[...] = jnp.zeros_like(out_ref)

        def sender(g, carry):
            digits = came_ref[g, second : second + 16, PB : 2 * PB].astype(jnp.float32)
            number = (digits[0:1] * float(LANES) + digits[1:2]).astype(jnp.int32)

            def block(h, total):
                token = lax.broadcasted_iota(jnp.int32, (span, tok), 0) + h * span
                picks = (token == number).astype(jnp.float32).astype(jnp.bfloat16)
                return total + jnp.dot(flipped_ref[h], picks, preferred_element_type=jnp.float32)

            rows = lax.fori_loop(0, groups, block, jnp.zeros((PB, tok), jnp.float32))
            out_ref[...] += jnp.dot(
                rows.astype(jnp.bfloat16), teach_ref[g], preferred_element_type=jnp.float32
            )
            return carry

        lax.fori_loop(0, n_dp, sender, 0)

    return pl.pallas_call(
        kernel,
        in_specs=[VMEM, VMEM],
        out_specs=VMEM,
        out_shape=struct((PB, wide), jnp.float32),
        scratch_shapes=[pltpu.VMEM((groups, PB, span), jnp.bfloat16)],
        compiler_params=params(24),
        cost_estimate=cost(0, 1024),
        name="projector",
    )(came, teach)


def final_product(first, last, hb, cols):
    n_dp, count = last.shape[:2]
    blocks = (last.shape[2] - cols) // (2 * hb)

    def kernel(first_ref, last_ref, gate_ref, up_ref):
        def group(g, total):
            here = pl.ds(g * GROUP, GROUP)
            for b in range(blocks):
                size = count
                if b < blocks - 1:
                    size = min(count, FIRST - b * count)
                    feats = first_ref[here, b * count : b * count + size, 2 * PB :]
                else:
                    feats = last_ref[here, :, 2 * blocks * hb :]
                grads = last_ref[here, :size, 2 * b * hb : 2 * (b + 1) * hb]
                total = total + contract_rows(
                    grads.reshape(GROUP * size, 2 * hb), feats.reshape(GROUP * size, cols)
                )
            return total

        total = jnp.zeros((2 * hb, cols), jnp.float32)
        if n_dp == GROUP:
            total = group(0, total)
        else:
            total = lax.fori_loop(0, n_dp // GROUP, group, total)
        gate_ref[...] = total[:hb]
        up_ref[...] = total[hb:]

    return pl.pallas_call(
        kernel,
        in_specs=[VMEM] * 2,
        out_specs=[VMEM] * 2,
        out_shape=[struct((hb, cols), jnp.float32)] * 2,
        compiler_params=params(24),
        cost_estimate=cost(0, 1024),
        name="final_product",
    )(first, last)


def body(
    teacher_rows, row_map, student_hidden, projected, mlp_input, gate_bucket, up_bucket, down_bucket
):
    tok = row_map.shape[0]
    n_dp = lax.axis_size("dp")
    n_t = lax.axis_size("tensor")
    hb, width = down_bucket.shape[0], student_hidden.shape[1]
    cols = width * n_t // n_dp
    factor = 1.0 / math.sqrt(tok * n_dp)
    rows = hb // GROUP

    right, left, two, digits, here, away, teach = prepare(
        row_map, teacher_rows, mlp_input, student_hidden, projected, down_bucket, n_dp, n_t, factor
    )
    before, beyond = shift(right, n_t, 1), shift(left, n_t, -1)
    away = shift(away, n_t, 2)
    teach = lax.all_to_all(teach, "dp", split_axis=0, concat_axis=0, tiled=True)

    mine = stack_rows([here, before, away, beyond], rows, width)
    one = shift(before, n_t, 1)
    others = [swap(mine, n_dp, mask) for mask in (2, 4, 6)]
    near = stack_rows([mine] + others, n_t * rows, width, after=[teach, one])
    far = swap(near, n_dp, 1)

    sent, pre = features(
        [right, before, one, beyond], gate_bucket, up_bucket, n_dp, digits, after=[near]
    )
    came_first = lax.all_to_all(sent, "dp", split_axis=0, concat_axis=0, tiled=True)

    before, beyond = shift(two, n_t, 1), shift(two, n_t, -1)
    one = shift(before, n_t, 1)
    partial = partial_products(
        near, far, student_hidden, projected, n_t, rows, factor, after=[pre, before, beyond]
    )
    acts = [partial[0]] + [shift(partial[k], n_t, -k) for k in range(1, n_t)]

    sent = features([two, before, one, beyond], gate_bucket, up_bucket, n_dp, rest=(pre, acts))
    came_last = lax.all_to_all(sent, "dp", split_axis=0, concat_axis=0, tiled=True)
    grad_proj = projector(came_first, teach)
    grad_gate, grad_up = final_product(came_first, came_last, hb, cols)
    return (grad_proj[:, None, :], grad_gate, grad_up)


def solution(mesh):
    in_specs = (
        P("dp", "tensor"),
        P("dp"),
        P("dp", "tensor"),
        P("dp", "tensor"),
        P("dp", "tensor"),
        P(None, "tensor"),
        P(None, "tensor"),
        P("tensor", None),
    )
    out_specs = (P(None, "tensor", "dp"), P("tensor", "dp"), P("tensor", "dp"))
    return jax.shard_map(body, mesh=mesh, in_specs=in_specs, out_specs=out_specs, check_vma=False)
```

time: 123 us -> 129 us (1.049)
  waiting for transfers between devices: 43.3 us -> 59.8 us
  local copies, waits for them, and re-layouts: 19.6 us -> 3.98 us
  Pallas kernels: 13.9 us -> 23.1 us
  starting transfers between devices: 44.5 us -> 40.9 us
    unnamed x45 -> x31, local copies, waits for them, and re-layouts: 19.6 us -> 3.98 us
    ppermute x12 -> x10, waiting for transfers between devices: 21.2 us -> 33.2 us  [shift(): lax.ppermute(x, 'tensor', [(i, (i + by) % count) for i in range(count)])]
    pallas_call x5 -> x3, Pallas kernels: 5.05 us -> 13.8 us  [the longest x2 10.5 us: features(): pl.pallas_call(kernel, in_specs=[VMEM] * n_t + [pl.BlockSpec(memory_space...]
    ppermute x12 -> x10, starting transfers between devices: 27.3 us -> 23.6 us  [shift(): lax.ppermute(x, 'tensor', [(i, (i + by) % count) for i in range(count)])]
    all_to_all x2, waiting for transfers between devices: 11.5 us -> 15 us  [body(): lax.all_to_all(sent, 'dp', split_axis=0, concat_axis=0, tiled=True)]
  transfers between devices with their start and end apart: 19 -> 17, of which waited for: 9 -> 9; matrix products, arithmetic and copies ran while one was open for 1% -> 1% of each run, Pallas kernels for 7% -> 9%
where the time goes in v2:
time: 129 us
  waiting for transfers between devices  59.8 us (46%)
  starting transfers between devices  40.9 us (32%)
  Pallas kernels  23.1 us (18%)
  local copies, waits for them, and re-layouts  3.98 us (3%)
    ppermute x10, waiting for transfers between devices, shift(): lax.ppermute(x, 'tensor', [(i, (i + by) % count) for i in range(count)])  33.2 us
    ppermute x10, starting transfers between devices, shift(): lax.ppermute(x, 'tensor', [(i, (i + by) % count) for i in range(count)])  23.6 us
    all_to_all x2, waiting for transfers between devices, body(): lax.all_to_all(sent, 'dp', split_axis=0, concat_axis=0, tiled=True)  15 us
    ppermute x4, waiting for transfers between devices, swap(): return lax.ppermute(x, 'dp', [(i, i ^ mask) for i in range(count)])  11.6 us
    pallas_call x2, Pallas kernels, features(): pl.pallas_call(kernel, in_specs=[VMEM] * n_t + [pl.BlockSpec(memory_space...  10.5 us
    all_to_all x2, starting transfers between devices, body(): lax.all_to_all(sent, 'dp', split_axis=0, concat_axis=0, tiled=True)  8.01 us
    all_to_all x1, starting transfers between devices, body(): teach = lax.all_to_all(teach, 'dp', split_axis=0, concat_axis=0, tiled=True)  5.31 us
    unnamed x31, local copies, waits for them, and re-layouts  3.98 us
  transfers between devices with their start and end apart: 17, of which 9 were waited for; matrix products, arithmetic and copies ran while one was open for 1% of the time, Pallas kernels for 9%

profile of v2, /device:TPU:0, one launch (start us, length us, event | category | flops | bytes accessed | tf_op | source)
XLA Modules:
  0.0 128.7 jit_solution(4089383578608103332)
XLA Ops:
  0.6 3.1 %prepare.1 = (bf16[96,2304]{1,0:T(8,128)(2,1)}, bf16[96,2304]{1,0:T(8,128)(2,1)}, bf16[48,2048]{1,0:T(8,128)(2,1)}, bf16[16,128]{1,0:T(8,128)(2,1)}, bf16[16,204...) custom-call(s32[1,128]{1,0:T(1,128)} %bitcast.3, bf16[128,4096]{1,0:T(8,128)(2,1)} %t_ref.1, ...), custom_call_target="tpu_custom_call" | custom-call | bytes 1024 | tf_op jit(solution)/shard_map/prepare/pallas_call | solution.py:109
  3.8 5.3 %all-to-all-start = ((bf16[8,128,512]{2,1,0:T(8,128)(2,1)}), bf16[8,128,512]{2,1,0:T(8,128)(2,1)S(1)}, u32[]{:S(2)}, u32[]{:S(2)}) async-start(bf16[8,128,512]{2,1,0:T(8,128)(2,1)} %get-tuple-element.23), calls=%async_computation | async-start | bytes 2097152 | tf_op jit(solution)/shard_map/all_to_all | solution.py:368
  9.1 1.6 %collective-permute-start = (bf16[96,2304]{1,0:T(8,128)(2,1)S(1)}, bf16[96,2304]{1,0:T(8,128)(2,1)S(1)}, u32[]{:S(2)}, u32[]{:S(2)}) collective-permute-start(bf16[96,2304]{1,0:T(8,128)(2,1)S(1)} %copy-done.7), channel_id=1, source_target_pairs={{0,1},{1,2},{2,3},{3,0},{4,5},{5,6},{6,7},{7,4},{8,9},{9,10},{10,1... | collective-permute-start | bytes 1327112 | tf_op jit(solution)/shard_map/ppermute | solution.py:32
  10.7 2.2 %collective-permute-start.2 = (bf16[96,2304]{1,0:T(8,128)(2,1)S(1)}, bf16[96,2304]{1,0:T(8,128)(2,1)S(1)}, u32[]{:S(2)}, u32[]{:S(2)}) collective-permute-start(bf16[96,2304]{1,0:T(8,128)(2,1)S(1)} %copy-done.13), channel_id=1, source_target_pairs={{0,3},{1,0},{2,1},{3,2},{4,7},{5,4},{6,5},{7,6},{8,11},{9,8},{10,9... | collective-permute-start | bytes 1327112 | tf_op jit(solution)/shard_map/ppermute | solution.py:32
  13.0 11.0 %collective-permute-done.refs_1_ = bf16[96,2304]{1,0:T(8,128)(2,1)S(1)} collective-permute-done((bf16[96,2304]{1,0:T(8,128)(2,1)S(1)}, bf16[96,2304]{1,0:T(8,128)(2,1)S(1)}, u32[]{:S(2)}, u32[]{:S(2)}) %collective-permute-start) | collective-permute-done | bytes 442400 | tf_op jit(solution)/shard_map/ppermute | solution.py:32
  24.0 11.1 %collective-permute-start.3 = (bf16[16,2048]{1,0:T(8,128)(2,1)S(1)}, bf16[16,2048]{1,0:T(8,128)(2,1)S(1)}, u32[]{:S(2)}, u32[]{:S(2)}) collective-permute-start(bf16[16,2048]{1,0:T(8,128)(2,1)S(1)} %copy-done.14), channel_id=1, source_target_pairs={{0,2},{1,3},{2,0},{3,1},{4,6},{5,7},{6,4},{7,5},{8,10},{9,11},{10,... | collective-permute-start | bytes 196616 | tf_op jit(solution)/shard_map/ppermute | solution.py:32
  35.1 10.2 %collective-permute-done.3.refs_2_ = bf16[16,2048]{1,0:T(8,128)(2,1)S(1)} collective-permute-done((bf16[16,2048]{1,0:T(8,128)(2,1)S(1)}, bf16[16,2048]{1,0:T(8,128)(2,1)S(1)}, u32[]{:S(2)}, u32[]{:S(2)}) %collective-permute-start.3) | collective-permute-done | bytes 65568 | tf_op jit(solution)/shard_map/ppermute | solution.py:32
  45.4 1.7 %collective-permute-start.4 = (bf16[64,2048]{1,0:T(8,128)(2,1)S(1)}, bf16[64,2048]{1,0:T(8,128)(2,1)S(1)}, u32[]{:S(2)}, u32[]{:S(2)}) collective-permute-start(bf16[64,2048]{1,0:T(8,128)(2,1)S(1)} %stack_rows.2.refs_0_), channel_id=1, source_target_pairs={{0,8},{4,12},{8,0},{12,4},{16,24},{20,28},{24,16},{28,20},{1,9},{5... | collective-permute-start | bytes 786440 | tf_op jit(solution)/shard_map/ppermute | solution.py:36
  47.1 1.5 %collective-permute-start.5 = (bf16[64,2048]{1,0:T(8,128)(2,1)S(1)}, bf16[64,2048]{1,0:T(8,128)(2,1)S(1)}, u32[]{:S(2)}, u32[]{:S(2)}) collective-permute-start(bf16[64,2048]{1,0:T(8,128)(2,1)S(1)} %stack_rows.2.refs_0_), channel_id=1, source_target_pairs={{0,16},{4,20},{8,24},{12,28},{16,0},{20,4},{24,8},{28,12},{1,17},{... | collective-permute-start | bytes 786440 | tf_op jit(solution)/shard_map/ppermute | solution.py:36
  48.6 0.4 collective-permute-start.6
  48.9 5.7 %collective-permute-done.4.refs_1_ = bf16[64,2048]{1,0:T(8,128)(2,1)S(1)} collective-permute-done((bf16[64,2048]{1,0:T(8,128)(2,1)S(1)}, bf16[64,2048]{1,0:T(8,128)(2,1)S(1)}, u32[]{:S(2)}, u32[]{:S(2)}) %collective-permute-start.4) | collective-permute-done | bytes 262176 | tf_op jit(solution)/shard_map/ppermute | solution.py:36
  54.6 5.9 %collective-permute-done.5.refs_2_ = bf16[64,2048]{1,0:T(8,128)(2,1)S(1)} collective-permute-done((bf16[64,2048]{1,0:T(8,128)(2,1)S(1)}, bf16[64,2048]{1,0:T(8,128)(2,1)S(1)}, u32[]{:S(2)}, u32[]{:S(2)}) %collective-permute-start.5) | collective-permute-done | bytes 262176 | tf_op jit(solution)/shard_map/ppermute | solution.py:36
  60.7 0.7 copy-done.3
  61.3 1.0 copy-done
  62.3 5.2 %first_features.1 = (bf16[8,80,1280]{2,1,0:T(8,128)(2,1)}, f32[80,256]{1,0:T(8,128)}) custom-call(bf16[96,2304]{1,0:T(8,128)(2,1)} %get-tuple-element.18.refs_0_, bf16[96,2304]{1,0:T(8,128)(2,1)} %copy-done.1, bf16[96,2304]{1,0:T(8,128)(2,1)} %copy-done.3, bf16[96,2304]{1,0:T(8,128)(2,1)} %copy-done.2, bf16[8192,128]{1,0:T(8,128)(2,1)} %refs_4_.3, ...), custom_call_target="tpu_custom_call" | custom-call | bytes 1024 | tf_op jit(solution)/shard_map/first_features/pallas_call | solution.py:248
  67.6 3.7 %all-to-all-start.1 = ((bf16[8,80,1280]{2,1,0:T(8,128)(2,1)}), bf16[8,80,1280]{2,1,0:T(8,128)(2,1)S(1)}, u32[]{:S(2)}, u32[]{:S(2)}) async-start(bf16[8,80,1280]{2,1,0:T(8,128)(2,1)} %get-tuple-element.24), calls=%async_computation.1 | async-start | bytes 3276800 | tf_op jit(solution)/shard_map/all_to_all | solution.py:379
  71.3 0.4 collective-permute-start.10
  71.7 3.8 %collective-permute-start.9 = (bf16[48,2048]{1,0:T(8,128)(2,1)S(1)}, bf16[48,2048]{1,0:T(8,128)(2,1)S(1)}, u32[]{:S(2)}, u32[]{:S(2)}) collective-permute-start(bf16[48,2048]{1,0:T(8,128)(2,1)S(1)} %copy-done.8), channel_id=1, source_target_pairs={{0,3},{1,0},{2,1},{3,2},{4,7},{5,4},{6,5},{7,6},{8,11},{9,8},{10,9... | collective-permute-start | bytes 589832 | tf_op jit(solution)/shard_map/ppermute | solution.py:32
  75.5 5.8 %collective-permute-done.7.refs_1_ = bf16[48,2048]{1,0:T(8,128)(2,1)S(1)} collective-permute-done((bf16[48,2048]{1,0:T(8,128)(2,1)S(1)}, bf16[48,2048]{1,0:T(8,128)(2,1)S(1)}, u32[]{:S(2)}, u32[]{:S(2)}) %collective-permute-start.7) | collective-permute-done | bytes 196640 | tf_op jit(solution)/shard_map/ppermute | solution.py:32
  81.3 1.6 %collective-permute-done.9.refs_2_.refs_3_ = bf16[48,2048]{1,0:T(8,128)(2,1)S(1)} collective-permute-done((bf16[48,2048]{1,0:T(8,128)(2,1)S(1)}, bf16[48,2048]{1,0:T(8,128)(2,1)S(1)}, u32[]{:S(2)}, u32[]{:S(2)}) %collective-permute-start.9) | collective-permute-done | bytes 196640 | tf_op jit(solution)/shard_map/ppermute | solution.py:32
  82.9 0.7 copy-done.6
  83.6 3.2 %partial_products.1 = (f32[128,128]{1,0:T(8,128)}, f32[128,128]{1,0:T(8,128)}, f32[128,128]{1,0:T(8,128)}, f32[128,128]{1,0:T(8,128)}) custom-call(bf16[256,2048]{1,0:T(8,128)(2,1)} %copy-done, bf16[256,2048]{1,0:T(8,128)(2,1)} %collective-permute-done.10.far_ref, bf16[128,2048]{1,0:T(8,128)(2,1)} %s_ref.3, bf16[128,2048]{1,0:T(8,128)(2,1)} %p_ref.3, ...), custom_call_target="tpu_custom_call" | custom-call | bytes 1024 | tf_op jit(solution)/shard_map/partial_products/pallas_call | solution.py:161
  86.8 2.6 %collective-permute-start.11 = (f32[128,128]{1,0:T(8,128)}, f32[128,128]{1,0:T(8,128)S(1)}, u32[]{:S(2)}, u32[]{:S(2)}) collective-permute-start(f32[128,128]{1,0:T(8,128)} %get-tuple-element.28), channel_id=1, source_target_pairs={{0,3},{1,0},{2,1},{3,2},{4,7},{5,4},{6,5},{7,6},{8,11},{9,8},{10,9... | collective-permute-start | bytes 196616 | tf_op jit(solution)/shard_map/ppermute | solution.py:32
  89.6 2.0 %collective-permute-start.13 = (f32[128,128]{1,0:T(8,128)}, f32[128,128]{1,0:T(8,128)S(1)}, u32[]{:S(2)}, u32[]{:S(2)}) collective-permute-start(f32[128,128]{1,0:T(8,128)} %get-tuple-element.30), channel_id=1, source_target_pairs={{0,1},{1,2},{2,3},{3,0},{4,5},{5,6},{6,7},{7,4},{8,9},{9,10},{10,1... | collective-permute-start | bytes 196616 | tf_op jit(solution)/shard_map/ppermute | solution.py:32
  91.9 4.4 %collective-permute-done.12.refs_9_ = f32[128,128]{1,0:T(8,128)S(1)} collective-permute-done((f32[128,128]{1,0:T(8,128)}, f32[128,128]{1,0:T(8,128)S(1)}, u32[]{:S(2)}, u32[]{:S(2)}) %collective-permute-start.12) | collective-permute-done | bytes 65568 | tf_op jit(solution)/shard_map/ppermute | solution.py:32
  96.3 0.6 copy-done.11
  97.0 5.3 %last_features.1 = bf16[8,48,1792]{2,1,0:T(8,128)(2,1)} custom-call(bf16[48,2048]{1,0:T(8,128)(2,1)} %get-tuple-element.25.refs_0_, bf16[48,2048]{1,0:T(8,128)(2,1)} %copy-done.5, bf16[48,2048]{1,0:T(8,128)(2,1)} %copy-done.9, bf16[48,2048]{1,0:T(8,128)(2,1)} %copy-done.6, bf16[8192,128]{1,0:T(8,128)(2,1)} %refs_4_.3, bf16[8192,128]{1,0:T(8,128)(2,1)} %refs_5_.3, ...), custom_call_target="tpu_custom_call" | custom-call | bytes 1024 | tf_op jit(solution)/shard_map/last_features/pallas_call | solution.py:248
  102.3 4.3 %all-to-all-start.2 = ((bf16[8,48,1792]{2,1,0:T(8,128)(2,1)}), bf16[8,48,1792]{2,1,0:T(8,128)(2,1)}, u32[]{:S(2)}, u32[]{:S(2)}) async-start(bf16[8,48,1792]{2,1,0:T(8,128)(2,1)} %last_features.1), calls=%async_computation.2 | async-start | bytes 2752512 | tf_op jit(solution)/shard_map/all_to_all | solution.py:389
  106.6 3.0 %projector.1 = f32[128,512]{1,0:T(8,128)S(1)} custom-call(bf16[8,80,1280]{2,1,0:T(8,128)(2,1)S(1)} %all-to-all-done.1.came_ref.first_ref, bf16[8,128,512]{2,1,0:T(8,128)(2,1)S(1)} %all-to-all-done.refs_4_.teach_ref), custom_call_target="tpu_custom_call" | custom-call | bytes 1024 | tf_op jit(solution)/shard_map/projector/pallas_call | solution.py:301
  109.6 1.0 copy.11
  110.6 15.0 %all-to-all-done.2.last_ref = bf16[8,48,1792]{2,1,0:T(8,128)(2,1)} async-done(((bf16[8,48,1792]{2,1,0:T(8,128)(2,1)}), bf16[8,48,1792]{2,1,0:T(8,128)(2,1)}, u32[]{:S(2)}, u32[]{:S(2)}) %all-to-all-start.2) | async-done | bytes 1376288 | tf_op jit(solution)/shard_map/all_to_all | solution.py:389
  125.5 3.1 %final_product.1 = (f32[128,1024]{1,0:T(8,128)}, f32[128,1024]{1,0:T(8,128)}) custom-call(bf16[8,80,1280]{2,1,0:T(8,128)(2,1)S(1)} %all-to-all-done.1.came_ref.first_ref, bf16[8,48,1792]{2,1,0:T(8,128)(2,1)} %all-to-all-done.2.last_ref), custom_call_target="tpu_custom_call" | custom-call | bytes 1024 | tf_op jit(solution)/shard_map/final_product/pallas_call | solution.py:341
  (41 shorter events, 0.7 us)
Async XLA Ops:
  3.7 5.4 %copy-start.7 = (bf16[96,2304]{1,0:T(8,128)(2,1)S(1)}, bf16[96,2304]{1,0:T(8,128)(2,1)}, u32[]{:S(2)}) copy-start(bf16[96,2304]{1,0:T(8,128)(2,1)} %get-tuple-element.18.refs_0_) | copy-start | bytes 1327108
  3.8 7.0 %copy-start.13 = (bf16[96,2304]{1,0:T(8,128)(2,1)S(1)}, bf16[96,2304]{1,0:T(8,128)(2,1)}, u32[]{:S(2)}) copy-start(bf16[96,2304]{1,0:T(8,128)(2,1)} %get-tuple-element.19) | copy-start | bytes 1327108
  3.8 20.2 %copy-start.14 = (bf16[16,2048]{1,0:T(8,128)(2,1)S(1)}, bf16[16,2048]{1,0:T(8,128)(2,1)}, u32[]{:S(2)}) copy-start(bf16[16,2048]{1,0:T(8,128)(2,1)} %get-tuple-element.22) | copy-start | bytes 196612
  3.8 41.5 %copy-start.4 = (bf16[16,2048]{1,0:T(8,128)(2,1)S(1)}, bf16[16,2048]{1,0:T(8,128)(2,1)}, u32[]{:S(2)}) copy-start(bf16[16,2048]{1,0:T(8,128)(2,1)} %get-tuple-element.21.refs_0_) | copy-start | bytes 196612
  3.8 56.8 %all-to-all-start = ((bf16[8,128,512]{2,1,0:T(8,128)(2,1)}), bf16[8,128,512]{2,1,0:T(8,128)(2,1)S(1)}, u32[]{:S(2)}, u32[]{:S(2)}) async-start(bf16[8,128,512]{2,1,0:T(8,128)(2,1)} %get-tuple-element.23), calls=%async_computation | async-start | bytes 2097152 | tf_op jit(solution)/shard_map/all_to_all | solution.py:368
  9.1 14.9 %collective-permute-start = (bf16[96,2304]{1,0:T(8,128)(2,1)S(1)}, bf16[96,2304]{1,0:T(8,128)(2,1)S(1)}, u32[]{:S(2)}, u32[]{:S(2)}) collective-permute-start(bf16[96,2304]{1,0:T(8,128)(2,1)S(1)} %copy-done.7), channel_id=1, source_target_pairs={{0,1},{1,2},{2,3},{3,0},{4,5},{5,6},{6,7},{7,4},{8,9},{9,10},{10,1... | collective-permute-start | bytes 1327112 | tf_op jit(solution)/shard_map/ppermute | solution.py:32
  10.7 34.6 %collective-permute-start.2 = (bf16[96,2304]{1,0:T(8,128)(2,1)S(1)}, bf16[96,2304]{1,0:T(8,128)(2,1)S(1)}, u32[]{:S(2)}, u32[]{:S(2)}) collective-permute-start(bf16[96,2304]{1,0:T(8,128)(2,1)S(1)} %copy-done.13), channel_id=1, source_target_pairs={{0,3},{1,0},{2,1},{3,2},{4,7},{5,4},{6,5},{7,6},{8,11},{9,8},{10,9... | collective-permute-start | bytes 1327112 | tf_op jit(solution)/shard_map/ppermute | solution.py:32
  24.0 36.7 %copy-start.1 = (bf16[96,2304]{1,0:T(8,128)(2,1)}, bf16[96,2304]{1,0:T(8,128)(2,1)S(1)}, u32[]{:S(2)}) copy-start(bf16[96,2304]{1,0:T(8,128)(2,1)S(1)} %collective-permute-done.refs_1_) | copy-start | bytes 1327108
  24.0 36.6 %collective-permute-start.1 = (bf16[96,2304]{1,0:T(8,128)(2,1)S(1)}, bf16[96,2304]{1,0:T(8,128)(2,1)S(1)}, u32[]{:S(2)}, u32[]{:S(2)}) collective-permute-start(bf16[96,2304]{1,0:T(8,128)(2,1)S(1)} %collective-permute-done.refs_1_), channel_id=1, source_target_pairs={{0,1},{1,2},{2,3},{3,0},{4,5},{5,6},{6,7},{7,4},{8,9},{9,10},{10,1... | collective-permute-start | bytes 1327112 | tf_op jit(solution)/shard_map/ppermute | solution.py:32
  24.0 21.3 %collective-permute-start.3 = (bf16[16,2048]{1,0:T(8,128)(2,1)S(1)}, bf16[16,2048]{1,0:T(8,128)(2,1)S(1)}, u32[]{:S(2)}, u32[]{:S(2)}) collective-permute-start(bf16[16,2048]{1,0:T(8,128)(2,1)S(1)} %copy-done.14), channel_id=1, source_target_pairs={{0,2},{1,3},{2,0},{3,1},{4,6},{5,7},{6,4},{7,5},{8,10},{9,11},{10,... | collective-permute-start | bytes 196616 | tf_op jit(solution)/shard_map/ppermute | solution.py:32
  45.3 15.3 %copy-start.2 = (bf16[96,2304]{1,0:T(8,128)(2,1)}, bf16[96,2304]{1,0:T(8,128)(2,1)S(1)}, u32[]{:S(2)}) copy-start(bf16[96,2304]{1,0:T(8,128)(2,1)S(1)} %collective-permute-done.2.refs_3_) | copy-start | bytes 1327108
  45.4 9.2 %collective-permute-start.4 = (bf16[64,2048]{1,0:T(8,128)(2,1)S(1)}, bf16[64,2048]{1,0:T(8,128)(2,1)S(1)}, u32[]{:S(2)}, u32[]{:S(2)}) collective-permute-start(bf16[64,2048]{1,0:T(8,128)(2,1)S(1)} %stack_rows.2.refs_0_), channel_id=1, source_target_pairs={{0,8},{4,12},{8,0},{12,4},{16,24},{20,28},{24,16},{28,20},{1,9},{5... | collective-permute-start | bytes 786440 | tf_op jit(solution)/shard_map/ppermute | solution.py:36
  47.1 13.5 %collective-permute-start.5 = (bf16[64,2048]{1,0:T(8,128)(2,1)S(1)}, bf16[64,2048]{1,0:T(8,128)(2,1)S(1)}, u32[]{:S(2)}, u32[]{:S(2)}) collective-permute-start(bf16[64,2048]{1,0:T(8,128)(2,1)S(1)} %stack_rows.2.refs_0_), channel_id=1, source_target_pairs={{0,16},{4,20},{8,24},{12,28},{16,0},{20,4},{24,8},{28,12},{1,17},{... | collective-permute-start | bytes 786440 | tf_op jit(solution)/shard_map/ppermute | solution.py:36
  48.6 12.0 %collective-permute-start.6 = (bf16[64,2048]{1,0:T(8,128)(2,1)S(1)}, bf16[64,2048]{1,0:T(8,128)(2,1)S(1)}, u32[]{:S(2)}, u32[]{:S(2)}) collective-permute-start(bf16[64,2048]{1,0:T(8,128)(2,1)S(1)} %stack_rows.2.refs_0_), channel_id=1, source_target_pairs={{0,24},{4,28},{8,16},{12,20},{16,8},{20,12},{24,0},{28,4},{1,25},{... | collective-permute-start | bytes 786440 | tf_op jit(solution)/shard_map/ppermute | solution.py:36
  60.5 0.8 copy-start.3
  61.3 1.0 copy-start
  67.6 4.2 %copy-start.8 = (bf16[48,2048]{1,0:T(8,128)(2,1)S(1)}, bf16[48,2048]{1,0:T(8,128)(2,1)}, u32[]{:S(2)}) copy-start(bf16[48,2048]{1,0:T(8,128)(2,1)} %get-tuple-element.25.refs_0_) | copy-start | bytes 589828
  67.6 34.7 %all-to-all-start.1 = ((bf16[8,80,1280]{2,1,0:T(8,128)(2,1)}), bf16[8,80,1280]{2,1,0:T(8,128)(2,1)S(1)}, u32[]{:S(2)}, u32[]{:S(2)}) async-start(bf16[8,80,1280]{2,1,0:T(8,128)(2,1)} %get-tuple-element.24), calls=%async_computation.1 | async-start | bytes 3276800 | tf_op jit(solution)/shard_map/all_to_all | solution.py:379
  71.3 11.6 %collective-permute-start.10 = (bf16[256,2048]{1,0:T(8,128)(2,1)}, bf16[256,2048]{1,0:T(8,128)(2,1)}, u32[]{:S(2)}, u32[]{:S(2)}) collective-permute-start(bf16[256,2048]{1,0:T(8,128)(2,1)} %copy-done), channel_id=1, source_target_pairs={{0,4},{4,0},{8,12},{12,8},{16,20},{20,16},{24,28},{28,24},{1,5},{5... | collective-permute-start | bytes 3145736 | tf_op jit(solution)/shard_map/ppermute | solution.py:36
  71.7 9.6 %collective-permute-start.7 = (bf16[48,2048]{1,0:T(8,128)(2,1)S(1)}, bf16[48,2048]{1,0:T(8,128)(2,1)S(1)}, u32[]{:S(2)}, u32[]{:S(2)}) collective-permute-start(bf16[48,2048]{1,0:T(8,128)(2,1)S(1)} %copy-done.8), channel_id=1, source_target_pairs={{0,1},{1,2},{2,3},{3,0},{4,5},{5,6},{6,7},{7,4},{8,9},{9,10},{10,1... | collective-permute-start | bytes 589832 | tf_op jit(solution)/shard_map/ppermute | solution.py:32
  71.7 11.2 %collective-permute-start.9 = (bf16[48,2048]{1,0:T(8,128)(2,1)S(1)}, bf16[48,2048]{1,0:T(8,128)(2,1)S(1)}, u32[]{:S(2)}, u32[]{:S(2)}) collective-permute-start(bf16[48,2048]{1,0:T(8,128)(2,1)S(1)} %copy-done.8), channel_id=1, source_target_pairs={{0,3},{1,0},{2,1},{3,2},{4,7},{5,4},{6,5},{7,6},{8,11},{9,8},{10,9... | collective-permute-start | bytes 589832 | tf_op jit(solution)/shard_map/ppermute | solution.py:32
  81.3 1.6 %copy-start.5 = (bf16[48,2048]{1,0:T(8,128)(2,1)}, bf16[48,2048]{1,0:T(8,128)(2,1)S(1)}, u32[]{:S(2)}) copy-start(bf16[48,2048]{1,0:T(8,128)(2,1)S(1)} %collective-permute-done.7.refs_1_) | copy-start | bytes 589828
  81.3 10.4 %collective-permute-start.8 = (bf16[48,2048]{1,0:T(8,128)(2,1)S(1)}, bf16[48,2048]{1,0:T(8,128)(2,1)S(1)}, u32[]{:S(2)}, u32[]{:S(2)}) collective-permute-start(bf16[48,2048]{1,0:T(8,128)(2,1)S(1)} %collective-permute-done.7.refs_1_), channel_id=1, source_target_pairs={{0,1},{1,2},{2,3},{3,0},{4,5},{5,6},{6,7},{7,4},{8,9},{9,10},{10,1... | collective-permute-start | bytes 589832 | tf_op jit(solution)/shard_map/ppermute | solution.py:32
  82.9 0.7 copy-start.6
  86.8 5.1 %collective-permute-start.11 = (f32[128,128]{1,0:T(8,128)}, f32[128,128]{1,0:T(8,128)S(1)}, u32[]{:S(2)}, u32[]{:S(2)}) collective-permute-start(f32[128,128]{1,0:T(8,128)} %get-tuple-element.28), channel_id=1, source_target_pairs={{0,3},{1,0},{2,1},{3,2},{4,7},{5,4},{6,5},{7,6},{8,11},{9,8},{10,9... | collective-permute-start | bytes 196616 | tf_op jit(solution)/shard_map/ppermute | solution.py:32
  89.4 6.9 %collective-permute-start.12 = (f32[128,128]{1,0:T(8,128)}, f32[128,128]{1,0:T(8,128)S(1)}, u32[]{:S(2)}, u32[]{:S(2)}) collective-permute-start(f32[128,128]{1,0:T(8,128)} %get-tuple-element.29), channel_id=1, source_target_pairs={{0,2},{1,3},{2,0},{3,1},{4,6},{5,7},{6,4},{7,5},{8,10},{9,11},{10,... | collective-permute-start | bytes 196616 | tf_op jit(solution)/shard_map/ppermute | solution.py:32
  89.6 6.7 %collective-permute-start.13 = (f32[128,128]{1,0:T(8,128)}, f32[128,128]{1,0:T(8,128)S(1)}, u32[]{:S(2)}, u32[]{:S(2)}) collective-permute-start(f32[128,128]{1,0:T(8,128)} %get-tuple-element.30), channel_id=1, source_target_pairs={{0,1},{1,2},{2,3},{3,0},{4,5},{5,6},{6,7},{7,4},{8,9},{9,10},{10,1... | collective-permute-start | bytes 196616 | tf_op jit(solution)/shard_map/ppermute | solution.py:32
  91.7 4.7 %copy-start.9 = (bf16[48,2048]{1,0:T(8,128)(2,1)}, bf16[48,2048]{1,0:T(8,128)(2,1)S(1)}, u32[]{:S(2)}) copy-start(bf16[48,2048]{1,0:T(8,128)(2,1)S(1)} %collective-permute-done.8.refs_2_) | copy-start | bytes 589828
  91.9 4.4 %copy-start.10 = (f32[128,128]{1,0:T(8,128)}, f32[128,128]{1,0:T(8,128)S(1)}, u32[]{:S(2)}) copy-start(f32[128,128]{1,0:T(8,128)S(1)} %collective-permute-done.11.refs_8_) | copy-start | bytes 196612
  96.3 0.6 copy-start.11
  96.3 0.7 copy-start.12
  102.3 23.2 %all-to-all-start.2 = ((bf16[8,48,1792]{2,1,0:T(8,128)(2,1)}), bf16[8,48,1792]{2,1,0:T(8,128)(2,1)}, u32[]{:S(2)}, u32[]{:S(2)}) async-start(bf16[8,48,1792]{2,1,0:T(8,128)(2,1)} %last_features.1), calls=%async_computation.2 | async-start | bytes 2752512 | tf_op jit(solution)/shard_map/all_to_all | solution.py:389

commit v3 on v2

v3 whole, which is shorter than its diff:
```python
import functools
import math

import jax
import jax.numpy as jnp
from jax import lax
from jax.experimental import pallas as pl
from jax.experimental.pallas import tpu as pltpu
from jax.sharding import PartitionSpec as P

PB = 128
LANES = 128
GROUP = 8
MIB = 1 << 20

VMEM = pl.BlockSpec(memory_space=pltpu.VMEM)


def params(mib):
    return pltpu.CompilerParams(vmem_limit_bytes=mib * MIB)


def room(*arrays):
    total = 0
    for a in arrays:
        lanes = pl.cdiv(a.shape[-1], LANES) * LANES
        total += math.prod(a.shape[:-1]) * lanes * jnp.dtype(a.dtype).itemsize
    return params(total // MIB + 5)


def cost(flops, nbytes):
    return pl.CostEstimate(flops=int(flops), bytes_accessed=int(nbytes), transcendentals=0)


def struct(shape, dtype=jnp.bfloat16):
    return jax.ShapeDtypeStruct(shape, dtype)


def shift(x, count, by):
    return lax.ppermute(x, "tensor", [(i, (i + by) % count) for i in range(count)])


def hop(x, pairs):
    return lax.ppermute(x, "tensor", pairs)


def swap(x, count, mask):
    return lax.ppermute(x, "dp", [(i, i ^ mask) for i in range(count)])


def contract_rows(left, right):
    return lax.dot_general(
        left, right, (((0,), (0,)), ((), ())), preferred_element_type=jnp.float32
    )


def contract_cols(left, right):
    return lax.dot_general(
        left, right, (((1,), (1,)), ((), ())), preferred_element_type=jnp.float32
    )


def scaled_difference(student, projected, factor):
    wide = student.astype(jnp.float32) - projected.astype(jnp.float32)
    return (wide * factor).astype(jnp.bfloat16)


def prepare(row_map, teacher, mlp_input, student, projected, down, n_dp, n_t, factor):
    tok, width = mlp_input.shape
    rows = down.shape[0] // GROUP
    wide = teacher.shape[1] // n_dp
    hbm = pl.BlockSpec(memory_space=pltpu.HBM)
    if wide % LANES:
        blocks = teacher.reshape(tok, n_dp, wide).transpose(1, 0, 2)
        numbers = jnp.stack([row_map // LANES, row_map % LANES]).astype(jnp.bfloat16)
        numbers = jnp.broadcast_to(numbers.reshape(1, -1, wide), (n_dp, 2 * tok // wide, wide))
        blocks = jnp.concatenate([blocks, numbers], axis=1)
        wide = 0

    def kernel(m_ref, t_ref, x_ref, s_ref, p_ref, d_ref, own_ref, *refs):
        pieces, outs = refs[:n_t], refs[n_t:-4]
        s_buf, p_buf, m_buf, sems = refs[-4:]
        row = pl.multiple_of((lax.axis_index("dp") % GROUP) * rows, rows)
        pairs = [
            (s_ref.at[:, :PB], s_buf),
            (p_ref.at[:, :PB], p_buf),
            (m_ref, m_buf),
            (x_ref, own_ref.at[:, :width]),
        ]
        for k in range(n_t):
            col = pl.multiple_of(((lax.axis_index("tensor") + k) % n_t) * width, width)
            pairs.append((d_ref.at[pl.ds(row, rows), pl.ds(col, width)], pieces[k]))
        if wide:
            for i in range(n_dp):
                pairs.append((t_ref.at[:, i * wide : (i + 1) * wide], outs[0].at[i, :tok]))
        copies = [
            pltpu.make_async_copy(src, dst, sems.at[i]) for i, (src, dst) in enumerate(pairs)
        ]
        for c in copies:
            c.start()
        for c in copies[:3]:
            c.wait()
        own_ref[:, width:] = scaled_difference(s_buf[...], p_buf[...], factor)
        line = lax.broadcasted_iota(jnp.int32, (16, tok), 0)
        number = jnp.broadcast_to(m_buf[...], (16, tok))
        high, low = number // LANES, number % LANES
        digits = jnp.where(line == 0, high, jnp.where(line == 1, low, 0))
        digits = digits.astype(jnp.float32).astype(jnp.bfloat16)
        if wide:
            for i in range(n_dp):
                outs[0][i, tok:, :] = jnp.zeros((16, wide), jnp.bfloat16)
                outs[0][i, tok:, :tok] = digits
        for c in copies[3:]:
            c.wait()

    shapes = [(tok, width + PB)] + [(rows, width)] * n_t
    if wide:
        shapes.append((n_dp, tok + 16, wide))
    out = pl.pallas_call(
        kernel,
        in_specs=[hbm] * 6,
        out_specs=[VMEM] * len(shapes),
        out_shape=[struct(s) for s in shapes],
        scratch_shapes=[
            pltpu.VMEM((tok, PB), jnp.bfloat16),
            pltpu.VMEM((tok, PB), jnp.bfloat16),
            pltpu.VMEM((1, tok), jnp.int32),
            pltpu.SemaphoreType.DMA((4 + n_t + n_dp,)),
        ],
        compiler_params=params(60),
        cost_estimate=cost(0, 1024),
        name="prepare",
    )(row_map.reshape(1, tok), teacher, mlp_input, student, projected, down)
    return out if wide else [*out, blocks]


def stack_rows(parts, rows, width, after=()):
    def kernel(*refs):
        out_ref = refs[-1]
        for i, ref in enumerate(refs[: len(parts)]):
            out_ref[i * rows : (i + 1) * rows] = ref[ref.shape[0] - rows :, :width]

    return pl.pallas_call(
        kernel,
        in_specs=[VMEM] * len(parts) + [pl.BlockSpec(memory_space=pl.ANY)] * len(after),
        out_specs=VMEM,
        out_shape=struct((len(parts) * rows, width)),
        compiler_params=room(*parts),
        cost_estimate=cost(0, 1024),
        name="stack_rows",
    )(*parts, *after)


def ordered(x, *after):
    def kernel(*refs):
        pass

    return pl.pallas_call(
        kernel,
        in_specs=[pl.BlockSpec(memory_space=pl.ANY)] * (1 + len(after)),
        out_specs=pl.BlockSpec(memory_space=pl.ANY),
        out_shape=struct(x.shape, x.dtype),
        input_output_aliases={0: 0},
        compiler_params=params(1),
        cost_estimate=cost(0, 1024),
        name="ordered",
    )(x, *after)


def partial_products(near, far, student, projected, n_t, rows, factor, after):
    tok, width = student.shape
    hb = rows * GROUP
    half = GROUP // 2

    def kernel(near_ref, far_ref, s_ref, p_ref, *refs):
        outs = refs[len(after) :]
        err = scaled_difference(s_ref[...], p_ref[...], factor)
        place = lax.axis_index("dp") % GROUP
        for side, ref in enumerate((near_ref, far_ref)):
            product = contract_cols(ref[...], err)
            for j in range(half):
                row = pl.multiple_of((place ^ (2 * j + side)) * rows, rows)
                for k in range(n_t):
                    at = (j * n_t + k) * rows
                    outs[k][pl.ds(row, rows), :] = product[at : at + rows]

    return pl.pallas_call(
        kernel,
        in_specs=[VMEM] * 4
        + [pl.BlockSpec(memory_space=pl.ANY)] * len(after),
        out_specs=[VMEM] * n_t,
        out_shape=[struct((hb, tok), jnp.float32)] * n_t,
        compiler_params=room(near, near, far, student, projected, student),
        cost_estimate=cost(0, 1024),
        name="partial_products",
    )(near, far, student, projected, *after)


def weight_copies(gate_ref, up_ref, w_ref, sems, slots, width):
    hb = gate_ref.shape[1]
    copies = []
    for i, slot in enumerate(slots):
        at = pl.ds(pl.multiple_of(slot * width, width), width)
        for j, ref in enumerate((gate_ref, up_ref)):
            dst = w_ref.at[i, :, j * hb : (j + 1) * hb]
            copies.append(pltpu.make_async_copy(ref.at[at], dst, sems.at[2 * i + j]))
    return copies


def place_slices(slices, places, width, n_t, n_dp):
    count = slices[0].shape[0]
    cols = width * n_t // n_dp
    per = width // cols

    def kernel(*refs):
        out_ref = refs[-1]
        for k, x_ref in zip(places, refs):
            slot = (lax.axis_index("tensor") + n_t - k) % n_t
            for b in range(per):
                out_ref[slot * per + b, :, PB:] = x_ref[:, b * cols : (b + 1) * cols]

            @pl.when(slot == 0)
            def _(x_ref=x_ref):
                for i in range(n_dp):
                    out_ref[i, :, :PB] = x_ref[:, width:]

    return pl.pallas_call(
        kernel,
        in_specs=[VMEM] * len(slices),
        out_specs=VMEM,
        out_shape=struct((n_dp, count, PB + cols)),
        compiler_params=room(*slices, struct((n_dp, count, PB + cols))),
        cost_estimate=cost(0, 1024),
        name="place_slices",
    )(*slices)


def place_last(payload, from_left, from_right, ends, width, n_t, after=()):
    n_dp = payload.shape[0]
    cols = width * n_t // n_dp
    per = width // cols
    aligned = cols % LANES == 0
    hbm = pl.BlockSpec(memory_space=pltpu.HBM)

    def kernel(in_ref, left_ref, right_ref, last_ref, first_ref, *refs):
        out_ref, sems = refs[len(after) :]
        t = lax.axis_index("tensor")
        if not aligned:
            out_ref[...] = in_ref[...]

        def place(ref, slot):
            if not aligned:
                for b in range(per):
                    out_ref[slot * per + b, :, PB:] = ref[:, b * cols : (b + 1) * cols]

                @pl.when(slot == 0)
                def _():
                    for i in range(n_dp):
                        out_ref[i, :, :PB] = ref[:, width:]

                return
            copies = []
            for b in range(per):
                src = ref.at[:, pl.ds(b * cols, cols)]
                dst = out_ref.at[slot * per + b, :, pl.ds(PB, cols)]
                copies.append(pltpu.make_async_copy(src, dst, sems.at[b]))
            for c in copies:
                c.start()

            @pl.when(slot == 0)
            def _():
                extra = []
                for i in range(n_dp):
                    src = ref.at[:, pl.ds(width, PB)]
                    dst = out_ref.at[i, :, pl.ds(0, PB)]
                    extra.append(pltpu.make_async_copy(src, dst, sems.at[per + i]))
                for c in extra:
                    c.start()
                for c in extra:
                    c.wait()

            for c in copies:
                c.wait()

        half = n_t // 2
        for ref, slot, here in (
            (left_ref, t - half, t >= half),
            (right_ref, t + half, t < half),
            (last_ref, 0, t == n_t - 1),
            (first_ref, n_t - 1, t == 0),
        ):
            pl.when(here)(functools.partial(place, ref, slot))

    return pl.pallas_call(
        kernel,
        in_specs=[hbm if aligned else VMEM]
        + [VMEM] * 4
        + [pl.BlockSpec(memory_space=pl.ANY)] * len(after),
        out_specs=hbm if aligned else VMEM,
        out_shape=struct(payload.shape),
        input_output_aliases={0: 0} if aligned else {},
        scratch_shapes=[pltpu.SemaphoreType.DMA((per + n_dp,))],
        compiler_params=room(from_left, from_left, from_left, from_left, *([] if aligned else [payload] * 2)),
        cost_estimate=cost(0, 1024),
        name="place_last",
    )(payload, from_left, from_right, *ends, *after)


def gate_and_up(slices, gate, up, n_t, after):
    count, width, hb = slices[0].shape[0], gate.shape[0] // n_t, gate.shape[1]
    n_s = len(slices)

    def kernel(*refs):
        xs, gate_ref, up_ref = refs[:n_s], refs[n_s], refs[n_s + 1]
        pre_ref, w_ref, sems = refs[-3:]
        t = lax.axis_index("tensor")
        slots = [t, (t + n_t - 1) % n_t, (t + 1) % n_t, (t + n_t // 2) % n_t]
        copies = weight_copies(gate_ref, up_ref, w_ref, sems, slots, width)
        for c in copies:
            c.start()
        left = jnp.where(t == 0, xs[6][:, :width], xs[1][:, :width])
        right = jnp.where(t == n_t - 1, xs[5][:, :width], xs[2][:, :width])
        away = jnp.where(t < n_t // 2, xs[4][:, :width], xs[3][:, :width])
        pre = jnp.zeros((count, 2 * hb), jnp.float32)
        for i, x in enumerate([xs[0][:, :width], left, right, away]):
            copies[2 * i].wait()
            copies[2 * i + 1].wait()
            pre += jnp.dot(x, w_ref[i], preferred_element_type=jnp.float32)
        pre_ref[...] = pre

    return pl.pallas_call(
        kernel,
        in_specs=[VMEM] * n_s
        + [pl.BlockSpec(memory_space=pltpu.HBM)] * 2
        + [pl.BlockSpec(memory_space=pl.ANY)] * len(after),
        out_specs=VMEM,
        out_shape=struct((count, 2 * hb), jnp.float32),
        scratch_shapes=[
            pltpu.VMEM((n_t, width, 2 * hb), jnp.bfloat16),
            pltpu.SemaphoreType.DMA((2 * n_t,)),
        ],
        compiler_params=room(*slices, gate, up, *slices[:2]),
        cost_estimate=cost(0, 1024),
        name="gate_and_up",
    )(*slices, gate, up, *after)


def gradients(pre, acts):
    count, hb = pre.shape[0], pre.shape[1] // 2

    def kernel(pre_ref, *refs):
        act_refs, out_ref = refs[:-1], refs[-1]
        act = act_refs[0][...]
        for ref in act_refs[1:]:
            act += ref[...]
        act = act.T
        gate_pre, up_pre = pre_ref[:, :hb], pre_ref[:, hb:]
        s = jax.nn.sigmoid(gate_pre)
        gate_grad = act * up_pre * s * (1.0 + gate_pre * (1.0 - s))
        up_grad = act * gate_pre * s
        out_ref[:, :hb] = gate_grad.astype(jnp.bfloat16)
        out_ref[:, hb:] = up_grad.astype(jnp.bfloat16)

    return pl.pallas_call(
        kernel,
        in_specs=[VMEM] * (1 + len(acts)),
        out_specs=VMEM,
        out_shape=struct((count, 2 * hb)),
        compiler_params=room(pre, *acts, pre, pre, pre),
        cost_estimate=cost(0, 1024),
        name="gradients",
    )(pre, *acts)


def projector(came, teach, tok):
    n_dp, _, wide = teach.shape
    groups = n_dp // GROUP
    span = GROUP * tok
    digits = teach[:, tok:]
    if wide < tok:
        digits = digits.reshape(n_dp, 2, tok)
        digits = jnp.pad(digits, ((0, 0), (0, 14), (0, 0)))
        teach = teach[:, :tok]

    def kernel(came_ref, teach_ref, digits_ref, out_ref, flipped_ref):
        def flip(g, carry):
            bucket = came_ref[pl.ds(g * GROUP, GROUP), :, :PB].reshape(span, PB)
            flipped_ref[g] = bucket.astype(jnp.float32).T.astype(jnp.bfloat16)
            return carry

        lax.fori_loop(0, groups, flip, 0)
        out_ref[...] = jnp.zeros_like(out_ref)

        def sender(g, carry):
            lines = digits_ref[g, :, :tok].astype(jnp.float32)
            number = (lines[0:1] * float(LANES) + lines[1:2]).astype(jnp.int32)

            def block(h, total):
                token = lax.broadcasted_iota(jnp.int32, (span, tok), 0) + h * span
                picks = (token == number).astype(jnp.float32).astype(jnp.bfloat16)
                return total + jnp.dot(flipped_ref[h], picks, preferred_element_type=jnp.float32)

            rows = lax.fori_loop(0, groups, block, jnp.zeros((PB, tok), jnp.float32))
            out_ref[...] += jnp.dot(
                rows.astype(jnp.bfloat16), teach_ref[g, :tok], preferred_element_type=jnp.float32
            )
            return carry

        lax.fori_loop(0, n_dp, sender, 0)

    return pl.pallas_call(
        kernel,
        in_specs=[VMEM] * 3,
        out_specs=VMEM,
        out_shape=struct((PB, wide), jnp.float32),
        scratch_shapes=[pltpu.VMEM((groups, PB, span), jnp.bfloat16)],
        compiler_params=params(24),
        cost_estimate=cost(0, 1024),
        name="projector",
    )(came, teach, digits)


def final_product(feats, grads, masks):
    n_dp, count = feats.shape[:2]
    hb, cols = grads[0].shape[-1] // 2, feats.shape[2] - PB

    def kernel(feats_ref, *refs):
        grad_refs, (gate_ref, up_ref) = refs[: len(grads)], refs[len(grads) : len(grads) + 2]

        def group(g, total):
            here = pl.ds(g * GROUP, GROUP)
            left = left_ref[here].reshape(GROUP * count, 2 * hb)
            right = feats_ref[here, :, PB:].reshape(GROUP * count, cols)
            return total + contract_rows(left, right)

        total = jnp.zeros((2 * hb, cols), jnp.float32)
        if masks:
            left_ref = refs[-1]
            for mask, ref in zip(masks, grad_refs):
                left_ref[lax.axis_index("dp") ^ mask] = ref[...]
            total = group(0, total)
        else:
            left_ref = grad_refs[0]
            total = lax.fori_loop(0, n_dp // GROUP, group, total)
        gate_ref[...] = total[:hb]
        up_ref[...] = total[hb:]

    return pl.pallas_call(
        kernel,
        in_specs=[VMEM] * (1 + len(grads)),
        out_specs=[VMEM] * 2,
        out_shape=[struct((hb, cols), jnp.float32)] * 2,
        scratch_shapes=[pltpu.VMEM((n_dp, count, 2 * hb), jnp.bfloat16)] if masks else [],
        compiler_params=params(40),
        cost_estimate=cost(0, 1024),
        name="final_product",
    )(feats, *grads)


def body(
    teacher_rows, row_map, student_hidden, projected, mlp_input, gate_bucket, up_bucket, down_bucket
):
    tok = row_map.shape[0]
    n_dp = lax.axis_size("dp")
    n_t = lax.axis_size("tensor")
    hb, width = down_bucket.shape[0], student_hidden.shape[1]
    cols = width * n_t // n_dp
    factor = 1.0 / math.sqrt(tok * n_dp)
    rows = hb // GROUP

    own, *pieces, teach = prepare(
        row_map, teacher_rows, mlp_input, student_hidden, projected, down_bucket, n_dp, n_t, factor
    )
    rightward = [(i, i + 1) for i in range(n_t - 1)]
    leftward = [(i + 1, i) for i in range(n_t - 1)]
    teach = lax.all_to_all(teach, "dp", split_axis=0, concat_axis=0, tiled=True)
    from_left, from_right = hop(own, rightward), hop(own, leftward)
    mine = stack_rows(
        [pieces[0]] + [shift(pieces[k], n_t, k) for k in range(1, n_t)], rows, width
    )
    others = [swap(mine, n_dp, mask) for mask in (2, 4, 6)]

    from_left, from_right = ordered(from_left, mine), ordered(from_right, mine)
    far_left, far_right = hop(from_left, rightward[1:]), hop(from_right, leftward[:-1])
    ends = [hop(far_left, rightward[-1:]), hop(far_right, leftward[:1])]

    near = stack_rows([mine] + others, n_t * rows, width, after=[teach])
    far = swap(near, n_dp, 1)
    partial = partial_products(near, far, student_hidden, projected, n_t, rows, factor, after=[])
    acts = [partial[0]] + [shift(partial[k], n_t, -k) for k in range(1, n_t)]

    sent = place_slices([own, from_left, from_right], [0, 1, n_t - 1], width, n_t, n_dp)
    sent = place_last(sent, far_left, far_right, ends, width, n_t, after=[partial[0]])
    feats = lax.all_to_all(sent, "dp", split_axis=0, concat_axis=0, tiled=True)

    slices = [own, from_left, from_right, far_left, far_right, *ends]
    pre = gate_and_up(slices, gate_bucket, up_bucket, n_t, after=[sent])
    grads = gradients(pre, acts)
    masks = list(range(n_dp)) if n_dp == GROUP else []
    if masks:
        grads = [grads] + [swap(grads, n_dp, mask) for mask in masks[1:]]
    else:
        grads = [lax.all_gather(grads, "dp")]
    grad_proj = projector(feats, teach, tok)
    grad_gate, grad_up = final_product(feats, grads, masks)
    return (grad_proj[:, None, :], grad_gate, grad_up)


def solution(mesh):
    in_specs = (
        P("dp", "tensor"),
        P("dp"),
        P("dp", "tensor"),
        P("dp", "tensor"),
        P("dp", "tensor"),
        P(None, "tensor"),
        P(None, "tensor"),
        P("tensor", None),
    )
    out_specs = (P(None, "tensor", "dp"), P("tensor", "dp"), P("tensor", "dp"))
    return jax.shard_map(body, mesh=mesh, in_specs=in_specs, out_specs=out_specs, check_vma=False)
```

time: 129 us -> 119 us (0.922)
  the two profiles are of different devices: /device:TPU:0 before, /device:TPU:25 now
where the time goes in v3:
time: 119 us; the launch traced here: 118 us
  starting transfers between devices  38.3 us (32%)
  waiting for transfers between devices  37.8 us (32%)
  local copies, waits for them, and re-layouts  22.8 us (19%)
  Pallas kernels  18.5 us (16%)
    unnamed x75, local copies, waits for them, and re-layouts  22.1 us
    ppermute x6, waiting for transfers between devices, shift(): lax.ppermute(x, 'tensor', [(i, (i + by) % count) for i in range(count)])  16.2 us
    ppermute x11, starting transfers between devices, swap(): return lax.ppermute(x, 'dp', [(i, i ^ mask) for i in range(count)])  14.5 us
    ppermute x11, waiting for transfers between devices, swap(): return lax.ppermute(x, 'dp', [(i, i ^ mask) for i in range(count)])  11.9 us
    ppermute x6, waiting for transfers between devices, hop(): return lax.ppermute(x, 'tensor', pairs)  9.61 us
    ppermute x6, starting transfers between devices, hop(): return lax.ppermute(x, 'tensor', pairs)  8.11 us
    ppermute x6, starting transfers between devices, shift(): lax.ppermute(x, 'tensor', [(i, (i + by) % count) for i in range(count)])  6.72 us
    all_to_all x1, starting transfers between devices, body(): teach = lax.all_to_all(teach, 'dp', split_axis=0, concat_axis=0, tiled=True)  4.54 us
  transfers between devices with their start and end apart: 25, of which 6 were waited for; matrix products, arithmetic and copies ran while one was open for 1% of the time, Pallas kernels for 8%

profile of v3, /device:TPU:25, one launch (start us, length us, event | category | flops | bytes accessed | tf_op | source)
XLA Modules:
  0.0 118.4 jit_solution(1377535037571551929)
XLA Ops:
  0.6 2.9 %prepare.1 = (bf16[128,2176]{1,0:T(8,128)(2,1)}, bf16[16,2048]{1,0:T(8,128)(2,1)}, bf16[16,2048]{1,0:T(8,128)(2,1)}, bf16[16,2048]{1,0:T(8,128)(2,1)}, bf16[16,2...) custom-call(s32[1,128]{1,0:T(1,128)} %bitcast.3, bf16[128,4096]{1,0:T(8,128)(2,1)} %t_ref.1, bf16[128,2048]{1,0:T(8,128)(2,1)} %x_ref.1, ...), custom_call_target="tpu_custom_call" | custom-call | bytes 1024 | tf_op jit(solution)/shard_map/prepare/pallas_call | solution.py:119
  3.6 4.5 %all-to-all-start = ((bf16[8,144,512]{2,1,0:T(8,128)(2,1)}), bf16[8,144,512]{2,1,0:T(8,128)(2,1)S(1)}, u32[]{:S(2)}, u32[]{:S(2)}) async-start(bf16[8,144,512]{2,1,0:T(8,128)(2,1)} %get-tuple-element.20), calls=%async_computation | async-start | bytes 2359296 | tf_op jit(solution)/shard_map/all_to_all | solution.py:476
  8.2 2.1 %collective-permute-start.4 = (bf16[128,2176]{1,0:T(8,128)(2,1)S(1)}, bf16[128,2176]{1,0:T(8,128)(2,1)S(1)}, u32[]{:S(2)}, u32[]{:S(2)}) collective-permute-start(bf16[128,2176]{1,0:T(8,128)(2,1)S(1)} %copy-done.6), channel_id=1, source_target_pairs={{1,0},{2,1},{3,2},{5,4},{6,5},{7,6},{9,8},{10,9},{11,10},{13,12},{... | collective-permute-start | bytes 1671176 | tf_op jit(solution)/shard_map/ppermute | solution.py:44
  10.3 1.3 %collective-permute-start = (bf16[128,2176]{1,0:T(8,128)(2,1)S(1)}, bf16[128,2176]{1,0:T(8,128)(2,1)S(1)}, u32[]{:S(2)}, u32[]{:S(2)}) collective-permute-start(bf16[128,2176]{1,0:T(8,128)(2,1)S(1)} %copy-done.6), channel_id=1, source_target_pairs={{0,1},{1,2},{2,3},{4,5},{5,6},{6,7},{8,9},{9,10},{10,11},{12,13},{... | collective-permute-start | bytes 1671176 | tf_op jit(solution)/shard_map/ppermute | solution.py:44
  11.6 1.9 %collective-permute-start.1 = (bf16[16,2048]{1,0:T(8,128)(2,1)S(1)}, bf16[16,2048]{1,0:T(8,128)(2,1)S(1)}, u32[]{:S(2)}, u32[]{:S(2)}) collective-permute-start(bf16[16,2048]{1,0:T(8,128)(2,1)S(1)} %copy-done.36), channel_id=1, source_target_pairs={{0,1},{1,2},{2,3},{3,0},{4,5},{5,6},{6,7},{7,4},{8,9},{9,10},{10,1... | collective-permute-start | bytes 196616 | tf_op jit(solution)/shard_map/ppermute | solution.py:40
  13.5 1.4 %collective-permute-start.2 = (bf16[16,2048]{1,0:T(8,128)(2,1)S(1)}, bf16[16,2048]{1,0:T(8,128)(2,1)S(1)}, u32[]{:S(2)}, u32[]{:S(2)}) collective-permute-start(bf16[16,2048]{1,0:T(8,128)(2,1)S(1)} %copy-done.35), channel_id=1, source_target_pairs={{0,2},{1,3},{2,0},{3,1},{4,6},{5,7},{6,4},{7,5},{8,10},{9,11},{10,... | collective-permute-start | bytes 196616 | tf_op jit(solution)/shard_map/ppermute | solution.py:40
  15.1 12.5 %collective-permute-done.1.refs_1_ = bf16[16,2048]{1,0:T(8,128)(2,1)S(1)} collective-permute-done((bf16[16,2048]{1,0:T(8,128)(2,1)S(1)}, bf16[16,2048]{1,0:T(8,128)(2,1)S(1)}, u32[]{:S(2)}, u32[]{:S(2)}) %collective-permute-start.1) | collective-permute-done | bytes 65568 | tf_op jit(solution)/shard_map/ppermute | solution.py:40
  27.5 3.8 %collective-permute-done.2.refs_2_ = bf16[16,2048]{1,0:T(8,128)(2,1)S(1)} collective-permute-done((bf16[16,2048]{1,0:T(8,128)(2,1)S(1)}, bf16[16,2048]{1,0:T(8,128)(2,1)S(1)}, u32[]{:S(2)}, u32[]{:S(2)}) %collective-permute-start.2) | collective-permute-done | bytes 65568 | tf_op jit(solution)/shard_map/ppermute | solution.py:40
  31.3 1.1 collective-permute-start.10
  32.4 1.2 collective-permute-start.11
  34.0 1.5 %collective-permute-start.6 = (bf16[128,2176]{1,0:T(8,128)(2,1)S(1)}, bf16[128,2176]{1,0:T(8,128)(2,1)}, u32[]{:S(2)}, u32[]{:S(2)}) collective-permute-start(bf16[128,2176]{1,0:T(8,128)(2,1)S(1)} %ordered.3.refs_2_), channel_id=1, source_target_pairs={{1,0},{2,1},{5,4},{6,5},{9,8},{10,9},{13,12},{14,13},{17,16},{18,1... | collective-permute-start | bytes 1671176 | tf_op jit(solution)/shard_map/ppermute | solution.py:44
  35.5 1.3 %collective-permute-start.5 = (bf16[128,2176]{1,0:T(8,128)(2,1)S(1)}, bf16[128,2176]{1,0:T(8,128)(2,1)}, u32[]{:S(2)}, u32[]{:S(2)}) collective-permute-start(bf16[128,2176]{1,0:T(8,128)(2,1)S(1)} %ordered.2.refs_1_), channel_id=1, source_target_pairs={{1,2},{2,3},{5,6},{6,7},{9,10},{10,11},{13,14},{14,15},{17,18},{18... | collective-permute-start | bytes 1671176 | tf_op jit(solution)/shard_map/ppermute | solution.py:44
  36.8 5.8 %collective-permute-done.10.refs_2_ = bf16[64,2048]{1,0:T(8,128)(2,1)S(1)} collective-permute-done((bf16[64,2048]{1,0:T(8,128)(2,1)S(1)}, bf16[64,2048]{1,0:T(8,128)(2,1)S(1)}, u32[]{:S(2)}, u32[]{:S(2)}) %collective-permute-start.10) | collective-permute-done | bytes 262176 | tf_op jit(solution)/shard_map/ppermute | solution.py:48
  49.1 2.7 %collective-permute-start.12 = (bf16[256,2048]{1,0:T(8,128)(2,1)S(1)}, bf16[256,2048]{1,0:T(8,128)(2,1)S(1)}, u32[]{:S(2)}, u32[]{:S(2)}) collective-permute-start(bf16[256,2048]{1,0:T(8,128)(2,1)S(1)} %stack_rows.3.near_ref), channel_id=1, source_target_pairs={{0,4},{4,0},{8,12},{12,8},{16,20},{20,16},{24,28},{28,24},{1,5},{5... | collective-permute-start | bytes 3145736 | tf_op jit(solution)/shard_map/ppermute | solution.py:48
  52.5 1.3 %collective-permute-start.7 = (bf16[128,2176]{1,0:T(8,128)(2,1)}, bf16[128,2176]{1,0:T(8,128)(2,1)S(1)}, u32[]{:S(2)}, u32[]{:S(2)}) collective-permute-start(bf16[128,2176]{1,0:T(8,128)(2,1)} %collective-permute-done.5.left_ref.refs_3_), channel_id=1, source_target_pairs={{2,3},{6,7},{10,11},{14,15},{18,19},{22,23},{26,27},{30,31}} | collective-permute-start | bytes 1671176 | tf_op jit(solution)/shard_map/ppermute | solution.py:44
  54.9 1.6 %place_slices.1.in_ref = bf16[8,128,1152]{2,1,0:T(8,128)(2,1)} custom-call(bf16[128,2176]{1,0:T(8,128)(2,1)S(1)} %copy-done.7, bf16[128,2176]{1,0:T(8,128)(2,1)S(1)} %ordered.2.refs_1_, bf16[128,2176]{1,0:T(8,128)(2,1)S(1)} %ordered.3.refs_2_), custom_call_target="tpu_custom_call" | custom-call | bytes 1024 | tf_op jit(solution)/shard_map/place_slices/pallas_call | solution.py:227
  59.1 9.6 %collective-permute-done.7.last_ref.refs_5_ = bf16[128,2176]{1,0:T(8,128)(2,1)S(1)} collective-permute-done((bf16[128,2176]{1,0:T(8,128)(2,1)}, bf16[128,2176]{1,0:T(8,128)(2,1)S(1)}, u32[]{:S(2)}, u32[]{:S(2)}) %collective-permute-start.7) | collective-permute-done | bytes 557088 | tf_op jit(solution)/shard_map/ppermute | solution.py:44
  68.7 3.0 %place_last.1.refs_9_ = bf16[8,128,1152]{2,1,0:T(8,128)(2,1)} custom-call(bf16[8,128,1152]{2,1,0:T(8,128)(2,1)} %place_slices.1.in_ref, bf16[128,2176]{1,0:T(8,128)(2,1)} %collective-permute-done.5.left_ref.refs_3_, bf16[128,2176]{1,0:T(8,128)(2,1)} %collective-permute-done.6.right_ref.refs_4_, ...), custom_call_target="tpu_custom_call", output_to_operand_aliasing={{}: (0, {})} | custom-call | bytes 1024 | tf_op jit(solution)/shard_map/place_last/pallas_call | solution.py:294
  73.4 4.5 %all-to-all-start.1 = ((bf16[8,128,1152]{2,1,0:T(8,128)(2,1)}), bf16[8,128,1152]{2,1,0:T(8,128)(2,1)S(1)}, u32[]{:S(2)}, u32[]{:S(2)}) async-start(bf16[8,128,1152]{2,1,0:T(8,128)(2,1)} %place_last.1.refs_9_), calls=%async_computation.1 | async-start | bytes 4718592 | tf_op jit(solution)/shard_map/all_to_all | solution.py:494
  77.9 3.3 %collective-permute-start.15 = (f32[128,128]{1,0:T(8,128)}, f32[128,128]{1,0:T(8,128)S(1)}, u32[]{:S(2)}, u32[]{:S(2)}) collective-permute-start(f32[128,128]{1,0:T(8,128)} %copy-done.31), channel_id=1, source_target_pairs={{0,1},{1,2},{2,3},{3,0},{4,5},{5,6},{6,7},{7,4},{8,9},{9,10},{10,1... | collective-permute-start | bytes 196616 | tf_op jit(solution)/shard_map/ppermute | solution.py:40
  81.1 1.1 copy-done.1
  82.2 1.1 copy-done.3
  86.4 1.6 %copy-done.13 = bf16[8192,128]{1,0:T(8,128)(2,1)S(1)} copy-done((bf16[8192,128]{1,0:T(8,128)(2,1)S(1)}, bf16[8192,128]{1,0:T(8,128)(2,1)}, u32[]{:S(2)}) %copy-start.13) | copy-done | bytes 2097176
  88.0 1.6 %copy-done.14 = bf16[8192,128]{1,0:T(8,128)(2,1)S(1)} copy-done((bf16[8192,128]{1,0:T(8,128)(2,1)S(1)}, bf16[8192,128]{1,0:T(8,128)(2,1)}, u32[]{:S(2)}) %copy-start.14) | copy-done | bytes 2097176
  89.6 3.7 %gate_and_up.1.pre_ref = f32[128,256]{1,0:T(8,128)S(1)} custom-call(bf16[128,2176]{1,0:T(8,128)(2,1)S(1)} %copy-done.8, bf16[128,2176]{1,0:T(8,128)(2,1)S(1)} %copy-done.1, bf16[128,2176]{1,0:T(8,128)(2,1)S(1)} %copy-done.3, bf16[128,2176]{1,0:T(8,128)(2,1)} %collective-permute-done.5.left_ref.refs_3_, ...), custom_call_target="tpu_custom_call" | custom-call | bytes 1024 | tf_op jit(solution)/shard_map/gate_and_up/pallas_call | solution.py:331
  94.8 1.6 %collective-permute-start.17 = (bf16[128,256]{1,0:T(8,128)(2,1)}, bf16[128,256]{1,0:T(8,128)(2,1)S(1)}, u32[]{:S(2)}, u32[]{:S(2)}) collective-permute-start(bf16[128,256]{1,0:T(8,128)(2,1)} %gradients.1.refs_0_), channel_id=1, source_target_pairs={{0,8},{4,12},{8,0},{12,4},{16,24},{20,28},{24,16},{28,20},{1,9},{5... | collective-permute-start | bytes 196616 | tf_op jit(solution)/shard_map/ppermute | solution.py:48
  96.5 1.6 %collective-permute-start.19 = (bf16[128,256]{1,0:T(8,128)(2,1)}, bf16[128,256]{1,0:T(8,128)(2,1)}, u32[]{:S(2)}, u32[]{:S(2)}) collective-permute-start(bf16[128,256]{1,0:T(8,128)(2,1)} %gradients.1.refs_0_), channel_id=1, source_target_pairs={{0,16},{4,20},{8,24},{12,28},{16,0},{20,4},{24,8},{28,12},{1,17},{... | collective-permute-start | bytes 196616 | tf_op jit(solution)/shard_map/ppermute | solution.py:48
  99.1 2.4 %collective-permute-start.21 = (bf16[128,256]{1,0:T(8,128)(2,1)}, bf16[128,256]{1,0:T(8,128)(2,1)}, u32[]{:S(2)}, u32[]{:S(2)}) collective-permute-start(bf16[128,256]{1,0:T(8,128)(2,1)} %gradients.1.refs_0_), channel_id=1, source_target_pairs={{0,24},{4,28},{8,16},{12,20},{16,8},{20,12},{24,0},{28,4},{1,25},{... | collective-permute-start | bytes 196616 | tf_op jit(solution)/shard_map/ppermute | solution.py:48
  101.5 5.6 %collective-permute-done.17.refs_2_ = bf16[128,256]{1,0:T(8,128)(2,1)S(1)} collective-permute-done((bf16[128,256]{1,0:T(8,128)(2,1)}, bf16[128,256]{1,0:T(8,128)(2,1)S(1)}, u32[]{:S(2)}, u32[]{:S(2)}) %collective-permute-start.17) | collective-permute-done | bytes 65568 | tf_op jit(solution)/shard_map/ppermute | solution.py:48
  107.7 2.3 %collective-permute-start.22 = (bf16[128,256]{1,0:T(8,128)(2,1)}, bf16[128,256]{1,0:T(8,128)(2,1)}, u32[]{:S(2)}, u32[]{:S(2)}) collective-permute-start(bf16[128,256]{1,0:T(8,128)(2,1)} %gradients.1.refs_0_), channel_id=1, source_target_pairs={{0,28},{4,24},{8,20},{12,16},{16,12},{20,8},{24,4},{28,0},{1,29},{... | collective-permute-start | bytes 196616 | tf_op jit(solution)/shard_map/ppermute | solution.py:48
  111.6 3.0 %projector.1 = f32[128,512]{1,0:T(8,128)S(1)} custom-call(bf16[8,128,1152]{2,1,0:T(8,128)(2,1)S(1)} %all-to-all-done.1.came_ref.feats_ref, bf16[8,144,512]{2,1,0:T(8,128)(2,1)S(1)} %all-to-all-done.refs_4_.teach_ref, bf16[8,16,512]{2,1,0:T(8,128)(2,1)S(1)} %copy-done.17), custom_call_target="tpu_custom_call" | custom-call | bytes 1024 | tf_op jit(solution)/shard_map/projector/pallas_call | solution.py:411
  115.6 2.7 %final_product.1 = (f32[128,1024]{1,0:T(8,128)}, f32[128,1024]{1,0:T(8,128)}) custom-call(bf16[8,128,1152]{2,1,0:T(8,128)(2,1)S(1)} %all-to-all-done.1.came_ref.feats_ref, bf16[128,256]{1,0:T(8,128)(2,1)} %gradients.1.refs_0_, bf16[128,256]{1,0:T(8,128)(2,1)S(1)} %copy-done.27, bf16[128,256]{1,0:T(8,128)(2,1)S(1)} %copy-done.29, ...), custom_call_target="tpu_custom_call" | custom-call | bytes 1024 | tf_op jit(solution)/shard_map/final_product/pallas_call | solution.py:448
  (106 shorter events, 22.1 us)
Async XLA Ops:
  3.6 9.9 %copy-start.35 = (bf16[16,2048]{1,0:T(8,128)(2,1)S(1)}, bf16[16,2048]{1,0:T(8,128)(2,1)}, u32[]{:S(2)}) copy-start(bf16[16,2048]{1,0:T(8,128)(2,1)} %get-tuple-element.18) | copy-start | bytes 196612
  3.6 11.3 %copy-start.34 = (bf16[16,2048]{1,0:T(8,128)(2,1)S(1)}, bf16[16,2048]{1,0:T(8,128)(2,1)}, u32[]{:S(2)}) copy-start(bf16[16,2048]{1,0:T(8,128)(2,1)} %get-tuple-element.19) | copy-start | bytes 196612
  3.6 27.7 %copy-start.30 = (bf16[16,2048]{1,0:T(8,128)(2,1)S(1)}, bf16[16,2048]{1,0:T(8,128)(2,1)}, u32[]{:S(2)}) copy-start(bf16[16,2048]{1,0:T(8,128)(2,1)} %get-tuple-element.16.refs_0_) | copy-start | bytes 196612
  3.6 41.6 %all-to-all-start = ((bf16[8,144,512]{2,1,0:T(8,128)(2,1)}), bf16[8,144,512]{2,1,0:T(8,128)(2,1)S(1)}, u32[]{:S(2)}, u32[]{:S(2)}) async-start(bf16[8,144,512]{2,1,0:T(8,128)(2,1)} %get-tuple-element.20), calls=%async_computation | async-start | bytes 2359296 | tf_op jit(solution)/shard_map/all_to_all | solution.py:476
  8.2 25.9 %collective-permute-start.4 = (bf16[128,2176]{1,0:T(8,128)(2,1)S(1)}, bf16[128,2176]{1,0:T(8,128)(2,1)S(1)}, u32[]{:S(2)}, u32[]{:S(2)}) collective-permute-start(bf16[128,2176]{1,0:T(8,128)(2,1)S(1)} %copy-done.6), channel_id=1, source_target_pairs={{1,0},{2,1},{3,2},{5,4},{6,5},{7,6},{9,8},{10,9},{11,10},{13,12},{... | collective-permute-start | bytes 1671176 | tf_op jit(solution)/shard_map/ppermute | solution.py:44
  10.3 25.2 %collective-permute-start = (bf16[128,2176]{1,0:T(8,128)(2,1)S(1)}, bf16[128,2176]{1,0:T(8,128)(2,1)S(1)}, u32[]{:S(2)}, u32[]{:S(2)}) collective-permute-start(bf16[128,2176]{1,0:T(8,128)(2,1)S(1)} %copy-done.6), channel_id=1, source_target_pairs={{0,1},{1,2},{2,3},{4,5},{5,6},{6,7},{8,9},{9,10},{10,11},{12,13},{... | collective-permute-start | bytes 1671176 | tf_op jit(solution)/shard_map/ppermute | solution.py:44
  11.6 15.9 %collective-permute-start.1 = (bf16[16,2048]{1,0:T(8,128)(2,1)S(1)}, bf16[16,2048]{1,0:T(8,128)(2,1)S(1)}, u32[]{:S(2)}, u32[]{:S(2)}) collective-permute-start(bf16[16,2048]{1,0:T(8,128)(2,1)S(1)} %copy-done.36), channel_id=1, source_target_pairs={{0,1},{1,2},{2,3},{3,0},{4,5},{5,6},{6,7},{7,4},{8,9},{9,10},{10,1... | collective-permute-start | bytes 196616 | tf_op jit(solution)/shard_map/ppermute | solution.py:40
  13.5 17.8 %collective-permute-start.2 = (bf16[16,2048]{1,0:T(8,128)(2,1)S(1)}, bf16[16,2048]{1,0:T(8,128)(2,1)S(1)}, u32[]{:S(2)}, u32[]{:S(2)}) collective-permute-start(bf16[16,2048]{1,0:T(8,128)(2,1)S(1)} %copy-done.35), channel_id=1, source_target_pairs={{0,2},{1,3},{2,0},{3,1},{4,6},{5,7},{6,4},{7,5},{8,10},{9,11},{10,... | collective-permute-start | bytes 196616 | tf_op jit(solution)/shard_map/ppermute | solution.py:40
  14.9 16.4 %collective-permute-start.3 = (bf16[16,2048]{1,0:T(8,128)(2,1)S(1)}, bf16[16,2048]{1,0:T(8,128)(2,1)S(1)}, u32[]{:S(2)}, u32[]{:S(2)}) collective-permute-start(bf16[16,2048]{1,0:T(8,128)(2,1)S(1)} %copy-done.34), channel_id=1, source_target_pairs={{0,3},{1,0},{2,1},{3,2},{4,7},{5,4},{6,5},{7,6},{8,11},{9,8},{10,9... | collective-permute-start | bytes 196616 | tf_op jit(solution)/shard_map/ppermute | solution.py:40
  31.3 13.2 %copy-start.4 = (bf16[64,2048]{1,0:T(8,128)(2,1)}, bf16[64,2048]{1,0:T(8,128)(2,1)S(1)}, u32[]{:S(2)}) copy-start(bf16[64,2048]{1,0:T(8,128)(2,1)S(1)} %stack_rows.2.refs_1_.refs_0_) | copy-start | bytes 786436
  31.3 11.2 %collective-permute-start.10 = (bf16[64,2048]{1,0:T(8,128)(2,1)S(1)}, bf16[64,2048]{1,0:T(8,128)(2,1)S(1)}, u32[]{:S(2)}, u32[]{:S(2)}) collective-permute-start(bf16[64,2048]{1,0:T(8,128)(2,1)S(1)} %stack_rows.2.refs_1_.refs_0_), channel_id=1, source_target_pairs={{0,16},{4,20},{8,24},{12,28},{16,0},{20,4},{24,8},{28,12},{1,17},{... | collective-permute-start | bytes 786440 | tf_op jit(solution)/shard_map/ppermute | solution.py:48
  32.4 10.9 %collective-permute-start.11 = (bf16[64,2048]{1,0:T(8,128)(2,1)S(1)}, bf16[64,2048]{1,0:T(8,128)(2,1)S(1)}, u32[]{:S(2)}, u32[]{:S(2)}) collective-permute-start(bf16[64,2048]{1,0:T(8,128)(2,1)S(1)} %stack_rows.2.refs_1_.refs_0_), channel_id=1, source_target_pairs={{0,24},{4,28},{8,16},{12,20},{16,8},{20,12},{24,0},{28,4},{1,25},{... | collective-permute-start | bytes 786440 | tf_op jit(solution)/shard_map/ppermute | solution.py:48
  33.6 10.9 %collective-permute-start.9 = (bf16[64,2048]{1,0:T(8,128)(2,1)S(1)}, bf16[64,2048]{1,0:T(8,128)(2,1)S(1)}, u32[]{:S(2)}, u32[]{:S(2)}) collective-permute-start(bf16[64,2048]{1,0:T(8,128)(2,1)S(1)} %stack_rows.2.refs_1_.refs_0_), channel_id=1, source_target_pairs={{0,8},{4,12},{8,0},{12,4},{16,24},{20,28},{24,16},{28,20},{1,9},{5... | collective-permute-start | bytes 786440 | tf_op jit(solution)/shard_map/ppermute | solution.py:48
  34.0 19.8 %copy-start.2 = (bf16[128,2176]{1,0:T(8,128)(2,1)}, bf16[128,2176]{1,0:T(8,128)(2,1)S(1)}, u32[]{:S(2)}) copy-start(bf16[128,2176]{1,0:T(8,128)(2,1)S(1)} %ordered.3.refs_2_) | copy-start | bytes 1671172
  34.0 17.8 %collective-permute-start.6 = (bf16[128,2176]{1,0:T(8,128)(2,1)S(1)}, bf16[128,2176]{1,0:T(8,128)(2,1)}, u32[]{:S(2)}, u32[]{:S(2)}) collective-permute-start(bf16[128,2176]{1,0:T(8,128)(2,1)S(1)} %ordered.3.refs_2_), channel_id=1, source_target_pairs={{1,0},{2,1},{5,4},{6,5},{9,8},{10,9},{13,12},{14,13},{17,16},{18,1... | collective-permute-start | bytes 1671176 | tf_op jit(solution)/shard_map/ppermute | solution.py:44
  35.5 20.9 %copy-start = (bf16[128,2176]{1,0:T(8,128)(2,1)}, bf16[128,2176]{1,0:T(8,128)(2,1)S(1)}, u32[]{:S(2)}) copy-start(bf16[128,2176]{1,0:T(8,128)(2,1)S(1)} %ordered.2.refs_1_) | copy-start | bytes 1671172
  35.5 17.0 %collective-permute-start.5 = (bf16[128,2176]{1,0:T(8,128)(2,1)S(1)}, bf16[128,2176]{1,0:T(8,128)(2,1)}, u32[]{:S(2)}, u32[]{:S(2)}) collective-permute-start(bf16[128,2176]{1,0:T(8,128)(2,1)S(1)} %ordered.2.refs_1_), channel_id=1, source_target_pairs={{1,2},{2,3},{5,6},{6,7},{9,10},{10,11},{13,14},{14,15},{17,18},{18... | collective-permute-start | bytes 1671176 | tf_op jit(solution)/shard_map/ppermute | solution.py:44
  49.1 7.4 %collective-permute-start.12 = (bf16[256,2048]{1,0:T(8,128)(2,1)S(1)}, bf16[256,2048]{1,0:T(8,128)(2,1)S(1)}, u32[]{:S(2)}, u32[]{:S(2)}) collective-permute-start(bf16[256,2048]{1,0:T(8,128)(2,1)S(1)} %stack_rows.3.near_ref), channel_id=1, source_target_pairs={{0,4},{4,0},{8,12},{12,8},{16,20},{20,16},{24,28},{28,24},{1,5},{5... | collective-permute-start | bytes 3145736 | tf_op jit(solution)/shard_map/ppermute | solution.py:48
  51.8 7.3 %collective-permute-start.8 = (bf16[128,2176]{1,0:T(8,128)(2,1)}, bf16[128,2176]{1,0:T(8,128)(2,1)S(1)}, u32[]{:S(2)}, u32[]{:S(2)}) collective-permute-start(bf16[128,2176]{1,0:T(8,128)(2,1)} %collective-permute-done.6.right_ref.refs_4_), channel_id=1, source_target_pairs={{1,0},{5,4},{9,8},{13,12},{17,16},{21,20},{25,24},{29,28}} | collective-permute-start | bytes 1671176 | tf_op jit(solution)/shard_map/ppermute | solution.py:44
  52.5 16.2 %collective-permute-start.7 = (bf16[128,2176]{1,0:T(8,128)(2,1)}, bf16[128,2176]{1,0:T(8,128)(2,1)S(1)}, u32[]{:S(2)}, u32[]{:S(2)}) collective-permute-start(bf16[128,2176]{1,0:T(8,128)(2,1)} %collective-permute-done.5.left_ref.refs_3_), channel_id=1, source_target_pairs={{2,3},{6,7},{10,11},{14,15},{18,19},{22,23},{26,27},{30,31}} | collective-permute-start | bytes 1671176 | tf_op jit(solution)/shard_map/ppermute | solution.py:44
  59.1 12.6 %copy-start.18 = (f32[128,128]{1,0:T(8,128)}, f32[128,128]{1,0:T(8,128)S(1)}, u32[]{:S(2)}) copy-start(f32[128,128]{1,0:T(8,128)S(1)} %get-tuple-element.21.refs_0_) | copy-start | bytes 196612
  73.4 37.3 %all-to-all-start.1 = ((bf16[8,128,1152]{2,1,0:T(8,128)(2,1)}), bf16[8,128,1152]{2,1,0:T(8,128)(2,1)S(1)}, u32[]{:S(2)}, u32[]{:S(2)}) async-start(bf16[8,128,1152]{2,1,0:T(8,128)(2,1)} %place_last.1.refs_9_), calls=%async_computation.1 | async-start | bytes 4718592 | tf_op jit(solution)/shard_map/all_to_all | solution.py:494
  77.9 15.5 %collective-permute-start.13 = (f32[128,128]{1,0:T(8,128)}, f32[128,128]{1,0:T(8,128)S(1)}, u32[]{:S(2)}, u32[]{:S(2)}) collective-permute-start(f32[128,128]{1,0:T(8,128)} %copy-done.33), channel_id=1, source_target_pairs={{0,3},{1,0},{2,1},{3,2},{4,7},{5,4},{6,5},{7,6},{8,11},{9,8},{10,9... | collective-permute-start | bytes 196616 | tf_op jit(solution)/shard_map/ppermute | solution.py:40
  77.9 15.5 %collective-permute-start.14 = (f32[128,128]{1,0:T(8,128)}, f32[128,128]{1,0:T(8,128)S(1)}, u32[]{:S(2)}, u32[]{:S(2)}) collective-permute-start(f32[128,128]{1,0:T(8,128)} %copy-done.32), channel_id=1, source_target_pairs={{0,2},{1,3},{2,0},{3,1},{4,6},{5,7},{6,4},{7,5},{8,10},{9,11},{10,... | collective-permute-start | bytes 196616 | tf_op jit(solution)/shard_map/ppermute | solution.py:40
  77.9 15.5 %collective-permute-start.15 = (f32[128,128]{1,0:T(8,128)}, f32[128,128]{1,0:T(8,128)S(1)}, u32[]{:S(2)}, u32[]{:S(2)}) collective-permute-start(f32[128,128]{1,0:T(8,128)} %copy-done.31), channel_id=1, source_target_pairs={{0,1},{1,2},{2,3},{3,0},{4,5},{5,6},{6,7},{7,4},{8,9},{9,10},{10,1... | collective-permute-start | bytes 196616 | tf_op jit(solution)/shard_map/ppermute | solution.py:40
  94.1 4.4 %collective-permute-start.16 = (bf16[128,256]{1,0:T(8,128)(2,1)}, bf16[128,256]{1,0:T(8,128)(2,1)S(1)}, u32[]{:S(2)}, u32[]{:S(2)}) collective-permute-start(bf16[128,256]{1,0:T(8,128)(2,1)} %gradients.1.refs_0_), channel_id=1, source_target_pairs={{0,4},{4,0},{8,12},{12,8},{16,20},{20,16},{24,28},{28,24},{1,5},{5... | collective-permute-start | bytes 196616 | tf_op jit(solution)/shard_map/ppermute | solution.py:48
  94.8 12.3 %collective-permute-start.17 = (bf16[128,256]{1,0:T(8,128)(2,1)}, bf16[128,256]{1,0:T(8,128)(2,1)S(1)}, u32[]{:S(2)}, u32[]{:S(2)}) collective-permute-start(bf16[128,256]{1,0:T(8,128)(2,1)} %gradients.1.refs_0_), channel_id=1, source_target_pairs={{0,8},{4,12},{8,0},{12,4},{16,24},{20,28},{24,16},{28,20},{1,9},{5... | collective-permute-start | bytes 196616 | tf_op jit(solution)/shard_map/ppermute | solution.py:48
  96.4 19.2 %collective-permute-start.18 = (bf16[128,256]{1,0:T(8,128)(2,1)}, bf16[128,256]{1,0:T(8,128)(2,1)}, u32[]{:S(2)}, u32[]{:S(2)}) collective-permute-start(bf16[128,256]{1,0:T(8,128)(2,1)} %gradients.1.refs_0_), channel_id=1, source_target_pairs={{0,12},{4,8},{8,4},{12,0},{16,28},{20,24},{24,20},{28,16},{1,13},{... | collective-permute-start | bytes 196616 | tf_op jit(solution)/shard_map/ppermute | solution.py:48
  96.5 19.1 %collective-permute-start.19 = (bf16[128,256]{1,0:T(8,128)(2,1)}, bf16[128,256]{1,0:T(8,128)(2,1)}, u32[]{:S(2)}, u32[]{:S(2)}) collective-permute-start(bf16[128,256]{1,0:T(8,128)(2,1)} %gradients.1.refs_0_), channel_id=1, source_target_pairs={{0,16},{4,20},{8,24},{12,28},{16,0},{20,4},{24,8},{28,12},{1,17},{... | collective-permute-start | bytes 196616 | tf_op jit(solution)/shard_map/ppermute | solution.py:48
  98.1 17.5 %collective-permute-start.20 = (bf16[128,256]{1,0:T(8,128)(2,1)}, bf16[128,256]{1,0:T(8,128)(2,1)}, u32[]{:S(2)}, u32[]{:S(2)}) collective-permute-start(bf16[128,256]{1,0:T(8,128)(2,1)} %gradients.1.refs_0_), channel_id=1, source_target_pairs={{0,20},{4,16},{8,28},{12,24},{16,4},{20,0},{24,12},{28,8},{1,21},{... | collective-permute-start | bytes 196616 | tf_op jit(solution)/shard_map/ppermute | solution.py:48
  99.1 16.5 %collective-permute-start.21 = (bf16[128,256]{1,0:T(8,128)(2,1)}, bf16[128,256]{1,0:T(8,128)(2,1)}, u32[]{:S(2)}, u32[]{:S(2)}) collective-permute-start(bf16[128,256]{1,0:T(8,128)(2,1)} %gradients.1.refs_0_), channel_id=1, source_target_pairs={{0,24},{4,28},{8,16},{12,20},{16,8},{20,12},{24,0},{28,4},{1,25},{... | collective-permute-start | bytes 196616 | tf_op jit(solution)/shard_map/ppermute | solution.py:48
  107.7 7.9 %collective-permute-start.22 = (bf16[128,256]{1,0:T(8,128)(2,1)}, bf16[128,256]{1,0:T(8,128)(2,1)}, u32[]{:S(2)}, u32[]{:S(2)}) collective-permute-start(bf16[128,256]{1,0:T(8,128)(2,1)} %gradients.1.refs_0_), channel_id=1, source_target_pairs={{0,28},{4,24},{8,20},{12,16},{16,12},{20,8},{24,4},{28,0},{1,29},{... | collective-permute-start | bytes 196616 | tf_op jit(solution)/shard_map/ppermute | solution.py:48
  (30 other events, 60.4 us)

commit v4 on v3

--- a/solution.py
+++ b/solution.py
@@ -18,14 +18,6 @@
 
 def params(mib):
     return pltpu.CompilerParams(vmem_limit_bytes=mib * MIB)
-
-
-def room(*arrays):
-    total = 0
-    for a in arrays:
-        lanes = pl.cdiv(a.shape[-1], LANES) * LANES
-        total += math.prod(a.shape[:-1]) * lanes * jnp.dtype(a.dtype).itemsize
-    return params(total // MIB + 5)
 
 
 def cost(flops, nbytes):
@@ -134,7 +126,7 @@
     return out if wide else [*out, blocks]
 
 
-def stack_rows(parts, rows, width, after=()):
+def stack_rows(parts, rows, width, mib, after=()):
     def kernel(*refs):
         out_ref = refs[-1]
         for i, ref in enumerate(refs[: len(parts)]):
@@ -145,7 +137,7 @@
         in_specs=[VMEM] * len(parts) + [pl.BlockSpec(memory_space=pl.ANY)] * len(after),
         out_specs=VMEM,
         out_shape=struct((len(parts) * rows, width)),
-        compiler_params=room(*parts),
+        compiler_params=params(mib),
         cost_estimate=cost(0, 1024),
         name="stack_rows",
     )(*parts, *after)
@@ -190,7 +182,7 @@
         + [pl.BlockSpec(memory_space=pl.ANY)] * len(after),
         out_specs=[VMEM] * n_t,
         out_shape=[struct((hb, tok), jnp.float32)] * n_t,
-        compiler_params=room(near, near, far, student, projected, student),
+        compiler_params=params(60),
         cost_estimate=cost(0, 1024),
         name="partial_products",
     )(near, far, student, projected, *after)
@@ -217,19 +209,14 @@
         for k, x_ref in zip(places, refs):
             slot = (lax.axis_index("tensor") + n_t - k) % n_t
             for b in range(per):
-                out_ref[slot * per + b, :, PB:] = x_ref[:, b * cols : (b + 1) * cols]
-
-            @pl.when(slot == 0)
-            def _(x_ref=x_ref):
-                for i in range(n_dp):
-                    out_ref[i, :, :PB] = x_ref[:, width:]
+                out_ref[slot * per + b] = x_ref[:, b * cols : (b + 1) * cols]
 
     return pl.pallas_call(
         kernel,
         in_specs=[VMEM] * len(slices),
         out_specs=VMEM,
-        out_shape=struct((n_dp, count, PB + cols)),
-        compiler_params=room(*slices, struct((n_dp, count, PB + cols))),
+        out_shape=struct((n_dp, count, cols)),
+        compiler_params=params(60),
         cost_estimate=cost(0, 1024),
         name="place_slices",
     )(*slices)
@@ -251,33 +238,15 @@
         def place(ref, slot):
             if not aligned:
                 for b in range(per):
-                    out_ref[slot * per + b, :, PB:] = ref[:, b * cols : (b + 1) * cols]
-
-                @pl.when(slot == 0)
-                def _():
-                    for i in range(n_dp):
-                        out_ref[i, :, :PB] = ref[:, width:]
-
+                    out_ref[slot * per + b] = ref[:, b * cols : (b + 1) * cols]
                 return
             copies = []
             for b in range(per):
                 src = ref.at[:, pl.ds(b * cols, cols)]
-                dst = out_ref.at[slot * per + b, :, pl.ds(PB, cols)]
+                dst = out_ref.at[slot * per + b]
                 copies.append(pltpu.make_async_copy(src, dst, sems.at[b]))
             for c in copies:
                 c.start()
-
-            @pl.when(slot == 0)
-            def _():
-                extra = []
-                for i in range(n_dp):
-                    src = ref.at[:, pl.ds(width, PB)]
-                    dst = out_ref.at[i, :, pl.ds(0, PB)]
-                    extra.append(pltpu.make_async_copy(src, dst, sems.at[per + i]))
-                for c in extra:
-                    c.start()
-                for c in extra:
-                    c.wait()
 
             for c in copies:
                 c.wait()
@@ -299,8 +268,8 @@
         out_specs=hbm if aligned else VMEM,
         out_shape=struct(payload.shape),
         input_output_aliases={0: 0} if aligned else {},
-        scratch_shapes=[pltpu.SemaphoreType.DMA((per + n_dp,))],
-        compiler_params=room(from_left, from_left, from_left, from_left, *([] if aligned else [payload] * 2)),
+        scratch_shapes=[pltpu.SemaphoreType.DMA((per,))],
+        compiler_params=params(60),
         cost_estimate=cost(0, 1024),
         name="place_last",
     )(payload, from_left, from_right, *ends, *after)
@@ -339,17 +308,17 @@
             pltpu.VMEM((n_t, width, 2 * hb), jnp.bfloat16),
             pltpu.SemaphoreType.DMA((2 * n_t,)),
         ],
-        compiler_params=room(*slices, gate, up, *slices[:2]),
+        compiler_params=params(60),
         cost_estimate=cost(0, 1024),
         name="gate_and_up",
     )(*slices, gate, up, *after)
 
 
-def gradients(pre, acts):
+def gradients(pre, acts, slices, width):
     count, hb = pre.shape[0], pre.shape[1] // 2
 
     def kernel(pre_ref, *refs):
-        act_refs, out_ref = refs[:-1], refs[-1]
+        act_refs, xs, out_ref = refs[: len(acts)], refs[len(acts) : -1], refs[-1]
         act = act_refs[0][...]
         for ref in act_refs[1:]:
             act += ref[...]
@@ -359,102 +328,117 @@
         gate_grad = act * up_pre * s * (1.0 + gate_pre * (1.0 - s))
         up_grad = act * gate_pre * s
         out_ref[:, :hb] = gate_grad.astype(jnp.bfloat16)
-        out_ref[:, hb:] = up_grad.astype(jnp.bfloat16)
-
-    return pl.pallas_call(
-        kernel,
-        in_specs=[VMEM] * (1 + len(acts)),
-        out_specs=VMEM,
-        out_shape=struct((count, 2 * hb)),
-        compiler_params=room(pre, *acts, pre, pre, pre),
+        out_ref[:, hb : 2 * hb] = up_grad.astype(jnp.bfloat16)
+        for i, ref in enumerate(xs):
+
+            @pl.when(lax.axis_index("tensor") == i)
+            def _(ref=ref):
+                out_ref[:, 2 * hb :] = ref[...]
+
+    bucket = pl.BlockSpec((count, PB), lambda i: (0, width // PB))
+
+    def whole(x):
+        return pl.BlockSpec(x.shape, lambda i: (0, 0))
+
+    return pl.pallas_call(
+        kernel,
+        grid=(1,),
+        in_specs=[whole(x) for x in (pre, *acts)] + [bucket] * len(slices),
+        out_specs=pl.BlockSpec((count, 2 * hb + PB), lambda i: (0, 0)),
+        out_shape=struct((count, 2 * hb + PB)),
+        compiler_params=params(60),
         cost_estimate=cost(0, 1024),
         name="gradients",
-    )(pre, *acts)
-
-
-def projector(came, teach, tok):
+    )(pre, *acts, *slices)
+
+
+def hand_over(teach, tok, after):
     n_dp, _, wide = teach.shape
     groups = n_dp // GROUP
     span = GROUP * tok
-    digits = teach[:, tok:]
+    digits = []
     if wide < tok:
-        digits = digits.reshape(n_dp, 2, tok)
-        digits = jnp.pad(digits, ((0, 0), (0, 14), (0, 0)))
-        teach = teach[:, :tok]
-
-    def kernel(came_ref, teach_ref, digits_ref, out_ref, flipped_ref):
-        def flip(g, carry):
-            bucket = came_ref[pl.ds(g * GROUP, GROUP), :, :PB].reshape(span, PB)
-            flipped_ref[g] = bucket.astype(jnp.float32).T.astype(jnp.bfloat16)
-            return carry
-
-        lax.fori_loop(0, groups, flip, 0)
-        out_ref[...] = jnp.zeros_like(out_ref)
-
-        def sender(g, carry):
-            lines = digits_ref[g, :, :tok].astype(jnp.float32)
-            number = (lines[0:1] * float(LANES) + lines[1:2]).astype(jnp.int32)
-
-            def block(h, total):
+        digits = teach[:, tok:].reshape(n_dp, 2, tok)
+        digits = [jnp.pad(digits, ((0, 0), (0, 14), (0, 0)))]
+
+    def kernel(*refs):
+        teach_ref, (out_ref, total_ref) = refs[0], refs[-2:]
+
+        def receivers(h, carry):
+            total_ref[...] = jnp.zeros_like(total_ref)
+
+            def sender(g, carry):
+                lines = refs[1][g] if digits else teach_ref[g, tok : tok + 16, :tok]
+                lines = lines.astype(jnp.float32)
+                number = (lines[0:1] * float(LANES) + lines[1:2]).astype(jnp.int32)
                 token = lax.broadcasted_iota(jnp.int32, (span, tok), 0) + h * span
                 picks = (token == number).astype(jnp.float32).astype(jnp.bfloat16)
-                return total + jnp.dot(flipped_ref[h], picks, preferred_element_type=jnp.float32)
-
-            rows = lax.fori_loop(0, groups, block, jnp.zeros((PB, tok), jnp.float32))
-            out_ref[...] += jnp.dot(
-                rows.astype(jnp.bfloat16), teach_ref[g, :tok], preferred_element_type=jnp.float32
+                total_ref[...] += jnp.dot(
+                    picks, teach_ref[g, :tok], preferred_element_type=jnp.float32
+                )
+                return carry
+
+            lax.fori_loop(0, n_dp, sender, 0)
+            out_ref[pl.ds(h * GROUP, GROUP)] = (
+                total_ref[...].astype(jnp.bfloat16).reshape(GROUP, tok, wide)
             )
             return carry
 
-        lax.fori_loop(0, n_dp, sender, 0)
-
-    return pl.pallas_call(
-        kernel,
-        in_specs=[VMEM] * 3,
+        lax.fori_loop(0, groups, receivers, 0)
+
+    return pl.pallas_call(
+        kernel,
+        in_specs=[VMEM] * (1 + len(digits)) + [pl.BlockSpec(memory_space=pl.ANY)] * len(after),
         out_specs=VMEM,
-        out_shape=struct((PB, wide), jnp.float32),
-        scratch_shapes=[pltpu.VMEM((groups, PB, span), jnp.bfloat16)],
-        compiler_params=params(24),
-        cost_estimate=cost(0, 1024),
-        name="projector",
-    )(came, teach, digits)
-
-
-def final_product(feats, grads, masks):
-    n_dp, count = feats.shape[:2]
-    hb, cols = grads[0].shape[-1] // 2, feats.shape[2] - PB
-
-    def kernel(feats_ref, *refs):
-        grad_refs, (gate_ref, up_ref) = refs[: len(grads)], refs[len(grads) : len(grads) + 2]
-
-        def group(g, total):
+        out_shape=struct((n_dp, tok, wide)),
+        scratch_shapes=[pltpu.VMEM((span, wide), jnp.float32)],
+        compiler_params=params(60),
+        cost_estimate=cost(0, 1024),
+        name="hand_over",
+    )(teach, *digits, *after)
+
+
+def final_product(feats, handed, grads, masks):
+    n_dp, count, cols = feats.shape
+    wide = handed.shape[2]
+    hb = (grads[0].shape[-1] - PB) // 2
+
+    def kernel(feats_ref, handed_ref, *refs):
+        grad_refs, (proj_ref, gate_ref, up_ref) = refs[: len(grads)], refs[len(grads) : len(grads) + 3]
+
+        def group(g, totals):
             here = pl.ds(g * GROUP, GROUP)
-            left = left_ref[here].reshape(GROUP * count, 2 * hb)
-            right = feats_ref[here, :, PB:].reshape(GROUP * count, cols)
-            return total + contract_rows(left, right)
-
-        total = jnp.zeros((2 * hb, cols), jnp.float32)
+            left = left_ref[here].reshape(GROUP * count, 2 * hb + PB)
+            right = feats_ref[here].reshape(GROUP * count, cols)
+            rows = handed_ref[here].reshape(GROUP * count, wide)
+            return (
+                totals[0] + contract_rows(left[:, : 2 * hb], right),
+                totals[1] + contract_rows(left[:, 2 * hb :], rows),
+            )
+
+        totals = (jnp.zeros((2 * hb, cols), jnp.float32), jnp.zeros((PB, wide), jnp.float32))
         if masks:
             left_ref = refs[-1]
             for mask, ref in zip(masks, grad_refs):
                 left_ref[lax.axis_index("dp") ^ mask] = ref[...]
-            total = group(0, total)
+            totals = group(0, totals)
         else:
             left_ref = grad_refs[0]
-            total = lax.fori_loop(0, n_dp // GROUP, group, total)
-        gate_ref[...] = total[:hb]
-        up_ref[...] = total[hb:]
-
-    return pl.pallas_call(
-        kernel,
-        in_specs=[VMEM] * (1 + len(grads)),
-        out_specs=[VMEM] * 2,
-        out_shape=[struct((hb, cols), jnp.float32)] * 2,
-        scratch_shapes=[pltpu.VMEM((n_dp, count, 2 * hb), jnp.bfloat16)] if masks else [],
+            totals = lax.fori_loop(0, n_dp // GROUP, group, totals)
+        gate_ref[...] = totals[0][:hb]
+        up_ref[...] = totals[0][hb:]
+        proj_ref[...] = totals[1].reshape(PB, 1, wide)
+
+    return pl.pallas_call(
+        kernel,
+        in_specs=[VMEM] * (2 + len(grads)),
+        out_specs=[VMEM] * 3,
+        out_shape=[struct((PB, 1, wide), jnp.float32)] + [struct((hb, cols), jnp.float32)] * 2,
+        scratch_shapes=[pltpu.VMEM((n_dp, count, 2 * hb + PB), jnp.bfloat16)] if masks else [],
         compiler_params=params(40),
         cost_estimate=cost(0, 1024),
         name="final_product",
-    )(feats, *grads)
+    )(feats, handed, *grads)
 
 
 def body(
@@ -476,7 +460,7 @@
     teach = lax.all_to_all(teach, "dp", split_axis=0, concat_axis=0, tiled=True)
     from_left, from_right = hop(own, rightward), hop(own, leftward)
     mine = stack_rows(
-        [pieces[0]] + [shift(pieces[k], n_t, k) for k in range(1, n_t)], rows, width
+        [pieces[0]] + [shift(pieces[k], n_t, k) for k in range(1, n_t)], rows, width, 8
     )
     others = [swap(mine, n_dp, mask) for mask in (2, 4, 6)]
 
@@ -484,7 +468,9 @@
     far_left, far_right = hop(from_left, rightward[1:]), hop(from_right, leftward[:-1])
     ends = [hop(far_left, rightward[-1:]), hop(far_right, leftward[:1])]
 
-    near = stack_rows([mine] + others, n_t * rows, width, after=[teach])
+    near = stack_rows(
+        [mine] + others, n_t * rows, width, 60, after=[teach, far_left, far_right]
+    )
     far = swap(near, n_dp, 1)
     partial = partial_products(near, far, student_hidden, projected, n_t, rows, factor, after=[])
     acts = [partial[0]] + [shift(partial[k], n_t, -k) for k in range(1, n_t)]
@@ -495,15 +481,14 @@
 
     slices = [own, from_left, from_right, far_left, far_right, *ends]
     pre = gate_and_up(slices, gate_bucket, up_bucket, n_t, after=[sent])
-    grads = gradients(pre, acts)
+    grads = gradients(pre, acts, [own, from_left, far_left, ends[0]], width)
     masks = list(range(n_dp)) if n_dp == GROUP else []
     if masks:
         grads = [grads] + [swap(grads, n_dp, mask) for mask in masks[1:]]
     else:
         grads = [lax.all_gather(grads, "dp")]
-    grad_proj = projector(feats, teach, tok)
-    grad_gate, grad_up = final_product(feats, grads, masks)
-    return (grad_proj[:, None, :], grad_gate, grad_up)
+    handed = hand_over(teach, tok, after=[sent])
+    return final_product(feats, handed, grads, masks)
 
 
 def solution(mesh):

time: 119 us -> 117 us (0.983)
  the two profiles are of different devices: /device:TPU:25 before, /device:TPU:0 now
where the time goes in v4:
time: 117 us; the launch traced here: 116 us
  waiting for transfers between devices  40.7 us (35%)
  starting transfers between devices  37.9 us (32%)
  Pallas kernels  29.6 us (25%)
  local copies, waits for them, and re-layouts  7.03 us (6%)
    ppermute x11, waiting for transfers between devices, swap(): return lax.ppermute(x, 'dp', [(i, i ^ mask) for i in range(count)])  21.8 us
    ppermute x6, waiting for transfers between devices, hop(): return lax.ppermute(x, 'tensor', pairs)  11.2 us
    ppermute x6, starting transfers between devices, hop(): return lax.ppermute(x, 'tensor', pairs)  11 us
    ppermute x6, starting transfers between devices, shift(): lax.ppermute(x, 'tensor', [(i, (i + by) % count) for i in range(count)])  9.54 us
    ppermute x11, starting transfers between devices, swap(): return lax.ppermute(x, 'dp', [(i, i ^ mask) for i in range(count)])  9.43 us
    ppermute x6, waiting for transfers between devices, shift(): lax.ppermute(x, 'tensor', [(i, (i + by) % count) for i in range(count)])  7.6 us
    unnamed x44, local copies, waits for them, and re-layouts  7.03 us
    pallas_call x1, Pallas kernels, hand_over(): pl.pallas_call(kernel, in_specs=[VMEM] * (1 + len(digits)) + [pl.BlockSpe...  5.81 us
  transfers between devices with their start and end apart: 25, of which 8 were waited for; matrix products, arithmetic and copies ran while one was open for 0% of the time, Pallas kernels for 17%

profile of v4, /device:TPU:0, one launch (start us, length us, event | category | flops | bytes accessed | tf_op | source)
XLA Modules:
  0.0 116.2 jit_solution(18114174266882791095)
XLA Ops:
  0.6 3.0 %prepare.1 = (bf16[128,2176]{1,0:T(8,128)(2,1)}, bf16[16,2048]{1,0:T(8,128)(2,1)}, bf16[16,2048]{1,0:T(8,128)(2,1)}, bf16[16,2048]{1,0:T(8,128)(2,1)}, bf16[16,2...) custom-call(s32[1,128]{1,0:T(1,128)} %bitcast.1, bf16[128,4096]{1,0:T(8,128)(2,1)} %t_ref.1, bf16[128,2048]{1,0:T(8,128)(2,1)} %x_ref.1, ...), custom_call_target="tpu_custom_call" | custom-call | bytes 1024 | tf_op jit(solution)/shard_map/prepare/pallas_call | solution.py:111
  3.6 1.4 %collective-permute-start.4 = (bf16[128,2176]{1,0:T(8,128)(2,1)}, bf16[128,2176]{1,0:T(8,128)(2,1)S(1)}, u32[]{:S(2)}, u32[]{:S(2)}) collective-permute-start(bf16[128,2176]{1,0:T(8,128)(2,1)} %get-tuple-element.13.refs_0_.refs_4_), channel_id=1, source_target_pairs={{1,0},{2,1},{3,2},{5,4},{6,5},{7,6},{9,8},{10,9},{11,10},{13,12},{... | collective-permute-start | bytes 1671176 | tf_op jit(solution)/shard_map/ppermute | solution.py:36
  5.1 5.6 %collective-permute-start = (bf16[128,2176]{1,0:T(8,128)(2,1)}, bf16[128,2176]{1,0:T(8,128)(2,1)S(1)}, u32[]{:S(2)}, u32[]{:S(2)}) collective-permute-start(bf16[128,2176]{1,0:T(8,128)(2,1)} %get-tuple-element.13.refs_0_.refs_4_), channel_id=1, source_target_pairs={{0,1},{1,2},{2,3},{4,5},{5,6},{6,7},{8,9},{9,10},{10,11},{12,13},{... | collective-permute-start | bytes 1671176 | tf_op jit(solution)/shard_map/ppermute | solution.py:36
  10.7 4.2 %all-to-all-start = ((bf16[8,144,512]{2,1,0:T(8,128)(2,1)}), bf16[8,144,512]{2,1,0:T(8,128)(2,1)S(1)}, u32[]{:S(2)}, u32[]{:S(2)}) async-start(bf16[8,144,512]{2,1,0:T(8,128)(2,1)} %get-tuple-element.18), calls=%async_computation | async-start | bytes 2359296 | tf_op jit(solution)/shard_map/all_to_all | solution.py:460
  14.9 1.6 %collective-permute-start.1 = (bf16[16,2048]{1,0:T(8,128)(2,1)S(1)}, bf16[16,2048]{1,0:T(8,128)(2,1)S(1)}, u32[]{:S(2)}, u32[]{:S(2)}) collective-permute-start(bf16[16,2048]{1,0:T(8,128)(2,1)S(1)} %copy-done.21), channel_id=1, source_target_pairs={{0,1},{1,2},{2,3},{3,0},{4,5},{5,6},{6,7},{7,4},{8,9},{9,10},{10,1... | collective-permute-start | bytes 196616 | tf_op jit(solution)/shard_map/ppermute | solution.py:32
  16.5 1.1 collective-permute-start.2
  17.6 2.8 %collective-permute-start.3 = (bf16[16,2048]{1,0:T(8,128)(2,1)S(1)}, bf16[16,2048]{1,0:T(8,128)(2,1)S(1)}, u32[]{:S(2)}, u32[]{:S(2)}) collective-permute-start(bf16[16,2048]{1,0:T(8,128)(2,1)S(1)} %copy-done.18), channel_id=1, source_target_pairs={{0,3},{1,0},{2,1},{3,2},{4,7},{5,4},{6,5},{7,6},{8,11},{9,8},{10,9... | collective-permute-start | bytes 196616 | tf_op jit(solution)/shard_map/ppermute | solution.py:32
  20.4 5.8 %collective-permute-done.1.refs_1_ = bf16[16,2048]{1,0:T(8,128)(2,1)S(1)} collective-permute-done((bf16[16,2048]{1,0:T(8,128)(2,1)S(1)}, bf16[16,2048]{1,0:T(8,128)(2,1)S(1)}, u32[]{:S(2)}, u32[]{:S(2)}) %collective-permute-start.1) | collective-permute-done | bytes 65568 | tf_op jit(solution)/shard_map/ppermute | solution.py:32
  26.3 1.3 %collective-permute-done.2.refs_2_ = bf16[16,2048]{1,0:T(8,128)(2,1)S(1)} collective-permute-done((bf16[16,2048]{1,0:T(8,128)(2,1)S(1)}, bf16[16,2048]{1,0:T(8,128)(2,1)S(1)}, u32[]{:S(2)}, u32[]{:S(2)}) %collective-permute-start.2) | collective-permute-done | bytes 65568 | tf_op jit(solution)/shard_map/ppermute | solution.py:32
  27.7 1.3 %collective-permute-start.6 = (bf16[128,2176]{1,0:T(8,128)(2,1)S(1)}, bf16[128,2176]{1,0:T(8,128)(2,1)}, u32[]{:S(2)}, u32[]{:S(2)}) collective-permute-start(bf16[128,2176]{1,0:T(8,128)(2,1)S(1)} %ordered.3.refs_2_), channel_id=1, source_target_pairs={{1,0},{2,1},{5,4},{6,5},{9,8},{10,9},{13,12},{14,13},{17,16},{18,1... | collective-permute-start | bytes 1671176 | tf_op jit(solution)/shard_map/ppermute | solution.py:36
  29.7 2.5 %collective-permute-start.11 = (bf16[64,2048]{1,0:T(8,128)(2,1)S(1)}, bf16[64,2048]{1,0:T(8,128)(2,1)S(1)}, u32[]{:S(2)}, u32[]{:S(2)}) collective-permute-start(bf16[64,2048]{1,0:T(8,128)(2,1)S(1)} %stack_rows.2.refs_1_.refs_0_), channel_id=1, source_target_pairs={{0,24},{4,28},{8,16},{12,20},{16,8},{20,12},{24,0},{28,4},{1,25},{... | collective-permute-start | bytes 786440 | tf_op jit(solution)/shard_map/ppermute | solution.py:40
  33.3 6.7 %collective-permute-done.11.refs_3_ = bf16[64,2048]{1,0:T(8,128)(2,1)S(1)} collective-permute-done((bf16[64,2048]{1,0:T(8,128)(2,1)S(1)}, bf16[64,2048]{1,0:T(8,128)(2,1)S(1)}, u32[]{:S(2)}, u32[]{:S(2)}) %collective-permute-start.11) | collective-permute-done | bytes 262176 | tf_op jit(solution)/shard_map/ppermute | solution.py:40
  40.0 2.9 %collective-permute-done.10.refs_2_ = bf16[64,2048]{1,0:T(8,128)(2,1)S(1)} collective-permute-done((bf16[64,2048]{1,0:T(8,128)(2,1)S(1)}, bf16[64,2048]{1,0:T(8,128)(2,1)S(1)}, u32[]{:S(2)}, u32[]{:S(2)}) %collective-permute-start.10) | collective-permute-done | bytes 262176 | tf_op jit(solution)/shard_map/ppermute | solution.py:40
  45.4 2.2 %stack_rows.3.near_ref = bf16[256,2048]{1,0:T(8,128)(2,1)} custom-call(bf16[64,2048]{1,0:T(8,128)(2,1)} %copy-done.2, bf16[64,2048]{1,0:T(8,128)(2,1)} %collective-permute-done.9.refs_1_, bf16[64,2048]{1,0:T(8,128)(2,1)} %copy-done.12, bf16[64,2048]{1,0:T(8,128)(2,1)} %copy-done.11, bf16[8,144,512]{2,1,0:T(8,128)(2,1)} %copy-done.6, ...), custom_call_target="tpu_custom_call" | custom-call | bytes 1024 | tf_op jit(solution)/shard_map/stack_rows/pallas_call | solution.py:135
  47.7 1.3 %collective-permute-start.8 = (bf16[128,2176]{1,0:T(8,128)(2,1)}, bf16[128,2176]{1,0:T(8,128)(2,1)S(1)}, u32[]{:S(2)}, u32[]{:S(2)}) collective-permute-start(bf16[128,2176]{1,0:T(8,128)(2,1)} %collective-permute-done.6.refs_6_.right_ref.refs_4_), channel_id=1, source_target_pairs={{1,0},{5,4},{9,8},{13,12},{17,16},{21,20},{25,24},{29,28}} | collective-permute-start | bytes 1671176 | tf_op jit(solution)/shard_map/ppermute | solution.py:36
  49.7 2.8 %place_slices.1.in_ref = bf16[8,128,1024]{2,1,0:T(8,128)(2,1)} custom-call(bf16[128,2176]{1,0:T(8,128)(2,1)} %get-tuple-element.13.refs_0_.refs_4_, bf16[128,2176]{1,0:T(8,128)(2,1)} %copy-done, bf16[128,2176]{1,0:T(8,128)(2,1)} %copy-done.1), custom_call_target="tpu_custom_call" | custom-call | bytes 1024 | tf_op jit(solution)/shard_map/place_slices/pallas_call | solution.py:214
  52.5 1.0 copy-done.10
  53.5 3.2 %partial_products.1 = (f32[128,128]{1,0:T(8,128)}, f32[128,128]{1,0:T(8,128)}, f32[128,128]{1,0:T(8,128)}, f32[128,128]{1,0:T(8,128)}) custom-call(bf16[256,2048]{1,0:T(8,128)(2,1)} %stack_rows.3.near_ref, bf16[256,2048]{1,0:T(8,128)(2,1)} %copy-done.10, bf16[128,2048]{1,0:T(8,128)(2,1)} %s_ref.3, bf16[128,2048]{1,0:T(8,128)(2,1)} %p_ref.3), custom_call_target="tpu_custom_call" | custom-call | bytes 1024 | tf_op jit(solution)/shard_map/partial_products/pallas_call | solution.py:179
  56.7 11.2 %collective-permute-done.8.first_ref.refs_6_ = bf16[128,2176]{1,0:T(8,128)(2,1)S(1)} collective-permute-done((bf16[128,2176]{1,0:T(8,128)(2,1)}, bf16[128,2176]{1,0:T(8,128)(2,1)S(1)}, u32[]{:S(2)}, u32[]{:S(2)}) %collective-permute-start.8) | collective-permute-done | bytes 557088 | tf_op jit(solution)/shard_map/ppermute | solution.py:36
  68.9 3.2 %place_last.1.refs_1_.refs_9_ = bf16[8,128,1024]{2,1,0:T(8,128)(2,1)} custom-call(bf16[8,128,1024]{2,1,0:T(8,128)(2,1)} %place_slices.1.in_ref, bf16[128,2176]{1,0:T(8,128)(2,1)} %copy-done.7, bf16[128,2176]{1,0:T(8,128)(2,1)} %collective-permute-done.6.refs_6_.right_ref.refs_4_, bf16[128,2176]{1,0:T(8,128)(2,1)} %copy-done.8, ...), custom_call_target="tpu_custom_call", output_to_operand_aliasing={{}: (0, {})} | custom-call | bytes 1024 | tf_op jit(solution)/shard_map/place_last/pallas_call | solution.py:263
  72.2 3.7 %all-to-all-start.1 = ((bf16[8,128,1024]{2,1,0:T(8,128)(2,1)}), bf16[8,128,1024]{2,1,0:T(8,128)(2,1)S(1)}, u32[]{:S(2)}, u32[]{:S(2)}) async-start(bf16[8,128,1024]{2,1,0:T(8,128)(2,1)} %place_last.1.refs_1_.refs_9_), calls=%async_computation.1 | async-start | bytes 4194304 | tf_op jit(solution)/shard_map/all_to_all | solution.py:480
  75.9 3.3 %collective-permute-start.13 = (f32[128,128]{1,0:T(8,128)S(1)}, f32[128,128]{1,0:T(8,128)S(1)}, u32[]{:S(2)}, u32[]{:S(2)}) collective-permute-start(f32[128,128]{1,0:T(8,128)S(1)} %copy-done.19), channel_id=1, source_target_pairs={{0,3},{1,0},{2,1},{3,2},{4,7},{5,4},{6,5},{7,6},{8,11},{9,8},{10,9... | collective-permute-start | bytes 196616 | tf_op jit(solution)/shard_map/ppermute | solution.py:32
  79.9 5.7 %gate_and_up.1.pre_ref = f32[128,256]{1,0:T(8,128)} custom-call(bf16[128,2176]{1,0:T(8,128)(2,1)} %get-tuple-element.13.refs_0_.refs_4_, bf16[128,2176]{1,0:T(8,128)(2,1)} %copy-done, bf16[128,2176]{1,0:T(8,128)(2,1)} %copy-done.1, bf16[128,2176]{1,0:T(8,128)(2,1)} %copy-done.7, bf16[128,2176]{1,0:T(8,128)(2,1)} %collective-permute-done.6.refs_6_.right_ref.refs_4_, ...), custom_call_target="tpu_custom_call" | custom-call | bytes 1024 | tf_op jit(solution)/shard_map/gate_and_up/pallas_call | solution.py:300
  87.4 1.8 %gradients.1.refs_0_ = bf16[128,384]{1,0:T(8,128)(2,1)} custom-call(f32[128,256]{1,0:T(8,128)} %gate_and_up.1.pre_ref, f32[128,128]{1,0:T(8,128)} %get-tuple-element.19.refs_0_, f32[128,128]{1,0:T(8,128)} %copy-done.13, f32[128,128]{1,0:T(8,128)} %copy-done.14, f32[128,128]{1,0:T(8,128)} %copy-done.15, bf16[128,2176]{1,0:T(8,128)(2,1)} %get-tuple-element.13.refs_0_.refs_4_, ...), custom_call_target="tpu_custom_call" | custom-call | bytes 1024 | tf_op jit(solution)/shard_map/gradients/pallas_call | solution.py:343
  89.1 1.6 %collective-permute-start.22 = (bf16[128,384]{1,0:T(8,128)(2,1)}, bf16[128,384]{1,0:T(8,128)(2,1)S(1)}, u32[]{:S(2)}, u32[]{:S(2)}) collective-permute-start(bf16[128,384]{1,0:T(8,128)(2,1)} %gradients.1.refs_0_), channel_id=1, source_target_pairs={{0,28},{4,24},{8,20},{12,16},{16,12},{20,8},{24,4},{28,0},{1,29},{... | collective-permute-start | bytes 294920 | tf_op jit(solution)/shard_map/ppermute | solution.py:40
  90.7 1.1 collective-permute-start.21
  91.8 1.4 %collective-permute-start.20 = (bf16[128,384]{1,0:T(8,128)(2,1)}, bf16[128,384]{1,0:T(8,128)(2,1)S(1)}, u32[]{:S(2)}, u32[]{:S(2)}) collective-permute-start(bf16[128,384]{1,0:T(8,128)(2,1)} %gradients.1.refs_0_), channel_id=1, source_target_pairs={{0,20},{4,16},{8,28},{12,24},{16,4},{20,0},{24,12},{28,8},{1,21},{... | collective-permute-start | bytes 294920 | tf_op jit(solution)/shard_map/ppermute | solution.py:40
  94.4 9.8 %collective-permute-done.22.refs_7_ = bf16[128,384]{1,0:T(8,128)(2,1)S(1)} collective-permute-done((bf16[128,384]{1,0:T(8,128)(2,1)}, bf16[128,384]{1,0:T(8,128)(2,1)S(1)}, u32[]{:S(2)}, u32[]{:S(2)}) %collective-permute-start.22) | collective-permute-done | bytes 98336 | tf_op jit(solution)/shard_map/ppermute | solution.py:40
  104.8 2.4 %collective-permute-done.21.refs_6_ = bf16[128,384]{1,0:T(8,128)(2,1)S(1)} collective-permute-done((bf16[128,384]{1,0:T(8,128)(2,1)}, bf16[128,384]{1,0:T(8,128)(2,1)S(1)}, u32[]{:S(2)}, u32[]{:S(2)}) %collective-permute-start.21) | collective-permute-done | bytes 98336 | tf_op jit(solution)/shard_map/ppermute | solution.py:40
  107.2 5.8 %hand_over.1.handed_ref = bf16[8,128,512]{2,1,0:T(8,128)(2,1)} custom-call(bf16[8,144,512]{2,1,0:T(8,128)(2,1)} %copy-done.6, bf16[8,128,1024]{2,1,0:T(8,128)(2,1)} %place_last.1.refs_1_.refs_9_), custom_call_target="tpu_custom_call" | custom-call | bytes 1024 | tf_op jit(solution)/shard_map/hand_over/pallas_call | solution.py:389
  113.1 1.2 %copy-done.3 = bf16[8,128,512]{2,1,0:T(8,128)(2,1)S(1)} copy-done((bf16[8,128,512]{2,1,0:T(8,128)(2,1)S(1)}, bf16[8,128,512]{2,1,0:T(8,128)(2,1)}, u32[]{:S(2)}) %copy-start.3) | copy-done | bytes 1048600
  114.3 1.8 %final_product.1 = (f32[128,1,512]{2,1,0:T(1,128)}, f32[128,1024]{1,0:T(8,128)}, f32[128,1024]{1,0:T(8,128)}) custom-call(bf16[8,128,1024]{2,1,0:T(8,128)(2,1)S(1)} %all-to-all-done.1.feats_ref, bf16[8,128,512]{2,1,0:T(8,128)(2,1)S(1)} %copy-done.3, bf16[128,384]{1,0:T(8,128)(2,1)S(1)} %copy-done.4, bf16[128,384]{1,0:T(8,128)(2,1)S(1)} %collective-permute-done.16.refs_1_, ...), custom_call_target="tpu_custom_call" | custom-call | bytes 1024 | tf_op jit(solution)/shard_map/final_product/pallas_call | solution.py:432
  (74 shorter events, 10.2 us)
Async XLA Ops:
  3.6 12.8 %copy-start.20 = (bf16[16,2048]{1,0:T(8,128)(2,1)S(1)}, bf16[16,2048]{1,0:T(8,128)(2,1)}, u32[]{:S(2)}) copy-start(bf16[16,2048]{1,0:T(8,128)(2,1)} %get-tuple-element.16) | copy-start | bytes 196612
  3.6 14.0 %copy-start.18 = (bf16[16,2048]{1,0:T(8,128)(2,1)S(1)}, bf16[16,2048]{1,0:T(8,128)(2,1)}, u32[]{:S(2)}) copy-start(bf16[16,2048]{1,0:T(8,128)(2,1)} %get-tuple-element.17) | copy-start | bytes 196612
  3.6 24.0 %copy-start.5 = (bf16[16,2048]{1,0:T(8,128)(2,1)S(1)}, bf16[16,2048]{1,0:T(8,128)(2,1)}, u32[]{:S(2)}) copy-start(bf16[16,2048]{1,0:T(8,128)(2,1)} %get-tuple-element.14.refs_0_) | copy-start | bytes 196612
  3.6 24.0 %collective-permute-start.4 = (bf16[128,2176]{1,0:T(8,128)(2,1)}, bf16[128,2176]{1,0:T(8,128)(2,1)S(1)}, u32[]{:S(2)}, u32[]{:S(2)}) collective-permute-start(bf16[128,2176]{1,0:T(8,128)(2,1)} %get-tuple-element.13.refs_0_.refs_4_), channel_id=1, source_target_pairs={{1,0},{2,1},{3,2},{5,4},{6,5},{7,6},{9,8},{10,9},{11,10},{13,12},{... | collective-permute-start | bytes 1671176 | tf_op jit(solution)/shard_map/ppermute | solution.py:36
  5.1 23.9 %collective-permute-start = (bf16[128,2176]{1,0:T(8,128)(2,1)}, bf16[128,2176]{1,0:T(8,128)(2,1)S(1)}, u32[]{:S(2)}, u32[]{:S(2)}) collective-permute-start(bf16[128,2176]{1,0:T(8,128)(2,1)} %get-tuple-element.13.refs_0_.refs_4_), channel_id=1, source_target_pairs={{0,1},{1,2},{2,3},{4,5},{5,6},{6,7},{8,9},{9,10},{10,11},{12,13},{... | collective-permute-start | bytes 1671176 | tf_op jit(solution)/shard_map/ppermute | solution.py:36
  10.7 32.9 %all-to-all-start = ((bf16[8,144,512]{2,1,0:T(8,128)(2,1)}), bf16[8,144,512]{2,1,0:T(8,128)(2,1)S(1)}, u32[]{:S(2)}, u32[]{:S(2)}) async-start(bf16[8,144,512]{2,1,0:T(8,128)(2,1)} %get-tuple-element.18), calls=%async_computation | async-start | bytes 2359296 | tf_op jit(solution)/shard_map/all_to_all | solution.py:460
  14.9 11.4 %collective-permute-start.1 = (bf16[16,2048]{1,0:T(8,128)(2,1)S(1)}, bf16[16,2048]{1,0:T(8,128)(2,1)S(1)}, u32[]{:S(2)}, u32[]{:S(2)}) collective-permute-start(bf16[16,2048]{1,0:T(8,128)(2,1)S(1)} %copy-done.21), channel_id=1, source_target_pairs={{0,1},{1,2},{2,3},{3,0},{4,5},{5,6},{6,7},{7,4},{8,9},{9,10},{10,1... | collective-permute-start | bytes 196616 | tf_op jit(solution)/shard_map/ppermute | solution.py:32
  16.5 11.2 %collective-permute-start.2 = (bf16[16,2048]{1,0:T(8,128)(2,1)S(1)}, bf16[16,2048]{1,0:T(8,128)(2,1)S(1)}, u32[]{:S(2)}, u32[]{:S(2)}) collective-permute-start(bf16[16,2048]{1,0:T(8,128)(2,1)S(1)} %copy-done.20), channel_id=1, source_target_pairs={{0,2},{1,3},{2,0},{3,1},{4,6},{5,7},{6,4},{7,5},{8,10},{9,11},{10,... | collective-permute-start | bytes 196616 | tf_op jit(solution)/shard_map/ppermute | solution.py:32
  17.6 10.0 %collective-permute-start.3 = (bf16[16,2048]{1,0:T(8,128)(2,1)S(1)}, bf16[16,2048]{1,0:T(8,128)(2,1)S(1)}, u32[]{:S(2)}, u32[]{:S(2)}) collective-permute-start(bf16[16,2048]{1,0:T(8,128)(2,1)S(1)} %copy-done.18), channel_id=1, source_target_pairs={{0,3},{1,0},{2,1},{3,2},{4,7},{5,4},{6,5},{7,6},{8,11},{9,8},{10,9... | collective-permute-start | bytes 196616 | tf_op jit(solution)/shard_map/ppermute | solution.py:32
  27.6 16.0 %copy-start.2 = (bf16[64,2048]{1,0:T(8,128)(2,1)}, bf16[64,2048]{1,0:T(8,128)(2,1)S(1)}, u32[]{:S(2)}) copy-start(bf16[64,2048]{1,0:T(8,128)(2,1)S(1)} %stack_rows.2.refs_1_.refs_0_) | copy-start | bytes 786436
  27.7 20.0 %copy-start.1 = (bf16[128,2176]{1,0:T(8,128)(2,1)}, bf16[128,2176]{1,0:T(8,128)(2,1)S(1)}, u32[]{:S(2)}) copy-start(bf16[128,2176]{1,0:T(8,128)(2,1)S(1)} %ordered.3.refs_2_) | copy-start | bytes 1671172
  27.7 15.9 %collective-permute-start.6 = (bf16[128,2176]{1,0:T(8,128)(2,1)S(1)}, bf16[128,2176]{1,0:T(8,128)(2,1)}, u32[]{:S(2)}, u32[]{:S(2)}) collective-permute-start(bf16[128,2176]{1,0:T(8,128)(2,1)S(1)} %ordered.3.refs_2_), channel_id=1, source_target_pairs={{1,0},{2,1},{5,4},{6,5},{9,8},{10,9},{13,12},{14,13},{17,16},{18,1... | collective-permute-start | bytes 1671176 | tf_op jit(solution)/shard_map/ppermute | solution.py:36
  29.0 18.7 %copy-start = (bf16[128,2176]{1,0:T(8,128)(2,1)}, bf16[128,2176]{1,0:T(8,128)(2,1)S(1)}, u32[]{:S(2)}) copy-start(bf16[128,2176]{1,0:T(8,128)(2,1)S(1)} %ordered.2.refs_1_.refs_5_) | copy-start | bytes 1671172
  29.0 14.6 %collective-permute-start.5 = (bf16[128,2176]{1,0:T(8,128)(2,1)S(1)}, bf16[128,2176]{1,0:T(8,128)(2,1)S(1)}, u32[]{:S(2)}, u32[]{:S(2)}) collective-permute-start(bf16[128,2176]{1,0:T(8,128)(2,1)S(1)} %ordered.2.refs_1_.refs_5_), channel_id=1, source_target_pairs={{1,2},{2,3},{5,6},{6,7},{9,10},{10,11},{13,14},{14,15},{17,18},{18... | collective-permute-start | bytes 1671176 | tf_op jit(solution)/shard_map/ppermute | solution.py:36
  29.7 10.2 %collective-permute-start.11 = (bf16[64,2048]{1,0:T(8,128)(2,1)S(1)}, bf16[64,2048]{1,0:T(8,128)(2,1)S(1)}, u32[]{:S(2)}, u32[]{:S(2)}) collective-permute-start(bf16[64,2048]{1,0:T(8,128)(2,1)S(1)} %stack_rows.2.refs_1_.refs_0_), channel_id=1, source_target_pairs={{0,24},{4,28},{8,16},{12,20},{16,8},{20,12},{24,0},{28,4},{1,25},{... | collective-permute-start | bytes 786440 | tf_op jit(solution)/shard_map/ppermute | solution.py:40
  32.2 10.7 %collective-permute-start.10 = (bf16[64,2048]{1,0:T(8,128)(2,1)S(1)}, bf16[64,2048]{1,0:T(8,128)(2,1)S(1)}, u32[]{:S(2)}, u32[]{:S(2)}) collective-permute-start(bf16[64,2048]{1,0:T(8,128)(2,1)S(1)} %stack_rows.2.refs_1_.refs_0_), channel_id=1, source_target_pairs={{0,16},{4,20},{8,24},{12,28},{16,0},{20,4},{24,8},{28,12},{1,17},{... | collective-permute-start | bytes 786440 | tf_op jit(solution)/shard_map/ppermute | solution.py:40
  32.7 10.9 %collective-permute-start.9 = (bf16[64,2048]{1,0:T(8,128)(2,1)S(1)}, bf16[64,2048]{1,0:T(8,128)(2,1)}, u32[]{:S(2)}, u32[]{:S(2)}) collective-permute-start(bf16[64,2048]{1,0:T(8,128)(2,1)S(1)} %stack_rows.2.refs_1_.refs_0_), channel_id=1, source_target_pairs={{0,8},{4,12},{8,0},{12,4},{16,24},{20,28},{24,16},{28,20},{1,9},{5... | collective-permute-start | bytes 786440 | tf_op jit(solution)/shard_map/ppermute | solution.py:40
  47.7 4.9 %collective-permute-start.12 = (bf16[256,2048]{1,0:T(8,128)(2,1)}, bf16[256,2048]{1,0:T(8,128)(2,1)S(1)}, u32[]{:S(2)}, u32[]{:S(2)}) collective-permute-start(bf16[256,2048]{1,0:T(8,128)(2,1)} %stack_rows.3.near_ref), channel_id=1, source_target_pairs={{0,4},{4,0},{8,12},{12,8},{16,20},{20,16},{24,28},{28,24},{1,5},{5... | collective-permute-start | bytes 3145736 | tf_op jit(solution)/shard_map/ppermute | solution.py:40
  47.7 20.3 %collective-permute-start.8 = (bf16[128,2176]{1,0:T(8,128)(2,1)}, bf16[128,2176]{1,0:T(8,128)(2,1)S(1)}, u32[]{:S(2)}, u32[]{:S(2)}) collective-permute-start(bf16[128,2176]{1,0:T(8,128)(2,1)} %collective-permute-done.6.refs_6_.right_ref.refs_4_), channel_id=1, source_target_pairs={{1,0},{5,4},{9,8},{13,12},{17,16},{21,20},{25,24},{29,28}} | collective-permute-start | bytes 1671176 | tf_op jit(solution)/shard_map/ppermute | solution.py:36
  49.0 19.0 %collective-permute-start.7 = (bf16[128,2176]{1,0:T(8,128)(2,1)}, bf16[128,2176]{1,0:T(8,128)(2,1)S(1)}, u32[]{:S(2)}, u32[]{:S(2)}) collective-permute-start(bf16[128,2176]{1,0:T(8,128)(2,1)} %copy-done.7), channel_id=1, source_target_pairs={{2,3},{6,7},{10,11},{14,15},{18,19},{22,23},{26,27},{30,31}} | collective-permute-start | bytes 1671176 | tf_op jit(solution)/shard_map/ppermute | solution.py:36
  72.2 40.9 %all-to-all-start.1 = ((bf16[8,128,1024]{2,1,0:T(8,128)(2,1)}), bf16[8,128,1024]{2,1,0:T(8,128)(2,1)S(1)}, u32[]{:S(2)}, u32[]{:S(2)}) async-start(bf16[8,128,1024]{2,1,0:T(8,128)(2,1)} %place_last.1.refs_1_.refs_9_), calls=%async_computation.1 | async-start | bytes 4194304 | tf_op jit(solution)/shard_map/all_to_all | solution.py:480
  75.9 9.7 %collective-permute-start.13 = (f32[128,128]{1,0:T(8,128)S(1)}, f32[128,128]{1,0:T(8,128)S(1)}, u32[]{:S(2)}, u32[]{:S(2)}) collective-permute-start(f32[128,128]{1,0:T(8,128)S(1)} %copy-done.19), channel_id=1, source_target_pairs={{0,3},{1,0},{2,1},{3,2},{4,7},{5,4},{6,5},{7,6},{8,11},{9,8},{10,9... | collective-permute-start | bytes 196616 | tf_op jit(solution)/shard_map/ppermute | solution.py:32
  79.3 6.8 %collective-permute-start.14 = (f32[128,128]{1,0:T(8,128)S(1)}, f32[128,128]{1,0:T(8,128)S(1)}, u32[]{:S(2)}, u32[]{:S(2)}) collective-permute-start(f32[128,128]{1,0:T(8,128)S(1)} %copy-done.17), channel_id=1, source_target_pairs={{0,2},{1,3},{2,0},{3,1},{4,6},{5,7},{6,4},{7,5},{8,10},{9,11},{10,... | collective-permute-start | bytes 196616 | tf_op jit(solution)/shard_map/ppermute | solution.py:32
  79.3 6.8 %collective-permute-start.15 = (f32[128,128]{1,0:T(8,128)S(1)}, f32[128,128]{1,0:T(8,128)S(1)}, u32[]{:S(2)}, u32[]{:S(2)}) collective-permute-start(f32[128,128]{1,0:T(8,128)S(1)} %copy-done.16), channel_id=1, source_target_pairs={{0,1},{1,2},{2,3},{3,0},{4,5},{5,6},{6,7},{7,4},{8,9},{9,10},{10,1... | collective-permute-start | bytes 196616 | tf_op jit(solution)/shard_map/ppermute | solution.py:32
  89.1 24.0 %copy-start.4 = (bf16[128,384]{1,0:T(8,128)(2,1)S(1)}, bf16[128,384]{1,0:T(8,128)(2,1)}, u32[]{:S(2)}) copy-start(bf16[128,384]{1,0:T(8,128)(2,1)} %gradients.1.refs_0_) | copy-start | bytes 294916
  89.1 15.1 %collective-permute-start.22 = (bf16[128,384]{1,0:T(8,128)(2,1)}, bf16[128,384]{1,0:T(8,128)(2,1)S(1)}, u32[]{:S(2)}, u32[]{:S(2)}) collective-permute-start(bf16[128,384]{1,0:T(8,128)(2,1)} %gradients.1.refs_0_), channel_id=1, source_target_pairs={{0,28},{4,24},{8,20},{12,16},{16,12},{20,8},{24,4},{28,0},{1,29},{... | collective-permute-start | bytes 294920 | tf_op jit(solution)/shard_map/ppermute | solution.py:40
  90.7 16.5 %collective-permute-start.21 = (bf16[128,384]{1,0:T(8,128)(2,1)}, bf16[128,384]{1,0:T(8,128)(2,1)S(1)}, u32[]{:S(2)}, u32[]{:S(2)}) collective-permute-start(bf16[128,384]{1,0:T(8,128)(2,1)} %gradients.1.refs_0_), channel_id=1, source_target_pairs={{0,24},{4,28},{8,16},{12,20},{16,8},{20,12},{24,0},{28,4},{1,25},{... | collective-permute-start | bytes 294920 | tf_op jit(solution)/shard_map/ppermute | solution.py:40
  91.8 21.2 %collective-permute-start.20 = (bf16[128,384]{1,0:T(8,128)(2,1)}, bf16[128,384]{1,0:T(8,128)(2,1)S(1)}, u32[]{:S(2)}, u32[]{:S(2)}) collective-permute-start(bf16[128,384]{1,0:T(8,128)(2,1)} %gradients.1.refs_0_), channel_id=1, source_target_pairs={{0,20},{4,16},{8,28},{12,24},{16,4},{20,0},{24,12},{28,8},{1,21},{... | collective-permute-start | bytes 294920 | tf_op jit(solution)/shard_map/ppermute | solution.py:40
  93.2 19.9 %collective-permute-start.19 = (bf16[128,384]{1,0:T(8,128)(2,1)}, bf16[128,384]{1,0:T(8,128)(2,1)S(1)}, u32[]{:S(2)}, u32[]{:S(2)}) collective-permute-start(bf16[128,384]{1,0:T(8,128)(2,1)} %gradients.1.refs_0_), channel_id=1, source_target_pairs={{0,16},{4,20},{8,24},{12,28},{16,0},{20,4},{24,8},{28,12},{1,17},{... | collective-permute-start | bytes 294920 | tf_op jit(solution)/shard_map/ppermute | solution.py:40
  93.5 19.5 %collective-permute-start.18 = (bf16[128,384]{1,0:T(8,128)(2,1)}, bf16[128,384]{1,0:T(8,128)(2,1)S(1)}, u32[]{:S(2)}, u32[]{:S(2)}) collective-permute-start(bf16[128,384]{1,0:T(8,128)(2,1)} %gradients.1.refs_0_), channel_id=1, source_target_pairs={{0,12},{4,8},{8,4},{12,0},{16,28},{20,24},{24,20},{28,16},{1,13},{... | collective-permute-start | bytes 294920 | tf_op jit(solution)/shard_map/ppermute | solution.py:40
  104.2 8.8 %collective-permute-start.17 = (bf16[128,384]{1,0:T(8,128)(2,1)}, bf16[128,384]{1,0:T(8,128)(2,1)S(1)}, u32[]{:S(2)}, u32[]{:S(2)}) collective-permute-start(bf16[128,384]{1,0:T(8,128)(2,1)} %gradients.1.refs_0_), channel_id=1, source_target_pairs={{0,8},{4,12},{8,0},{12,4},{16,24},{20,28},{24,16},{28,20},{1,9},{5... | collective-permute-start | bytes 294920 | tf_op jit(solution)/shard_map/ppermute | solution.py:40
  107.2 5.8 %collective-permute-start.16 = (bf16[128,384]{1,0:T(8,128)(2,1)}, bf16[128,384]{1,0:T(8,128)(2,1)S(1)}, u32[]{:S(2)}, u32[]{:S(2)}) collective-permute-start(bf16[128,384]{1,0:T(8,128)(2,1)} %gradients.1.refs_0_), channel_id=1, source_target_pairs={{0,4},{4,0},{8,12},{12,8},{16,20},{20,16},{24,28},{28,24},{1,5},{5... | collective-permute-start | bytes 294920 | tf_op jit(solution)/shard_map/ppermute | solution.py:40
  (15 other events, 41.4 us)

commit v5 on v4

--- a/solution.py
+++ b/solution.py
@@ -352,7 +352,7 @@
     )(pre, *acts, *slices)
 
 
-def hand_over(teach, tok, after):
+def hand_over(teach, tok):
     n_dp, _, wide = teach.shape
     groups = n_dp // GROUP
     span = GROUP * tok
@@ -388,14 +388,14 @@
 
     return pl.pallas_call(
         kernel,
-        in_specs=[VMEM] * (1 + len(digits)) + [pl.BlockSpec(memory_space=pl.ANY)] * len(after),
+        in_specs=[VMEM] * (1 + len(digits)),
         out_specs=VMEM,
         out_shape=struct((n_dp, tok, wide)),
         scratch_shapes=[pltpu.VMEM((span, wide), jnp.float32)],
         compiler_params=params(60),
         cost_estimate=cost(0, 1024),
         name="hand_over",
-    )(teach, *digits, *after)
+    )(teach, *digits)
 
 
 def final_product(feats, handed, grads, masks):
@@ -420,7 +420,8 @@
         if masks:
             left_ref = refs[-1]
             for mask, ref in zip(masks, grad_refs):
-                left_ref[lax.axis_index("dp") ^ mask] = ref[...]
+                left_ref[lax.axis_index("dp") ^ mask] = ref[:count]
+                left_ref[lax.axis_index("dp") ^ mask ^ 1] = ref[count:]
             totals = group(0, totals)
         else:
             left_ref = grad_refs[0]
@@ -468,8 +469,9 @@
     far_left, far_right = hop(from_left, rightward[1:]), hop(from_right, leftward[:-1])
     ends = [hop(far_left, rightward[-1:]), hop(far_right, leftward[:1])]
 
+    handed = hand_over(teach, tok)
     near = stack_rows(
-        [mine] + others, n_t * rows, width, 60, after=[teach, far_left, far_right]
+        [mine] + others, n_t * rows, width, 60, after=[handed, far_left, far_right]
     )
     far = swap(near, n_dp, 1)
     partial = partial_products(near, far, student_hidden, projected, n_t, rows, factor, after=[])
@@ -482,12 +484,12 @@
     slices = [own, from_left, from_right, far_left, far_right, *ends]
     pre = gate_and_up(slices, gate_bucket, up_bucket, n_t, after=[sent])
     grads = gradients(pre, acts, [own, from_left, far_left, ends[0]], width)
-    masks = list(range(n_dp)) if n_dp == GROUP else []
+    masks = [0, 2, 4, 6] if n_dp == GROUP else []
     if masks:
-        grads = [grads] + [swap(grads, n_dp, mask) for mask in masks[1:]]
+        pair = stack_rows([grads, swap(grads, n_dp, 1)], tok, grads.shape[1], 8)
+        grads = [pair] + [swap(pair, n_dp, mask) for mask in masks[1:]]
     else:
         grads = [lax.all_gather(grads, "dp")]
-    handed = hand_over(teach, tok, after=[sent])
     return final_product(feats, handed, grads, masks)
 
 

time: 117 us -> 115 us (0.983)
  local copies, waits for them, and re-layouts: 7.03 us -> 9.24 us
  waiting for transfers between devices: 40.7 us -> 38.5 us
  starting transfers between devices: 37.9 us -> 35.9 us
    ppermute x11 -> x8, starting transfers between devices: 9.43 us -> 7.11 us  [swap(): return lax.ppermute(x, 'dp', [(i, i ^ mask) for i in range(count)])]
    unnamed x44 -> x54, local copies, waits for them, and re-layouts: 7.03 us -> 9.24 us
    ppermute x11 -> x8, waiting for transfers between devices: 21.8 us -> 20.9 us  [swap(): return lax.ppermute(x, 'dp', [(i, i ^ mask) for i in range(count)])]
  transfers between devices with their start and end apart: 25 -> 22, of which waited for: 8 -> 9; matrix products, arithmetic and copies ran while one was open for 0% -> 0% of each run, Pallas kernels for 17% -> 17%
where the time goes in v5:
time: 115 us; the launch traced here: 114 us
  waiting for transfers between devices  38.5 us (33%)
  starting transfers between devices  35.9 us (31%)
  Pallas kernels  29.6 us (26%)
  local copies, waits for them, and re-layouts  9.24 us (8%)
    ppermute x8, waiting for transfers between devices, swap(): return lax.ppermute(x, 'dp', [(i, i ^ mask) for i in range(count)])  20.9 us
    ppermute x6, starting transfers between devices, hop(): return lax.ppermute(x, 'tensor', pairs)  11 us
    ppermute x6, waiting for transfers between devices, hop(): return lax.ppermute(x, 'tensor', pairs)  10.6 us
    ppermute x6, starting transfers between devices, shift(): lax.ppermute(x, 'tensor', [(i, (i + by) % count) for i in range(count)])  9.8 us
    unnamed x54, local copies, waits for them, and re-layouts  9.24 us
    ppermute x8, starting transfers between devices, swap(): return lax.ppermute(x, 'dp', [(i, i ^ mask) for i in range(count)])  7.11 us
    ppermute x6, waiting for transfers between devices, shift(): lax.ppermute(x, 'tensor', [(i, (i + by) % count) for i in range(count)])  7.05 us
    pallas_call x1, Pallas kernels, hand_over(): pl.pallas_call(kernel, in_specs=[VMEM] * (1 + len(digits)), out_specs=VME...  5.84 us
  transfers between devices with their start and end apart: 22, of which 9 were waited for; matrix products, arithmetic and copies ran while one was open for 0% of the time, Pallas kernels for 17%

profile of v5, /device:TPU:0, one launch (start us, length us, event | category | flops | bytes accessed | tf_op | source)
XLA Modules:
  0.0 114.2 jit_solution(9696974920404248277)
XLA Ops:
  0.6 2.9 %prepare.1 = (bf16[128,2176]{1,0:T(8,128)(2,1)}, bf16[16,2048]{1,0:T(8,128)(2,1)}, bf16[16,2048]{1,0:T(8,128)(2,1)}, bf16[16,2048]{1,0:T(8,128)(2,1)}, bf16[16,2...) custom-call(s32[1,128]{1,0:T(1,128)} %bitcast.1, bf16[128,4096]{1,0:T(8,128)(2,1)} %t_ref.1, bf16[128,2048]{1,0:T(8,128)(2,1)} %x_ref.1, ...), custom_call_target="tpu_custom_call" | custom-call | bytes 1024 | tf_op jit(solution)/shard_map/prepare/pallas_call | solution.py:111
  3.6 1.4 %collective-permute-start.4 = (bf16[128,2176]{1,0:T(8,128)(2,1)}, bf16[128,2176]{1,0:T(8,128)(2,1)S(1)}, u32[]{:S(2)}, u32[]{:S(2)}) collective-permute-start(bf16[128,2176]{1,0:T(8,128)(2,1)} %get-tuple-element.13.refs_0_.refs_4_), channel_id=1, source_target_pairs={{1,0},{2,1},{3,2},{5,4},{6,5},{7,6},{9,8},{10,9},{11,10},{13,12},{... | collective-permute-start | bytes 1671176 | tf_op jit(solution)/shard_map/ppermute | solution.py:36
  5.0 5.6 %collective-permute-start = (bf16[128,2176]{1,0:T(8,128)(2,1)}, bf16[128,2176]{1,0:T(8,128)(2,1)S(1)}, u32[]{:S(2)}, u32[]{:S(2)}) collective-permute-start(bf16[128,2176]{1,0:T(8,128)(2,1)} %get-tuple-element.13.refs_0_.refs_4_), channel_id=1, source_target_pairs={{0,1},{1,2},{2,3},{4,5},{5,6},{6,7},{8,9},{9,10},{10,11},{12,13},{... | collective-permute-start | bytes 1671176 | tf_op jit(solution)/shard_map/ppermute | solution.py:36
  10.6 4.3 %all-to-all-start = ((bf16[8,144,512]{2,1,0:T(8,128)(2,1)}), bf16[8,144,512]{2,1,0:T(8,128)(2,1)}, u32[]{:S(2)}, u32[]{:S(2)}) async-start(bf16[8,144,512]{2,1,0:T(8,128)(2,1)} %get-tuple-element.18), calls=%async_computation | async-start | bytes 2359296 | tf_op jit(solution)/shard_map/all_to_all | solution.py:461
  14.9 2.0 %collective-permute-start.1 = (bf16[16,2048]{1,0:T(8,128)(2,1)S(1)}, bf16[16,2048]{1,0:T(8,128)(2,1)S(1)}, u32[]{:S(2)}, u32[]{:S(2)}) collective-permute-start(bf16[16,2048]{1,0:T(8,128)(2,1)S(1)} %copy-done.26), channel_id=1, source_target_pairs={{0,1},{1,2},{2,3},{3,0},{4,5},{5,6},{6,7},{7,4},{8,9},{9,10},{10,1... | collective-permute-start | bytes 196616 | tf_op jit(solution)/shard_map/ppermute | solution.py:32
  17.0 1.1 collective-permute-start.2
  18.1 2.8 %collective-permute-start.3 = (bf16[16,2048]{1,0:T(8,128)(2,1)S(1)}, bf16[16,2048]{1,0:T(8,128)(2,1)S(1)}, u32[]{:S(2)}, u32[]{:S(2)}) collective-permute-start(bf16[16,2048]{1,0:T(8,128)(2,1)S(1)} %copy-done.23), channel_id=1, source_target_pairs={{0,3},{1,0},{2,1},{3,2},{4,7},{5,4},{6,5},{7,6},{8,11},{9,8},{10,9... | collective-permute-start | bytes 196616 | tf_op jit(solution)/shard_map/ppermute | solution.py:32
  20.9 5.3 %collective-permute-done.1.refs_1_ = bf16[16,2048]{1,0:T(8,128)(2,1)S(1)} collective-permute-done((bf16[16,2048]{1,0:T(8,128)(2,1)S(1)}, bf16[16,2048]{1,0:T(8,128)(2,1)S(1)}, u32[]{:S(2)}, u32[]{:S(2)}) %collective-permute-start.1) | collective-permute-done | bytes 65568 | tf_op jit(solution)/shard_map/ppermute | solution.py:32
  26.2 1.3 %collective-permute-done.2.refs_2_ = bf16[16,2048]{1,0:T(8,128)(2,1)S(1)} collective-permute-done((bf16[16,2048]{1,0:T(8,128)(2,1)S(1)}, bf16[16,2048]{1,0:T(8,128)(2,1)S(1)}, u32[]{:S(2)}, u32[]{:S(2)}) %collective-permute-start.2) | collective-permute-done | bytes 65568 | tf_op jit(solution)/shard_map/ppermute | solution.py:32
  27.7 1.3 %collective-permute-start.6 = (bf16[128,2176]{1,0:T(8,128)(2,1)S(1)}, bf16[128,2176]{1,0:T(8,128)(2,1)S(1)}, u32[]{:S(2)}, u32[]{:S(2)}) collective-permute-start(bf16[128,2176]{1,0:T(8,128)(2,1)S(1)} %ordered.3.refs_2_), channel_id=1, source_target_pairs={{1,0},{2,1},{5,4},{6,5},{9,8},{10,9},{13,12},{14,13},{17,16},{18,1... | collective-permute-start | bytes 1671176 | tf_op jit(solution)/shard_map/ppermute | solution.py:36
  29.7 2.5 %collective-permute-start.11 = (bf16[64,2048]{1,0:T(8,128)(2,1)S(1)}, bf16[64,2048]{1,0:T(8,128)(2,1)S(1)}, u32[]{:S(2)}, u32[]{:S(2)}) collective-permute-start(bf16[64,2048]{1,0:T(8,128)(2,1)S(1)} %stack_rows.3.refs_1_.refs_0_), channel_id=1, source_target_pairs={{0,24},{4,28},{8,16},{12,20},{16,8},{20,12},{24,0},{28,4},{1,25},{... | collective-permute-start | bytes 786440 | tf_op jit(solution)/shard_map/ppermute | solution.py:40
  33.3 5.8 %hand_over.1.refs_4_.handed_ref = bf16[8,128,512]{2,1,0:T(8,128)(2,1)} custom-call(bf16[8,144,512]{2,1,0:T(8,128)(2,1)} %all-to-all-done.refs_0_), custom_call_target="tpu_custom_call" | custom-call | bytes 1024 | tf_op jit(solution)/shard_map/hand_over/pallas_call | solution.py:389
  39.9 2.9 %collective-permute-done.10.refs_2_ = bf16[64,2048]{1,0:T(8,128)(2,1)S(1)} collective-permute-done((bf16[64,2048]{1,0:T(8,128)(2,1)S(1)}, bf16[64,2048]{1,0:T(8,128)(2,1)S(1)}, u32[]{:S(2)}, u32[]{:S(2)}) %collective-permute-start.10) | collective-permute-done | bytes 262176 | tf_op jit(solution)/shard_map/ppermute | solution.py:40
  44.7 2.2 %stack_rows.4.near_ref = bf16[256,2048]{1,0:T(8,128)(2,1)} custom-call(bf16[64,2048]{1,0:T(8,128)(2,1)} %copy-done.3, bf16[64,2048]{1,0:T(8,128)(2,1)} %copy-done.17, bf16[64,2048]{1,0:T(8,128)(2,1)} %copy-done.16, bf16[64,2048]{1,0:T(8,128)(2,1)} %copy-done.15, bf16[8,128,512]{2,1,0:T(8,128)(2,1)} %hand_over.1.refs_4_.handed_ref, ...), custom_call_target="tpu_custom_call" | custom-call | bytes 1024 | tf_op jit(solution)/shard_map/stack_rows/pallas_call | solution.py:135
  46.9 1.3 %collective-permute-start.8 = (bf16[128,2176]{1,0:T(8,128)(2,1)}, bf16[128,2176]{1,0:T(8,128)(2,1)S(1)}, u32[]{:S(2)}, u32[]{:S(2)}) collective-permute-start(bf16[128,2176]{1,0:T(8,128)(2,1)} %copy-done.12), channel_id=1, source_target_pairs={{1,0},{5,4},{9,8},{13,12},{17,16},{21,20},{25,24},{29,28}} | collective-permute-start | bytes 1671176 | tf_op jit(solution)/shard_map/ppermute | solution.py:36
  49.0 2.8 %place_slices.1.in_ref = bf16[8,128,1024]{2,1,0:T(8,128)(2,1)} custom-call(bf16[128,2176]{1,0:T(8,128)(2,1)} %get-tuple-element.13.refs_0_.refs_4_, bf16[128,2176]{1,0:T(8,128)(2,1)} %copy-done.1, bf16[128,2176]{1,0:T(8,128)(2,1)} %copy-done.2), custom_call_target="tpu_custom_call" | custom-call | bytes 1024 | tf_op jit(solution)/shard_map/place_slices/pallas_call | solution.py:214
  51.8 1.0 copy-done.14
  52.8 3.2 %partial_products.1 = (f32[128,128]{1,0:T(8,128)}, f32[128,128]{1,0:T(8,128)}, f32[128,128]{1,0:T(8,128)}, f32[128,128]{1,0:T(8,128)}) custom-call(bf16[256,2048]{1,0:T(8,128)(2,1)} %stack_rows.4.near_ref, bf16[256,2048]{1,0:T(8,128)(2,1)} %copy-done.14, bf16[128,2048]{1,0:T(8,128)(2,1)} %s_ref.3, bf16[128,2048]{1,0:T(8,128)(2,1)} %p_ref.3), custom_call_target="tpu_custom_call" | custom-call | bytes 1024 | tf_op jit(solution)/shard_map/partial_products/pallas_call | solution.py:179
  56.0 10.5 %collective-permute-done.8.first_ref.refs_6_ = bf16[128,2176]{1,0:T(8,128)(2,1)S(1)} collective-permute-done((bf16[128,2176]{1,0:T(8,128)(2,1)}, bf16[128,2176]{1,0:T(8,128)(2,1)S(1)}, u32[]{:S(2)}, u32[]{:S(2)}) %collective-permute-start.8) | collective-permute-done | bytes 557088 | tf_op jit(solution)/shard_map/ppermute | solution.py:36
  67.6 3.2 %place_last.1.refs_9_ = bf16[8,128,1024]{2,1,0:T(8,128)(2,1)} custom-call(bf16[8,128,1024]{2,1,0:T(8,128)(2,1)} %place_slices.1.in_ref, bf16[128,2176]{1,0:T(8,128)(2,1)} %copy-done.10, bf16[128,2176]{1,0:T(8,128)(2,1)} %copy-done.12, bf16[128,2176]{1,0:T(8,128)(2,1)} %copy-done.11, bf16[128,2176]{1,0:T(8,128)(2,1)} %copy-done.13, ...), custom_call_target="tpu_custom_call", output_to_operand_aliasing={{}: (0, {})} | custom-call | bytes 1024 | tf_op jit(solution)/shard_map/place_last/pallas_call | solution.py:263
  70.8 3.7 %all-to-all-start.1 = ((bf16[8,128,1024]{2,1,0:T(8,128)(2,1)}), bf16[8,128,1024]{2,1,0:T(8,128)(2,1)S(1)}, u32[]{:S(2)}, u32[]{:S(2)}) async-start(bf16[8,128,1024]{2,1,0:T(8,128)(2,1)} %place_last.1.refs_9_), calls=%async_computation.1 | async-start | bytes 4194304 | tf_op jit(solution)/shard_map/all_to_all | solution.py:482
  74.6 3.1 %collective-permute-start.13 = (f32[128,128]{1,0:T(8,128)S(1)}, f32[128,128]{1,0:T(8,128)S(1)}, u32[]{:S(2)}, u32[]{:S(2)}) collective-permute-start(f32[128,128]{1,0:T(8,128)S(1)} %copy-done.24), channel_id=1, source_target_pairs={{0,3},{1,0},{2,1},{3,2},{4,7},{5,4},{6,5},{7,6},{8,11},{9,8},{10,9... | collective-permute-start | bytes 196616 | tf_op jit(solution)/shard_map/ppermute | solution.py:32
  78.4 5.7 %gate_and_up.1.pre_ref = f32[128,256]{1,0:T(8,128)} custom-call(bf16[128,2176]{1,0:T(8,128)(2,1)} %get-tuple-element.13.refs_0_.refs_4_, bf16[128,2176]{1,0:T(8,128)(2,1)} %copy-done.1, bf16[128,2176]{1,0:T(8,128)(2,1)} %copy-done.2, bf16[128,2176]{1,0:T(8,128)(2,1)} %copy-done.10, bf16[128,2176]{1,0:T(8,128)(2,1)} %copy-done.12, ...), custom_call_target="tpu_custom_call" | custom-call | bytes 1024 | tf_op jit(solution)/shard_map/gate_and_up/pallas_call | solution.py:300
  85.8 1.8 %gradients.1.refs_0_ = bf16[128,384]{1,0:T(8,128)(2,1)} custom-call(f32[128,256]{1,0:T(8,128)} %gate_and_up.1.pre_ref, f32[128,128]{1,0:T(8,128)} %get-tuple-element.19.refs_0_, f32[128,128]{1,0:T(8,128)} %copy-done.18, f32[128,128]{1,0:T(8,128)} %copy-done.19, f32[128,128]{1,0:T(8,128)} %copy-done.20, bf16[128,2176]{1,0:T(8,128)(2,1)} %get-tuple-element.13.refs_0_.refs_4_, ...), custom_call_target="tpu_custom_call" | custom-call | bytes 1024 | tf_op jit(solution)/shard_map/gradients/pallas_call | solution.py:343
  87.6 1.5 %collective-permute-done.16.refs_1_ = bf16[128,384]{1,0:T(8,128)(2,1)S(1)} collective-permute-done((bf16[128,384]{1,0:T(8,128)(2,1)}, bf16[128,384]{1,0:T(8,128)(2,1)S(1)}, u32[]{:S(2)}, u32[]{:S(2)}) %collective-permute-start.16) | collective-permute-done | bytes 98336 | tf_op jit(solution)/shard_map/ppermute | solution.py:40
  89.1 0.9 copy-done.4
  90.0 2.7 %collective-permute-start.19 = (bf16[256,384]{1,0:T(8,128)(2,1)S(1)}, bf16[256,384]{1,0:T(8,128)(2,1)S(1)}, u32[]{:S(2)}, u32[]{:S(2)}) collective-permute-start(bf16[256,384]{1,0:T(8,128)(2,1)S(1)} %stack_rows.5.refs_0_), channel_id=1, source_target_pairs={{0,24},{4,28},{8,16},{12,20},{16,8},{20,12},{24,0},{28,4},{1,25},{... | collective-permute-start | bytes 589832 | tf_op jit(solution)/shard_map/ppermute | solution.py:40
  93.6 12.3 %collective-permute-done.19.refs_3_ = bf16[256,384]{1,0:T(8,128)(2,1)S(1)} collective-permute-done((bf16[256,384]{1,0:T(8,128)(2,1)S(1)}, bf16[256,384]{1,0:T(8,128)(2,1)S(1)}, u32[]{:S(2)}, u32[]{:S(2)}) %collective-permute-start.19) | collective-permute-done | bytes 196640 | tf_op jit(solution)/shard_map/ppermute | solution.py:40
  105.9 3.3 %collective-permute-done.18.refs_2_ = bf16[256,384]{1,0:T(8,128)(2,1)S(1)} collective-permute-done((bf16[256,384]{1,0:T(8,128)(2,1)S(1)}, bf16[256,384]{1,0:T(8,128)(2,1)S(1)}, u32[]{:S(2)}, u32[]{:S(2)}) %collective-permute-start.18) | collective-permute-done | bytes 196640 | tf_op jit(solution)/shard_map/ppermute | solution.py:40
  110.5 0.9 copy-done.6
  111.4 0.9 copy-done.8
  112.4 1.8 %final_product.1 = (f32[128,1,512]{2,1,0:T(1,128)}, f32[128,1024]{1,0:T(8,128)}, f32[128,1024]{1,0:T(8,128)}) custom-call(bf16[8,128,1024]{2,1,0:T(8,128)(2,1)S(1)} %all-to-all-done.1.feats_ref, bf16[8,128,512]{2,1,0:T(8,128)(2,1)S(1)} %copy-done, bf16[256,384]{1,0:T(8,128)(2,1)S(1)} %stack_rows.5.refs_0_, bf16[256,384]{1,0:T(8,128)(2,1)S(1)} %copy-done.8, ...), custom_call_target="tpu_custom_call" | custom-call | bytes 1024 | tf_op jit(solution)/shard_map/final_product/pallas_call | solution.py:433
  (79 shorter events, 10.8 us)
Async XLA Ops:
  3.6 11.4 %copy-start.26 = (bf16[16,2048]{1,0:T(8,128)(2,1)S(1)}, bf16[16,2048]{1,0:T(8,128)(2,1)}, u32[]{:S(2)}) copy-start(bf16[16,2048]{1,0:T(8,128)(2,1)} %get-tuple-element.15) | copy-start | bytes 196612
  3.6 13.4 %copy-start.25 = (bf16[16,2048]{1,0:T(8,128)(2,1)S(1)}, bf16[16,2048]{1,0:T(8,128)(2,1)}, u32[]{:S(2)}) copy-start(bf16[16,2048]{1,0:T(8,128)(2,1)} %get-tuple-element.16) | copy-start | bytes 196612
  3.6 14.5 %copy-start.23 = (bf16[16,2048]{1,0:T(8,128)(2,1)S(1)}, bf16[16,2048]{1,0:T(8,128)(2,1)}, u32[]{:S(2)}) copy-start(bf16[16,2048]{1,0:T(8,128)(2,1)} %get-tuple-element.17) | copy-start | bytes 196612
  3.6 24.0 %copy-start.9 = (bf16[16,2048]{1,0:T(8,128)(2,1)S(1)}, bf16[16,2048]{1,0:T(8,128)(2,1)}, u32[]{:S(2)}) copy-start(bf16[16,2048]{1,0:T(8,128)(2,1)} %get-tuple-element.14.refs_0_) | copy-start | bytes 196612
  3.6 24.0 %collective-permute-start.4 = (bf16[128,2176]{1,0:T(8,128)(2,1)}, bf16[128,2176]{1,0:T(8,128)(2,1)S(1)}, u32[]{:S(2)}, u32[]{:S(2)}) collective-permute-start(bf16[128,2176]{1,0:T(8,128)(2,1)} %get-tuple-element.13.refs_0_.refs_4_), channel_id=1, source_target_pairs={{1,0},{2,1},{3,2},{5,4},{6,5},{7,6},{9,8},{10,9},{11,10},{13,12},{... | collective-permute-start | bytes 1671176 | tf_op jit(solution)/shard_map/ppermute | solution.py:36
  5.0 23.9 %collective-permute-start = (bf16[128,2176]{1,0:T(8,128)(2,1)}, bf16[128,2176]{1,0:T(8,128)(2,1)S(1)}, u32[]{:S(2)}, u32[]{:S(2)}) collective-permute-start(bf16[128,2176]{1,0:T(8,128)(2,1)} %get-tuple-element.13.refs_0_.refs_4_), channel_id=1, source_target_pairs={{0,1},{1,2},{2,3},{4,5},{5,6},{6,7},{8,9},{9,10},{10,11},{12,13},{... | collective-permute-start | bytes 1671176 | tf_op jit(solution)/shard_map/ppermute | solution.py:36
  10.6 22.6 %all-to-all-start = ((bf16[8,144,512]{2,1,0:T(8,128)(2,1)}), bf16[8,144,512]{2,1,0:T(8,128)(2,1)}, u32[]{:S(2)}, u32[]{:S(2)}) async-start(bf16[8,144,512]{2,1,0:T(8,128)(2,1)} %get-tuple-element.18), calls=%async_computation | async-start | bytes 2359296 | tf_op jit(solution)/shard_map/all_to_all | solution.py:461
  14.9 11.3 %collective-permute-start.1 = (bf16[16,2048]{1,0:T(8,128)(2,1)S(1)}, bf16[16,2048]{1,0:T(8,128)(2,1)S(1)}, u32[]{:S(2)}, u32[]{:S(2)}) collective-permute-start(bf16[16,2048]{1,0:T(8,128)(2,1)S(1)} %copy-done.26), channel_id=1, source_target_pairs={{0,1},{1,2},{2,3},{3,0},{4,5},{5,6},{6,7},{7,4},{8,9},{9,10},{10,1... | collective-permute-start | bytes 196616 | tf_op jit(solution)/shard_map/ppermute | solution.py:32
  17.0 10.6 %collective-permute-start.2 = (bf16[16,2048]{1,0:T(8,128)(2,1)S(1)}, bf16[16,2048]{1,0:T(8,128)(2,1)S(1)}, u32[]{:S(2)}, u32[]{:S(2)}) collective-permute-start(bf16[16,2048]{1,0:T(8,128)(2,1)S(1)} %copy-done.25), channel_id=1, source_target_pairs={{0,2},{1,3},{2,0},{3,1},{4,6},{5,7},{6,4},{7,5},{8,10},{9,11},{10,... | collective-permute-start | bytes 196616 | tf_op jit(solution)/shard_map/ppermute | solution.py:32
  18.1 9.5 %collective-permute-start.3 = (bf16[16,2048]{1,0:T(8,128)(2,1)S(1)}, bf16[16,2048]{1,0:T(8,128)(2,1)S(1)}, u32[]{:S(2)}, u32[]{:S(2)}) collective-permute-start(bf16[16,2048]{1,0:T(8,128)(2,1)S(1)} %copy-done.23), channel_id=1, source_target_pairs={{0,3},{1,0},{2,1},{3,2},{4,7},{5,4},{6,5},{7,6},{8,11},{9,8},{10,9... | collective-permute-start | bytes 196616 | tf_op jit(solution)/shard_map/ppermute | solution.py:32
  27.6 11.5 %copy-start.3 = (bf16[64,2048]{1,0:T(8,128)(2,1)}, bf16[64,2048]{1,0:T(8,128)(2,1)S(1)}, u32[]{:S(2)}) copy-start(bf16[64,2048]{1,0:T(8,128)(2,1)S(1)} %stack_rows.3.refs_1_.refs_0_) | copy-start | bytes 786436
  27.7 19.3 %copy-start.2 = (bf16[128,2176]{1,0:T(8,128)(2,1)}, bf16[128,2176]{1,0:T(8,128)(2,1)S(1)}, u32[]{:S(2)}) copy-start(bf16[128,2176]{1,0:T(8,128)(2,1)S(1)} %ordered.3.refs_2_) | copy-start | bytes 1671172
  27.7 15.2 %collective-permute-start.6 = (bf16[128,2176]{1,0:T(8,128)(2,1)S(1)}, bf16[128,2176]{1,0:T(8,128)(2,1)S(1)}, u32[]{:S(2)}, u32[]{:S(2)}) collective-permute-start(bf16[128,2176]{1,0:T(8,128)(2,1)S(1)} %ordered.3.refs_2_), channel_id=1, source_target_pairs={{1,0},{2,1},{5,4},{6,5},{9,8},{10,9},{13,12},{14,13},{17,16},{18,1... | collective-permute-start | bytes 1671176 | tf_op jit(solution)/shard_map/ppermute | solution.py:36
  29.0 18.0 %copy-start.1 = (bf16[128,2176]{1,0:T(8,128)(2,1)}, bf16[128,2176]{1,0:T(8,128)(2,1)S(1)}, u32[]{:S(2)}) copy-start(bf16[128,2176]{1,0:T(8,128)(2,1)S(1)} %ordered.2.refs_1_.refs_5_) | copy-start | bytes 1671172
  29.0 13.9 %collective-permute-start.5 = (bf16[128,2176]{1,0:T(8,128)(2,1)S(1)}, bf16[128,2176]{1,0:T(8,128)(2,1)S(1)}, u32[]{:S(2)}, u32[]{:S(2)}) collective-permute-start(bf16[128,2176]{1,0:T(8,128)(2,1)S(1)} %ordered.2.refs_1_.refs_5_), channel_id=1, source_target_pairs={{1,2},{2,3},{5,6},{6,7},{9,10},{10,11},{13,14},{14,15},{17,18},{18... | collective-permute-start | bytes 1671176 | tf_op jit(solution)/shard_map/ppermute | solution.py:36
  29.7 10.2 %collective-permute-start.11 = (bf16[64,2048]{1,0:T(8,128)(2,1)S(1)}, bf16[64,2048]{1,0:T(8,128)(2,1)S(1)}, u32[]{:S(2)}, u32[]{:S(2)}) collective-permute-start(bf16[64,2048]{1,0:T(8,128)(2,1)S(1)} %stack_rows.3.refs_1_.refs_0_), channel_id=1, source_target_pairs={{0,24},{4,28},{8,16},{12,20},{16,8},{20,12},{24,0},{28,4},{1,25},{... | collective-permute-start | bytes 786440 | tf_op jit(solution)/shard_map/ppermute | solution.py:40
  32.2 10.7 %collective-permute-start.10 = (bf16[64,2048]{1,0:T(8,128)(2,1)S(1)}, bf16[64,2048]{1,0:T(8,128)(2,1)S(1)}, u32[]{:S(2)}, u32[]{:S(2)}) collective-permute-start(bf16[64,2048]{1,0:T(8,128)(2,1)S(1)} %stack_rows.3.refs_1_.refs_0_), channel_id=1, source_target_pairs={{0,16},{4,20},{8,24},{12,28},{16,0},{20,4},{24,8},{28,12},{1,17},{... | collective-permute-start | bytes 786440 | tf_op jit(solution)/shard_map/ppermute | solution.py:40
  32.7 10.2 %collective-permute-start.9 = (bf16[64,2048]{1,0:T(8,128)(2,1)S(1)}, bf16[64,2048]{1,0:T(8,128)(2,1)S(1)}, u32[]{:S(2)}, u32[]{:S(2)}) collective-permute-start(bf16[64,2048]{1,0:T(8,128)(2,1)S(1)} %stack_rows.3.refs_1_.refs_0_), channel_id=1, source_target_pairs={{0,8},{4,12},{8,0},{12,4},{16,24},{20,28},{24,16},{28,20},{1,9},{5... | collective-permute-start | bytes 786440 | tf_op jit(solution)/shard_map/ppermute | solution.py:40
  46.9 4.9 %collective-permute-start.12 = (bf16[256,2048]{1,0:T(8,128)(2,1)}, bf16[256,2048]{1,0:T(8,128)(2,1)S(1)}, u32[]{:S(2)}, u32[]{:S(2)}) collective-permute-start(bf16[256,2048]{1,0:T(8,128)(2,1)} %stack_rows.4.near_ref), channel_id=1, source_target_pairs={{0,4},{4,0},{8,12},{12,8},{16,20},{20,16},{24,28},{28,24},{1,5},{5... | collective-permute-start | bytes 3145736 | tf_op jit(solution)/shard_map/ppermute | solution.py:40
  46.9 19.6 %collective-permute-start.8 = (bf16[128,2176]{1,0:T(8,128)(2,1)}, bf16[128,2176]{1,0:T(8,128)(2,1)S(1)}, u32[]{:S(2)}, u32[]{:S(2)}) collective-permute-start(bf16[128,2176]{1,0:T(8,128)(2,1)} %copy-done.12), channel_id=1, source_target_pairs={{1,0},{5,4},{9,8},{13,12},{17,16},{21,20},{25,24},{29,28}} | collective-permute-start | bytes 1671176 | tf_op jit(solution)/shard_map/ppermute | solution.py:36
  48.2 18.3 %collective-permute-start.7 = (bf16[128,2176]{1,0:T(8,128)(2,1)}, bf16[128,2176]{1,0:T(8,128)(2,1)S(1)}, u32[]{:S(2)}, u32[]{:S(2)}) collective-permute-start(bf16[128,2176]{1,0:T(8,128)(2,1)} %copy-done.10), channel_id=1, source_target_pairs={{2,3},{6,7},{10,11},{14,15},{18,19},{22,23},{26,27},{30,31}} | collective-permute-start | bytes 1671176 | tf_op jit(solution)/shard_map/ppermute | solution.py:36
  70.8 6.9 %copy-start.22 = (f32[128,128]{1,0:T(8,128)S(1)}, f32[128,128]{1,0:T(8,128)}, u32[]{:S(2)}) copy-start(f32[128,128]{1,0:T(8,128)} %get-tuple-element.21) | copy-start | bytes 196612
  70.8 6.9 %copy-start.21 = (f32[128,128]{1,0:T(8,128)S(1)}, f32[128,128]{1,0:T(8,128)}, u32[]{:S(2)}) copy-start(f32[128,128]{1,0:T(8,128)} %get-tuple-element.22) | copy-start | bytes 196612
  70.8 39.7 %all-to-all-start.1 = ((bf16[8,128,1024]{2,1,0:T(8,128)(2,1)}), bf16[8,128,1024]{2,1,0:T(8,128)(2,1)S(1)}, u32[]{:S(2)}, u32[]{:S(2)}) async-start(bf16[8,128,1024]{2,1,0:T(8,128)(2,1)} %place_last.1.refs_9_), calls=%async_computation.1 | async-start | bytes 4194304 | tf_op jit(solution)/shard_map/all_to_all | solution.py:482
  74.6 9.6 %collective-permute-start.13 = (f32[128,128]{1,0:T(8,128)S(1)}, f32[128,128]{1,0:T(8,128)S(1)}, u32[]{:S(2)}, u32[]{:S(2)}) collective-permute-start(f32[128,128]{1,0:T(8,128)S(1)} %copy-done.24), channel_id=1, source_target_pairs={{0,3},{1,0},{2,1},{3,2},{4,7},{5,4},{6,5},{7,6},{8,11},{9,8},{10,9... | collective-permute-start | bytes 196616 | tf_op jit(solution)/shard_map/ppermute | solution.py:32
  77.7 6.8 %collective-permute-start.14 = (f32[128,128]{1,0:T(8,128)S(1)}, f32[128,128]{1,0:T(8,128)S(1)}, u32[]{:S(2)}, u32[]{:S(2)}) collective-permute-start(f32[128,128]{1,0:T(8,128)S(1)} %copy-done.22), channel_id=1, source_target_pairs={{0,2},{1,3},{2,0},{3,1},{4,6},{5,7},{6,4},{7,5},{8,10},{9,11},{10,... | collective-permute-start | bytes 196616 | tf_op jit(solution)/shard_map/ppermute | solution.py:32
  77.7 6.8 %collective-permute-start.15 = (f32[128,128]{1,0:T(8,128)S(1)}, f32[128,128]{1,0:T(8,128)S(1)}, u32[]{:S(2)}, u32[]{:S(2)}) collective-permute-start(f32[128,128]{1,0:T(8,128)S(1)} %copy-done.21), channel_id=1, source_target_pairs={{0,1},{1,2},{2,3},{3,0},{4,5},{5,6},{6,7},{7,4},{8,9},{9,10},{10,1... | collective-permute-start | bytes 196616 | tf_op jit(solution)/shard_map/ppermute | solution.py:32
  84.1 26.4 %copy-start = (bf16[8,128,512]{2,1,0:T(8,128)(2,1)S(1)}, bf16[8,128,512]{2,1,0:T(8,128)(2,1)}, u32[]{:S(2)}) copy-start(bf16[8,128,512]{2,1,0:T(8,128)(2,1)} %hand_over.1.refs_4_.handed_ref) | copy-start | bytes 3145732
  87.6 1.5 %collective-permute-start.16 = (bf16[128,384]{1,0:T(8,128)(2,1)}, bf16[128,384]{1,0:T(8,128)(2,1)S(1)}, u32[]{:S(2)}, u32[]{:S(2)}) collective-permute-start(bf16[128,384]{1,0:T(8,128)(2,1)} %gradients.1.refs_0_), channel_id=1, source_target_pairs={{0,4},{4,0},{8,12},{12,8},{16,20},{20,16},{24,28},{28,24},{1,5},{5... | collective-permute-start | bytes 294920 | tf_op jit(solution)/shard_map/ppermute | solution.py:40
  90.0 15.8 %collective-permute-start.19 = (bf16[256,384]{1,0:T(8,128)(2,1)S(1)}, bf16[256,384]{1,0:T(8,128)(2,1)S(1)}, u32[]{:S(2)}, u32[]{:S(2)}) collective-permute-start(bf16[256,384]{1,0:T(8,128)(2,1)S(1)} %stack_rows.5.refs_0_), channel_id=1, source_target_pairs={{0,24},{4,28},{8,16},{12,20},{16,8},{20,12},{24,0},{28,4},{1,25},{... | collective-permute-start | bytes 589832 | tf_op jit(solution)/shard_map/ppermute | solution.py:40
  92.7 16.5 %collective-permute-start.18 = (bf16[256,384]{1,0:T(8,128)(2,1)S(1)}, bf16[256,384]{1,0:T(8,128)(2,1)S(1)}, u32[]{:S(2)}, u32[]{:S(2)}) collective-permute-start(bf16[256,384]{1,0:T(8,128)(2,1)S(1)} %stack_rows.5.refs_0_), channel_id=1, source_target_pairs={{0,16},{4,20},{8,24},{12,28},{16,0},{20,4},{24,8},{28,12},{1,17},{... | collective-permute-start | bytes 589832 | tf_op jit(solution)/shard_map/ppermute | solution.py:40
  93.2 16.6 %collective-permute-start.17 = (bf16[256,384]{1,0:T(8,128)(2,1)S(1)}, bf16[256,384]{1,0:T(8,128)(2,1)S(1)}, u32[]{:S(2)}, u32[]{:S(2)}) collective-permute-start(bf16[256,384]{1,0:T(8,128)(2,1)S(1)} %stack_rows.5.refs_0_), channel_id=1, source_target_pairs={{0,8},{4,12},{8,0},{12,4},{16,24},{20,28},{24,16},{28,20},{1,9},{5... | collective-permute-start | bytes 589832 | tf_op jit(solution)/shard_map/ppermute | solution.py:40
  (17 other events, 18.9 us)

commit v6 on v5

--- a/solution.py
+++ b/solution.py
@@ -420,8 +420,9 @@
         if masks:
             left_ref = refs[-1]
             for mask, ref in zip(masks, grad_refs):
-                left_ref[lax.axis_index("dp") ^ mask] = ref[:count]
-                left_ref[lax.axis_index("dp") ^ mask ^ 1] = ref[count:]
+                for j in range(GROUP // 2):
+                    place = lax.axis_index("dp") ^ mask ^ (2 * j)
+                    left_ref[place] = ref[j * count : (j + 1) * count]
             totals = group(0, totals)
         else:
             left_ref = grad_refs[0]
@@ -436,7 +437,7 @@
         out_specs=[VMEM] * 3,
         out_shape=[struct((PB, 1, wide), jnp.float32)] + [struct((hb, cols), jnp.float32)] * 2,
         scratch_shapes=[pltpu.VMEM((n_dp, count, 2 * hb + PB), jnp.bfloat16)] if masks else [],
-        compiler_params=params(40),
+        compiler_params=params(60),
         cost_estimate=cost(0, 1024),
         name="final_product",
     )(feats, handed, *grads)
@@ -459,35 +460,34 @@
     rightward = [(i, i + 1) for i in range(n_t - 1)]
     leftward = [(i + 1, i) for i in range(n_t - 1)]
     teach = lax.all_to_all(teach, "dp", split_axis=0, concat_axis=0, tiled=True)
-    from_left, from_right = hop(own, rightward), hop(own, leftward)
     mine = stack_rows(
         [pieces[0]] + [shift(pieces[k], n_t, k) for k in range(1, n_t)], rows, width, 8
     )
     others = [swap(mine, n_dp, mask) for mask in (2, 4, 6)]
 
-    from_left, from_right = ordered(from_left, mine), ordered(from_right, mine)
+    own = ordered(own, mine)
+    from_left, from_right = hop(own, rightward), hop(own, leftward)
     far_left, far_right = hop(from_left, rightward[1:]), hop(from_right, leftward[:-1])
     ends = [hop(far_left, rightward[-1:]), hop(far_right, leftward[:1])]
 
     handed = hand_over(teach, tok)
-    near = stack_rows(
-        [mine] + others, n_t * rows, width, 60, after=[handed, far_left, far_right]
-    )
+    near = stack_rows([mine] + others, n_t * rows, width, 60)
     far = swap(near, n_dp, 1)
     partial = partial_products(near, far, student_hidden, projected, n_t, rows, factor, after=[])
     acts = [partial[0]] + [shift(partial[k], n_t, -k) for k in range(1, n_t)]
 
     sent = place_slices([own, from_left, from_right], [0, 1, n_t - 1], width, n_t, n_dp)
-    sent = place_last(sent, far_left, far_right, ends, width, n_t, after=[partial[0]])
+    sent = place_last(sent, far_left, far_right, ends, width, n_t, after=[partial[0], handed])
     feats = lax.all_to_all(sent, "dp", split_axis=0, concat_axis=0, tiled=True)
 
     slices = [own, from_left, from_right, far_left, far_right, *ends]
     pre = gate_and_up(slices, gate_bucket, up_bucket, n_t, after=[sent])
     grads = gradients(pre, acts, [own, from_left, far_left, ends[0]], width)
-    masks = [0, 2, 4, 6] if n_dp == GROUP else []
+    masks = [0, 1] if n_dp == GROUP else []
     if masks:
-        pair = stack_rows([grads, swap(grads, n_dp, 1)], tok, grads.shape[1], 8)
-        grads = [pair] + [swap(pair, n_dp, mask) for mask in masks[1:]]
+        near = [grads] + [swap(grads, n_dp, mask) for mask in (2, 4, 6)]
+        near = stack_rows(near, tok, grads.shape[1], 8)
+        grads = [near, swap(near, n_dp, 1)]
     else:
         grads = [lax.all_gather(grads, "dp")]
     return final_product(feats, handed, grads, masks)

time: 115 us -> 119 us (1.035)
  Pallas kernels: 29.6 us -> 31.7 us
    all_to_all x1, waiting for transfers between devices: 0.01 us -> 7.1 us  [body(): teach = lax.all_to_all(teach, 'dp', split_axis=0, concat_axis=0, tiled=True)]
    ppermute x8, waiting for transfers between devices: 20.9 us -> 15 us  [swap(): return lax.ppermute(x, 'dp', [(i, i ^ mask) for i in range(count)])]
    ppermute x6, waiting for transfers between devices: 7.05 us -> 4.34 us  [shift(): lax.ppermute(x, 'tensor', [(i, (i + by) % count) for i in range(count)])]
    ppermute x6, starting transfers between devices: 9.8 us -> 12 us  [shift(): lax.ppermute(x, 'tensor', [(i, (i + by) % count) for i in range(count)])]
    pallas_call x1, Pallas kernels: 1.84 us -> 3.89 us  [final_product(): pl.pallas_call(kernel, in_specs=[VMEM] * (2 + len(grads)), out_specs=[VME...]
    ppermute x6, waiting for transfers between devices: 10.6 us -> 11.8 us  [hop(): return lax.ppermute(x, 'tensor', pairs)]
    unnamed x54 -> x48, local copies, waits for them, and re-layouts: 9.24 us -> 10.4 us
  transfers between devices with their start and end apart: 22 -> 22, of which waited for: 9 -> 12; matrix products, arithmetic and copies ran while one was open for 0% -> 0% of each run, Pallas kernels for 17% -> 18%
where the time goes in v6:
time: 119 us; the launch traced here: 118 us
  waiting for transfers between devices  38.3 us (32%)
  starting transfers between devices  36.3 us (31%)
  Pallas kernels  31.7 us (27%)
  local copies, waits for them, and re-layouts  10.4 us (9%)
    ppermute x8, waiting for transfers between devices, swap(): return lax.ppermute(x, 'dp', [(i, i ^ mask) for i in range(count)])  15 us
    ppermute x6, starting transfers between devices, shift(): lax.ppermute(x, 'tensor', [(i, (i + by) % count) for i in range(count)])  12 us
    ppermute x6, waiting for transfers between devices, hop(): return lax.ppermute(x, 'tensor', pairs)  11.8 us
    unnamed x48, local copies, waits for them, and re-layouts  10.4 us
    ppermute x6, starting transfers between devices, hop(): return lax.ppermute(x, 'tensor', pairs)  9.81 us
    ppermute x8, starting transfers between devices, swap(): return lax.ppermute(x, 'dp', [(i, i ^ mask) for i in range(count)])  7.13 us
    all_to_all x1, waiting for transfers between devices, body(): teach = lax.all_to_all(teach, 'dp', split_axis=0, concat_axis=0, tiled=True)  7.1 us
    pallas_call x1, Pallas kernels, hand_over(): pl.pallas_call(kernel, in_specs=[VMEM] * (1 + len(digits)), out_specs=VME...  5.81 us
  transfers between devices with their start and end apart: 22, of which 12 were waited for; matrix products, arithmetic and copies ran while one was open for 0% of the time, Pallas kernels for 18%

profile of v6, /device:TPU:0, one launch (start us, length us, event | category | flops | bytes accessed | tf_op | source)
XLA Modules:
  0.0 117.5 jit_solution(565893341072729709)
XLA Ops:
  0.6 2.9 %prepare.1 = (bf16[128,2176]{1,0:T(8,128)(2,1)}, bf16[16,2048]{1,0:T(8,128)(2,1)}, bf16[16,2048]{1,0:T(8,128)(2,1)}, bf16[16,2048]{1,0:T(8,128)(2,1)}, bf16[16,2...) custom-call(s32[1,128]{1,0:T(1,128)} %bitcast.1, bf16[128,4096]{1,0:T(8,128)(2,1)} %t_ref.1, bf16[128,2048]{1,0:T(8,128)(2,1)} %x_ref.1, ...), custom_call_target="tpu_custom_call" | custom-call | bytes 1024 | tf_op jit(solution)/shard_map/prepare/pallas_call | solution.py:111
  3.6 3.1 %collective-permute-start = (bf16[16,2048]{1,0:T(8,128)(2,1)}, bf16[16,2048]{1,0:T(8,128)(2,1)S(1)}, u32[]{:S(2)}, u32[]{:S(2)}) collective-permute-start(bf16[16,2048]{1,0:T(8,128)(2,1)} %get-tuple-element.15), channel_id=1, source_target_pairs={{0,1},{1,2},{2,3},{3,0},{4,5},{5,6},{6,7},{7,4},{8,9},{9,10},{10,1... | collective-permute-start | bytes 196616 | tf_op jit(solution)/shard_map/ppermute | solution.py:32
  6.6 2.6 %collective-permute-start.1 = (bf16[16,2048]{1,0:T(8,128)(2,1)}, bf16[16,2048]{1,0:T(8,128)(2,1)S(1)}, u32[]{:S(2)}, u32[]{:S(2)}) collective-permute-start(bf16[16,2048]{1,0:T(8,128)(2,1)} %get-tuple-element.16), channel_id=1, source_target_pairs={{0,2},{1,3},{2,0},{3,1},{4,6},{5,7},{6,4},{7,5},{8,10},{9,11},{10,... | collective-permute-start | bytes 196616 | tf_op jit(solution)/shard_map/ppermute | solution.py:32
  9.2 1.3 %collective-permute-start.2 = (bf16[16,2048]{1,0:T(8,128)(2,1)}, bf16[16,2048]{1,0:T(8,128)(2,1)S(1)}, u32[]{:S(2)}, u32[]{:S(2)}) collective-permute-start(bf16[16,2048]{1,0:T(8,128)(2,1)} %get-tuple-element.17), channel_id=1, source_target_pairs={{0,3},{1,0},{2,1},{3,2},{4,7},{5,4},{6,5},{7,6},{8,11},{9,8},{10,9... | collective-permute-start | bytes 196616 | tf_op jit(solution)/shard_map/ppermute | solution.py:32
  11.4 2.5 %collective-permute-done.1.refs_2_ = bf16[16,2048]{1,0:T(8,128)(2,1)S(1)} collective-permute-done((bf16[16,2048]{1,0:T(8,128)(2,1)}, bf16[16,2048]{1,0:T(8,128)(2,1)S(1)}, u32[]{:S(2)}, u32[]{:S(2)}) %collective-permute-start.1) | collective-permute-done | bytes 65568 | tf_op jit(solution)/shard_map/ppermute | solution.py:32
  15.0 1.1 copy-done
  17.0 1.3 %collective-permute-start.4 = (bf16[128,2176]{1,0:T(8,128)(2,1)}, bf16[128,2176]{1,0:T(8,128)(2,1)S(1)}, u32[]{:S(2)}, u32[]{:S(2)}) collective-permute-start(bf16[128,2176]{1,0:T(8,128)(2,1)} %copy-done.1), channel_id=1, source_target_pairs={{1,0},{2,1},{3,2},{5,4},{6,5},{7,6},{9,8},{10,9},{11,10},{13,12},{... | collective-permute-start | bytes 1671176 | tf_op jit(solution)/shard_map/ppermute | solution.py:36
  18.3 4.6 %collective-permute-start.3 = (bf16[128,2176]{1,0:T(8,128)(2,1)}, bf16[128,2176]{1,0:T(8,128)(2,1)S(1)}, u32[]{:S(2)}, u32[]{:S(2)}) collective-permute-start(bf16[128,2176]{1,0:T(8,128)(2,1)} %copy-done.1), channel_id=1, source_target_pairs={{0,1},{1,2},{2,3},{4,5},{5,6},{6,7},{8,9},{9,10},{10,11},{12,13},{... | collective-permute-start | bytes 1671176 | tf_op jit(solution)/shard_map/ppermute | solution.py:36
  22.8 2.6 %collective-permute-start.11 = (bf16[64,2048]{1,0:T(8,128)(2,1)S(1)}, bf16[64,2048]{1,0:T(8,128)(2,1)S(1)}, u32[]{:S(2)}, u32[]{:S(2)}) collective-permute-start(bf16[64,2048]{1,0:T(8,128)(2,1)S(1)} %stack_rows.3.refs_1_.refs_0_), channel_id=1, source_target_pairs={{0,24},{4,28},{8,16},{12,20},{16,8},{20,12},{24,0},{28,4},{1,25},{... | collective-permute-start | bytes 786440 | tf_op jit(solution)/shard_map/ppermute | solution.py:40
  26.4 7.0 %collective-permute-done.4.refs_2_ = bf16[128,2176]{1,0:T(8,128)(2,1)S(1)} collective-permute-done((bf16[128,2176]{1,0:T(8,128)(2,1)}, bf16[128,2176]{1,0:T(8,128)(2,1)S(1)}, u32[]{:S(2)}, u32[]{:S(2)}) %collective-permute-start.4) | collective-permute-done | bytes 557088 | tf_op jit(solution)/shard_map/ppermute | solution.py:36
  33.4 1.3 %collective-permute-start.6 = (bf16[128,2176]{1,0:T(8,128)(2,1)S(1)}, bf16[128,2176]{1,0:T(8,128)(2,1)S(1)}, u32[]{:S(2)}, u32[]{:S(2)}) collective-permute-start(bf16[128,2176]{1,0:T(8,128)(2,1)S(1)} %collective-permute-done.4.refs_2_), channel_id=1, source_target_pairs={{1,0},{2,1},{5,4},{6,5},{9,8},{10,9},{13,12},{14,13},{17,16},{18,1... | collective-permute-start | bytes 1671176 | tf_op jit(solution)/shard_map/ppermute | solution.py:36
  35.4 1.4 %collective-permute-done.10.refs_2_ = bf16[64,2048]{1,0:T(8,128)(2,1)S(1)} collective-permute-done((bf16[64,2048]{1,0:T(8,128)(2,1)S(1)}, bf16[64,2048]{1,0:T(8,128)(2,1)S(1)}, u32[]{:S(2)}, u32[]{:S(2)}) %collective-permute-start.10) | collective-permute-done | bytes 262176 | tf_op jit(solution)/shard_map/ppermute | solution.py:40
  38.3 2.2 %stack_rows.4.near_ref = bf16[256,2048]{1,0:T(8,128)(2,1)} custom-call(bf16[64,2048]{1,0:T(8,128)(2,1)} %copy-done.2, bf16[64,2048]{1,0:T(8,128)(2,1)} %copy-done.17, bf16[64,2048]{1,0:T(8,128)(2,1)} %copy-done.16, bf16[64,2048]{1,0:T(8,128)(2,1)} %copy-done.15), custom_call_target="tpu_custom_call" | custom-call | bytes 1024 | tf_op jit(solution)/shard_map/stack_rows/pallas_call | solution.py:135
  40.6 3.6 %all-to-all-start = ((bf16[8,144,512]{2,1,0:T(8,128)(2,1)}), bf16[8,144,512]{2,1,0:T(8,128)(2,1)S(1)}, u32[]{:S(2)}, u32[]{:S(2)}) async-start(bf16[8,144,512]{2,1,0:T(8,128)(2,1)} %get-tuple-element.19), calls=%async_computation | async-start | bytes 2359296 | tf_op jit(solution)/shard_map/all_to_all | solution.py:462
  44.1 4.8 %collective-permute-done.6.right_ref.refs_4_ = bf16[128,2176]{1,0:T(8,128)(2,1)S(1)} collective-permute-done((bf16[128,2176]{1,0:T(8,128)(2,1)S(1)}, bf16[128,2176]{1,0:T(8,128)(2,1)S(1)}, u32[]{:S(2)}, u32[]{:S(2)}) %collective-permute-start.6) | collective-permute-done | bytes 557088 | tf_op jit(solution)/shard_map/ppermute | solution.py:36
  48.9 1.3 %collective-permute-start.8 = (bf16[128,2176]{1,0:T(8,128)(2,1)S(1)}, bf16[128,2176]{1,0:T(8,128)(2,1)S(1)}, u32[]{:S(2)}, u32[]{:S(2)}) collective-permute-start(bf16[128,2176]{1,0:T(8,128)(2,1)S(1)} %collective-permute-done.6.right_ref.refs_4_), channel_id=1, source_target_pairs={{1,0},{5,4},{9,8},{13,12},{17,16},{21,20},{25,24},{29,28}} | collective-permute-start | bytes 1671176 | tf_op jit(solution)/shard_map/ppermute | solution.py:36
  50.9 2.8 %place_slices.1.in_ref = bf16[8,128,1024]{2,1,0:T(8,128)(2,1)} custom-call(bf16[128,2176]{1,0:T(8,128)(2,1)} %copy-done.1, bf16[128,2176]{1,0:T(8,128)(2,1)} %copy-done.7, bf16[128,2176]{1,0:T(8,128)(2,1)} %copy-done.11), custom_call_target="tpu_custom_call" | custom-call | bytes 1024 | tf_op jit(solution)/shard_map/place_slices/pallas_call | solution.py:214
  53.8 7.1 %all-to-all-done.refs_0_ = bf16[8,144,512]{2,1,0:T(8,128)(2,1)S(1)} async-done(((bf16[8,144,512]{2,1,0:T(8,128)(2,1)}), bf16[8,144,512]{2,1,0:T(8,128)(2,1)S(1)}, u32[]{:S(2)}, u32[]{:S(2)}) %all-to-all-start) | async-done | bytes 1179680 | tf_op jit(solution)/shard_map/all_to_all | solution.py:462
  60.9 1.0 copy-done.10
  61.9 5.8 %hand_over.1.refs_1_.handed_ref = bf16[8,128,512]{2,1,0:T(8,128)(2,1)} custom-call(bf16[8,144,512]{2,1,0:T(8,128)(2,1)} %copy-done.10), custom_call_target="tpu_custom_call" | custom-call | bytes 1024 | tf_op jit(solution)/shard_map/hand_over/pallas_call | solution.py:389
  67.7 3.2 %partial_products.1 = (f32[128,128]{1,0:T(8,128)}, f32[128,128]{1,0:T(8,128)}, f32[128,128]{1,0:T(8,128)}, f32[128,128]{1,0:T(8,128)}) custom-call(bf16[256,2048]{1,0:T(8,128)(2,1)} %stack_rows.4.near_ref, bf16[256,2048]{1,0:T(8,128)(2,1)} %collective-permute-done.12.far_ref, bf16[128,2048]{1,0:T(8,128)(2,1)} %s_ref.3, bf16[128,2048]{1,0:T(8,128)(2,1)} %p_ref.3), custom_call_target="tpu_custom_call" | custom-call | bytes 1024 | tf_op jit(solution)/shard_map/partial_products/pallas_call | solution.py:179
  71.9 3.2 %place_last.1.refs_9_ = bf16[8,128,1024]{2,1,0:T(8,128)(2,1)} custom-call(bf16[8,128,1024]{2,1,0:T(8,128)(2,1)} %place_slices.1.in_ref, bf16[128,2176]{1,0:T(8,128)(2,1)} %copy-done.8, bf16[128,2176]{1,0:T(8,128)(2,1)} %copy-done.12, bf16[128,2176]{1,0:T(8,128)(2,1)} %copy-done.9, bf16[128,2176]{1,0:T(8,128)(2,1)} %copy-done.13, ...), custom_call_target="tpu_custom_call", output_to_operand_aliasing={{}: (0, {})} | custom-call | bytes 1024 | tf_op jit(solution)/shard_map/place_last/pallas_call | solution.py:263
  75.2 3.7 %all-to-all-start.1 = ((bf16[8,128,1024]{2,1,0:T(8,128)(2,1)}), bf16[8,128,1024]{2,1,0:T(8,128)(2,1)S(1)}, u32[]{:S(2)}, u32[]{:S(2)}) async-start(bf16[8,128,1024]{2,1,0:T(8,128)(2,1)} %place_last.1.refs_9_), calls=%async_computation.1 | async-start | bytes 4194304 | tf_op jit(solution)/shard_map/all_to_all | solution.py:481
  78.9 2.6 %collective-permute-start.13 = (f32[128,128]{1,0:T(8,128)S(1)}, f32[128,128]{1,0:T(8,128)S(1)}, u32[]{:S(2)}, u32[]{:S(2)}) collective-permute-start(f32[128,128]{1,0:T(8,128)S(1)} %copy-done.23), channel_id=1, source_target_pairs={{0,3},{1,0},{2,1},{3,2},{4,7},{5,4},{6,5},{7,6},{8,11},{9,8},{10,9... | collective-permute-start | bytes 196616 | tf_op jit(solution)/shard_map/ppermute | solution.py:32
  81.5 2.4 %collective-permute-start.14 = (f32[128,128]{1,0:T(8,128)S(1)}, f32[128,128]{1,0:T(8,128)S(1)}, u32[]{:S(2)}, u32[]{:S(2)}) collective-permute-start(f32[128,128]{1,0:T(8,128)S(1)} %copy-done.22), channel_id=1, source_target_pairs={{0,2},{1,3},{2,0},{3,1},{4,6},{5,7},{6,4},{7,5},{8,10},{9,11},{10,... | collective-permute-start | bytes 196616 | tf_op jit(solution)/shard_map/ppermute | solution.py:32
  84.0 5.7 %gate_and_up.1.pre_ref = f32[128,256]{1,0:T(8,128)} custom-call(bf16[128,2176]{1,0:T(8,128)(2,1)} %copy-done.1, bf16[128,2176]{1,0:T(8,128)(2,1)} %copy-done.7, bf16[128,2176]{1,0:T(8,128)(2,1)} %copy-done.11, bf16[128,2176]{1,0:T(8,128)(2,1)} %copy-done.8, bf16[128,2176]{1,0:T(8,128)(2,1)} %copy-done.12, bf16[128,2176]{1,0:T(8,128)(2,1)} %copy-done.9, ...), custom_call_target="tpu_custom_call" | custom-call | bytes 1024 | tf_op jit(solution)/shard_map/gate_and_up/pallas_call | solution.py:300
  91.7 1.8 %gradients.1.refs_0_ = bf16[128,384]{1,0:T(8,128)(2,1)} custom-call(f32[128,256]{1,0:T(8,128)} %gate_and_up.1.pre_ref, f32[128,128]{1,0:T(8,128)} %get-tuple-element.18.refs_0_, f32[128,128]{1,0:T(8,128)} %copy-done.18, f32[128,128]{1,0:T(8,128)} %copy-done.19, f32[128,128]{1,0:T(8,128)} %copy-done.20, bf16[128,2176]{1,0:T(8,128)(2,1)} %copy-done.1, ...), custom_call_target="tpu_custom_call" | custom-call | bytes 1024 | tf_op jit(solution)/shard_map/gradients/pallas_call | solution.py:343
  93.5 2.6 %collective-permute-start.18 = (bf16[128,384]{1,0:T(8,128)(2,1)}, bf16[128,384]{1,0:T(8,128)(2,1)S(1)}, u32[]{:S(2)}, u32[]{:S(2)}) collective-permute-start(bf16[128,384]{1,0:T(8,128)(2,1)} %gradients.1.refs_0_), channel_id=1, source_target_pairs={{0,24},{4,28},{8,16},{12,20},{16,8},{20,12},{24,0},{28,4},{1,25},{... | collective-permute-start | bytes 294920 | tf_op jit(solution)/shard_map/ppermute | solution.py:40
  97.0 11.1 %collective-permute-done.18.refs_3_ = bf16[128,384]{1,0:T(8,128)(2,1)S(1)} collective-permute-done((bf16[128,384]{1,0:T(8,128)(2,1)}, bf16[128,384]{1,0:T(8,128)(2,1)S(1)}, u32[]{:S(2)}, u32[]{:S(2)}) %collective-permute-start.18) | collective-permute-done | bytes 98336 | tf_op jit(solution)/shard_map/ppermute | solution.py:40
  109.9 1.7 %collective-permute-done.19.refs_1_ = bf16[512,384]{1,0:T(8,128)(2,1)S(1)} collective-permute-done((bf16[512,384]{1,0:T(8,128)(2,1)S(1)}, bf16[512,384]{1,0:T(8,128)(2,1)S(1)}, u32[]{:S(2)}, u32[]{:S(2)}) %collective-permute-start.19) | collective-permute-done | bytes 393248 | tf_op jit(solution)/shard_map/ppermute | solution.py:40
  112.3 1.3 %copy-done.6 = bf16[8,128,1024]{2,1,0:T(8,128)(2,1)} copy-done((bf16[8,128,1024]{2,1,0:T(8,128)(2,1)}, bf16[8,128,1024]{2,1,0:T(8,128)(2,1)S(1)}, u32[]{:S(2)}) %copy-start.6) | copy-done | bytes 2097176
  113.6 3.9 %final_product.1 = (f32[128,1,512]{2,1,0:T(1,128)}, f32[128,1024]{1,0:T(8,128)}, f32[128,1024]{1,0:T(8,128)}) custom-call(bf16[8,128,1024]{2,1,0:T(8,128)(2,1)} %copy-done.6, bf16[8,128,512]{2,1,0:T(8,128)(2,1)} %hand_over.1.refs_1_.handed_ref, bf16[512,384]{1,0:T(8,128)(2,1)} %copy-done.3, bf16[512,384]{1,0:T(8,128)(2,1)} %copy-done.14), custom_call_target="tpu_custom_call" | custom-call | bytes 1024 | tf_op jit(solution)/shard_map/final_product/pallas_call | solution.py:434
  (72 shorter events, 12.9 us)
Async XLA Ops:
  3.6 7.8 %collective-permute-start = (bf16[16,2048]{1,0:T(8,128)(2,1)}, bf16[16,2048]{1,0:T(8,128)(2,1)S(1)}, u32[]{:S(2)}, u32[]{:S(2)}) collective-permute-start(bf16[16,2048]{1,0:T(8,128)(2,1)} %get-tuple-element.15), channel_id=1, source_target_pairs={{0,1},{1,2},{2,3},{3,0},{4,5},{5,6},{6,7},{7,4},{8,9},{9,10},{10,1... | collective-permute-start | bytes 196616 | tf_op jit(solution)/shard_map/ppermute | solution.py:32
  6.6 7.3 %collective-permute-start.1 = (bf16[16,2048]{1,0:T(8,128)(2,1)}, bf16[16,2048]{1,0:T(8,128)(2,1)S(1)}, u32[]{:S(2)}, u32[]{:S(2)}) collective-permute-start(bf16[16,2048]{1,0:T(8,128)(2,1)} %get-tuple-element.16), channel_id=1, source_target_pairs={{0,2},{1,3},{2,0},{3,1},{4,6},{5,7},{6,4},{7,5},{8,10},{9,11},{10,... | collective-permute-start | bytes 196616 | tf_op jit(solution)/shard_map/ppermute | solution.py:32
  9.2 4.9 %collective-permute-start.2 = (bf16[16,2048]{1,0:T(8,128)(2,1)}, bf16[16,2048]{1,0:T(8,128)(2,1)S(1)}, u32[]{:S(2)}, u32[]{:S(2)}) collective-permute-start(bf16[16,2048]{1,0:T(8,128)(2,1)} %get-tuple-element.17), channel_id=1, source_target_pairs={{0,3},{1,0},{2,1},{3,2},{4,7},{5,4},{6,5},{7,6},{8,11},{9,8},{10,9... | collective-permute-start | bytes 196616 | tf_op jit(solution)/shard_map/ppermute | solution.py:32
  15.0 21.9 %copy-start.2 = (bf16[64,2048]{1,0:T(8,128)(2,1)}, bf16[64,2048]{1,0:T(8,128)(2,1)S(1)}, u32[]{:S(2)}) copy-start(bf16[64,2048]{1,0:T(8,128)(2,1)S(1)} %stack_rows.3.refs_1_.refs_0_) | copy-start | bytes 786436
  17.0 16.4 %collective-permute-start.4 = (bf16[128,2176]{1,0:T(8,128)(2,1)}, bf16[128,2176]{1,0:T(8,128)(2,1)S(1)}, u32[]{:S(2)}, u32[]{:S(2)}) collective-permute-start(bf16[128,2176]{1,0:T(8,128)(2,1)} %copy-done.1), channel_id=1, source_target_pairs={{1,0},{2,1},{3,2},{5,4},{6,5},{7,6},{9,8},{10,9},{11,10},{13,12},{... | collective-permute-start | bytes 1671176 | tf_op jit(solution)/shard_map/ppermute | solution.py:36
  18.3 16.4 %collective-permute-start.3 = (bf16[128,2176]{1,0:T(8,128)(2,1)}, bf16[128,2176]{1,0:T(8,128)(2,1)S(1)}, u32[]{:S(2)}, u32[]{:S(2)}) collective-permute-start(bf16[128,2176]{1,0:T(8,128)(2,1)} %copy-done.1), channel_id=1, source_target_pairs={{0,1},{1,2},{2,3},{4,5},{5,6},{6,7},{8,9},{9,10},{10,11},{12,13},{... | collective-permute-start | bytes 1671176 | tf_op jit(solution)/shard_map/ppermute | solution.py:36
  22.8 12.6 %collective-permute-start.11 = (bf16[64,2048]{1,0:T(8,128)(2,1)S(1)}, bf16[64,2048]{1,0:T(8,128)(2,1)S(1)}, u32[]{:S(2)}, u32[]{:S(2)}) collective-permute-start(bf16[64,2048]{1,0:T(8,128)(2,1)S(1)} %stack_rows.3.refs_1_.refs_0_), channel_id=1, source_target_pairs={{0,24},{4,28},{8,16},{12,20},{16,8},{20,12},{24,0},{28,4},{1,25},{... | collective-permute-start | bytes 786440 | tf_op jit(solution)/shard_map/ppermute | solution.py:40
  25.4 11.5 %collective-permute-start.10 = (bf16[64,2048]{1,0:T(8,128)(2,1)S(1)}, bf16[64,2048]{1,0:T(8,128)(2,1)S(1)}, u32[]{:S(2)}, u32[]{:S(2)}) collective-permute-start(bf16[64,2048]{1,0:T(8,128)(2,1)S(1)} %stack_rows.3.refs_1_.refs_0_), channel_id=1, source_target_pairs={{0,16},{4,20},{8,24},{12,28},{16,0},{20,4},{24,8},{28,12},{1,17},{... | collective-permute-start | bytes 786440 | tf_op jit(solution)/shard_map/ppermute | solution.py:40
  25.9 11.0 %collective-permute-start.9 = (bf16[64,2048]{1,0:T(8,128)(2,1)S(1)}, bf16[64,2048]{1,0:T(8,128)(2,1)S(1)}, u32[]{:S(2)}, u32[]{:S(2)}) collective-permute-start(bf16[64,2048]{1,0:T(8,128)(2,1)S(1)} %stack_rows.3.refs_1_.refs_0_), channel_id=1, source_target_pairs={{0,8},{4,12},{8,0},{12,4},{16,24},{20,28},{24,16},{28,20},{1,9},{5... | collective-permute-start | bytes 786440 | tf_op jit(solution)/shard_map/ppermute | solution.py:40
  33.4 7.2 %copy-start.11 = (bf16[128,2176]{1,0:T(8,128)(2,1)}, bf16[128,2176]{1,0:T(8,128)(2,1)S(1)}, u32[]{:S(2)}) copy-start(bf16[128,2176]{1,0:T(8,128)(2,1)S(1)} %collective-permute-done.4.refs_2_) | copy-start | bytes 1671172
  33.4 15.5 %collective-permute-start.6 = (bf16[128,2176]{1,0:T(8,128)(2,1)S(1)}, bf16[128,2176]{1,0:T(8,128)(2,1)S(1)}, u32[]{:S(2)}, u32[]{:S(2)}) collective-permute-start(bf16[128,2176]{1,0:T(8,128)(2,1)S(1)} %collective-permute-done.4.refs_2_), channel_id=1, source_target_pairs={{1,0},{2,1},{5,4},{6,5},{9,8},{10,9},{13,12},{14,13},{17,16},{18,1... | collective-permute-start | bytes 1671176 | tf_op jit(solution)/shard_map/ppermute | solution.py:36
  34.7 5.9 %copy-start.7 = (bf16[128,2176]{1,0:T(8,128)(2,1)}, bf16[128,2176]{1,0:T(8,128)(2,1)S(1)}, u32[]{:S(2)}) copy-start(bf16[128,2176]{1,0:T(8,128)(2,1)S(1)} %collective-permute-done.3.refs_1_.refs_5_) | copy-start | bytes 1671172
  34.7 15.5 %collective-permute-start.5 = (bf16[128,2176]{1,0:T(8,128)(2,1)S(1)}, bf16[128,2176]{1,0:T(8,128)(2,1)S(1)}, u32[]{:S(2)}, u32[]{:S(2)}) collective-permute-start(bf16[128,2176]{1,0:T(8,128)(2,1)S(1)} %collective-permute-done.3.refs_1_.refs_5_), channel_id=1, source_target_pairs={{1,2},{2,3},{5,6},{6,7},{9,10},{10,11},{13,14},{14,15},{17,18},{18... | collective-permute-start | bytes 1671176 | tf_op jit(solution)/shard_map/ppermute | solution.py:36
  35.4 1.5 %copy-start.15 = (bf16[64,2048]{1,0:T(8,128)(2,1)}, bf16[64,2048]{1,0:T(8,128)(2,1)S(1)}, u32[]{:S(2)}) copy-start(bf16[64,2048]{1,0:T(8,128)(2,1)S(1)} %collective-permute-done.11.refs_3_) | copy-start | bytes 786436
  40.5 27.2 %collective-permute-start.12 = (bf16[256,2048]{1,0:T(8,128)(2,1)}, bf16[256,2048]{1,0:T(8,128)(2,1)}, u32[]{:S(2)}, u32[]{:S(2)}) collective-permute-start(bf16[256,2048]{1,0:T(8,128)(2,1)} %stack_rows.4.near_ref), channel_id=1, source_target_pairs={{0,4},{4,0},{8,12},{12,8},{16,20},{20,16},{24,28},{28,24},{1,5},{5... | collective-permute-start | bytes 3145736 | tf_op jit(solution)/shard_map/ppermute | solution.py:40
  40.6 20.3 %all-to-all-start = ((bf16[8,144,512]{2,1,0:T(8,128)(2,1)}), bf16[8,144,512]{2,1,0:T(8,128)(2,1)S(1)}, u32[]{:S(2)}, u32[]{:S(2)}) async-start(bf16[8,144,512]{2,1,0:T(8,128)(2,1)} %get-tuple-element.19), calls=%async_computation | async-start | bytes 2359296 | tf_op jit(solution)/shard_map/all_to_all | solution.py:462
  48.9 18.8 %copy-start.12 = (bf16[128,2176]{1,0:T(8,128)(2,1)}, bf16[128,2176]{1,0:T(8,128)(2,1)S(1)}, u32[]{:S(2)}) copy-start(bf16[128,2176]{1,0:T(8,128)(2,1)S(1)} %collective-permute-done.6.right_ref.refs_4_) | copy-start | bytes 1671172
  48.9 22.0 %collective-permute-start.8 = (bf16[128,2176]{1,0:T(8,128)(2,1)S(1)}, bf16[128,2176]{1,0:T(8,128)(2,1)S(1)}, u32[]{:S(2)}, u32[]{:S(2)}) collective-permute-start(bf16[128,2176]{1,0:T(8,128)(2,1)S(1)} %collective-permute-done.6.right_ref.refs_4_), channel_id=1, source_target_pairs={{1,0},{5,4},{9,8},{13,12},{17,16},{21,20},{25,24},{29,28}} | collective-permute-start | bytes 1671176 | tf_op jit(solution)/shard_map/ppermute | solution.py:36
  50.2 17.5 %copy-start.8 = (bf16[128,2176]{1,0:T(8,128)(2,1)}, bf16[128,2176]{1,0:T(8,128)(2,1)S(1)}, u32[]{:S(2)}) copy-start(bf16[128,2176]{1,0:T(8,128)(2,1)S(1)} %collective-permute-done.5.left_ref.refs_3_.refs_6_) | copy-start | bytes 1671172
  50.2 20.7 %collective-permute-start.7 = (bf16[128,2176]{1,0:T(8,128)(2,1)S(1)}, bf16[128,2176]{1,0:T(8,128)(2,1)S(1)}, u32[]{:S(2)}, u32[]{:S(2)}) collective-permute-start(bf16[128,2176]{1,0:T(8,128)(2,1)S(1)} %collective-permute-done.5.left_ref.refs_3_.refs_6_), channel_id=1, source_target_pairs={{2,3},{6,7},{10,11},{14,15},{18,19},{22,23},{26,27},{30,31}} | collective-permute-start | bytes 1671176 | tf_op jit(solution)/shard_map/ppermute | solution.py:36
  75.1 3.8 %copy-start.23 = (f32[128,128]{1,0:T(8,128)S(1)}, f32[128,128]{1,0:T(8,128)}, u32[]{:S(2)}) copy-start(f32[128,128]{1,0:T(8,128)} %get-tuple-element.20) | copy-start | bytes 196612
  75.2 6.4 %copy-start.22 = (f32[128,128]{1,0:T(8,128)S(1)}, f32[128,128]{1,0:T(8,128)}, u32[]{:S(2)}) copy-start(f32[128,128]{1,0:T(8,128)} %get-tuple-element.21) | copy-start | bytes 196612
  75.2 8.8 %copy-start.21 = (f32[128,128]{1,0:T(8,128)S(1)}, f32[128,128]{1,0:T(8,128)}, u32[]{:S(2)}) copy-start(f32[128,128]{1,0:T(8,128)} %get-tuple-element.22) | copy-start | bytes 196612
  75.2 36.4 %all-to-all-start.1 = ((bf16[8,128,1024]{2,1,0:T(8,128)(2,1)}), bf16[8,128,1024]{2,1,0:T(8,128)(2,1)S(1)}, u32[]{:S(2)}, u32[]{:S(2)}) async-start(bf16[8,128,1024]{2,1,0:T(8,128)(2,1)} %place_last.1.refs_9_), calls=%async_computation.1 | async-start | bytes 4194304 | tf_op jit(solution)/shard_map/all_to_all | solution.py:481
  78.9 10.8 %collective-permute-start.13 = (f32[128,128]{1,0:T(8,128)S(1)}, f32[128,128]{1,0:T(8,128)S(1)}, u32[]{:S(2)}, u32[]{:S(2)}) collective-permute-start(f32[128,128]{1,0:T(8,128)S(1)} %copy-done.23), channel_id=1, source_target_pairs={{0,3},{1,0},{2,1},{3,2},{4,7},{5,4},{6,5},{7,6},{8,11},{9,8},{10,9... | collective-permute-start | bytes 196616 | tf_op jit(solution)/shard_map/ppermute | solution.py:32
  81.5 9.0 %collective-permute-start.14 = (f32[128,128]{1,0:T(8,128)S(1)}, f32[128,128]{1,0:T(8,128)S(1)}, u32[]{:S(2)}, u32[]{:S(2)}) collective-permute-start(f32[128,128]{1,0:T(8,128)S(1)} %copy-done.22), channel_id=1, source_target_pairs={{0,2},{1,3},{2,0},{3,1},{4,6},{5,7},{6,4},{7,5},{8,10},{9,11},{10,... | collective-permute-start | bytes 196616 | tf_op jit(solution)/shard_map/ppermute | solution.py:32
  84.0 6.5 %collective-permute-start.15 = (f32[128,128]{1,0:T(8,128)S(1)}, f32[128,128]{1,0:T(8,128)S(1)}, u32[]{:S(2)}, u32[]{:S(2)}) collective-permute-start(f32[128,128]{1,0:T(8,128)S(1)} %copy-done.21), channel_id=1, source_target_pairs={{0,1},{1,2},{2,3},{3,0},{4,5},{5,6},{6,7},{7,4},{8,9},{9,10},{10,1... | collective-permute-start | bytes 196616 | tf_op jit(solution)/shard_map/ppermute | solution.py:32
  93.5 14.6 %collective-permute-start.18 = (bf16[128,384]{1,0:T(8,128)(2,1)}, bf16[128,384]{1,0:T(8,128)(2,1)S(1)}, u32[]{:S(2)}, u32[]{:S(2)}) collective-permute-start(bf16[128,384]{1,0:T(8,128)(2,1)} %gradients.1.refs_0_), channel_id=1, source_target_pairs={{0,24},{4,28},{8,16},{12,20},{16,8},{20,12},{24,0},{28,4},{1,25},{... | collective-permute-start | bytes 294920 | tf_op jit(solution)/shard_map/ppermute | solution.py:40
  96.1 12.6 %collective-permute-start.17 = (bf16[128,384]{1,0:T(8,128)(2,1)}, bf16[128,384]{1,0:T(8,128)(2,1)S(1)}, u32[]{:S(2)}, u32[]{:S(2)}) collective-permute-start(bf16[128,384]{1,0:T(8,128)(2,1)} %gradients.1.refs_0_), channel_id=1, source_target_pairs={{0,16},{4,20},{8,24},{12,28},{16,0},{20,4},{24,8},{28,12},{1,17},{... | collective-permute-start | bytes 294920 | tf_op jit(solution)/shard_map/ppermute | solution.py:40
  96.7 12.2 %collective-permute-start.16 = (bf16[128,384]{1,0:T(8,128)(2,1)}, bf16[128,384]{1,0:T(8,128)(2,1)S(1)}, u32[]{:S(2)}, u32[]{:S(2)}) collective-permute-start(bf16[128,384]{1,0:T(8,128)(2,1)} %gradients.1.refs_0_), channel_id=1, source_target_pairs={{0,8},{4,12},{8,0},{12,4},{16,24},{20,28},{24,16},{28,20},{1,9},{5... | collective-permute-start | bytes 294920 | tf_op jit(solution)/shard_map/ppermute | solution.py:40
  109.8 1.8 %copy-start.3 = (bf16[512,384]{1,0:T(8,128)(2,1)}, bf16[512,384]{1,0:T(8,128)(2,1)S(1)}, u32[]{:S(2)}) copy-start(bf16[512,384]{1,0:T(8,128)(2,1)S(1)} %stack_rows.5.refs_0_) | copy-start | bytes 1179652
  109.8 1.8 %collective-permute-start.19 = (bf16[512,384]{1,0:T(8,128)(2,1)S(1)}, bf16[512,384]{1,0:T(8,128)(2,1)S(1)}, u32[]{:S(2)}, u32[]{:S(2)}) collective-permute-start(bf16[512,384]{1,0:T(8,128)(2,1)S(1)} %stack_rows.5.refs_0_), channel_id=1, source_target_pairs={{0,4},{4,0},{8,12},{12,8},{16,20},{20,16},{24,28},{28,24},{1,5},{5... | collective-permute-start | bytes 1179656 | tf_op jit(solution)/shard_map/ppermute | solution.py:40
  (14 other events, 12.0 us)

commit v7 on v5

--- a/solution.py
+++ b/solution.py
@@ -199,7 +199,7 @@
     return copies
 
 
-def place_slices(slices, places, width, n_t, n_dp):
+def place_slices(slices, places, width, n_t, n_dp, after):
     count = slices[0].shape[0]
     cols = width * n_t // n_dp
     per = width // cols
@@ -213,13 +213,13 @@
 
     return pl.pallas_call(
         kernel,
-        in_specs=[VMEM] * len(slices),
+        in_specs=[VMEM] * len(slices) + [pl.BlockSpec(memory_space=pl.ANY)] * len(after),
         out_specs=VMEM,
         out_shape=struct((n_dp, count, cols)),
         compiler_params=params(60),
         cost_estimate=cost(0, 1024),
         name="place_slices",
-    )(*slices)
+    )(*slices, *after)
 
 
 def place_last(payload, from_left, from_right, ends, width, n_t, after=()):
@@ -459,26 +459,24 @@
     rightward = [(i, i + 1) for i in range(n_t - 1)]
     leftward = [(i + 1, i) for i in range(n_t - 1)]
     teach = lax.all_to_all(teach, "dp", split_axis=0, concat_axis=0, tiled=True)
-    from_left, from_right = hop(own, rightward), hop(own, leftward)
     mine = stack_rows(
         [pieces[0]] + [shift(pieces[k], n_t, k) for k in range(1, n_t)], rows, width, 8
     )
     others = [swap(mine, n_dp, mask) for mask in (2, 4, 6)]
 
-    from_left, from_right = ordered(from_left, mine), ordered(from_right, mine)
+    own = ordered(own, mine)
+    from_left, from_right = hop(own, rightward), hop(own, leftward)
     far_left, far_right = hop(from_left, rightward[1:]), hop(from_right, leftward[:-1])
     ends = [hop(far_left, rightward[-1:]), hop(far_right, leftward[:1])]
 
     handed = hand_over(teach, tok)
-    near = stack_rows(
-        [mine] + others, n_t * rows, width, 60, after=[handed, far_left, far_right]
-    )
+    near = stack_rows([mine] + others, n_t * rows, width, 60)
     far = swap(near, n_dp, 1)
     partial = partial_products(near, far, student_hidden, projected, n_t, rows, factor, after=[])
     acts = [partial[0]] + [shift(partial[k], n_t, -k) for k in range(1, n_t)]
 
-    sent = place_slices([own, from_left, from_right], [0, 1, n_t - 1], width, n_t, n_dp)
-    sent = place_last(sent, far_left, far_right, ends, width, n_t, after=[partial[0]])
+    sent = place_slices([own, from_left, from_right], [0, 1, n_t - 1], width, n_t, n_dp, [])
+    sent = place_last(sent, far_left, far_right, ends, width, n_t, after=[partial[0], teach])
     feats = lax.all_to_all(sent, "dp", split_axis=0, concat_axis=0, tiled=True)
 
     slices = [own, from_left, from_right, far_left, far_right, *ends]

time: 115 us -> 113 us (0.983)
  starting transfers between devices: 35.9 us -> 32.3 us
  waiting for transfers between devices: 38.5 us -> 40.9 us
    ppermute x6, waiting for transfers between devices: 10.6 us -> 20.7 us  [hop(): return lax.ppermute(x, 'tensor', pairs)]
    ppermute x8, waiting for transfers between devices: 20.9 us -> 13.5 us  [swap(): return lax.ppermute(x, 'dp', [(i, i ^ mask) for i in range(count)])]
    ppermute x6, waiting for transfers between devices: 7.05 us -> 3.91 us  [shift(): lax.ppermute(x, 'tensor', [(i, (i + by) % count) for i in range(count)])]
    all_to_all x1, waiting for transfers between devices: 0.01 us -> 2.87 us  [body(): teach = lax.all_to_all(teach, 'dp', split_axis=0, concat_axis=0, tiled=True)]
    ppermute x6, starting transfers between devices: 11 us -> 8.75 us  [hop(): return lax.ppermute(x, 'tensor', pairs)]
    unnamed x54 -> x44, local copies, waits for them, and re-layouts: 9.24 us -> 8.46 us
  transfers between devices with their start and end apart: 22 -> 22, of which waited for: 9 -> 12; matrix products, arithmetic and copies ran while one was open for 0% -> 0% of each run, Pallas kernels for 17% -> 19%
where the time goes in v7:
time: 113 us; the launch traced here: 112 us
  waiting for transfers between devices  40.9 us (36%)
  starting transfers between devices  32.3 us (29%)
  Pallas kernels  29.6 us (26%)
  local copies, waits for them, and re-layouts  8.46 us (7%)
    ppermute x6, waiting for transfers between devices, hop(): return lax.ppermute(x, 'tensor', pairs)  20.7 us
    ppermute x8, waiting for transfers between devices, swap(): return lax.ppermute(x, 'dp', [(i, i ^ mask) for i in range(count)])  13.5 us
    ppermute x6, starting transfers between devices, shift(): lax.ppermute(x, 'tensor', [(i, (i + by) % count) for i in range(count)])  9.14 us
    ppermute x6, starting transfers between devices, hop(): return lax.ppermute(x, 'tensor', pairs)  8.75 us
    unnamed x44, local copies, waits for them, and re-layouts  8.46 us
    ppermute x8, starting transfers between devices, swap(): return lax.ppermute(x, 'dp', [(i, i ^ mask) for i in range(count)])  7.11 us
    pallas_call x1, Pallas kernels, hand_over(): pl.pallas_call(kernel, in_specs=[VMEM] * (1 + len(digits)), out_specs=VME...  5.83 us
    pallas_call x1, Pallas kernels, gate_and_up(): pl.pallas_call(kernel, in_specs=[VMEM] * n_s + [pl.BlockSpec(memory_space...  5.73 us
  transfers between devices with their start and end apart: 22, of which 12 were waited for; matrix products, arithmetic and copies ran while one was open for 0% of the time, Pallas kernels for 19%

profile of v7, /device:TPU:0, one launch (start us, length us, event | category | flops | bytes accessed | tf_op | source)
XLA Modules:
  0.0 112.2 jit_solution(16005659137145199672)
XLA Ops:
  0.6 2.9 %prepare.1 = (bf16[128,2176]{1,0:T(8,128)(2,1)}, bf16[16,2048]{1,0:T(8,128)(2,1)}, bf16[16,2048]{1,0:T(8,128)(2,1)}, bf16[16,2048]{1,0:T(8,128)(2,1)}, bf16[16,2...) custom-call(s32[1,128]{1,0:T(1,128)} %bitcast.1, bf16[128,4096]{1,0:T(8,128)(2,1)} %t_ref.1, bf16[128,2048]{1,0:T(8,128)(2,1)} %x_ref.1, ...), custom_call_target="tpu_custom_call" | custom-call | bytes 1024 | tf_op jit(solution)/shard_map/prepare/pallas_call | solution.py:111
  3.5 3.1 %collective-permute-start = (bf16[16,2048]{1,0:T(8,128)(2,1)}, bf16[16,2048]{1,0:T(8,128)(2,1)S(1)}, u32[]{:S(2)}, u32[]{:S(2)}) collective-permute-start(bf16[16,2048]{1,0:T(8,128)(2,1)} %get-tuple-element.15), channel_id=1, source_target_pairs={{0,1},{1,2},{2,3},{3,0},{4,5},{5,6},{6,7},{7,4},{8,9},{9,10},{10,1... | collective-permute-start | bytes 196616 | tf_op jit(solution)/shard_map/ppermute | solution.py:32
  6.6 2.6 %collective-permute-start.1 = (bf16[16,2048]{1,0:T(8,128)(2,1)}, bf16[16,2048]{1,0:T(8,128)(2,1)S(1)}, u32[]{:S(2)}, u32[]{:S(2)}) collective-permute-start(bf16[16,2048]{1,0:T(8,128)(2,1)} %get-tuple-element.16), channel_id=1, source_target_pairs={{0,2},{1,3},{2,0},{3,1},{4,6},{5,7},{6,4},{7,5},{8,10},{9,11},{10,... | collective-permute-start | bytes 196616 | tf_op jit(solution)/shard_map/ppermute | solution.py:32
  9.2 1.3 %collective-permute-start.2 = (bf16[16,2048]{1,0:T(8,128)(2,1)}, bf16[16,2048]{1,0:T(8,128)(2,1)S(1)}, u32[]{:S(2)}, u32[]{:S(2)}) collective-permute-start(bf16[16,2048]{1,0:T(8,128)(2,1)} %get-tuple-element.17), channel_id=1, source_target_pairs={{0,3},{1,0},{2,1},{3,2},{4,7},{5,4},{6,5},{7,6},{8,11},{9,8},{10,9... | collective-permute-start | bytes 196616 | tf_op jit(solution)/shard_map/ppermute | solution.py:32
  11.4 2.5 %collective-permute-done.1.refs_2_ = bf16[16,2048]{1,0:T(8,128)(2,1)S(1)} collective-permute-done((bf16[16,2048]{1,0:T(8,128)(2,1)}, bf16[16,2048]{1,0:T(8,128)(2,1)S(1)}, u32[]{:S(2)}, u32[]{:S(2)}) %collective-permute-start.1) | collective-permute-done | bytes 65568 | tf_op jit(solution)/shard_map/ppermute | solution.py:32
  17.0 3.5 %collective-permute-start.3 = (bf16[128,2176]{1,0:T(8,128)(2,1)}, bf16[128,2176]{1,0:T(8,128)(2,1)S(1)}, u32[]{:S(2)}, u32[]{:S(2)}) collective-permute-start(bf16[128,2176]{1,0:T(8,128)(2,1)} %copy-done.1), channel_id=1, source_target_pairs={{0,1},{1,2},{2,3},{4,5},{5,6},{6,7},{8,9},{9,10},{10,11},{12,13},{... | collective-permute-start | bytes 1671176 | tf_op jit(solution)/shard_map/ppermute | solution.py:36
  20.5 1.3 %collective-permute-start.4 = (bf16[128,2176]{1,0:T(8,128)(2,1)}, bf16[128,2176]{1,0:T(8,128)(2,1)S(1)}, u32[]{:S(2)}, u32[]{:S(2)}) collective-permute-start(bf16[128,2176]{1,0:T(8,128)(2,1)} %copy-done.1), channel_id=1, source_target_pairs={{1,0},{2,1},{3,2},{5,4},{6,5},{7,6},{9,8},{10,9},{11,10},{13,12},{... | collective-permute-start | bytes 1671176 | tf_op jit(solution)/shard_map/ppermute | solution.py:36
  21.8 1.6 %collective-permute-start.10 = (bf16[64,2048]{1,0:T(8,128)(2,1)S(1)}, bf16[64,2048]{1,0:T(8,128)(2,1)S(1)}, u32[]{:S(2)}, u32[]{:S(2)}) collective-permute-start(bf16[64,2048]{1,0:T(8,128)(2,1)S(1)} %stack_rows.3.refs_1_.refs_0_), channel_id=1, source_target_pairs={{0,16},{4,20},{8,24},{12,28},{16,0},{20,4},{24,8},{28,12},{1,17},{... | collective-permute-start | bytes 786440 | tf_op jit(solution)/shard_map/ppermute | solution.py:40
  23.4 1.4 %collective-permute-start.11 = (bf16[64,2048]{1,0:T(8,128)(2,1)S(1)}, bf16[64,2048]{1,0:T(8,128)(2,1)S(1)}, u32[]{:S(2)}, u32[]{:S(2)}) collective-permute-start(bf16[64,2048]{1,0:T(8,128)(2,1)S(1)} %stack_rows.3.refs_1_.refs_0_), channel_id=1, source_target_pairs={{0,24},{4,28},{8,16},{12,20},{16,8},{20,12},{24,0},{28,4},{1,25},{... | collective-permute-start | bytes 786440 | tf_op jit(solution)/shard_map/ppermute | solution.py:40
  25.4 7.4 %collective-permute-done.3.refs_1_.refs_5_ = bf16[128,2176]{1,0:T(8,128)(2,1)S(1)} collective-permute-done((bf16[128,2176]{1,0:T(8,128)(2,1)}, bf16[128,2176]{1,0:T(8,128)(2,1)S(1)}, u32[]{:S(2)}, u32[]{:S(2)}) %collective-permute-start.3) | collective-permute-done | bytes 557088 | tf_op jit(solution)/shard_map/ppermute | solution.py:36
  33.5 3.3 %collective-permute-done.4.refs_2_ = bf16[128,2176]{1,0:T(8,128)(2,1)S(1)} collective-permute-done((bf16[128,2176]{1,0:T(8,128)(2,1)}, bf16[128,2176]{1,0:T(8,128)(2,1)S(1)}, u32[]{:S(2)}, u32[]{:S(2)}) %collective-permute-start.4) | collective-permute-done | bytes 557088 | tf_op jit(solution)/shard_map/ppermute | solution.py:36
  36.8 1.3 %collective-permute-start.6 = (bf16[128,2176]{1,0:T(8,128)(2,1)S(1)}, bf16[128,2176]{1,0:T(8,128)(2,1)S(1)}, u32[]{:S(2)}, u32[]{:S(2)}) collective-permute-start(bf16[128,2176]{1,0:T(8,128)(2,1)S(1)} %collective-permute-done.4.refs_2_), channel_id=1, source_target_pairs={{1,0},{2,1},{5,4},{6,5},{9,8},{10,9},{13,12},{14,13},{17,16},{18,1... | collective-permute-start | bytes 1671176 | tf_op jit(solution)/shard_map/ppermute | solution.py:36
  39.6 2.2 %stack_rows.4.near_ref = bf16[256,2048]{1,0:T(8,128)(2,1)} custom-call(bf16[64,2048]{1,0:T(8,128)(2,1)} %copy-done.3, bf16[64,2048]{1,0:T(8,128)(2,1)} %copy-done.15, bf16[64,2048]{1,0:T(8,128)(2,1)} %copy-done.13, bf16[64,2048]{1,0:T(8,128)(2,1)} %copy-done.14), custom_call_target="tpu_custom_call" | custom-call | bytes 1024 | tf_op jit(solution)/shard_map/stack_rows/pallas_call | solution.py:135
  41.9 3.6 %all-to-all-start = ((bf16[8,144,512]{2,1,0:T(8,128)(2,1)}), bf16[8,144,512]{2,1,0:T(8,128)(2,1)S(1)}, u32[]{:S(2)}, u32[]{:S(2)}) async-start(bf16[8,144,512]{2,1,0:T(8,128)(2,1)} %get-tuple-element.19), calls=%async_computation | async-start | bytes 2359296 | tf_op jit(solution)/shard_map/all_to_all | solution.py:461
  46.2 5.8 %collective-permute-done.6.right_ref.refs_4_ = bf16[128,2176]{1,0:T(8,128)(2,1)S(1)} collective-permute-done((bf16[128,2176]{1,0:T(8,128)(2,1)S(1)}, bf16[128,2176]{1,0:T(8,128)(2,1)S(1)}, u32[]{:S(2)}, u32[]{:S(2)}) %collective-permute-start.6) | collective-permute-done | bytes 557088 | tf_op jit(solution)/shard_map/ppermute | solution.py:36
  52.0 1.3 %collective-permute-start.8 = (bf16[128,2176]{1,0:T(8,128)(2,1)S(1)}, bf16[128,2176]{1,0:T(8,128)(2,1)S(1)}, u32[]{:S(2)}, u32[]{:S(2)}) collective-permute-start(bf16[128,2176]{1,0:T(8,128)(2,1)S(1)} %collective-permute-done.6.right_ref.refs_4_), channel_id=1, source_target_pairs={{1,0},{5,4},{9,8},{13,12},{17,16},{21,20},{25,24},{29,28}} | collective-permute-start | bytes 1671176 | tf_op jit(solution)/shard_map/ppermute | solution.py:36
  53.3 2.8 %place_slices.1.in_ref = bf16[8,128,1024]{2,1,0:T(8,128)(2,1)} custom-call(bf16[128,2176]{1,0:T(8,128)(2,1)} %copy-done.1, bf16[128,2176]{1,0:T(8,128)(2,1)} %copy-done.7, bf16[128,2176]{1,0:T(8,128)(2,1)} %copy-done.10), custom_call_target="tpu_custom_call" | custom-call | bytes 1024 | tf_op jit(solution)/shard_map/place_slices/pallas_call | solution.py:214
  56.2 3.2 %partial_products.1 = (f32[128,128]{1,0:T(8,128)}, f32[128,128]{1,0:T(8,128)}, f32[128,128]{1,0:T(8,128)}, f32[128,128]{1,0:T(8,128)}) custom-call(bf16[256,2048]{1,0:T(8,128)(2,1)} %stack_rows.4.near_ref, bf16[256,2048]{1,0:T(8,128)(2,1)} %collective-permute-done.12.far_ref, bf16[128,2048]{1,0:T(8,128)(2,1)} %s_ref.3, bf16[128,2048]{1,0:T(8,128)(2,1)} %p_ref.3), custom_call_target="tpu_custom_call" | custom-call | bytes 1024 | tf_op jit(solution)/shard_map/partial_products/pallas_call | solution.py:179
  59.4 2.9 %all-to-all-done.refs_1_.refs_0_ = bf16[8,144,512]{2,1,0:T(8,128)(2,1)S(1)} async-done(((bf16[8,144,512]{2,1,0:T(8,128)(2,1)}), bf16[8,144,512]{2,1,0:T(8,128)(2,1)S(1)}, u32[]{:S(2)}, u32[]{:S(2)}) %all-to-all-start) | async-done | bytes 1179680 | tf_op jit(solution)/shard_map/all_to_all | solution.py:461
  62.3 4.0 %collective-permute-done.8.first_ref.refs_6_ = bf16[128,2176]{1,0:T(8,128)(2,1)S(1)} collective-permute-done((bf16[128,2176]{1,0:T(8,128)(2,1)S(1)}, bf16[128,2176]{1,0:T(8,128)(2,1)S(1)}, u32[]{:S(2)}, u32[]{:S(2)}) %collective-permute-start.8) | collective-permute-done | bytes 557088 | tf_op jit(solution)/shard_map/ppermute | solution.py:36
  67.1 3.2 %place_last.1.refs_9_ = bf16[8,128,1024]{2,1,0:T(8,128)(2,1)} custom-call(bf16[8,128,1024]{2,1,0:T(8,128)(2,1)} %place_slices.1.in_ref, bf16[128,2176]{1,0:T(8,128)(2,1)} %copy-done.8, bf16[128,2176]{1,0:T(8,128)(2,1)} %copy-done.11, bf16[128,2176]{1,0:T(8,128)(2,1)} %copy-done.9, bf16[128,2176]{1,0:T(8,128)(2,1)} %copy-done.12, ...), custom_call_target="tpu_custom_call", output_to_operand_aliasing={{}: (0, {})} | custom-call | bytes 1024 | tf_op jit(solution)/shard_map/place_last/pallas_call | solution.py:263
  70.3 3.7 %all-to-all-start.1 = ((bf16[8,128,1024]{2,1,0:T(8,128)(2,1)}), bf16[8,128,1024]{2,1,0:T(8,128)(2,1)S(1)}, u32[]{:S(2)}, u32[]{:S(2)}) async-start(bf16[8,128,1024]{2,1,0:T(8,128)(2,1)} %place_last.1.refs_9_), calls=%async_computation.1 | async-start | bytes 4194304 | tf_op jit(solution)/shard_map/all_to_all | solution.py:480
  74.4 1.9 %collective-permute-start.15 = (f32[128,128]{1,0:T(8,128)S(1)}, f32[128,128]{1,0:T(8,128)S(1)}, u32[]{:S(2)}, u32[]{:S(2)}) collective-permute-start(f32[128,128]{1,0:T(8,128)S(1)} %copy-done.19), channel_id=1, source_target_pairs={{0,1},{1,2},{2,3},{3,0},{4,5},{5,6},{6,7},{7,4},{8,9},{9,10},{10,1... | collective-permute-start | bytes 196616 | tf_op jit(solution)/shard_map/ppermute | solution.py:32
  76.3 5.7 %gate_and_up.1.pre_ref = f32[128,256]{1,0:T(8,128)} custom-call(bf16[128,2176]{1,0:T(8,128)(2,1)} %copy-done.1, bf16[128,2176]{1,0:T(8,128)(2,1)} %copy-done.7, bf16[128,2176]{1,0:T(8,128)(2,1)} %copy-done.10, bf16[128,2176]{1,0:T(8,128)(2,1)} %copy-done.8, bf16[128,2176]{1,0:T(8,128)(2,1)} %copy-done.11, bf16[128,2176]{1,0:T(8,128)(2,1)} %copy-done.9, ...), custom_call_target="tpu_custom_call" | custom-call | bytes 1024 | tf_op jit(solution)/shard_map/gate_and_up/pallas_call | solution.py:300
  83.6 1.8 %gradients.1.refs_0_ = bf16[128,384]{1,0:T(8,128)(2,1)} custom-call(f32[128,256]{1,0:T(8,128)} %gate_and_up.1.pre_ref, f32[128,128]{1,0:T(8,128)} %get-tuple-element.18.refs_0_, f32[128,128]{1,0:T(8,128)} %copy-done.16, f32[128,128]{1,0:T(8,128)} %copy-done.17, f32[128,128]{1,0:T(8,128)} %copy-done.18, bf16[128,2176]{1,0:T(8,128)(2,1)} %copy-done.1, ...), custom_call_target="tpu_custom_call" | custom-call | bytes 1024 | tf_op jit(solution)/shard_map/gradients/pallas_call | solution.py:343
  85.4 1.5 %collective-permute-done.16.refs_1_ = bf16[128,384]{1,0:T(8,128)(2,1)S(1)} collective-permute-done((bf16[128,384]{1,0:T(8,128)(2,1)}, bf16[128,384]{1,0:T(8,128)(2,1)S(1)}, u32[]{:S(2)}, u32[]{:S(2)}) %collective-permute-start.16) | collective-permute-done | bytes 98336 | tf_op jit(solution)/shard_map/ppermute | solution.py:40
  87.8 1.8 %collective-permute-start.17 = (bf16[256,384]{1,0:T(8,128)(2,1)S(1)}, bf16[256,384]{1,0:T(8,128)(2,1)S(1)}, u32[]{:S(2)}, u32[]{:S(2)}) collective-permute-start(bf16[256,384]{1,0:T(8,128)(2,1)S(1)} %stack_rows.5.refs_0_), channel_id=1, source_target_pairs={{0,8},{4,12},{8,0},{12,4},{16,24},{20,28},{24,16},{28,20},{1,9},{5... | collective-permute-start | bytes 589832 | tf_op jit(solution)/shard_map/ppermute | solution.py:40
  89.6 1.5 %collective-permute-start.18 = (bf16[256,384]{1,0:T(8,128)(2,1)S(1)}, bf16[256,384]{1,0:T(8,128)(2,1)S(1)}, u32[]{:S(2)}, u32[]{:S(2)}) collective-permute-start(bf16[256,384]{1,0:T(8,128)(2,1)S(1)} %stack_rows.5.refs_0_), channel_id=1, source_target_pairs={{0,16},{4,20},{8,24},{12,28},{16,0},{20,4},{24,8},{28,12},{1,17},{... | collective-permute-start | bytes 589832 | tf_op jit(solution)/shard_map/ppermute | solution.py:40
  91.4 5.8 %hand_over.1.handed_ref = bf16[8,128,512]{2,1,0:T(8,128)(2,1)} custom-call(bf16[8,144,512]{2,1,0:T(8,128)(2,1)} %copy-done.6), custom_call_target="tpu_custom_call" | custom-call | bytes 1024 | tf_op jit(solution)/shard_map/hand_over/pallas_call | solution.py:389
  97.2 7.3 %collective-permute-done.17.refs_1_ = bf16[256,384]{1,0:T(8,128)(2,1)S(1)} collective-permute-done((bf16[256,384]{1,0:T(8,128)(2,1)S(1)}, bf16[256,384]{1,0:T(8,128)(2,1)S(1)}, u32[]{:S(2)}, u32[]{:S(2)}) %collective-permute-start.17) | collective-permute-done | bytes 196640 | tf_op jit(solution)/shard_map/ppermute | solution.py:40
  104.5 4.7 %collective-permute-done.19.refs_3_ = bf16[256,384]{1,0:T(8,128)(2,1)S(1)} collective-permute-done((bf16[256,384]{1,0:T(8,128)(2,1)S(1)}, bf16[256,384]{1,0:T(8,128)(2,1)S(1)}, u32[]{:S(2)}, u32[]{:S(2)}) %collective-permute-start.19) | collective-permute-done | bytes 196640 | tf_op jit(solution)/shard_map/ppermute | solution.py:40
  110.4 1.8 %final_product.1 = (f32[128,1,512]{2,1,0:T(1,128)}, f32[128,1024]{1,0:T(8,128)}, f32[128,1024]{1,0:T(8,128)}) custom-call(bf16[8,128,1024]{2,1,0:T(8,128)(2,1)S(1)} %all-to-all-done.1.feats_ref, bf16[8,128,512]{2,1,0:T(8,128)(2,1)S(1)} %copy-done.2, bf16[256,384]{1,0:T(8,128)(2,1)S(1)} %stack_rows.5.refs_0_, ...), custom_call_target="tpu_custom_call" | custom-call | bytes 1024 | tf_op jit(solution)/shard_map/final_product/pallas_call | solution.py:433
  (68 shorter events, 12.3 us)
Async XLA Ops:
  3.5 7.8 %collective-permute-start = (bf16[16,2048]{1,0:T(8,128)(2,1)}, bf16[16,2048]{1,0:T(8,128)(2,1)S(1)}, u32[]{:S(2)}, u32[]{:S(2)}) collective-permute-start(bf16[16,2048]{1,0:T(8,128)(2,1)} %get-tuple-element.15), channel_id=1, source_target_pairs={{0,1},{1,2},{2,3},{3,0},{4,5},{5,6},{6,7},{7,4},{8,9},{9,10},{10,1... | collective-permute-start | bytes 196616 | tf_op jit(solution)/shard_map/ppermute | solution.py:32
  6.6 7.3 %collective-permute-start.1 = (bf16[16,2048]{1,0:T(8,128)(2,1)}, bf16[16,2048]{1,0:T(8,128)(2,1)S(1)}, u32[]{:S(2)}, u32[]{:S(2)}) collective-permute-start(bf16[16,2048]{1,0:T(8,128)(2,1)} %get-tuple-element.16), channel_id=1, source_target_pairs={{0,2},{1,3},{2,0},{3,1},{4,6},{5,7},{6,4},{7,5},{8,10},{9,11},{10,... | collective-permute-start | bytes 196616 | tf_op jit(solution)/shard_map/ppermute | solution.py:32
  9.2 4.9 %collective-permute-start.2 = (bf16[16,2048]{1,0:T(8,128)(2,1)}, bf16[16,2048]{1,0:T(8,128)(2,1)S(1)}, u32[]{:S(2)}, u32[]{:S(2)}) collective-permute-start(bf16[16,2048]{1,0:T(8,128)(2,1)} %get-tuple-element.17), channel_id=1, source_target_pairs={{0,3},{1,0},{2,1},{3,2},{4,7},{5,4},{6,5},{7,6},{8,11},{9,8},{10,9... | collective-permute-start | bytes 196616 | tf_op jit(solution)/shard_map/ppermute | solution.py:32
  15.0 23.2 %copy-start.3 = (bf16[64,2048]{1,0:T(8,128)(2,1)}, bf16[64,2048]{1,0:T(8,128)(2,1)S(1)}, u32[]{:S(2)}) copy-start(bf16[64,2048]{1,0:T(8,128)(2,1)S(1)} %stack_rows.3.refs_1_.refs_0_) | copy-start | bytes 786436
  17.0 15.8 %collective-permute-start.3 = (bf16[128,2176]{1,0:T(8,128)(2,1)}, bf16[128,2176]{1,0:T(8,128)(2,1)S(1)}, u32[]{:S(2)}, u32[]{:S(2)}) collective-permute-start(bf16[128,2176]{1,0:T(8,128)(2,1)} %copy-done.1), channel_id=1, source_target_pairs={{0,1},{1,2},{2,3},{4,5},{5,6},{6,7},{8,9},{9,10},{10,11},{12,13},{... | collective-permute-start | bytes 1671176 | tf_op jit(solution)/shard_map/ppermute | solution.py:36
  20.5 16.3 %collective-permute-start.4 = (bf16[128,2176]{1,0:T(8,128)(2,1)}, bf16[128,2176]{1,0:T(8,128)(2,1)S(1)}, u32[]{:S(2)}, u32[]{:S(2)}) collective-permute-start(bf16[128,2176]{1,0:T(8,128)(2,1)} %copy-done.1), channel_id=1, source_target_pairs={{1,0},{2,1},{3,2},{5,4},{6,5},{7,6},{9,8},{10,9},{11,10},{13,12},{... | collective-permute-start | bytes 1671176 | tf_op jit(solution)/shard_map/ppermute | solution.py:36
  21.8 16.3 %collective-permute-start.10 = (bf16[64,2048]{1,0:T(8,128)(2,1)S(1)}, bf16[64,2048]{1,0:T(8,128)(2,1)S(1)}, u32[]{:S(2)}, u32[]{:S(2)}) collective-permute-start(bf16[64,2048]{1,0:T(8,128)(2,1)S(1)} %stack_rows.3.refs_1_.refs_0_), channel_id=1, source_target_pairs={{0,16},{4,20},{8,24},{12,28},{16,0},{20,4},{24,8},{28,12},{1,17},{... | collective-permute-start | bytes 786440 | tf_op jit(solution)/shard_map/ppermute | solution.py:40
  23.4 14.7 %collective-permute-start.11 = (bf16[64,2048]{1,0:T(8,128)(2,1)S(1)}, bf16[64,2048]{1,0:T(8,128)(2,1)S(1)}, u32[]{:S(2)}, u32[]{:S(2)}) collective-permute-start(bf16[64,2048]{1,0:T(8,128)(2,1)S(1)} %stack_rows.3.refs_1_.refs_0_), channel_id=1, source_target_pairs={{0,24},{4,28},{8,16},{12,20},{16,8},{20,12},{24,0},{28,4},{1,25},{... | collective-permute-start | bytes 786440 | tf_op jit(solution)/shard_map/ppermute | solution.py:40
  24.8 13.3 %collective-permute-start.9 = (bf16[64,2048]{1,0:T(8,128)(2,1)S(1)}, bf16[64,2048]{1,0:T(8,128)(2,1)S(1)}, u32[]{:S(2)}, u32[]{:S(2)}) collective-permute-start(bf16[64,2048]{1,0:T(8,128)(2,1)S(1)} %stack_rows.3.refs_1_.refs_0_), channel_id=1, source_target_pairs={{0,8},{4,12},{8,0},{12,4},{16,24},{20,28},{24,16},{28,20},{1,9},{5... | collective-permute-start | bytes 786440 | tf_op jit(solution)/shard_map/ppermute | solution.py:40
  32.8 9.1 %copy-start.7 = (bf16[128,2176]{1,0:T(8,128)(2,1)}, bf16[128,2176]{1,0:T(8,128)(2,1)S(1)}, u32[]{:S(2)}) copy-start(bf16[128,2176]{1,0:T(8,128)(2,1)S(1)} %collective-permute-done.3.refs_1_.refs_5_) | copy-start | bytes 1671172
  32.8 12.7 %collective-permute-start.5 = (bf16[128,2176]{1,0:T(8,128)(2,1)S(1)}, bf16[128,2176]{1,0:T(8,128)(2,1)S(1)}, u32[]{:S(2)}, u32[]{:S(2)}) collective-permute-start(bf16[128,2176]{1,0:T(8,128)(2,1)S(1)} %collective-permute-done.3.refs_1_.refs_5_), channel_id=1, source_target_pairs={{1,2},{2,3},{5,6},{6,7},{9,10},{10,11},{13,14},{14,15},{17,18},{18... | collective-permute-start | bytes 1671176 | tf_op jit(solution)/shard_map/ppermute | solution.py:36
  36.8 5.1 %copy-start.10 = (bf16[128,2176]{1,0:T(8,128)(2,1)}, bf16[128,2176]{1,0:T(8,128)(2,1)S(1)}, u32[]{:S(2)}) copy-start(bf16[128,2176]{1,0:T(8,128)(2,1)S(1)} %collective-permute-done.4.refs_2_) | copy-start | bytes 1671172
  36.8 15.2 %collective-permute-start.6 = (bf16[128,2176]{1,0:T(8,128)(2,1)S(1)}, bf16[128,2176]{1,0:T(8,128)(2,1)S(1)}, u32[]{:S(2)}, u32[]{:S(2)}) collective-permute-start(bf16[128,2176]{1,0:T(8,128)(2,1)S(1)} %collective-permute-done.4.refs_2_), channel_id=1, source_target_pairs={{1,0},{2,1},{5,4},{6,5},{9,8},{10,9},{13,12},{14,13},{17,16},{18,1... | collective-permute-start | bytes 1671176 | tf_op jit(solution)/shard_map/ppermute | solution.py:36
  41.9 14.3 %collective-permute-start.12 = (bf16[256,2048]{1,0:T(8,128)(2,1)}, bf16[256,2048]{1,0:T(8,128)(2,1)}, u32[]{:S(2)}, u32[]{:S(2)}) collective-permute-start(bf16[256,2048]{1,0:T(8,128)(2,1)} %stack_rows.4.near_ref), channel_id=1, source_target_pairs={{0,4},{4,0},{8,12},{12,8},{16,20},{20,16},{24,28},{28,24},{1,5},{5... | collective-permute-start | bytes 3145736 | tf_op jit(solution)/shard_map/ppermute | solution.py:40
  41.9 20.4 %all-to-all-start = ((bf16[8,144,512]{2,1,0:T(8,128)(2,1)}), bf16[8,144,512]{2,1,0:T(8,128)(2,1)S(1)}, u32[]{:S(2)}, u32[]{:S(2)}) async-start(bf16[8,144,512]{2,1,0:T(8,128)(2,1)} %get-tuple-element.19), calls=%async_computation | async-start | bytes 2359296 | tf_op jit(solution)/shard_map/all_to_all | solution.py:461
  45.5 13.9 %copy-start.8 = (bf16[128,2176]{1,0:T(8,128)(2,1)}, bf16[128,2176]{1,0:T(8,128)(2,1)S(1)}, u32[]{:S(2)}) copy-start(bf16[128,2176]{1,0:T(8,128)(2,1)S(1)} %collective-permute-done.5.left_ref.refs_3_.refs_6_) | copy-start | bytes 1671172
  45.5 16.8 %collective-permute-start.7 = (bf16[128,2176]{1,0:T(8,128)(2,1)S(1)}, bf16[128,2176]{1,0:T(8,128)(2,1)S(1)}, u32[]{:S(2)}, u32[]{:S(2)}) collective-permute-start(bf16[128,2176]{1,0:T(8,128)(2,1)S(1)} %collective-permute-done.5.left_ref.refs_3_.refs_6_), channel_id=1, source_target_pairs={{2,3},{6,7},{10,11},{14,15},{18,19},{22,23},{26,27},{30,31}} | collective-permute-start | bytes 1671176 | tf_op jit(solution)/shard_map/ppermute | solution.py:36
  52.0 7.4 %copy-start.11 = (bf16[128,2176]{1,0:T(8,128)(2,1)}, bf16[128,2176]{1,0:T(8,128)(2,1)S(1)}, u32[]{:S(2)}) copy-start(bf16[128,2176]{1,0:T(8,128)(2,1)S(1)} %collective-permute-done.6.right_ref.refs_4_) | copy-start | bytes 1671172
  52.0 14.3 %collective-permute-start.8 = (bf16[128,2176]{1,0:T(8,128)(2,1)S(1)}, bf16[128,2176]{1,0:T(8,128)(2,1)S(1)}, u32[]{:S(2)}, u32[]{:S(2)}) collective-permute-start(bf16[128,2176]{1,0:T(8,128)(2,1)S(1)} %collective-permute-done.6.right_ref.refs_4_), channel_id=1, source_target_pairs={{1,0},{5,4},{9,8},{13,12},{17,16},{21,20},{25,24},{29,28}} | collective-permute-start | bytes 1671176 | tf_op jit(solution)/shard_map/ppermute | solution.py:36
  62.3 4.1 %copy-start.6 = (bf16[8,144,512]{2,1,0:T(8,128)(2,1)}, bf16[8,144,512]{2,1,0:T(8,128)(2,1)S(1)}, u32[]{:S(2)}) copy-start(bf16[8,144,512]{2,1,0:T(8,128)(2,1)S(1)} %all-to-all-done.refs_1_.refs_0_) | copy-start | bytes 3538948
  62.3 4.1 %copy-start.9 = (bf16[128,2176]{1,0:T(8,128)(2,1)}, bf16[128,2176]{1,0:T(8,128)(2,1)S(1)}, u32[]{:S(2)}) copy-start(bf16[128,2176]{1,0:T(8,128)(2,1)S(1)} %collective-permute-done.7.last_ref.refs_5_.refs_7_) | copy-start | bytes 1671172
  70.3 3.8 %copy-start.21 = (f32[128,128]{1,0:T(8,128)S(1)}, f32[128,128]{1,0:T(8,128)}, u32[]{:S(2)}) copy-start(f32[128,128]{1,0:T(8,128)} %get-tuple-element.20) | copy-start | bytes 196612
  70.3 3.9 %copy-start.20 = (f32[128,128]{1,0:T(8,128)S(1)}, f32[128,128]{1,0:T(8,128)}, u32[]{:S(2)}) copy-start(f32[128,128]{1,0:T(8,128)} %get-tuple-element.21) | copy-start | bytes 196612
  70.3 4.0 %copy-start.19 = (f32[128,128]{1,0:T(8,128)S(1)}, f32[128,128]{1,0:T(8,128)}, u32[]{:S(2)}) copy-start(f32[128,128]{1,0:T(8,128)} %get-tuple-element.22) | copy-start | bytes 196612
  70.3 38.8 %all-to-all-start.1 = ((bf16[8,128,1024]{2,1,0:T(8,128)(2,1)}), bf16[8,128,1024]{2,1,0:T(8,128)(2,1)S(1)}, u32[]{:S(2)}, u32[]{:S(2)}) async-start(bf16[8,128,1024]{2,1,0:T(8,128)(2,1)} %place_last.1.refs_9_), calls=%async_computation.1 | async-start | bytes 4194304 | tf_op jit(solution)/shard_map/all_to_all | solution.py:480
  74.1 7.9 %collective-permute-start.13 = (f32[128,128]{1,0:T(8,128)S(1)}, f32[128,128]{1,0:T(8,128)S(1)}, u32[]{:S(2)}, u32[]{:S(2)}) collective-permute-start(f32[128,128]{1,0:T(8,128)S(1)} %copy-done.21), channel_id=1, source_target_pairs={{0,3},{1,0},{2,1},{3,2},{4,7},{5,4},{6,5},{7,6},{8,11},{9,8},{10,9... | collective-permute-start | bytes 196616 | tf_op jit(solution)/shard_map/ppermute | solution.py:32
  74.2 8.2 %collective-permute-start.14 = (f32[128,128]{1,0:T(8,128)S(1)}, f32[128,128]{1,0:T(8,128)S(1)}, u32[]{:S(2)}, u32[]{:S(2)}) collective-permute-start(f32[128,128]{1,0:T(8,128)S(1)} %copy-done.20), channel_id=1, source_target_pairs={{0,2},{1,3},{2,0},{3,1},{4,6},{5,7},{6,4},{7,5},{8,10},{9,11},{10,... | collective-permute-start | bytes 196616 | tf_op jit(solution)/shard_map/ppermute | solution.py:32
  74.4 8.0 %collective-permute-start.15 = (f32[128,128]{1,0:T(8,128)S(1)}, f32[128,128]{1,0:T(8,128)S(1)}, u32[]{:S(2)}, u32[]{:S(2)}) collective-permute-start(f32[128,128]{1,0:T(8,128)S(1)} %copy-done.19), channel_id=1, source_target_pairs={{0,1},{1,2},{2,3},{3,0},{4,5},{5,6},{6,7},{7,4},{8,9},{9,10},{10,1... | collective-permute-start | bytes 196616 | tf_op jit(solution)/shard_map/ppermute | solution.py:32
  85.4 1.5 %collective-permute-start.16 = (bf16[128,384]{1,0:T(8,128)(2,1)}, bf16[128,384]{1,0:T(8,128)(2,1)S(1)}, u32[]{:S(2)}, u32[]{:S(2)}) collective-permute-start(bf16[128,384]{1,0:T(8,128)(2,1)} %gradients.1.refs_0_), channel_id=1, source_target_pairs={{0,4},{4,0},{8,12},{12,8},{16,20},{20,16},{24,28},{28,24},{1,5},{5... | collective-permute-start | bytes 294920 | tf_op jit(solution)/shard_map/ppermute | solution.py:40
  87.8 16.7 %collective-permute-start.17 = (bf16[256,384]{1,0:T(8,128)(2,1)S(1)}, bf16[256,384]{1,0:T(8,128)(2,1)S(1)}, u32[]{:S(2)}, u32[]{:S(2)}) collective-permute-start(bf16[256,384]{1,0:T(8,128)(2,1)S(1)} %stack_rows.5.refs_0_), channel_id=1, source_target_pairs={{0,8},{4,12},{8,0},{12,4},{16,24},{20,28},{24,16},{28,20},{1,9},{5... | collective-permute-start | bytes 589832 | tf_op jit(solution)/shard_map/ppermute | solution.py:40
  89.6 14.9 %collective-permute-start.18 = (bf16[256,384]{1,0:T(8,128)(2,1)S(1)}, bf16[256,384]{1,0:T(8,128)(2,1)S(1)}, u32[]{:S(2)}, u32[]{:S(2)}) collective-permute-start(bf16[256,384]{1,0:T(8,128)(2,1)S(1)} %stack_rows.5.refs_0_), channel_id=1, source_target_pairs={{0,16},{4,20},{8,24},{12,28},{16,0},{20,4},{24,8},{28,12},{1,17},{... | collective-permute-start | bytes 589832 | tf_op jit(solution)/shard_map/ppermute | solution.py:40
  91.1 18.0 %collective-permute-start.19 = (bf16[256,384]{1,0:T(8,128)(2,1)S(1)}, bf16[256,384]{1,0:T(8,128)(2,1)S(1)}, u32[]{:S(2)}, u32[]{:S(2)}) collective-permute-start(bf16[256,384]{1,0:T(8,128)(2,1)S(1)} %stack_rows.5.refs_0_), channel_id=1, source_target_pairs={{0,24},{4,28},{8,16},{12,20},{16,8},{20,12},{24,0},{28,4},{1,25},{... | collective-permute-start | bytes 589832 | tf_op jit(solution)/shard_map/ppermute | solution.py:40
  (12 other events, 9.8 us)

commit v8 on v7

--- a/solution.py
+++ b/solution.py
@@ -153,7 +153,7 @@
         out_specs=pl.BlockSpec(memory_space=pl.ANY),
         out_shape=struct(x.shape, x.dtype),
         input_output_aliases={0: 0},
-        compiler_params=params(1),
+        compiler_params=params(60),
         cost_estimate=cost(0, 1024),
         name="ordered",
     )(x, *after)

time: 113 us -> 112 us (level)
  local copies, waits for them, and re-layouts: 8.46 us -> 7.2 us
    unnamed x44 -> x40, local copies, waits for them, and re-layouts: 8.46 us -> 7.2 us
  transfers between devices with their start and end apart: 22 -> 22, of which waited for: 12 -> 12; matrix products, arithmetic and copies ran while one was open for 0% -> 0% of each run, Pallas kernels for 19% -> 20%
where the time goes in v8:
time: 112 us; the launch traced here: 111 us
  waiting for transfers between devices  40.9 us (37%)
  starting transfers between devices  32.3 us (29%)
  Pallas kernels  29.6 us (26%)
  local copies, waits for them, and re-layouts  7.2 us (6%)
    ppermute x6, waiting for transfers between devices, hop(): return lax.ppermute(x, 'tensor', pairs)  20.7 us
    ppermute x8, waiting for transfers between devices, swap(): return lax.ppermute(x, 'dp', [(i, i ^ mask) for i in range(count)])  13.5 us
    ppermute x6, starting transfers between devices, shift(): lax.ppermute(x, 'tensor', [(i, (i + by) % count) for i in range(count)])  9.14 us
    ppermute x6, starting transfers between devices, hop(): return lax.ppermute(x, 'tensor', pairs)  8.75 us
    unnamed x40, local copies, waits for them, and re-layouts  7.2 us
    ppermute x8, starting transfers between devices, swap(): return lax.ppermute(x, 'dp', [(i, i ^ mask) for i in range(count)])  7.11 us
    pallas_call x1, Pallas kernels, hand_over(): pl.pallas_call(kernel, in_specs=[VMEM] * (1 + len(digits)), out_specs=VME...  5.85 us
    pallas_call x1, Pallas kernels, gate_and_up(): pl.pallas_call(kernel, in_specs=[VMEM] * n_s + [pl.BlockSpec(memory_space...  5.73 us
  transfers between devices with their start and end apart: 22, of which 12 were waited for; matrix products, arithmetic and copies ran while one was open for 0% of the time, Pallas kernels for 20%

profile of v8, /device:TPU:0, one launch (start us, length us, event | category | flops | bytes accessed | tf_op | source)
XLA Modules:
  0.0 110.9 jit_solution(13812125362944347037)
XLA Ops:
  0.6 2.9 %prepare.1 = (bf16[128,2176]{1,0:T(8,128)(2,1)}, bf16[16,2048]{1,0:T(8,128)(2,1)}, bf16[16,2048]{1,0:T(8,128)(2,1)}, bf16[16,2048]{1,0:T(8,128)(2,1)}, bf16[16,2...) custom-call(s32[1,128]{1,0:T(1,128)} %bitcast.1, bf16[128,4096]{1,0:T(8,128)(2,1)} %t_ref.1, bf16[128,2048]{1,0:T(8,128)(2,1)} %x_ref.1, ...), custom_call_target="tpu_custom_call" | custom-call | bytes 1024 | tf_op jit(solution)/shard_map/prepare/pallas_call | solution.py:111
  3.5 3.1 %collective-permute-start = (bf16[16,2048]{1,0:T(8,128)(2,1)}, bf16[16,2048]{1,0:T(8,128)(2,1)S(1)}, u32[]{:S(2)}, u32[]{:S(2)}) collective-permute-start(bf16[16,2048]{1,0:T(8,128)(2,1)} %get-tuple-element.15), channel_id=1, source_target_pairs={{0,1},{1,2},{2,3},{3,0},{4,5},{5,6},{6,7},{7,4},{8,9},{9,10},{10,1... | collective-permute-start | bytes 196616 | tf_op jit(solution)/shard_map/ppermute | solution.py:32
  6.6 2.6 %collective-permute-start.1 = (bf16[16,2048]{1,0:T(8,128)(2,1)}, bf16[16,2048]{1,0:T(8,128)(2,1)S(1)}, u32[]{:S(2)}, u32[]{:S(2)}) collective-permute-start(bf16[16,2048]{1,0:T(8,128)(2,1)} %get-tuple-element.16), channel_id=1, source_target_pairs={{0,2},{1,3},{2,0},{3,1},{4,6},{5,7},{6,4},{7,5},{8,10},{9,11},{10,... | collective-permute-start | bytes 196616 | tf_op jit(solution)/shard_map/ppermute | solution.py:32
  9.2 1.3 %collective-permute-start.2 = (bf16[16,2048]{1,0:T(8,128)(2,1)}, bf16[16,2048]{1,0:T(8,128)(2,1)S(1)}, u32[]{:S(2)}, u32[]{:S(2)}) collective-permute-start(bf16[16,2048]{1,0:T(8,128)(2,1)} %get-tuple-element.17), channel_id=1, source_target_pairs={{0,3},{1,0},{2,1},{3,2},{4,7},{5,4},{6,5},{7,6},{8,11},{9,8},{10,9... | collective-permute-start | bytes 196616 | tf_op jit(solution)/shard_map/ppermute | solution.py:32
  11.4 2.5 %collective-permute-done.1.refs_2_ = bf16[16,2048]{1,0:T(8,128)(2,1)S(1)} collective-permute-done((bf16[16,2048]{1,0:T(8,128)(2,1)}, bf16[16,2048]{1,0:T(8,128)(2,1)S(1)}, u32[]{:S(2)}, u32[]{:S(2)}) %collective-permute-start.1) | collective-permute-done | bytes 65568 | tf_op jit(solution)/shard_map/ppermute | solution.py:32
  15.7 3.5 %collective-permute-start.3 = (bf16[128,2176]{1,0:T(8,128)(2,1)}, bf16[128,2176]{1,0:T(8,128)(2,1)S(1)}, u32[]{:S(2)}, u32[]{:S(2)}) collective-permute-start(bf16[128,2176]{1,0:T(8,128)(2,1)} %ordered.1.refs_0_.refs_4_), channel_id=1, source_target_pairs={{0,1},{1,2},{2,3},{4,5},{5,6},{6,7},{8,9},{9,10},{10,11},{12,13},{... | collective-permute-start | bytes 1671176 | tf_op jit(solution)/shard_map/ppermute | solution.py:36
  19.2 1.3 %collective-permute-start.4 = (bf16[128,2176]{1,0:T(8,128)(2,1)}, bf16[128,2176]{1,0:T(8,128)(2,1)S(1)}, u32[]{:S(2)}, u32[]{:S(2)}) collective-permute-start(bf16[128,2176]{1,0:T(8,128)(2,1)} %ordered.1.refs_0_.refs_4_), channel_id=1, source_target_pairs={{1,0},{2,1},{3,2},{5,4},{6,5},{7,6},{9,8},{10,9},{11,10},{13,12},{... | collective-permute-start | bytes 1671176 | tf_op jit(solution)/shard_map/ppermute | solution.py:36
  20.5 1.6 %collective-permute-start.10 = (bf16[64,2048]{1,0:T(8,128)(2,1)}, bf16[64,2048]{1,0:T(8,128)(2,1)S(1)}, u32[]{:S(2)}, u32[]{:S(2)}) collective-permute-start(bf16[64,2048]{1,0:T(8,128)(2,1)} %copy-done.1), channel_id=1, source_target_pairs={{0,16},{4,20},{8,24},{12,28},{16,0},{20,4},{24,8},{28,12},{1,17},{... | collective-permute-start | bytes 786440 | tf_op jit(solution)/shard_map/ppermute | solution.py:40
  22.1 1.4 %collective-permute-start.11 = (bf16[64,2048]{1,0:T(8,128)(2,1)}, bf16[64,2048]{1,0:T(8,128)(2,1)S(1)}, u32[]{:S(2)}, u32[]{:S(2)}) collective-permute-start(bf16[64,2048]{1,0:T(8,128)(2,1)} %copy-done.1), channel_id=1, source_target_pairs={{0,24},{4,28},{8,16},{12,20},{16,8},{20,12},{24,0},{28,4},{1,25},{... | collective-permute-start | bytes 786440 | tf_op jit(solution)/shard_map/ppermute | solution.py:40
  24.1 7.4 %collective-permute-done.3.refs_1_.refs_5_ = bf16[128,2176]{1,0:T(8,128)(2,1)S(1)} collective-permute-done((bf16[128,2176]{1,0:T(8,128)(2,1)}, bf16[128,2176]{1,0:T(8,128)(2,1)S(1)}, u32[]{:S(2)}, u32[]{:S(2)}) %collective-permute-start.3) | collective-permute-done | bytes 557088 | tf_op jit(solution)/shard_map/ppermute | solution.py:36
  32.2 3.3 %collective-permute-done.4.refs_2_ = bf16[128,2176]{1,0:T(8,128)(2,1)S(1)} collective-permute-done((bf16[128,2176]{1,0:T(8,128)(2,1)}, bf16[128,2176]{1,0:T(8,128)(2,1)S(1)}, u32[]{:S(2)}, u32[]{:S(2)}) %collective-permute-start.4) | collective-permute-done | bytes 557088 | tf_op jit(solution)/shard_map/ppermute | solution.py:36
  35.5 1.3 %collective-permute-start.6 = (bf16[128,2176]{1,0:T(8,128)(2,1)S(1)}, bf16[128,2176]{1,0:T(8,128)(2,1)S(1)}, u32[]{:S(2)}, u32[]{:S(2)}) collective-permute-start(bf16[128,2176]{1,0:T(8,128)(2,1)S(1)} %collective-permute-done.4.refs_2_), channel_id=1, source_target_pairs={{1,0},{2,1},{5,4},{6,5},{9,8},{10,9},{13,12},{14,13},{17,16},{18,1... | collective-permute-start | bytes 1671176 | tf_op jit(solution)/shard_map/ppermute | solution.py:36
  38.3 2.2 %stack_rows.4.near_ref = bf16[256,2048]{1,0:T(8,128)(2,1)} custom-call(bf16[64,2048]{1,0:T(8,128)(2,1)} %copy-done.1, bf16[64,2048]{1,0:T(8,128)(2,1)} %copy-done.13, bf16[64,2048]{1,0:T(8,128)(2,1)} %copy-done.11, bf16[64,2048]{1,0:T(8,128)(2,1)} %copy-done.12), custom_call_target="tpu_custom_call" | custom-call | bytes 1024 | tf_op jit(solution)/shard_map/stack_rows/pallas_call | solution.py:135
  40.6 3.6 %all-to-all-start = ((bf16[8,144,512]{2,1,0:T(8,128)(2,1)}), bf16[8,144,512]{2,1,0:T(8,128)(2,1)S(1)}, u32[]{:S(2)}, u32[]{:S(2)}) async-start(bf16[8,144,512]{2,1,0:T(8,128)(2,1)} %get-tuple-element.19), calls=%async_computation | async-start | bytes 2359296 | tf_op jit(solution)/shard_map/all_to_all | solution.py:461
  44.9 5.8 %collective-permute-done.6.right_ref.refs_4_ = bf16[128,2176]{1,0:T(8,128)(2,1)S(1)} collective-permute-done((bf16[128,2176]{1,0:T(8,128)(2,1)S(1)}, bf16[128,2176]{1,0:T(8,128)(2,1)S(1)}, u32[]{:S(2)}, u32[]{:S(2)}) %collective-permute-start.6) | collective-permute-done | bytes 557088 | tf_op jit(solution)/shard_map/ppermute | solution.py:36
  50.7 1.3 %collective-permute-start.8 = (bf16[128,2176]{1,0:T(8,128)(2,1)S(1)}, bf16[128,2176]{1,0:T(8,128)(2,1)S(1)}, u32[]{:S(2)}, u32[]{:S(2)}) collective-permute-start(bf16[128,2176]{1,0:T(8,128)(2,1)S(1)} %collective-permute-done.6.right_ref.refs_4_), channel_id=1, source_target_pairs={{1,0},{5,4},{9,8},{13,12},{17,16},{21,20},{25,24},{29,28}} | collective-permute-start | bytes 1671176 | tf_op jit(solution)/shard_map/ppermute | solution.py:36
  52.0 2.9 %place_slices.1.in_ref = bf16[8,128,1024]{2,1,0:T(8,128)(2,1)} custom-call(bf16[128,2176]{1,0:T(8,128)(2,1)} %ordered.1.refs_0_.refs_4_, bf16[128,2176]{1,0:T(8,128)(2,1)} %copy-done.5, bf16[128,2176]{1,0:T(8,128)(2,1)} %copy-done.8), custom_call_target="tpu_custom_call" | custom-call | bytes 1024 | tf_op jit(solution)/shard_map/place_slices/pallas_call | solution.py:214
  54.9 3.2 %partial_products.1 = (f32[128,128]{1,0:T(8,128)}, f32[128,128]{1,0:T(8,128)}, f32[128,128]{1,0:T(8,128)}, f32[128,128]{1,0:T(8,128)}) custom-call(bf16[256,2048]{1,0:T(8,128)(2,1)} %stack_rows.4.near_ref, bf16[256,2048]{1,0:T(8,128)(2,1)} %collective-permute-done.12.far_ref, bf16[128,2048]{1,0:T(8,128)(2,1)} %s_ref.3, bf16[128,2048]{1,0:T(8,128)(2,1)} %p_ref.3), custom_call_target="tpu_custom_call" | custom-call | bytes 1024 | tf_op jit(solution)/shard_map/partial_products/pallas_call | solution.py:179
  58.1 2.9 %all-to-all-done.refs_1_.refs_0_ = bf16[8,144,512]{2,1,0:T(8,128)(2,1)S(1)} async-done(((bf16[8,144,512]{2,1,0:T(8,128)(2,1)}), bf16[8,144,512]{2,1,0:T(8,128)(2,1)S(1)}, u32[]{:S(2)}, u32[]{:S(2)}) %all-to-all-start) | async-done | bytes 1179680 | tf_op jit(solution)/shard_map/all_to_all | solution.py:461
  61.0 4.1 %collective-permute-done.8.first_ref.refs_6_ = bf16[128,2176]{1,0:T(8,128)(2,1)S(1)} collective-permute-done((bf16[128,2176]{1,0:T(8,128)(2,1)S(1)}, bf16[128,2176]{1,0:T(8,128)(2,1)S(1)}, u32[]{:S(2)}, u32[]{:S(2)}) %collective-permute-start.8) | collective-permute-done | bytes 557088 | tf_op jit(solution)/shard_map/ppermute | solution.py:36
  65.8 3.2 %place_last.1.refs_9_ = bf16[8,128,1024]{2,1,0:T(8,128)(2,1)} custom-call(bf16[8,128,1024]{2,1,0:T(8,128)(2,1)} %place_slices.1.in_ref, bf16[128,2176]{1,0:T(8,128)(2,1)} %copy-done.6, bf16[128,2176]{1,0:T(8,128)(2,1)} %copy-done.9, bf16[128,2176]{1,0:T(8,128)(2,1)} %copy-done.7, bf16[128,2176]{1,0:T(8,128)(2,1)} %copy-done.10, ...), custom_call_target="tpu_custom_call", output_to_operand_aliasing={{}: (0, {})} | custom-call | bytes 1024 | tf_op jit(solution)/shard_map/place_last/pallas_call | solution.py:263
  69.0 3.7 %all-to-all-start.1 = ((bf16[8,128,1024]{2,1,0:T(8,128)(2,1)}), bf16[8,128,1024]{2,1,0:T(8,128)(2,1)S(1)}, u32[]{:S(2)}, u32[]{:S(2)}) async-start(bf16[8,128,1024]{2,1,0:T(8,128)(2,1)} %place_last.1.refs_9_), calls=%async_computation.1 | async-start | bytes 4194304 | tf_op jit(solution)/shard_map/all_to_all | solution.py:480
  73.1 1.9 %collective-permute-start.15 = (f32[128,128]{1,0:T(8,128)S(1)}, f32[128,128]{1,0:T(8,128)S(1)}, u32[]{:S(2)}, u32[]{:S(2)}) collective-permute-start(f32[128,128]{1,0:T(8,128)S(1)} %copy-done.17), channel_id=1, source_target_pairs={{0,1},{1,2},{2,3},{3,0},{4,5},{5,6},{6,7},{7,4},{8,9},{9,10},{10,1... | collective-permute-start | bytes 196616 | tf_op jit(solution)/shard_map/ppermute | solution.py:32
  75.0 5.7 %gate_and_up.1.pre_ref = f32[128,256]{1,0:T(8,128)} custom-call(bf16[128,2176]{1,0:T(8,128)(2,1)} %ordered.1.refs_0_.refs_4_, bf16[128,2176]{1,0:T(8,128)(2,1)} %copy-done.5, bf16[128,2176]{1,0:T(8,128)(2,1)} %copy-done.8, bf16[128,2176]{1,0:T(8,128)(2,1)} %copy-done.6, bf16[128,2176]{1,0:T(8,128)(2,1)} %copy-done.9, bf16[128,2176]{1,0:T(8,128)(2,1)} %copy-done.7, ...), custom_call_target="tpu_custom_call" | custom-call | bytes 1024 | tf_op jit(solution)/shard_map/gate_and_up/pallas_call | solution.py:300
  82.3 1.8 %gradients.1.refs_0_ = bf16[128,384]{1,0:T(8,128)(2,1)} custom-call(f32[128,256]{1,0:T(8,128)} %gate_and_up.1.pre_ref, f32[128,128]{1,0:T(8,128)} %get-tuple-element.18.refs_0_, f32[128,128]{1,0:T(8,128)} %copy-done.14, f32[128,128]{1,0:T(8,128)} %copy-done.15, f32[128,128]{1,0:T(8,128)} %copy-done.16, bf16[128,2176]{1,0:T(8,128)(2,1)} %ordered.1.refs_0_.refs_4_, ...), custom_call_target="tpu_custom_call" | custom-call | bytes 1024 | tf_op jit(solution)/shard_map/gradients/pallas_call | solution.py:343
  84.1 1.5 %collective-permute-done.16.refs_1_ = bf16[128,384]{1,0:T(8,128)(2,1)S(1)} collective-permute-done((bf16[128,384]{1,0:T(8,128)(2,1)}, bf16[128,384]{1,0:T(8,128)(2,1)S(1)}, u32[]{:S(2)}, u32[]{:S(2)}) %collective-permute-start.16) | collective-permute-done | bytes 98336 | tf_op jit(solution)/shard_map/ppermute | solution.py:40
  86.5 1.8 %collective-permute-start.17 = (bf16[256,384]{1,0:T(8,128)(2,1)S(1)}, bf16[256,384]{1,0:T(8,128)(2,1)S(1)}, u32[]{:S(2)}, u32[]{:S(2)}) collective-permute-start(bf16[256,384]{1,0:T(8,128)(2,1)S(1)} %stack_rows.5.refs_0_), channel_id=1, source_target_pairs={{0,8},{4,12},{8,0},{12,4},{16,24},{20,28},{24,16},{28,20},{1,9},{5... | collective-permute-start | bytes 589832 | tf_op jit(solution)/shard_map/ppermute | solution.py:40
  88.3 1.5 %collective-permute-start.18 = (bf16[256,384]{1,0:T(8,128)(2,1)S(1)}, bf16[256,384]{1,0:T(8,128)(2,1)S(1)}, u32[]{:S(2)}, u32[]{:S(2)}) collective-permute-start(bf16[256,384]{1,0:T(8,128)(2,1)S(1)} %stack_rows.5.refs_0_), channel_id=1, source_target_pairs={{0,16},{4,20},{8,24},{12,28},{16,0},{20,4},{24,8},{28,12},{1,17},{... | collective-permute-start | bytes 589832 | tf_op jit(solution)/shard_map/ppermute | solution.py:40
  90.1 5.8 %hand_over.1.handed_ref = bf16[8,128,512]{2,1,0:T(8,128)(2,1)} custom-call(bf16[8,144,512]{2,1,0:T(8,128)(2,1)} %copy-done.4), custom_call_target="tpu_custom_call" | custom-call | bytes 1024 | tf_op jit(solution)/shard_map/hand_over/pallas_call | solution.py:389
  95.9 7.3 %collective-permute-done.17.refs_1_ = bf16[256,384]{1,0:T(8,128)(2,1)S(1)} collective-permute-done((bf16[256,384]{1,0:T(8,128)(2,1)S(1)}, bf16[256,384]{1,0:T(8,128)(2,1)S(1)}, u32[]{:S(2)}, u32[]{:S(2)}) %collective-permute-start.17) | collective-permute-done | bytes 196640 | tf_op jit(solution)/shard_map/ppermute | solution.py:40
  103.2 4.7 %collective-permute-done.19.refs_3_ = bf16[256,384]{1,0:T(8,128)(2,1)S(1)} collective-permute-done((bf16[256,384]{1,0:T(8,128)(2,1)S(1)}, bf16[256,384]{1,0:T(8,128)(2,1)S(1)}, u32[]{:S(2)}, u32[]{:S(2)}) %collective-permute-start.19) | collective-permute-done | bytes 196640 | tf_op jit(solution)/shard_map/ppermute | solution.py:40
  109.1 1.8 %final_product.1 = (f32[128,1,512]{2,1,0:T(1,128)}, f32[128,1024]{1,0:T(8,128)}, f32[128,1024]{1,0:T(8,128)}) custom-call(bf16[8,128,1024]{2,1,0:T(8,128)(2,1)S(1)} %all-to-all-done.1.feats_ref, bf16[8,128,512]{2,1,0:T(8,128)(2,1)S(1)} %copy-done, bf16[256,384]{1,0:T(8,128)(2,1)S(1)} %stack_rows.5.refs_0_, ...), custom_call_target="tpu_custom_call" | custom-call | bytes 1024 | tf_op jit(solution)/shard_map/final_product/pallas_call | solution.py:433
  (64 shorter events, 11.1 us)
Async XLA Ops:
  3.5 7.8 %collective-permute-start = (bf16[16,2048]{1,0:T(8,128)(2,1)}, bf16[16,2048]{1,0:T(8,128)(2,1)S(1)}, u32[]{:S(2)}, u32[]{:S(2)}) collective-permute-start(bf16[16,2048]{1,0:T(8,128)(2,1)} %get-tuple-element.15), channel_id=1, source_target_pairs={{0,1},{1,2},{2,3},{3,0},{4,5},{5,6},{6,7},{7,4},{8,9},{9,10},{10,1... | collective-permute-start | bytes 196616 | tf_op jit(solution)/shard_map/ppermute | solution.py:32
  6.6 7.3 %collective-permute-start.1 = (bf16[16,2048]{1,0:T(8,128)(2,1)}, bf16[16,2048]{1,0:T(8,128)(2,1)S(1)}, u32[]{:S(2)}, u32[]{:S(2)}) collective-permute-start(bf16[16,2048]{1,0:T(8,128)(2,1)} %get-tuple-element.16), channel_id=1, source_target_pairs={{0,2},{1,3},{2,0},{3,1},{4,6},{5,7},{6,4},{7,5},{8,10},{9,11},{10,... | collective-permute-start | bytes 196616 | tf_op jit(solution)/shard_map/ppermute | solution.py:32
  9.2 4.9 %collective-permute-start.2 = (bf16[16,2048]{1,0:T(8,128)(2,1)}, bf16[16,2048]{1,0:T(8,128)(2,1)S(1)}, u32[]{:S(2)}, u32[]{:S(2)}) collective-permute-start(bf16[16,2048]{1,0:T(8,128)(2,1)} %get-tuple-element.17), channel_id=1, source_target_pairs={{0,3},{1,0},{2,1},{3,2},{4,7},{5,4},{6,5},{7,6},{8,11},{9,8},{10,9... | collective-permute-start | bytes 196616 | tf_op jit(solution)/shard_map/ppermute | solution.py:32
  15.7 15.8 %collective-permute-start.3 = (bf16[128,2176]{1,0:T(8,128)(2,1)}, bf16[128,2176]{1,0:T(8,128)(2,1)S(1)}, u32[]{:S(2)}, u32[]{:S(2)}) collective-permute-start(bf16[128,2176]{1,0:T(8,128)(2,1)} %ordered.1.refs_0_.refs_4_), channel_id=1, source_target_pairs={{0,1},{1,2},{2,3},{4,5},{5,6},{6,7},{8,9},{9,10},{10,11},{12,13},{... | collective-permute-start | bytes 1671176 | tf_op jit(solution)/shard_map/ppermute | solution.py:36
  19.2 16.3 %collective-permute-start.4 = (bf16[128,2176]{1,0:T(8,128)(2,1)}, bf16[128,2176]{1,0:T(8,128)(2,1)S(1)}, u32[]{:S(2)}, u32[]{:S(2)}) collective-permute-start(bf16[128,2176]{1,0:T(8,128)(2,1)} %ordered.1.refs_0_.refs_4_), channel_id=1, source_target_pairs={{1,0},{2,1},{3,2},{5,4},{6,5},{7,6},{9,8},{10,9},{11,10},{13,12},{... | collective-permute-start | bytes 1671176 | tf_op jit(solution)/shard_map/ppermute | solution.py:36
  20.5 16.3 %collective-permute-start.10 = (bf16[64,2048]{1,0:T(8,128)(2,1)}, bf16[64,2048]{1,0:T(8,128)(2,1)S(1)}, u32[]{:S(2)}, u32[]{:S(2)}) collective-permute-start(bf16[64,2048]{1,0:T(8,128)(2,1)} %copy-done.1), channel_id=1, source_target_pairs={{0,16},{4,20},{8,24},{12,28},{16,0},{20,4},{24,8},{28,12},{1,17},{... | collective-permute-start | bytes 786440 | tf_op jit(solution)/shard_map/ppermute | solution.py:40
  22.1 14.7 %collective-permute-start.11 = (bf16[64,2048]{1,0:T(8,128)(2,1)}, bf16[64,2048]{1,0:T(8,128)(2,1)S(1)}, u32[]{:S(2)}, u32[]{:S(2)}) collective-permute-start(bf16[64,2048]{1,0:T(8,128)(2,1)} %copy-done.1), channel_id=1, source_target_pairs={{0,24},{4,28},{8,16},{12,20},{16,8},{20,12},{24,0},{28,4},{1,25},{... | collective-permute-start | bytes 786440 | tf_op jit(solution)/shard_map/ppermute | solution.py:40
  23.5 13.3 %collective-permute-start.9 = (bf16[64,2048]{1,0:T(8,128)(2,1)}, bf16[64,2048]{1,0:T(8,128)(2,1)S(1)}, u32[]{:S(2)}, u32[]{:S(2)}) collective-permute-start(bf16[64,2048]{1,0:T(8,128)(2,1)} %copy-done.1), channel_id=1, source_target_pairs={{0,8},{4,12},{8,0},{12,4},{16,24},{20,28},{24,16},{28,20},{1,9},{5... | collective-permute-start | bytes 786440 | tf_op jit(solution)/shard_map/ppermute | solution.py:40
  31.5 9.1 %copy-start.5 = (bf16[128,2176]{1,0:T(8,128)(2,1)}, bf16[128,2176]{1,0:T(8,128)(2,1)S(1)}, u32[]{:S(2)}) copy-start(bf16[128,2176]{1,0:T(8,128)(2,1)S(1)} %collective-permute-done.3.refs_1_.refs_5_) | copy-start | bytes 1671172
  31.5 12.7 %collective-permute-start.5 = (bf16[128,2176]{1,0:T(8,128)(2,1)S(1)}, bf16[128,2176]{1,0:T(8,128)(2,1)S(1)}, u32[]{:S(2)}, u32[]{:S(2)}) collective-permute-start(bf16[128,2176]{1,0:T(8,128)(2,1)S(1)} %collective-permute-done.3.refs_1_.refs_5_), channel_id=1, source_target_pairs={{1,2},{2,3},{5,6},{6,7},{9,10},{10,11},{13,14},{14,15},{17,18},{18... | collective-permute-start | bytes 1671176 | tf_op jit(solution)/shard_map/ppermute | solution.py:36
  35.5 5.0 %copy-start.8 = (bf16[128,2176]{1,0:T(8,128)(2,1)}, bf16[128,2176]{1,0:T(8,128)(2,1)S(1)}, u32[]{:S(2)}) copy-start(bf16[128,2176]{1,0:T(8,128)(2,1)S(1)} %collective-permute-done.4.refs_2_) | copy-start | bytes 1671172
  35.5 15.2 %collective-permute-start.6 = (bf16[128,2176]{1,0:T(8,128)(2,1)S(1)}, bf16[128,2176]{1,0:T(8,128)(2,1)S(1)}, u32[]{:S(2)}, u32[]{:S(2)}) collective-permute-start(bf16[128,2176]{1,0:T(8,128)(2,1)S(1)} %collective-permute-done.4.refs_2_), channel_id=1, source_target_pairs={{1,0},{2,1},{5,4},{6,5},{9,8},{10,9},{13,12},{14,13},{17,16},{18,1... | collective-permute-start | bytes 1671176 | tf_op jit(solution)/shard_map/ppermute | solution.py:36
  40.6 14.3 %collective-permute-start.12 = (bf16[256,2048]{1,0:T(8,128)(2,1)}, bf16[256,2048]{1,0:T(8,128)(2,1)}, u32[]{:S(2)}, u32[]{:S(2)}) collective-permute-start(bf16[256,2048]{1,0:T(8,128)(2,1)} %stack_rows.4.near_ref), channel_id=1, source_target_pairs={{0,4},{4,0},{8,12},{12,8},{16,20},{20,16},{24,28},{28,24},{1,5},{5... | collective-permute-start | bytes 3145736 | tf_op jit(solution)/shard_map/ppermute | solution.py:40
  40.6 20.4 %all-to-all-start = ((bf16[8,144,512]{2,1,0:T(8,128)(2,1)}), bf16[8,144,512]{2,1,0:T(8,128)(2,1)S(1)}, u32[]{:S(2)}, u32[]{:S(2)}) async-start(bf16[8,144,512]{2,1,0:T(8,128)(2,1)} %get-tuple-element.19), calls=%async_computation | async-start | bytes 2359296 | tf_op jit(solution)/shard_map/all_to_all | solution.py:461
  44.2 13.9 %copy-start.6 = (bf16[128,2176]{1,0:T(8,128)(2,1)}, bf16[128,2176]{1,0:T(8,128)(2,1)S(1)}, u32[]{:S(2)}) copy-start(bf16[128,2176]{1,0:T(8,128)(2,1)S(1)} %collective-permute-done.5.left_ref.refs_3_.refs_6_) | copy-start | bytes 1671172
  44.2 16.8 %collective-permute-start.7 = (bf16[128,2176]{1,0:T(8,128)(2,1)S(1)}, bf16[128,2176]{1,0:T(8,128)(2,1)S(1)}, u32[]{:S(2)}, u32[]{:S(2)}) collective-permute-start(bf16[128,2176]{1,0:T(8,128)(2,1)S(1)} %collective-permute-done.5.left_ref.refs_3_.refs_6_), channel_id=1, source_target_pairs={{2,3},{6,7},{10,11},{14,15},{18,19},{22,23},{26,27},{30,31}} | collective-permute-start | bytes 1671176 | tf_op jit(solution)/shard_map/ppermute | solution.py:36
  50.7 7.4 %copy-start.9 = (bf16[128,2176]{1,0:T(8,128)(2,1)}, bf16[128,2176]{1,0:T(8,128)(2,1)S(1)}, u32[]{:S(2)}) copy-start(bf16[128,2176]{1,0:T(8,128)(2,1)S(1)} %collective-permute-done.6.right_ref.refs_4_) | copy-start | bytes 1671172
  50.7 14.3 %collective-permute-start.8 = (bf16[128,2176]{1,0:T(8,128)(2,1)S(1)}, bf16[128,2176]{1,0:T(8,128)(2,1)S(1)}, u32[]{:S(2)}, u32[]{:S(2)}) collective-permute-start(bf16[128,2176]{1,0:T(8,128)(2,1)S(1)} %collective-permute-done.6.right_ref.refs_4_), channel_id=1, source_target_pairs={{1,0},{5,4},{9,8},{13,12},{17,16},{21,20},{25,24},{29,28}} | collective-permute-start | bytes 1671176 | tf_op jit(solution)/shard_map/ppermute | solution.py:36
  61.0 4.1 %copy-start.4 = (bf16[8,144,512]{2,1,0:T(8,128)(2,1)}, bf16[8,144,512]{2,1,0:T(8,128)(2,1)S(1)}, u32[]{:S(2)}) copy-start(bf16[8,144,512]{2,1,0:T(8,128)(2,1)S(1)} %all-to-all-done.refs_1_.refs_0_) | copy-start | bytes 3538948
  61.0 4.1 %copy-start.7 = (bf16[128,2176]{1,0:T(8,128)(2,1)}, bf16[128,2176]{1,0:T(8,128)(2,1)S(1)}, u32[]{:S(2)}) copy-start(bf16[128,2176]{1,0:T(8,128)(2,1)S(1)} %collective-permute-done.7.last_ref.refs_5_.refs_7_) | copy-start | bytes 1671172
  69.0 3.8 %copy-start.19 = (f32[128,128]{1,0:T(8,128)S(1)}, f32[128,128]{1,0:T(8,128)}, u32[]{:S(2)}) copy-start(f32[128,128]{1,0:T(8,128)} %get-tuple-element.20) | copy-start | bytes 196612
  69.0 3.9 %copy-start.18 = (f32[128,128]{1,0:T(8,128)S(1)}, f32[128,128]{1,0:T(8,128)}, u32[]{:S(2)}) copy-start(f32[128,128]{1,0:T(8,128)} %get-tuple-element.21) | copy-start | bytes 196612
  69.0 4.0 %copy-start.17 = (f32[128,128]{1,0:T(8,128)S(1)}, f32[128,128]{1,0:T(8,128)}, u32[]{:S(2)}) copy-start(f32[128,128]{1,0:T(8,128)} %get-tuple-element.22) | copy-start | bytes 196612
  69.0 38.8 %all-to-all-start.1 = ((bf16[8,128,1024]{2,1,0:T(8,128)(2,1)}), bf16[8,128,1024]{2,1,0:T(8,128)(2,1)S(1)}, u32[]{:S(2)}, u32[]{:S(2)}) async-start(bf16[8,128,1024]{2,1,0:T(8,128)(2,1)} %place_last.1.refs_9_), calls=%async_computation.1 | async-start | bytes 4194304 | tf_op jit(solution)/shard_map/all_to_all | solution.py:480
  72.8 7.9 %collective-permute-start.13 = (f32[128,128]{1,0:T(8,128)S(1)}, f32[128,128]{1,0:T(8,128)S(1)}, u32[]{:S(2)}, u32[]{:S(2)}) collective-permute-start(f32[128,128]{1,0:T(8,128)S(1)} %copy-done.19), channel_id=1, source_target_pairs={{0,3},{1,0},{2,1},{3,2},{4,7},{5,4},{6,5},{7,6},{8,11},{9,8},{10,9... | collective-permute-start | bytes 196616 | tf_op jit(solution)/shard_map/ppermute | solution.py:32
  72.9 8.2 %collective-permute-start.14 = (f32[128,128]{1,0:T(8,128)S(1)}, f32[128,128]{1,0:T(8,128)S(1)}, u32[]{:S(2)}, u32[]{:S(2)}) collective-permute-start(f32[128,128]{1,0:T(8,128)S(1)} %copy-done.18), channel_id=1, source_target_pairs={{0,2},{1,3},{2,0},{3,1},{4,6},{5,7},{6,4},{7,5},{8,10},{9,11},{10,... | collective-permute-start | bytes 196616 | tf_op jit(solution)/shard_map/ppermute | solution.py:32
  73.1 8.0 %collective-permute-start.15 = (f32[128,128]{1,0:T(8,128)S(1)}, f32[128,128]{1,0:T(8,128)S(1)}, u32[]{:S(2)}, u32[]{:S(2)}) collective-permute-start(f32[128,128]{1,0:T(8,128)S(1)} %copy-done.17), channel_id=1, source_target_pairs={{0,1},{1,2},{2,3},{3,0},{4,5},{5,6},{6,7},{7,4},{8,9},{9,10},{10,1... | collective-permute-start | bytes 196616 | tf_op jit(solution)/shard_map/ppermute | solution.py:32
  84.1 1.5 %collective-permute-start.16 = (bf16[128,384]{1,0:T(8,128)(2,1)}, bf16[128,384]{1,0:T(8,128)(2,1)S(1)}, u32[]{:S(2)}, u32[]{:S(2)}) collective-permute-start(bf16[128,384]{1,0:T(8,128)(2,1)} %gradients.1.refs_0_), channel_id=1, source_target_pairs={{0,4},{4,0},{8,12},{12,8},{16,20},{20,16},{24,28},{28,24},{1,5},{5... | collective-permute-start | bytes 294920 | tf_op jit(solution)/shard_map/ppermute | solution.py:40
  86.5 16.7 %collective-permute-start.17 = (bf16[256,384]{1,0:T(8,128)(2,1)S(1)}, bf16[256,384]{1,0:T(8,128)(2,1)S(1)}, u32[]{:S(2)}, u32[]{:S(2)}) collective-permute-start(bf16[256,384]{1,0:T(8,128)(2,1)S(1)} %stack_rows.5.refs_0_), channel_id=1, source_target_pairs={{0,8},{4,12},{8,0},{12,4},{16,24},{20,28},{24,16},{28,20},{1,9},{5... | collective-permute-start | bytes 589832 | tf_op jit(solution)/shard_map/ppermute | solution.py:40
  88.3 14.9 %collective-permute-start.18 = (bf16[256,384]{1,0:T(8,128)(2,1)S(1)}, bf16[256,384]{1,0:T(8,128)(2,1)S(1)}, u32[]{:S(2)}, u32[]{:S(2)}) collective-permute-start(bf16[256,384]{1,0:T(8,128)(2,1)S(1)} %stack_rows.5.refs_0_), channel_id=1, source_target_pairs={{0,16},{4,20},{8,24},{12,28},{16,0},{20,4},{24,8},{28,12},{1,17},{... | collective-permute-start | bytes 589832 | tf_op jit(solution)/shard_map/ppermute | solution.py:40
  89.8 18.0 %collective-permute-start.19 = (bf16[256,384]{1,0:T(8,128)(2,1)S(1)}, bf16[256,384]{1,0:T(8,128)(2,1)S(1)}, u32[]{:S(2)}, u32[]{:S(2)}) collective-permute-start(bf16[256,384]{1,0:T(8,128)(2,1)S(1)} %stack_rows.5.refs_0_), channel_id=1, source_target_pairs={{0,24},{4,28},{8,16},{12,20},{16,8},{20,12},{24,0},{28,4},{1,25},{... | collective-permute-start | bytes 589832 | tf_op jit(solution)/shard_map/ppermute | solution.py:40
  107.9 1.2 %copy-start = (bf16[8,128,512]{2,1,0:T(8,128)(2,1)S(1)}, bf16[8,128,512]{2,1,0:T(8,128)(2,1)}, u32[]{:S(2)}) copy-start(bf16[8,128,512]{2,1,0:T(8,128)(2,1)} %hand_over.1.handed_ref) | copy-start | bytes 3145732
  (10 other events, 7.3 us)

commit v9 on v8

--- a/solution.py
+++ b/solution.py
@@ -269,7 +269,7 @@
         out_shape=struct(payload.shape),
         input_output_aliases={0: 0} if aligned else {},
         scratch_shapes=[pltpu.SemaphoreType.DMA((per,))],
-        compiler_params=params(60),
+        compiler_params=params(12 if aligned else 60),
         cost_estimate=cost(0, 1024),
         name="place_last",
     )(payload, from_left, from_right, *ends, *after)

time: 112 us -> 111 us (level)
    unnamed x40 -> x38, local copies, waits for them, and re-layouts: 7.2 us -> 7.26 us
where the time goes in v9:
time: 111 us
  waiting for transfers between devices  41 us (37%)
  starting transfers between devices  32.3 us (29%)
  Pallas kernels  29.1 us (26%)
  local copies, waits for them, and re-layouts  7.26 us (7%)
    ppermute x6, waiting for transfers between devices, hop(): return lax.ppermute(x, 'tensor', pairs)  20.8 us
    ppermute x8, waiting for transfers between devices, swap(): return lax.ppermute(x, 'dp', [(i, i ^ mask) for i in range(count)])  13.5 us
    ppermute x6, starting transfers between devices, shift(): lax.ppermute(x, 'tensor', [(i, (i + by) % count) for i in range(count)])  9.12 us
    ppermute x6, starting transfers between devices, hop(): return lax.ppermute(x, 'tensor', pairs)  8.75 us
    unnamed x38, local copies, waits for them, and re-layouts  7.26 us
    ppermute x8, starting transfers between devices, swap(): return lax.ppermute(x, 'dp', [(i, i ^ mask) for i in range(count)])  7.11 us
    pallas_call x1, Pallas kernels, hand_over(): pl.pallas_call(kernel, in_specs=[VMEM] * (1 + len(digits)), out_specs=VME...  5.83 us
    pallas_call x1, Pallas kernels, gate_and_up(): pl.pallas_call(kernel, in_specs=[VMEM] * n_s + [pl.BlockSpec(memory_space...  5.73 us
  transfers between devices with their start and end apart: 22, of which 12 were waited for; matrix products, arithmetic and copies ran while one was open for 0% of the time, Pallas kernels for 20%

profile of v9, /device:TPU:0, one launch (start us, length us, event | category | flops | bytes accessed | tf_op | source)
XLA Modules:
  0.0 110.6 jit_solution(15457482835831971395)
XLA Ops:
  0.6 2.9 %prepare.1 = (bf16[128,2176]{1,0:T(8,128)(2,1)}, bf16[16,2048]{1,0:T(8,128)(2,1)}, bf16[16,2048]{1,0:T(8,128)(2,1)}, bf16[16,2048]{1,0:T(8,128)(2,1)}, bf16[16,2...) custom-call(s32[1,128]{1,0:T(1,128)} %bitcast.1, bf16[128,4096]{1,0:T(8,128)(2,1)} %t_ref.1, bf16[128,2048]{1,0:T(8,128)(2,1)} %x_ref.1, ...), custom_call_target="tpu_custom_call" | custom-call | bytes 1024 | tf_op jit(solution)/shard_map/prepare/pallas_call | solution.py:111
  3.5 3.1 %collective-permute-start = (bf16[16,2048]{1,0:T(8,128)(2,1)}, bf16[16,2048]{1,0:T(8,128)(2,1)S(1)}, u32[]{:S(2)}, u32[]{:S(2)}) collective-permute-start(bf16[16,2048]{1,0:T(8,128)(2,1)} %get-tuple-element.15), channel_id=1, source_target_pairs={{0,1},{1,2},{2,3},{3,0},{4,5},{5,6},{6,7},{7,4},{8,9},{9,10},{10,1... | collective-permute-start | bytes 196616 | tf_op jit(solution)/shard_map/ppermute | solution.py:32
  6.6 2.6 %collective-permute-start.1 = (bf16[16,2048]{1,0:T(8,128)(2,1)}, bf16[16,2048]{1,0:T(8,128)(2,1)S(1)}, u32[]{:S(2)}, u32[]{:S(2)}) collective-permute-start(bf16[16,2048]{1,0:T(8,128)(2,1)} %get-tuple-element.16), channel_id=1, source_target_pairs={{0,2},{1,3},{2,0},{3,1},{4,6},{5,7},{6,4},{7,5},{8,10},{9,11},{10,... | collective-permute-start | bytes 196616 | tf_op jit(solution)/shard_map/ppermute | solution.py:32
  9.2 1.3 %collective-permute-start.2 = (bf16[16,2048]{1,0:T(8,128)(2,1)}, bf16[16,2048]{1,0:T(8,128)(2,1)S(1)}, u32[]{:S(2)}, u32[]{:S(2)}) collective-permute-start(bf16[16,2048]{1,0:T(8,128)(2,1)} %get-tuple-element.17), channel_id=1, source_target_pairs={{0,3},{1,0},{2,1},{3,2},{4,7},{5,4},{6,5},{7,6},{8,11},{9,8},{10,9... | collective-permute-start | bytes 196616 | tf_op jit(solution)/shard_map/ppermute | solution.py:32
  11.4 2.5 %collective-permute-done.1.refs_2_ = bf16[16,2048]{1,0:T(8,128)(2,1)S(1)} collective-permute-done((bf16[16,2048]{1,0:T(8,128)(2,1)}, bf16[16,2048]{1,0:T(8,128)(2,1)S(1)}, u32[]{:S(2)}, u32[]{:S(2)}) %collective-permute-start.1) | collective-permute-done | bytes 65568 | tf_op jit(solution)/shard_map/ppermute | solution.py:32
  15.7 3.5 %collective-permute-start.3 = (bf16[128,2176]{1,0:T(8,128)(2,1)}, bf16[128,2176]{1,0:T(8,128)(2,1)S(1)}, u32[]{:S(2)}, u32[]{:S(2)}) collective-permute-start(bf16[128,2176]{1,0:T(8,128)(2,1)} %ordered.1.refs_0_.refs_4_), channel_id=1, source_target_pairs={{0,1},{1,2},{2,3},{4,5},{5,6},{6,7},{8,9},{9,10},{10,11},{12,13},{... | collective-permute-start | bytes 1671176 | tf_op jit(solution)/shard_map/ppermute | solution.py:36
  19.2 1.3 %collective-permute-start.4 = (bf16[128,2176]{1,0:T(8,128)(2,1)}, bf16[128,2176]{1,0:T(8,128)(2,1)S(1)}, u32[]{:S(2)}, u32[]{:S(2)}) collective-permute-start(bf16[128,2176]{1,0:T(8,128)(2,1)} %ordered.1.refs_0_.refs_4_), channel_id=1, source_target_pairs={{1,0},{2,1},{3,2},{5,4},{6,5},{7,6},{9,8},{10,9},{11,10},{13,12},{... | collective-permute-start | bytes 1671176 | tf_op jit(solution)/shard_map/ppermute | solution.py:36
  20.5 1.6 %collective-permute-start.10 = (bf16[64,2048]{1,0:T(8,128)(2,1)}, bf16[64,2048]{1,0:T(8,128)(2,1)S(1)}, u32[]{:S(2)}, u32[]{:S(2)}) collective-permute-start(bf16[64,2048]{1,0:T(8,128)(2,1)} %copy-done.4), channel_id=1, source_target_pairs={{0,16},{4,20},{8,24},{12,28},{16,0},{20,4},{24,8},{28,12},{1,17},{... | collective-permute-start | bytes 786440 | tf_op jit(solution)/shard_map/ppermute | solution.py:40
  22.1 1.4 %collective-permute-start.11 = (bf16[64,2048]{1,0:T(8,128)(2,1)}, bf16[64,2048]{1,0:T(8,128)(2,1)S(1)}, u32[]{:S(2)}, u32[]{:S(2)}) collective-permute-start(bf16[64,2048]{1,0:T(8,128)(2,1)} %copy-done.4), channel_id=1, source_target_pairs={{0,24},{4,28},{8,16},{12,20},{16,8},{20,12},{24,0},{28,4},{1,25},{... | collective-permute-start | bytes 786440 | tf_op jit(solution)/shard_map/ppermute | solution.py:40
  24.1 7.4 %collective-permute-done.3.refs_1_.refs_5_ = bf16[128,2176]{1,0:T(8,128)(2,1)S(1)} collective-permute-done((bf16[128,2176]{1,0:T(8,128)(2,1)}, bf16[128,2176]{1,0:T(8,128)(2,1)S(1)}, u32[]{:S(2)}, u32[]{:S(2)}) %collective-permute-start.3) | collective-permute-done | bytes 557088 | tf_op jit(solution)/shard_map/ppermute | solution.py:36
  32.2 3.3 %collective-permute-done.4.refs_2_ = bf16[128,2176]{1,0:T(8,128)(2,1)S(1)} collective-permute-done((bf16[128,2176]{1,0:T(8,128)(2,1)}, bf16[128,2176]{1,0:T(8,128)(2,1)S(1)}, u32[]{:S(2)}, u32[]{:S(2)}) %collective-permute-start.4) | collective-permute-done | bytes 557088 | tf_op jit(solution)/shard_map/ppermute | solution.py:36
  35.5 1.3 %collective-permute-start.6 = (bf16[128,2176]{1,0:T(8,128)(2,1)S(1)}, bf16[128,2176]{1,0:T(8,128)(2,1)S(1)}, u32[]{:S(2)}, u32[]{:S(2)}) collective-permute-start(bf16[128,2176]{1,0:T(8,128)(2,1)S(1)} %collective-permute-done.4.refs_2_), channel_id=1, source_target_pairs={{1,0},{2,1},{5,4},{6,5},{9,8},{10,9},{13,12},{14,13},{17,16},{18,1... | collective-permute-start | bytes 1671176 | tf_op jit(solution)/shard_map/ppermute | solution.py:36
  38.4 2.2 %stack_rows.4.near_ref = bf16[256,2048]{1,0:T(8,128)(2,1)} custom-call(bf16[64,2048]{1,0:T(8,128)(2,1)} %copy-done.4, bf16[64,2048]{1,0:T(8,128)(2,1)} %copy-done.13, bf16[64,2048]{1,0:T(8,128)(2,1)} %copy-done.11, bf16[64,2048]{1,0:T(8,128)(2,1)} %copy-done.12), custom_call_target="tpu_custom_call" | custom-call | bytes 1024 | tf_op jit(solution)/shard_map/stack_rows/pallas_call | solution.py:135
  40.6 3.6 %all-to-all-start = ((bf16[8,144,512]{2,1,0:T(8,128)(2,1)}), bf16[8,144,512]{2,1,0:T(8,128)(2,1)S(1)}, u32[]{:S(2)}, u32[]{:S(2)}) async-start(bf16[8,144,512]{2,1,0:T(8,128)(2,1)} %get-tuple-element.19), calls=%async_computation | async-start | bytes 2359296 | tf_op jit(solution)/shard_map/all_to_all | solution.py:461
  44.9 5.8 %collective-permute-done.6.right_ref.refs_4_ = bf16[128,2176]{1,0:T(8,128)(2,1)S(1)} collective-permute-done((bf16[128,2176]{1,0:T(8,128)(2,1)S(1)}, bf16[128,2176]{1,0:T(8,128)(2,1)S(1)}, u32[]{:S(2)}, u32[]{:S(2)}) %collective-permute-start.6) | collective-permute-done | bytes 557088 | tf_op jit(solution)/shard_map/ppermute | solution.py:36
  50.7 1.3 %collective-permute-start.8 = (bf16[128,2176]{1,0:T(8,128)(2,1)S(1)}, bf16[128,2176]{1,0:T(8,128)(2,1)}, u32[]{:S(2)}, u32[]{:S(2)}) collective-permute-start(bf16[128,2176]{1,0:T(8,128)(2,1)S(1)} %collective-permute-done.6.right_ref.refs_4_), channel_id=1, source_target_pairs={{1,0},{5,4},{9,8},{13,12},{17,16},{21,20},{25,24},{29,28}} | collective-permute-start | bytes 1671176 | tf_op jit(solution)/shard_map/ppermute | solution.py:36
  52.0 2.9 %place_slices.1.in_ref = bf16[8,128,1024]{2,1,0:T(8,128)(2,1)} custom-call(bf16[128,2176]{1,0:T(8,128)(2,1)} %ordered.1.refs_0_.refs_4_, bf16[128,2176]{1,0:T(8,128)(2,1)} %copy-done.9, bf16[128,2176]{1,0:T(8,128)(2,1)} %copy-done.10), custom_call_target="tpu_custom_call" | custom-call | bytes 1024 | tf_op jit(solution)/shard_map/place_slices/pallas_call | solution.py:214
  54.9 3.2 %partial_products.1 = (f32[128,128]{1,0:T(8,128)}, f32[128,128]{1,0:T(8,128)}, f32[128,128]{1,0:T(8,128)}, f32[128,128]{1,0:T(8,128)}) custom-call(bf16[256,2048]{1,0:T(8,128)(2,1)} %stack_rows.4.near_ref, bf16[256,2048]{1,0:T(8,128)(2,1)} %collective-permute-done.12.far_ref, bf16[128,2048]{1,0:T(8,128)(2,1)} %s_ref.3, bf16[128,2048]{1,0:T(8,128)(2,1)} %p_ref.3), custom_call_target="tpu_custom_call" | custom-call | bytes 1024 | tf_op jit(solution)/shard_map/partial_products/pallas_call | solution.py:179
  58.1 2.9 %all-to-all-done.refs_1_.refs_0_ = bf16[8,144,512]{2,1,0:T(8,128)(2,1)S(1)} async-done(((bf16[8,144,512]{2,1,0:T(8,128)(2,1)}), bf16[8,144,512]{2,1,0:T(8,128)(2,1)S(1)}, u32[]{:S(2)}, u32[]{:S(2)}) %all-to-all-start) | async-done | bytes 1179680 | tf_op jit(solution)/shard_map/all_to_all | solution.py:461
  61.0 4.2 %collective-permute-done.8.first_ref.refs_6_ = bf16[128,2176]{1,0:T(8,128)(2,1)} collective-permute-done((bf16[128,2176]{1,0:T(8,128)(2,1)S(1)}, bf16[128,2176]{1,0:T(8,128)(2,1)}, u32[]{:S(2)}, u32[]{:S(2)}) %collective-permute-start.8) | collective-permute-done | bytes 557088 | tf_op jit(solution)/shard_map/ppermute | solution.py:36
  66.0 2.7 %place_last.1.refs_9_ = bf16[8,128,1024]{2,1,0:T(8,128)(2,1)} custom-call(bf16[8,128,1024]{2,1,0:T(8,128)(2,1)} %place_slices.1.in_ref, bf16[128,2176]{1,0:T(8,128)(2,1)S(1)} %collective-permute-done.5.left_ref.refs_3_.refs_6_, bf16[128,2176]{1,0:T(8,128)(2,1)S(1)} %collective-permute-done.6.right_ref.refs_4_, ...), custom_call_target="tpu_custom_call", output_to_operand_aliasing={{}: (0, {})} | custom-call | bytes 1024 | tf_op jit(solution)/shard_map/place_last/pallas_call | solution.py:263
  68.7 3.7 %all-to-all-start.1 = ((bf16[8,128,1024]{2,1,0:T(8,128)(2,1)}), bf16[8,128,1024]{2,1,0:T(8,128)(2,1)S(1)}, u32[]{:S(2)}, u32[]{:S(2)}) async-start(bf16[8,128,1024]{2,1,0:T(8,128)(2,1)} %place_last.1.refs_9_), calls=%async_computation.1 | async-start | bytes 4194304 | tf_op jit(solution)/shard_map/all_to_all | solution.py:480
  72.6 2.0 %collective-permute-start.15 = (f32[128,128]{1,0:T(8,128)S(1)}, f32[128,128]{1,0:T(8,128)S(1)}, u32[]{:S(2)}, u32[]{:S(2)}) collective-permute-start(f32[128,128]{1,0:T(8,128)S(1)} %copy-done.17), channel_id=1, source_target_pairs={{0,1},{1,2},{2,3},{3,0},{4,5},{5,6},{6,7},{7,4},{8,9},{9,10},{10,1... | collective-permute-start | bytes 196616 | tf_op jit(solution)/shard_map/ppermute | solution.py:32
  74.6 5.7 %gate_and_up.1.pre_ref = f32[128,256]{1,0:T(8,128)} custom-call(bf16[128,2176]{1,0:T(8,128)(2,1)} %ordered.1.refs_0_.refs_4_, bf16[128,2176]{1,0:T(8,128)(2,1)} %copy-done.9, bf16[128,2176]{1,0:T(8,128)(2,1)} %copy-done.10, bf16[128,2176]{1,0:T(8,128)(2,1)} %copy-done.1, bf16[128,2176]{1,0:T(8,128)(2,1)} %copy-done.5, bf16[128,2176]{1,0:T(8,128)(2,1)} %copy-done.2, ...), custom_call_target="tpu_custom_call" | custom-call | bytes 1024 | tf_op jit(solution)/shard_map/gate_and_up/pallas_call | solution.py:300
  82.0 1.8 %gradients.1.refs_0_ = bf16[128,384]{1,0:T(8,128)(2,1)} custom-call(f32[128,256]{1,0:T(8,128)} %gate_and_up.1.pre_ref, f32[128,128]{1,0:T(8,128)} %get-tuple-element.18.refs_0_, f32[128,128]{1,0:T(8,128)} %copy-done.14, f32[128,128]{1,0:T(8,128)} %copy-done.15, f32[128,128]{1,0:T(8,128)} %copy-done.16, bf16[128,2176]{1,0:T(8,128)(2,1)} %ordered.1.refs_0_.refs_4_, ...), custom_call_target="tpu_custom_call" | custom-call | bytes 1024 | tf_op jit(solution)/shard_map/gradients/pallas_call | solution.py:343
  83.8 1.5 %collective-permute-done.16.refs_1_ = bf16[128,384]{1,0:T(8,128)(2,1)S(1)} collective-permute-done((bf16[128,384]{1,0:T(8,128)(2,1)}, bf16[128,384]{1,0:T(8,128)(2,1)S(1)}, u32[]{:S(2)}, u32[]{:S(2)}) %collective-permute-start.16) | collective-permute-done | bytes 98336 | tf_op jit(solution)/shard_map/ppermute | solution.py:40
  86.2 1.8 %collective-permute-start.17 = (bf16[256,384]{1,0:T(8,128)(2,1)S(1)}, bf16[256,384]{1,0:T(8,128)(2,1)S(1)}, u32[]{:S(2)}, u32[]{:S(2)}) collective-permute-start(bf16[256,384]{1,0:T(8,128)(2,1)S(1)} %stack_rows.5.refs_0_), channel_id=1, source_target_pairs={{0,8},{4,12},{8,0},{12,4},{16,24},{20,28},{24,16},{28,20},{1,9},{5... | collective-permute-start | bytes 589832 | tf_op jit(solution)/shard_map/ppermute | solution.py:40
  88.0 1.5 %collective-permute-start.18 = (bf16[256,384]{1,0:T(8,128)(2,1)S(1)}, bf16[256,384]{1,0:T(8,128)(2,1)S(1)}, u32[]{:S(2)}, u32[]{:S(2)}) collective-permute-start(bf16[256,384]{1,0:T(8,128)(2,1)S(1)} %stack_rows.5.refs_0_), channel_id=1, source_target_pairs={{0,16},{4,20},{8,24},{12,28},{16,0},{20,4},{24,8},{28,12},{1,17},{... | collective-permute-start | bytes 589832 | tf_op jit(solution)/shard_map/ppermute | solution.py:40
  89.7 5.8 %hand_over.1.handed_ref = bf16[8,128,512]{2,1,0:T(8,128)(2,1)} custom-call(bf16[8,144,512]{2,1,0:T(8,128)(2,1)} %copy-done), custom_call_target="tpu_custom_call" | custom-call | bytes 1024 | tf_op jit(solution)/shard_map/hand_over/pallas_call | solution.py:389
  95.6 7.3 %collective-permute-done.17.refs_1_ = bf16[256,384]{1,0:T(8,128)(2,1)S(1)} collective-permute-done((bf16[256,384]{1,0:T(8,128)(2,1)S(1)}, bf16[256,384]{1,0:T(8,128)(2,1)S(1)}, u32[]{:S(2)}, u32[]{:S(2)}) %collective-permute-start.17) | collective-permute-done | bytes 196640 | tf_op jit(solution)/shard_map/ppermute | solution.py:40
  102.9 4.7 %collective-permute-done.19.refs_3_ = bf16[256,384]{1,0:T(8,128)(2,1)S(1)} collective-permute-done((bf16[256,384]{1,0:T(8,128)(2,1)S(1)}, bf16[256,384]{1,0:T(8,128)(2,1)S(1)}, u32[]{:S(2)}, u32[]{:S(2)}) %collective-permute-start.19) | collective-permute-done | bytes 196640 | tf_op jit(solution)/shard_map/ppermute | solution.py:40
  108.7 1.8 %final_product.1 = (f32[128,1,512]{2,1,0:T(1,128)}, f32[128,1024]{1,0:T(8,128)}, f32[128,1024]{1,0:T(8,128)}) custom-call(bf16[8,128,1024]{2,1,0:T(8,128)(2,1)S(1)} %all-to-all-done.1.feats_ref, bf16[8,128,512]{2,1,0:T(8,128)(2,1)S(1)} %copy-done.3, bf16[256,384]{1,0:T(8,128)(2,1)S(1)} %stack_rows.5.refs_0_, ...), custom_call_target="tpu_custom_call" | custom-call | bytes 1024 | tf_op jit(solution)/shard_map/final_product/pallas_call | solution.py:433
  (62 shorter events, 11.0 us)
Async XLA Ops:
  3.5 7.8 %collective-permute-start = (bf16[16,2048]{1,0:T(8,128)(2,1)}, bf16[16,2048]{1,0:T(8,128)(2,1)S(1)}, u32[]{:S(2)}, u32[]{:S(2)}) collective-permute-start(bf16[16,2048]{1,0:T(8,128)(2,1)} %get-tuple-element.15), channel_id=1, source_target_pairs={{0,1},{1,2},{2,3},{3,0},{4,5},{5,6},{6,7},{7,4},{8,9},{9,10},{10,1... | collective-permute-start | bytes 196616 | tf_op jit(solution)/shard_map/ppermute | solution.py:32
  6.6 7.3 %collective-permute-start.1 = (bf16[16,2048]{1,0:T(8,128)(2,1)}, bf16[16,2048]{1,0:T(8,128)(2,1)S(1)}, u32[]{:S(2)}, u32[]{:S(2)}) collective-permute-start(bf16[16,2048]{1,0:T(8,128)(2,1)} %get-tuple-element.16), channel_id=1, source_target_pairs={{0,2},{1,3},{2,0},{3,1},{4,6},{5,7},{6,4},{7,5},{8,10},{9,11},{10,... | collective-permute-start | bytes 196616 | tf_op jit(solution)/shard_map/ppermute | solution.py:32
  9.2 4.9 %collective-permute-start.2 = (bf16[16,2048]{1,0:T(8,128)(2,1)}, bf16[16,2048]{1,0:T(8,128)(2,1)S(1)}, u32[]{:S(2)}, u32[]{:S(2)}) collective-permute-start(bf16[16,2048]{1,0:T(8,128)(2,1)} %get-tuple-element.17), channel_id=1, source_target_pairs={{0,3},{1,0},{2,1},{3,2},{4,7},{5,4},{6,5},{7,6},{8,11},{9,8},{10,9... | collective-permute-start | bytes 196616 | tf_op jit(solution)/shard_map/ppermute | solution.py:32
  15.7 15.8 %collective-permute-start.3 = (bf16[128,2176]{1,0:T(8,128)(2,1)}, bf16[128,2176]{1,0:T(8,128)(2,1)S(1)}, u32[]{:S(2)}, u32[]{:S(2)}) collective-permute-start(bf16[128,2176]{1,0:T(8,128)(2,1)} %ordered.1.refs_0_.refs_4_), channel_id=1, source_target_pairs={{0,1},{1,2},{2,3},{4,5},{5,6},{6,7},{8,9},{9,10},{10,11},{12,13},{... | collective-permute-start | bytes 1671176 | tf_op jit(solution)/shard_map/ppermute | solution.py:36
  19.2 16.3 %collective-permute-start.4 = (bf16[128,2176]{1,0:T(8,128)(2,1)}, bf16[128,2176]{1,0:T(8,128)(2,1)S(1)}, u32[]{:S(2)}, u32[]{:S(2)}) collective-permute-start(bf16[128,2176]{1,0:T(8,128)(2,1)} %ordered.1.refs_0_.refs_4_), channel_id=1, source_target_pairs={{1,0},{2,1},{3,2},{5,4},{6,5},{7,6},{9,8},{10,9},{11,10},{13,12},{... | collective-permute-start | bytes 1671176 | tf_op jit(solution)/shard_map/ppermute | solution.py:36
  20.5 16.3 %collective-permute-start.10 = (bf16[64,2048]{1,0:T(8,128)(2,1)}, bf16[64,2048]{1,0:T(8,128)(2,1)S(1)}, u32[]{:S(2)}, u32[]{:S(2)}) collective-permute-start(bf16[64,2048]{1,0:T(8,128)(2,1)} %copy-done.4), channel_id=1, source_target_pairs={{0,16},{4,20},{8,24},{12,28},{16,0},{20,4},{24,8},{28,12},{1,17},{... | collective-permute-start | bytes 786440 | tf_op jit(solution)/shard_map/ppermute | solution.py:40
  22.1 14.7 %collective-permute-start.11 = (bf16[64,2048]{1,0:T(8,128)(2,1)}, bf16[64,2048]{1,0:T(8,128)(2,1)S(1)}, u32[]{:S(2)}, u32[]{:S(2)}) collective-permute-start(bf16[64,2048]{1,0:T(8,128)(2,1)} %copy-done.4), channel_id=1, source_target_pairs={{0,24},{4,28},{8,16},{12,20},{16,8},{20,12},{24,0},{28,4},{1,25},{... | collective-permute-start | bytes 786440 | tf_op jit(solution)/shard_map/ppermute | solution.py:40
  23.5 13.3 %collective-permute-start.9 = (bf16[64,2048]{1,0:T(8,128)(2,1)}, bf16[64,2048]{1,0:T(8,128)(2,1)S(1)}, u32[]{:S(2)}, u32[]{:S(2)}) collective-permute-start(bf16[64,2048]{1,0:T(8,128)(2,1)} %copy-done.4), channel_id=1, source_target_pairs={{0,8},{4,12},{8,0},{12,4},{16,24},{20,28},{24,16},{28,20},{1,9},{5... | collective-permute-start | bytes 786440 | tf_op jit(solution)/shard_map/ppermute | solution.py:40
  31.5 9.1 %copy-start.9 = (bf16[128,2176]{1,0:T(8,128)(2,1)}, bf16[128,2176]{1,0:T(8,128)(2,1)S(1)}, u32[]{:S(2)}) copy-start(bf16[128,2176]{1,0:T(8,128)(2,1)S(1)} %collective-permute-done.3.refs_1_.refs_5_) | copy-start | bytes 1671172
  31.5 12.7 %collective-permute-start.5 = (bf16[128,2176]{1,0:T(8,128)(2,1)S(1)}, bf16[128,2176]{1,0:T(8,128)(2,1)S(1)}, u32[]{:S(2)}, u32[]{:S(2)}) collective-permute-start(bf16[128,2176]{1,0:T(8,128)(2,1)S(1)} %collective-permute-done.3.refs_1_.refs_5_), channel_id=1, source_target_pairs={{1,2},{2,3},{5,6},{6,7},{9,10},{10,11},{13,14},{14,15},{17,18},{18... | collective-permute-start | bytes 1671176 | tf_op jit(solution)/shard_map/ppermute | solution.py:36
  35.5 5.0 %copy-start.10 = (bf16[128,2176]{1,0:T(8,128)(2,1)}, bf16[128,2176]{1,0:T(8,128)(2,1)S(1)}, u32[]{:S(2)}) copy-start(bf16[128,2176]{1,0:T(8,128)(2,1)S(1)} %collective-permute-done.4.refs_2_) | copy-start | bytes 1671172
  35.5 15.2 %collective-permute-start.6 = (bf16[128,2176]{1,0:T(8,128)(2,1)S(1)}, bf16[128,2176]{1,0:T(8,128)(2,1)S(1)}, u32[]{:S(2)}, u32[]{:S(2)}) collective-permute-start(bf16[128,2176]{1,0:T(8,128)(2,1)S(1)} %collective-permute-done.4.refs_2_), channel_id=1, source_target_pairs={{1,0},{2,1},{5,4},{6,5},{9,8},{10,9},{13,12},{14,13},{17,16},{18,1... | collective-permute-start | bytes 1671176 | tf_op jit(solution)/shard_map/ppermute | solution.py:36
  40.6 14.3 %collective-permute-start.12 = (bf16[256,2048]{1,0:T(8,128)(2,1)}, bf16[256,2048]{1,0:T(8,128)(2,1)}, u32[]{:S(2)}, u32[]{:S(2)}) collective-permute-start(bf16[256,2048]{1,0:T(8,128)(2,1)} %stack_rows.4.near_ref), channel_id=1, source_target_pairs={{0,4},{4,0},{8,12},{12,8},{16,20},{20,16},{24,28},{28,24},{1,5},{5... | collective-permute-start | bytes 3145736 | tf_op jit(solution)/shard_map/ppermute | solution.py:40
  40.6 20.4 %all-to-all-start = ((bf16[8,144,512]{2,1,0:T(8,128)(2,1)}), bf16[8,144,512]{2,1,0:T(8,128)(2,1)S(1)}, u32[]{:S(2)}, u32[]{:S(2)}) async-start(bf16[8,144,512]{2,1,0:T(8,128)(2,1)} %get-tuple-element.19), calls=%async_computation | async-start | bytes 2359296 | tf_op jit(solution)/shard_map/all_to_all | solution.py:461
  44.2 20.9 %copy-start.1 = (bf16[128,2176]{1,0:T(8,128)(2,1)}, bf16[128,2176]{1,0:T(8,128)(2,1)S(1)}, u32[]{:S(2)}) copy-start(bf16[128,2176]{1,0:T(8,128)(2,1)S(1)} %collective-permute-done.5.left_ref.refs_3_.refs_6_) | copy-start | bytes 1671172
  44.2 16.8 %collective-permute-start.7 = (bf16[128,2176]{1,0:T(8,128)(2,1)S(1)}, bf16[128,2176]{1,0:T(8,128)(2,1)S(1)}, u32[]{:S(2)}, u32[]{:S(2)}) collective-permute-start(bf16[128,2176]{1,0:T(8,128)(2,1)S(1)} %collective-permute-done.5.left_ref.refs_3_.refs_6_), channel_id=1, source_target_pairs={{2,3},{6,7},{10,11},{14,15},{18,19},{22,23},{26,27},{30,31}} | collective-permute-start | bytes 1671176 | tf_op jit(solution)/shard_map/ppermute | solution.py:36
  50.7 14.4 %copy-start.5 = (bf16[128,2176]{1,0:T(8,128)(2,1)}, bf16[128,2176]{1,0:T(8,128)(2,1)S(1)}, u32[]{:S(2)}) copy-start(bf16[128,2176]{1,0:T(8,128)(2,1)S(1)} %collective-permute-done.6.right_ref.refs_4_) | copy-start | bytes 1671172
  50.7 14.4 %collective-permute-start.8 = (bf16[128,2176]{1,0:T(8,128)(2,1)S(1)}, bf16[128,2176]{1,0:T(8,128)(2,1)}, u32[]{:S(2)}, u32[]{:S(2)}) collective-permute-start(bf16[128,2176]{1,0:T(8,128)(2,1)S(1)} %collective-permute-done.6.right_ref.refs_4_), channel_id=1, source_target_pairs={{1,0},{5,4},{9,8},{13,12},{17,16},{21,20},{25,24},{29,28}} | collective-permute-start | bytes 1671176 | tf_op jit(solution)/shard_map/ppermute | solution.py:36
  61.0 7.7 %copy-start = (bf16[8,144,512]{2,1,0:T(8,128)(2,1)}, bf16[8,144,512]{2,1,0:T(8,128)(2,1)S(1)}, u32[]{:S(2)}) copy-start(bf16[8,144,512]{2,1,0:T(8,128)(2,1)S(1)} %all-to-all-done.refs_1_.refs_0_) | copy-start | bytes 3538948
  61.0 7.7 %copy-start.2 = (bf16[128,2176]{1,0:T(8,128)(2,1)}, bf16[128,2176]{1,0:T(8,128)(2,1)S(1)}, u32[]{:S(2)}) copy-start(bf16[128,2176]{1,0:T(8,128)(2,1)S(1)} %collective-permute-done.7.last_ref.refs_5_.refs_7_) | copy-start | bytes 1671172
  68.7 3.8 %copy-start.18 = (f32[128,128]{1,0:T(8,128)S(1)}, f32[128,128]{1,0:T(8,128)}, u32[]{:S(2)}) copy-start(f32[128,128]{1,0:T(8,128)} %get-tuple-element.21) | copy-start | bytes 196612
  68.7 3.9 %copy-start.17 = (f32[128,128]{1,0:T(8,128)S(1)}, f32[128,128]{1,0:T(8,128)}, u32[]{:S(2)}) copy-start(f32[128,128]{1,0:T(8,128)} %get-tuple-element.22) | copy-start | bytes 196612
  68.7 38.8 %all-to-all-start.1 = ((bf16[8,128,1024]{2,1,0:T(8,128)(2,1)}), bf16[8,128,1024]{2,1,0:T(8,128)(2,1)S(1)}, u32[]{:S(2)}, u32[]{:S(2)}) async-start(bf16[8,128,1024]{2,1,0:T(8,128)(2,1)} %place_last.1.refs_9_), calls=%async_computation.1 | async-start | bytes 4194304 | tf_op jit(solution)/shard_map/all_to_all | solution.py:480
  72.5 7.9 %collective-permute-start.13 = (f32[128,128]{1,0:T(8,128)}, f32[128,128]{1,0:T(8,128)S(1)}, u32[]{:S(2)}, u32[]{:S(2)}) collective-permute-start(f32[128,128]{1,0:T(8,128)} %get-tuple-element.20), channel_id=1, source_target_pairs={{0,3},{1,0},{2,1},{3,2},{4,7},{5,4},{6,5},{7,6},{8,11},{9,8},{10,9... | collective-permute-start | bytes 196616 | tf_op jit(solution)/shard_map/ppermute | solution.py:32
  72.5 8.2 %collective-permute-start.14 = (f32[128,128]{1,0:T(8,128)S(1)}, f32[128,128]{1,0:T(8,128)S(1)}, u32[]{:S(2)}, u32[]{:S(2)}) collective-permute-start(f32[128,128]{1,0:T(8,128)S(1)} %copy-done.18), channel_id=1, source_target_pairs={{0,2},{1,3},{2,0},{3,1},{4,6},{5,7},{6,4},{7,5},{8,10},{9,11},{10,... | collective-permute-start | bytes 196616 | tf_op jit(solution)/shard_map/ppermute | solution.py:32
  72.6 8.1 %collective-permute-start.15 = (f32[128,128]{1,0:T(8,128)S(1)}, f32[128,128]{1,0:T(8,128)S(1)}, u32[]{:S(2)}, u32[]{:S(2)}) collective-permute-start(f32[128,128]{1,0:T(8,128)S(1)} %copy-done.17), channel_id=1, source_target_pairs={{0,1},{1,2},{2,3},{3,0},{4,5},{5,6},{6,7},{7,4},{8,9},{9,10},{10,1... | collective-permute-start | bytes 196616 | tf_op jit(solution)/shard_map/ppermute | solution.py:32
  83.8 1.5 %collective-permute-start.16 = (bf16[128,384]{1,0:T(8,128)(2,1)}, bf16[128,384]{1,0:T(8,128)(2,1)S(1)}, u32[]{:S(2)}, u32[]{:S(2)}) collective-permute-start(bf16[128,384]{1,0:T(8,128)(2,1)} %gradients.1.refs_0_), channel_id=1, source_target_pairs={{0,4},{4,0},{8,12},{12,8},{16,20},{20,16},{24,28},{28,24},{1,5},{5... | collective-permute-start | bytes 294920 | tf_op jit(solution)/shard_map/ppermute | solution.py:40
  85.3 0.9 copy-start.6
  86.2 16.7 %collective-permute-start.17 = (bf16[256,384]{1,0:T(8,128)(2,1)S(1)}, bf16[256,384]{1,0:T(8,128)(2,1)S(1)}, u32[]{:S(2)}, u32[]{:S(2)}) collective-permute-start(bf16[256,384]{1,0:T(8,128)(2,1)S(1)} %stack_rows.5.refs_0_), channel_id=1, source_target_pairs={{0,8},{4,12},{8,0},{12,4},{16,24},{20,28},{24,16},{28,20},{1,9},{5... | collective-permute-start | bytes 589832 | tf_op jit(solution)/shard_map/ppermute | solution.py:40
  88.0 14.9 %collective-permute-start.18 = (bf16[256,384]{1,0:T(8,128)(2,1)S(1)}, bf16[256,384]{1,0:T(8,128)(2,1)S(1)}, u32[]{:S(2)}, u32[]{:S(2)}) collective-permute-start(bf16[256,384]{1,0:T(8,128)(2,1)S(1)} %stack_rows.5.refs_0_), channel_id=1, source_target_pairs={{0,16},{4,20},{8,24},{12,28},{16,0},{20,4},{24,8},{28,12},{1,17},{... | collective-permute-start | bytes 589832 | tf_op jit(solution)/shard_map/ppermute | solution.py:40
  89.5 18.0 %collective-permute-start.19 = (bf16[256,384]{1,0:T(8,128)(2,1)S(1)}, bf16[256,384]{1,0:T(8,128)(2,1)S(1)}, u32[]{:S(2)}, u32[]{:S(2)}) collective-permute-start(bf16[256,384]{1,0:T(8,128)(2,1)S(1)} %stack_rows.5.refs_0_), channel_id=1, source_target_pairs={{0,24},{4,28},{8,16},{12,20},{16,8},{20,12},{24,0},{28,4},{1,25},{... | collective-permute-start | bytes 589832 | tf_op jit(solution)/shard_map/ppermute | solution.py:40
  107.5 1.2 %copy-start.3 = (bf16[8,128,512]{2,1,0:T(8,128)(2,1)S(1)}, bf16[8,128,512]{2,1,0:T(8,128)(2,1)}, u32[]{:S(2)}) copy-start(bf16[8,128,512]{2,1,0:T(8,128)(2,1)} %hand_over.1.handed_ref) | copy-start | bytes 3145732
  (9 other events, 6.5 us)
